TPU v7x, 32 devices: a whole 2x2x4 slice. The times are simulated.
32 devices in a mesh: ctx: 8 (over z, core), fsdp: 4 (over y, x).
Axes of the slice: x: 2, y: 2, z: 4, core: 2. Of those that a mesh axis runs over, the one named last changes fastest.
Arguments:
- tokens: bfloat16 [4, 3072, 1536], P('fsdp', 'ctx'), may hold values from -6 to 6
- grad_out: bfloat16 [4, 3072, 1536], P('fsdp', 'ctx'), may hold values from -6 to 6
- order: int32 [4, 3072], P('fsdp'), may hold values from 0 to 3071, each once within a row
- lengths: int32 [4, 3], P('fsdp'), may hold values from 1 to 1536, 3072 in all within a row
- routes: int32 [4, 3072, 4], P('fsdp', 'ctx'), may hold values from 0 to 15, all different within a row
- gain_one: bfloat16 [1536], P('fsdp'), may hold values from 0.5 to 1.5
- gain_two: bfloat16 [1536], P('fsdp'), may hold values from 0.5 to 1.5
- w_query: bfloat16 [1536, 1536], P('fsdp'), may hold values from -0.21875 to 0.21875
- w_key: bfloat16 [1536, 256], P('fsdp'), may hold values from -0.21875 to 0.21875
- w_value: bfloat16 [1536, 256], P('fsdp'), may hold values from -0.15625 to 0.15625
- w_out: bfloat16 [1536, 1536], P('fsdp'), may hold values from -3.5 to 3.5
- w_router: bfloat16 [1536, 16], P('fsdp'), may hold values from -0.078125 to 0.078125
- w_gate: bfloat16 [16, 1536, 768], P('ctx', 'fsdp'), may hold values from -0.15625 to 0.15625
- w_up: bfloat16 [16, 1536, 768], P('ctx', 'fsdp'), may hold values from -0.15625 to 0.15625
- w_down: bfloat16 [16, 768, 1536], P('ctx', None, 'fsdp'), may hold values from -0.4375 to 0.4375
Outputs:
- output: bfloat16 [4, 3072, 1536], P('fsdp', 'ctx')
- input_grad: bfloat16 [4, 3072, 1536], P('fsdp', 'ctx')
- grad_gain_one: float32 [1536], P('fsdp')
- grad_gain_two: float32 [1536], P('fsdp')
- grad_query: float32 [1536, 1536], P('fsdp')
- grad_key: float32 [1536, 256], P('fsdp')
- grad_value: float32 [1536, 256], P('fsdp')
- grad_out_proj: float32 [1536, 1536], P('fsdp')
- grad_router: float32 [1536, 16], P('fsdp')
- grad_gate: float32 [16, 1536, 768], P('ctx', 'fsdp')
- grad_up: float32 [16, 1536, 768], P('ctx', 'fsdp')
- grad_down: float32 [16, 768, 1536], P('ctx', None, 'fsdp')
Inputs may be any that keep to these rules, and one draw needn't show every extreme that they name: `order`: each row is a permutation of the numbers below 3072. `lengths`: each row sums to 3072, and its largest entry is 1536. `routes`: each row names 4 different experts.
All inputs are finite; a program needn't handle non-finite values.
Results may differ from a plain program's by a relative error of at most 0.024.
Values may be sent and summed in bfloat16 or wider, within the bound.
A program may use at most 192 MiB of HBM per device.

v0:
```python
import jax
import jax.numpy as jnp
from jax import lax
from jax.sharding import PartitionSpec as P

QUERY_HEADS = 12
KVH = 2
HEAD_SIZE = 128


EPSILON = 1e-06
ROPE_BASE = 10000.0
MASKED = -1e30


def rms_scale(value_rows, gain):
    return (
        value_rows
        * lax.rsqrt(jnp.mean(value_rows * value_rows, axis=-1, keepdims=True) + EPSILON)
        * gain
    )


def rotate(value_rows, position):
    half_dim = value_rows.shape[-1] // 2
    freqs = ROPE_BASE ** (-2.0 * jnp.arange(half_dim).astype(jnp.float32) / value_rows.shape[-1])
    angles = position.astype(jnp.float32)[:, None] * freqs[None, :]
    cosine = jnp.cos(angles)[:, None, :]
    sine = jnp.sin(angles)[:, None, :]
    first = value_rows[..., :half_dim]
    second = value_rows[..., half_dim:]
    return jnp.concatenate(
        [first * cosine - second * sine, second * cosine + first * sine], axis=-1
    )


def token_tables(order_row, length_row):
    ends = jnp.cumsum(length_row)
    starts = ends - length_row
    doc_ids = jnp.sum((order_row[:, None] >= ends[None, :]).astype(jnp.int32), axis=1)
    seq_ids = jnp.arange(length_row.shape[0])
    doc_start = jnp.sum(jnp.where(doc_ids[:, None] == seq_ids[None, :], starts[None, :], 0), axis=1)
    return (doc_ids, order_row - doc_start)


def slot_ranks(orig_dev, route_onehot):
    earlier = (orig_dev[None, :] < orig_dev[:, None]).astype(jnp.bfloat16)
    per_token = jnp.sum(route_onehot, axis=1).astype(jnp.bfloat16)
    counts = jnp.dot(earlier, per_token, preferred_element_type=jnp.float32)
    return jnp.sum(counts[:, None, :] * route_onehot, axis=2).astype(jnp.int32)


def body(
    tokens,
    grad_out,
    order,
    lengths,
    routes,
    gain_one,
    gain_two,
    w_query,
    w_key,
    w_value,
    w_out,
    w_router,
    w_gate,
    w_up,
    w_down,
):
    ctx_count = lax.axis_size("ctx")
    ctx_index = lax.axis_index("ctx")
    tok_rows = tokens.shape[1]
    width = tokens.shape[2]
    group_rows = order.shape[1]
    top_count = routes.shape[2]
    local_experts = w_gate.shape[0]
    expert_count = local_experts * ctx_count
    capacity = 5 * tok_rows * top_count // (4 * expert_count)
    kblock = min(512, group_rows)
    block_count = group_rows // kblock
    per_group = QUERY_HEADS // KVH
    score_scale = HEAD_SIZE ** (-0.5)
    slot_count = expert_count * capacity
    pair_count = tok_rows * top_count
    gain_first, gain_second, query_full, key_full, value_full, out_full, router_full = (
        lax.all_gather(gain_one, "fsdp", axis=0, tiled=True),
        lax.all_gather(gain_two, "fsdp", axis=0, tiled=True),
        lax.all_gather(w_query, "fsdp", axis=0, tiled=True),
        lax.all_gather(w_key, "fsdp", axis=0, tiled=True),
        lax.all_gather(w_value, "fsdp", axis=0, tiled=True),
        lax.all_gather(w_out, "fsdp", axis=0, tiled=True),
        lax.all_gather(w_router, "fsdp", axis=0, tiled=True),
    )
    gate_full, up_full, down_full = (
        lax.all_gather(w_gate, "fsdp", axis=1, tiled=True),
        lax.all_gather(w_up, "fsdp", axis=1, tiled=True),
        lax.all_gather(w_down, "fsdp", axis=2, tiled=True),
    )
    doc_all, pos_all = token_tables(order[0], lengths[0])
    start_row = ctx_index * tok_rows
    orig_mine = lax.dynamic_slice_in_dim(order[0], start_row, tok_rows)
    doc_mine = lax.dynamic_slice_in_dim(doc_all, start_row, tok_rows)
    pos_mine = lax.dynamic_slice_in_dim(pos_all, start_row, tok_rows)
    inputs = tokens[0].astype(jnp.float32)
    gain_a = gain_first.astype(jnp.float32)
    gain_b = gain_second.astype(jnp.float32)
    hidden_one = rms_scale(inputs, gain_a).astype(jnp.bfloat16)
    query_pre = jnp.dot(hidden_one, query_full, preferred_element_type=jnp.float32)
    key_pre = jnp.dot(hidden_one, key_full, preferred_element_type=jnp.float32)
    value_pre = jnp.dot(hidden_one, value_full, preferred_element_type=jnp.float32)
    queries = rotate(query_pre.reshape(tok_rows, QUERY_HEADS, HEAD_SIZE), pos_mine).astype(
        jnp.bfloat16
    )
    keys_mine = (
        rotate(key_pre.reshape(tok_rows, KVH, HEAD_SIZE), pos_mine)
        .astype(jnp.bfloat16)
        .reshape(tok_rows, KVH * HEAD_SIZE)
    )
    values_mine = value_pre.astype(jnp.bfloat16)
    keys_all, values_all = (
        lax.all_gather(keys_mine, "ctx", axis=0, tiled=True),
        lax.all_gather(values_mine, "ctx", axis=0, tiled=True),
    )
    query_head_rows = queries.reshape(tok_rows, KVH, per_group, HEAD_SIZE)
    doc_blocks = doc_all.reshape(block_count, kblock)
    orig_blocks = order[0].reshape(block_count, kblock)

    def block_scores(key_tile, doc_block, orig_block):
        attention_scores = (
            jnp.einsum(
                "mjie,aje->jima", query_head_rows, key_tile, preferred_element_type=jnp.float32
            )
            * score_scale
        )
        allowed = (doc_mine[:, None] == doc_block[None, :]) & (
            orig_block[None, :] <= orig_mine[:, None]
        )
        return jnp.where(allowed[None, None], attention_scores, MASKED)

    key_blocks = keys_all.reshape(block_count, kblock, KVH, HEAD_SIZE)
    value_blocks = values_all.reshape(block_count, kblock, KVH, HEAD_SIZE)

    def stats_step(carry, partial_results):
        running_top, running_total = carry
        attention_scores = block_scores(partial_results[0], partial_results[1], partial_results[2])
        new_top = jnp.maximum(running_top, jnp.max(attention_scores, axis=-1))
        new_total = running_total * jnp.exp(running_top - new_top) + jnp.sum(
            jnp.exp(attention_scores - new_top[..., None]), axis=-1
        )
        return ((new_top, new_total), None)

    start_top = jnp.full((KVH, per_group, tok_rows), MASKED, jnp.float32)
    start_total = jnp.zeros((KVH, per_group, tok_rows), jnp.float32)
    stats, unused = lax.scan(
        stats_step, (start_top, start_total), (key_blocks, doc_blocks, orig_blocks)
    )
    log_total = stats[0] + jnp.log(stats[1])

    def value_step(accum, partial_results):
        attention_scores = block_scores(partial_results[0], partial_results[2], partial_results[3])
        attention_probs = jnp.exp(attention_scores - log_total[..., None]).astype(jnp.bfloat16)
        return (
            accum
            + jnp.einsum(
                "enjk,keo->jeno",
                attention_probs,
                partial_results[1],
                preferred_element_type=jnp.float32,
            ),
            None,
        )

    attended_total, unused = lax.scan(
        value_step,
        jnp.zeros((tok_rows, KVH, per_group, HEAD_SIZE), jnp.float32),
        (key_blocks, value_blocks, doc_blocks, orig_blocks),
    )
    attended = attended_total.reshape(tok_rows, QUERY_HEADS * HEAD_SIZE).astype(jnp.bfloat16)
    middle = inputs + jnp.dot(attended, out_full, preferred_element_type=jnp.float32)
    hidden_two = rms_scale(middle, gain_b).astype(jnp.bfloat16)
    logits = jnp.dot(hidden_two, router_full, preferred_element_type=jnp.float32)
    route_rows = routes[0]
    route_onehot = (route_rows[:, :, None] == jnp.arange(expert_count)[None, None, :]).astype(
        jnp.float32
    )
    chosen = jnp.sum(logits[:, None, :] * route_onehot, axis=2)
    gate_weights = jax.nn.softmax(chosen, axis=-1)
    ranks = slot_ranks(orig_mine, route_onehot)
    owner = route_rows // local_experts
    slot_local = route_rows % local_experts
    send_index = jnp.where(
        ranks < capacity, slot_local * (ctx_count * capacity) + owner * capacity + ranks, slot_count
    )
    pair_ids = jnp.arange(pair_count)
    pair_table = (
        jnp.full((slot_count + 1,), pair_count, jnp.int32)
        .at[send_index.reshape(-1)]
        .set(pair_ids)[:slot_count]
    )
    token_table = jnp.where(pair_table < pair_count, pair_table // top_count, tok_rows)
    hidden_pad = jnp.concatenate([hidden_two, jnp.zeros((1, width), jnp.bfloat16)], axis=0)
    outgoing = hidden_pad[token_table].reshape(local_experts, ctx_count, capacity, width)
    expert_rows = lax.all_to_all(outgoing, "ctx", split_axis=1, concat_axis=1, tiled=True).reshape(
        local_experts, ctx_count * capacity, width
    )
    gate_pre = jnp.einsum(
        "end,edf->enf", expert_rows, gate_full, preferred_element_type=jnp.float32
    )
    up_pre = jnp.einsum("end,edf->enf", expert_rows, up_full, preferred_element_type=jnp.float32)
    sigmoid_gate = jax.nn.sigmoid(gate_pre)
    silu_gate = gate_pre * sigmoid_gate
    inner = (silu_gate * up_pre).astype(jnp.bfloat16)
    expert_out = jnp.einsum(
        "enf,efd->end", inner, down_full, preferred_element_type=jnp.float32
    ).astype(jnp.bfloat16)
    back_rows = lax.all_to_all(
        expert_out.reshape(local_experts, ctx_count, capacity, width),
        "ctx",
        split_axis=1,
        concat_axis=1,
        tiled=True,
    )
    back_pad = jnp.concatenate(
        [back_rows.reshape(slot_count, width), jnp.zeros((1, width), jnp.bfloat16)], axis=0
    )
    picked = back_pad[send_index].astype(jnp.float32)
    result = middle + jnp.sum(gate_weights[:, :, None] * picked, axis=1)
    out_grad = grad_out[0].astype(jnp.float32)
    pair_grad = (gate_weights[:, :, None] * out_grad[:, None, :]).astype(jnp.bfloat16)
    gate_grad = jnp.sum(picked * out_grad[:, None, :], axis=-1)
    pair_pad = jnp.concatenate(
        [pair_grad.reshape(pair_count, width), jnp.zeros((1, width), jnp.bfloat16)], axis=0
    )
    grad_outgoing = pair_pad[pair_table].reshape(local_experts, ctx_count, capacity, width)
    expert_out_grad = lax.all_to_all(
        grad_outgoing, "ctx", split_axis=1, concat_axis=1, tiled=True
    ).reshape(local_experts, ctx_count * capacity, width)
    inner_grad = jnp.einsum(
        "end,efd->enf", expert_out_grad, down_full, preferred_element_type=jnp.float32
    )
    gate_pre_grad = (
        inner_grad * up_pre * sigmoid_gate * (1.0 + gate_pre * (1.0 - sigmoid_gate))
    ).astype(jnp.bfloat16)
    up_pre_grad = (inner_grad * silu_gate).astype(jnp.bfloat16)
    down_local = jnp.einsum(
        "enf,end->efd", inner, expert_out_grad, preferred_element_type=jnp.float32
    )
    gate_local = jnp.einsum(
        "end,enf->edf", expert_rows, gate_pre_grad, preferred_element_type=jnp.float32
    )
    up_local = jnp.einsum(
        "end,enf->edf", expert_rows, up_pre_grad, preferred_element_type=jnp.float32
    )
    row_grad = (
        jnp.einsum("enf,edf->end", gate_pre_grad, gate_full, preferred_element_type=jnp.float32)
        + jnp.einsum("enf,edf->end", up_pre_grad, up_full, preferred_element_type=jnp.float32)
    ).astype(jnp.bfloat16)
    incoming = lax.all_to_all(
        row_grad.reshape(local_experts, ctx_count, capacity, width),
        "ctx",
        split_axis=1,
        concat_axis=1,
        tiled=True,
    )
    incoming_pad = jnp.concatenate(
        [incoming.reshape(slot_count, width), jnp.zeros((1, width), jnp.bfloat16)], axis=0
    )
    expert_part = jnp.sum(incoming_pad[send_index].astype(jnp.float32), axis=1)
    chosen_grad = gate_weights * (
        gate_grad - jnp.sum(gate_weights * gate_grad, axis=-1, keepdims=True)
    )
    logit_grad = jnp.einsum("tk,tke->te", chosen_grad, route_onehot).astype(jnp.bfloat16)
    router_local = jnp.einsum(
        "td,te->de", hidden_two, logit_grad, preferred_element_type=jnp.float32
    )
    hidden_two_grad = expert_part + jnp.einsum(
        "te,de->td", logit_grad, router_full, preferred_element_type=jnp.float32
    )
    unused_two, norm_two_back = jax.vjp(rms_scale, middle, gain_b)
    middle_part, gain_two_local = norm_two_back(hidden_two_grad)
    middle_grad = out_grad + middle_part
    branch_grad = middle_grad.astype(jnp.bfloat16)
    out_local = jnp.einsum("tc,td->cd", attended, branch_grad, preferred_element_type=jnp.float32)
    attended_grad = jnp.einsum(
        "td,cd->tc", branch_grad, out_full, preferred_element_type=jnp.float32
    ).astype(jnp.bfloat16)
    head_gradients = attended_grad.reshape(tok_rows, KVH, per_group, HEAD_SIZE)
    row_correction = jnp.einsum(
        "nwym,nwym->wyn", head_gradients.astype(jnp.float32), attended_total
    )
    keys_back, values_back = (keys_all, values_all)
    back_key_blocks = keys_back.reshape(block_count, kblock, KVH, HEAD_SIZE)
    back_value_blocks = values_back.reshape(block_count, kblock, KVH, HEAD_SIZE)

    def grad_step(query_grad, partial_results):
        key_tile, value_tile, doc_block, orig_block = partial_results
        attention_scores = block_scores(key_tile, doc_block, orig_block)
        attention_probs = jnp.exp(attention_scores - log_total[..., None])
        lower_probs = attention_probs.astype(jnp.bfloat16)
        prob_grad = jnp.einsum(
            "mjie,aje->jima", head_gradients, value_tile, preferred_element_type=jnp.float32
        )
        score_gradient = (attention_probs * (prob_grad - row_correction[..., None])).astype(
            jnp.bfloat16
        )
        query_grad = (
            query_grad
            + jnp.einsum(
                "enjk,keo->jeno", score_gradient, key_tile, preferred_element_type=jnp.float32
            )
            * score_scale
        )
        key_grad = (
            jnp.einsum(
                "vknp,nvki->pvi",
                score_gradient,
                query_head_rows,
                preferred_element_type=jnp.float32,
            )
            * score_scale
        )
        value_grad = jnp.einsum(
            "vknp,nvki->pvi", lower_probs, head_gradients, preferred_element_type=jnp.float32
        )
        return (query_grad, (key_grad, value_grad))

    query_grad, block_grads = lax.scan(
        grad_step,
        jnp.zeros((tok_rows, KVH, per_group, HEAD_SIZE), jnp.float32),
        (back_key_blocks, back_value_blocks, doc_blocks, orig_blocks),
    )
    key_grads = block_grads[0].reshape(group_rows, KVH * HEAD_SIZE)
    value_grads = block_grads[1].reshape(group_rows, KVH * HEAD_SIZE)
    key_grad_mine, value_grad_mine = (
        lax.psum_scatter(
            key_grads.astype(jnp.bfloat16), "ctx", scatter_dimension=0, tiled=True
        ).astype(jnp.float32),
        lax.psum_scatter(
            value_grads.astype(jnp.bfloat16), "ctx", scatter_dimension=0, tiled=True
        ).astype(jnp.float32),
    )
    negative_pos = -pos_mine.astype(jnp.float32)
    query_pre_grad = (
        rotate(query_grad.reshape(tok_rows, QUERY_HEADS, HEAD_SIZE), negative_pos)
        .astype(jnp.bfloat16)
        .reshape(tok_rows, QUERY_HEADS * HEAD_SIZE)
    )
    key_pre_grad = (
        rotate(key_grad_mine.reshape(tok_rows, KVH, HEAD_SIZE), negative_pos)
        .astype(jnp.bfloat16)
        .reshape(tok_rows, KVH * HEAD_SIZE)
    )
    value_pre_grad = value_grad_mine.astype(jnp.bfloat16)
    query_local = jnp.einsum(
        "td,tc->dc", hidden_one, query_pre_grad, preferred_element_type=jnp.float32
    )
    key_local = jnp.einsum(
        "td,tc->dc", hidden_one, key_pre_grad, preferred_element_type=jnp.float32
    )
    value_local = jnp.einsum(
        "td,tc->dc", hidden_one, value_pre_grad, preferred_element_type=jnp.float32
    )
    hidden_one_grad = (
        jnp.einsum("tc,dc->td", query_pre_grad, query_full, preferred_element_type=jnp.float32)
        + jnp.einsum("tc,dc->td", key_pre_grad, key_full, preferred_element_type=jnp.float32)
        + jnp.einsum("tc,dc->td", value_pre_grad, value_full, preferred_element_type=jnp.float32)
    )
    unused_one, norm_one_back = jax.vjp(rms_scale, inputs, gain_a)
    input_part, gain_one_local = norm_one_back(hidden_one_grad)
    input_grad = (middle_grad + input_part).astype(jnp.bfloat16)
    dense_local = (
        gain_one_local,
        gain_two_local,
        query_local,
        key_local,
        value_local,
        out_local,
        router_local,
    )
    shares = (
        lax.psum_scatter(
            dense_local[0].astype(jnp.bfloat16), "fsdp", scatter_dimension=0, tiled=True
        ).astype(jnp.float32),
        lax.psum_scatter(
            dense_local[1].astype(jnp.bfloat16), "fsdp", scatter_dimension=0, tiled=True
        ).astype(jnp.float32),
        lax.psum_scatter(
            dense_local[2].astype(jnp.bfloat16), "fsdp", scatter_dimension=0, tiled=True
        ).astype(jnp.float32),
        lax.psum_scatter(
            dense_local[3].astype(jnp.bfloat16), "fsdp", scatter_dimension=0, tiled=True
        ).astype(jnp.float32),
        lax.psum_scatter(
            dense_local[4].astype(jnp.bfloat16), "fsdp", scatter_dimension=0, tiled=True
        ).astype(jnp.float32),
        lax.psum_scatter(
            dense_local[5].astype(jnp.bfloat16), "fsdp", scatter_dimension=0, tiled=True
        ).astype(jnp.float32),
        lax.psum_scatter(
            dense_local[6].astype(jnp.bfloat16), "fsdp", scatter_dimension=0, tiled=True
        ).astype(jnp.float32),
    )
    dense_grads = (
        lax.psum(shares[0].astype(jnp.bfloat16), "ctx").astype(jnp.float32),
        lax.psum(shares[1].astype(jnp.bfloat16), "ctx").astype(jnp.float32),
        lax.psum(shares[2].astype(jnp.bfloat16), "ctx").astype(jnp.float32),
        lax.psum(shares[3].astype(jnp.bfloat16), "ctx").astype(jnp.float32),
        lax.psum(shares[4].astype(jnp.bfloat16), "ctx").astype(jnp.float32),
        lax.psum(shares[5].astype(jnp.bfloat16), "ctx").astype(jnp.float32),
        lax.psum(shares[6].astype(jnp.bfloat16), "ctx").astype(jnp.float32),
    )
    gate_grad_out, up_grad_out, down_grad_out = (
        lax.psum_scatter(
            gate_local.astype(jnp.bfloat16), "fsdp", scatter_dimension=1, tiled=True
        ).astype(jnp.float32),
        lax.psum_scatter(
            up_local.astype(jnp.bfloat16), "fsdp", scatter_dimension=1, tiled=True
        ).astype(jnp.float32),
        lax.psum_scatter(
            down_local.astype(jnp.bfloat16), "fsdp", scatter_dimension=2, tiled=True
        ).astype(jnp.float32),
    )
    return (
        result.astype(jnp.bfloat16)[None],
        input_grad[None],
        dense_grads[0],
        dense_grads[1],
        dense_grads[2],
        dense_grads[3],
        dense_grads[4],
        dense_grads[5],
        dense_grads[6],
        gate_grad_out,
        up_grad_out,
        down_grad_out,
    )


def solution(mesh):
    placed = (
        P("fsdp", "ctx", None),
        P("fsdp", "ctx", None),
        P("fsdp", None),
        P("fsdp", None),
        P("fsdp", "ctx", None),
        P("fsdp"),
        P("fsdp"),
        P("fsdp", None),
        P("fsdp", None),
        P("fsdp", None),
        P("fsdp", None),
        P("fsdp", None),
        P("ctx", "fsdp", None),
        P("ctx", "fsdp", None),
        P("ctx", None, "fsdp"),
    )
    return jax.shard_map(
        body,
        mesh=mesh,
        in_specs=placed,
        out_specs=(
            P("fsdp", "ctx", None),
            P("fsdp", "ctx", None),
            P("fsdp"),
            P("fsdp"),
            P("fsdp", None),
            P("fsdp", None),
            P("fsdp", None),
            P("fsdp", None),
            P("fsdp", None),
            P("ctx", "fsdp", None),
            P("ctx", "fsdp", None),
            P("ctx", None, "fsdp"),
        ),
        check_vma=False,
    )
```

profile of v0, /device:TPU:0, one launch (start us, length us, event | category | flops | bytes accessed | tf_op | source)
XLA Modules:
  0.0 1656.3 jit_solution(16492565090258460497)
XLA Ops:
  11.7 9.5 all-gather
  21.2 12.1 all_gather.39
  37.2 10.5 all_gather.37
  52.8 7.7 all-gather.1
  61.1 8.3 all_gather.44
  71.1 5.3 mul.505
  76.4 12.0 mul.506
  97.6 50.3 %all-gather.14.cloned.1.call-done = bf16[1536,1536]{1,0:T(8,128)(2,1)} async-done(((bf16[384,1536]{1,0:T(8,128)(2,1)}), bf16[1536,1536]{1,0:T(8,128)(2,1)}) %all-gather.14.cloned.1.call-update) | async-done | bytes 4718608 | tf_op jit(solution)/shard_map/all_gather | solution.py:88
  147.9 6.8 copy.137
  165.1 71.0 %while.39 = (s32[]{:T(128)}, f32[2,6,384]{2,1,0:T(8,128)S(1)}, f32[2,6,384]{2,1,0:T(8,128)S(1)}, s32[384]{0:T(512)S(1)}, s32[6,512]{1,0:T(8,128)}, /*index=5*/s3...) while((s32[]{:T(128)}, f32[2,6,384]{2,1,0:T(8,128)S(1)}, ...), condition=%wide.region_7.8_spmd.clone, body=%wide.region_4.7_spmd.clone.sunk | while | flops 621107712 | bytes 21161088 | solution.py:154
  171.3 5.6 exponential_reduce_fusion.2
  183.1 5.6 exponential_reduce_fusion.2
  195.0 5.6 exponential_reduce_fusion.2
  206.8 5.6 exponential_reduce_fusion.2
  218.7 5.6 exponential_reduce_fusion.2
  230.5 5.6 exponential_reduce_fusion.2
  236.2 49.7 %while.40 = (s32[]{:T(128)}, f32[384,2,6,128]{0,3,2,1:T(8,128)}, bf16[6,512,2,128]{3,2,1,0:T(2,128)(2,1)}, s32[384]{0:T(512)S(1)}, s32[6,512]{1,0:T(8,128)}, /*i...) while((s32[]{:T(128)}, f32[384,2,6,128]{0,3,2,1:T(8,128)}, ...), condition=%wide.region_9.10_spmd.clone, body=%wide.region_8.9_spmd.clone.sunk | while | flops 1219166208 | bytes 7904395 | solution.py:173
  245.3 6.2 bitcast_add_fusion.4
  253.8 6.2 bitcast_add_fusion.4
  262.3 6.2 bitcast_add_fusion.4
  270.8 6.2 bitcast_add_fusion.4
  279.3 6.2 bitcast_add_fusion.4
  289.7 5.3 multiply_reduce_fusion.4
  297.8 6.2 scatter_custom_fusion
  310.9 16.2 gather_fusion.2
  327.1 5.7 copy.152
  338.8 7.7 gather_fusion
  346.6 6.4 copy.146
  353.0 115.1 %all-to-all-done.2 = bf16[2,8,120,1536]{3,2,0,1:T(8,128)(2,1)} async-done(((bf16[2,8,120,1536]{3,2,0,1:T(8,128)(2,1)}), bf16[2,8,120,1536]{3,2,0,1:T(8,128)(2,1)}, u32[]{:S(2)}, u32[]{:S(2)}) %all-to-all-start.2) | async-done | bytes 5898272 | tf_op jit(solution)/shard_map/all_to_all | solution.py:235
  473.6 5.7 copy.153
  479.2 124.1 %all-to-all-done = bf16[2,8,120,1536]{3,2,0,1:T(8,128)(2,1)} async-done(((bf16[2,8,120,1536]{3,2,0,1:T(8,128)(2,1)}), bf16[2,8,120,1536]{3,2,0,1:T(8,128)(2,1)}, u32[]{:S(2)}, u32[]{:S(2)}) %all-to-all-start) | async-done | bytes 5898272 | tf_op jit(solution)/shard_map/all_to_all | solution.py:203
  603.3 5.6 copy.147
  609.0 11.3 fusion.121
  620.3 11.3 fusion.122
  631.6 13.0 multiply_convert_fusion.1
  657.8 9.9 fusion.123
  667.7 11.4 add_convert_fusion
  682.3 106.0 %all-to-all-done.1 = bf16[2,8,120,1536]{3,2,0,1:T(8,128)(2,1)} async-done(((bf16[2,8,120,1536]{3,2,0,1:T(8,128)(2,1)}), bf16[2,8,120,1536]{3,2,0,1:T(8,128)(2,1)}, u32[]{:S(2)}, u32[]{:S(2)}) %all-to-all-start.1) | async-done | bytes 5898272 | tf_op jit(solution)/shard_map/all_to_all | solution.py:216
  799.5 13.8 gather_fusion.1
  813.3 9.7 reshape.878
  823.0 12.9 multiply_reduce_fusion
  836.9 86.7 %all-to-all-done.3 = bf16[2,8,120,1536]{3,2,0,1:T(8,128)(2,1)} async-done(((bf16[2,8,120,1536]{3,2,0,1:T(8,128)(2,1)}), bf16[2,8,120,1536]{3,2,0,1:T(8,128)(2,1)}, u32[]{:S(2)}, u32[]{:S(2)}) %all-to-all-start.3) | async-done | bytes 5898272 | tf_op jit(solution)/shard_map/all_to_all | solution.py:258
  929.6 13.8 gather_fusion.3
  943.4 9.8 reshape.879
  953.2 10.8 reduce_sum.186
  981.9 131.3 %while.41 = (s32[]{:T(128)}, f32[384,2,6,128]{0,3,2,1:T(8,128)S(1)}, bf16[6,512,2,128]{3,1,2,0:T(8,128)(2,1)}, bf16[6,512,2,128]{3,1,2,0:T(8,128)(2,1)}, bf16[6,...) while((s32[]{:T(128)}, ...), condition=%wide.region_23.24_spmd.clone, body=%wide.region_22.23_spmd.clone.sunk | while | flops 3045982208 | bytes 160529872 | solution.py:327
  1122.1 10.2 convolution_convert_fusion.3
  1132.3 12.6 copy.193
  1144.9 5.4 copy.202
  1150.4 9.5 convolution_convert_fusion.5
  1159.9 9.6 convolution_convert_fusion.4
  1187.7 6.9 convolution_convert_fusion
  1203.6 39.5 %reduce-scatter.33.cloned.1.call-done = bf16[384,1536]{1,0:T(8,128)(2,1)} async-done(((bf16[1536,1536]{1,0:T(8,128)(2,1)}), bf16[384,1536]{1,0:T(8,128)(2,1)}) %reduce-scatter.33.cloned.1.call-update) | async-done | bytes 1179664
  1249.5 53.6 %reduce-scatter.27.cloned.1.call-done = bf16[2,384,768]{2,1,0:T(8,128)(2,1)} async-done(((bf16[2,1536,768]{2,1,0:T(8,128)(2,1)}), bf16[2,384,768]{2,1,0:T(8,128)(2,1)}) %reduce-scatter.27.cloned.1.call-update) | async-done | bytes 1179664 | tf_op jit(solution)/shard_map/reduce_scatter | solution.py:413
  1306.0 57.1 %reduce-scatter.29.cloned.1.call-done = bf16[2,384,768]{2,1,0:T(8,128)(2,1)} async-done(((bf16[2,1536,768]{2,1,0:T(8,128)(2,1)}), bf16[2,384,768]{2,1,0:T(8,128)(2,1)}) %reduce-scatter.29.cloned.1.call-update) | async-done | bytes 1179664 | tf_op jit(solution)/shard_map/reduce_scatter | solution.py:416
  1365.9 5.8 fusion.124
  1371.7 19.2 %reduce-scatter.31.cloned.1.call-done = bf16[384,16]{1,0:T(8,128)(2,1)} async-done(((bf16[1536,16]{1,0:T(8,128)(2,1)}), bf16[384,16]{1,0:T(8,128)(2,1)}) %reduce-scatter.31.cloned.1.call-update) | async-done | bytes 12304
  1392.5 27.3 %reduce-scatter.21.cloned.1.call-done = bf16[384,256]{1,0:T(8,128)(2,1)} async-done(((bf16[1536,256]{1,0:T(8,128)(2,1)}), bf16[384,256]{1,0:T(8,128)(2,1)}) %reduce-scatter.21.cloned.1.call-update) | async-done | bytes 196624 | tf_op jit(solution)/shard_map/reduce_scatter | solution.py:390
  1419.8 28.9 %reduce-scatter.23.cloned.1.call-done = bf16[384,256]{1,0:T(8,128)(2,1)} async-done(((bf16[1536,256]{1,0:T(8,128)(2,1)}), bf16[384,256]{1,0:T(8,128)(2,1)}) %reduce-scatter.23.cloned.1.call-update) | async-done | bytes 196624 | tf_op jit(solution)/shard_map/reduce_scatter | solution.py:393
  1448.7 60.0 %reduce-scatter.25.cloned.1.call-done = bf16[384,1536]{1,0:T(8,128)(2,1)} async-done(((bf16[1536,1536]{1,0:T(8,128)(2,1)}), bf16[384,1536]{1,0:T(8,128)(2,1)}) %reduce-scatter.25.cloned.1.call-update) | async-done | bytes 1179664 | tf_op jit(solution)/shard_map/reduce_scatter | solution.py:396
  1508.6 60.0 %reduce-scatter.19.cloned.1.call-done = bf16[384,1536]{1,0:T(8,128)(2,1)} async-done(((bf16[1536,1536]{1,0:T(8,128)(2,1)}), bf16[384,1536]{1,0:T(8,128)(2,1)}) %reduce-scatter.19.cloned.1.call-update) | async-done | bytes 1179664 | tf_op jit(solution)/shard_map/reduce_scatter | solution.py:387
  1572.5 9.7 all-reduce.8
  1584.9 28.2 %all-reduce.6 = (bf16[384]{0:T(512)(128)(2,1)}, bf16[384]{0:T(512)(128)(2,1)}, bf16[384,16]{0,1:T(8,128)(2,1)}) all-reduce(bf16[384]{0:T(512)(128)(2,1)} %dynamic-slice.2, bf16[384]{0:T(512)(128)(2,1)} %dynamic-slice.4, bf16[384,16]{0,1:T(8,128)(2,1)} %copy.192), channel_id=1, replica_groups=mesh['ctx'=8,'fsdp'=4] {'ctx'}, use_global_device_ids=true, to_apply=%region_29.30 | all-reduce | flops 6912 | bytes 27648 | tf_op jit(solution)/shard_map/psum | solution.py:404
  1621.0 22.0 %all-reduce.11.cloned.1.call-done = (bf16[384,1536]{1,0:T(8,128)(2,1)}, bf16[384,256]{1,0:T(8,128)(2,1)}, bf16[384,256]{1,0:T(8,128)(2,1)}, bf16[384,1536]{1,0:T(8,128)(2,1)}) async-done(((bf16[384,1536]{1,0:T(8,128)(2,1)}, bf16[384,256]{1,0:T(8,128)(2,1)}, bf16[384,256]{1,0:T(8,128)(2,1)}, bf16[384,1536]{1,0:T(8,128)(2,1)}), (bf16[384,1536]{1,0:T(8,128)(2,1)}, bf16[384,256]{1,0:T(8,128)(2,1)}, ...) | async-done | bytes 2752528 | tf_op jit(solution)/shard_map/psum | solution.py:406
  (558 shorter events, 367.6 us)
Async XLA Ops:
  7.2 28.2 %copy-start.11 = (bf16[1,384,1536]{2,1,0:T(8,128)(2,1)S(1)}, bf16[1,384,1536]{2,1,0:T(8,128)(2,1)}, u32[]{:S(2)}) copy-start(bf16[1,384,1536]{2,1,0:T(8,128)(2,1)} %param.21) | copy-start | bytes 3538948
  7.2 26.5 %copy-start.58 = (s32[1,3072]{1,0:T(1,128)S(1)}, s32[1,3072]{1,0:T(1,128)}, u32[]{:S(2)}) copy-start(s32[1,3072]{1,0:T(1,128)} %param.23) | copy-start | bytes 36868
  7.2 81.7 %all-gather.12.cloned.1.call-start = ((), (), s32[]{:S(2)}) async-start(), calls=%async_computation.15 | async-start | bytes 1769472 | tf_op jit(solution)/shard_map/all_gather | solution.py:121
  11.0 25.1 %copy-start.72 = (f32[384]{0:T(512)}, f32[384]{0:T(512)S(1)}, u32[]{:S(2)}) copy-start(f32[384]{0:T(512)S(1)} %fusion.111) | copy-start | bytes 4612
  21.2 26.4 %copy-start.55 = (f32[1536]{0:T(1024)}, f32[1536]{0:T(1024)S(1)}, u32[]{:S(2)}) copy-start(f32[1536]{0:T(1024)S(1)} %reshape.884) | copy-start | bytes 18436
  36.1 11.5 copy-start.73
  37.1 57.0 %all-gather.10.cloned.1.call-start = ((), (), s32[]{:S(2)}) async-start(), calls=%async_computation.14 | async-start | bytes 1769472 | tf_op jit(solution)/shard_map/all_gather | solution.py:122
  47.7 13.4 copy-start.79
  47.7 21.7 %copy-start.50 = (s32[1,384,4]{1,2,0:T(4,128)S(1)}, s32[1,384,4]{1,2,0:T(4,128)}, u32[]{:S(2)}) copy-start(s32[1,384,4]{1,2,0:T(4,128)} %param.25) | copy-start | bytes 18436
  47.7 23.1 %copy-start.19 = (bf16[1,384,1536]{2,1,0:T(8,128)(2,1)S(1)}, bf16[1,384,1536]{2,1,0:T(8,128)(2,1)}, u32[]{:S(2)}) copy-start(bf16[1,384,1536]{2,1,0:T(8,128)(2,1)} %param.22) | copy-start | bytes 3538948
  49.0 98.9 %all-gather.14.cloned.1.call-start = ((), (), s32[]{:S(2)}) async-start(), calls=%async_computation.16 | async-start | bytes 5898240 | tf_op jit(solution)/shard_map/all_gather | solution.py:88
  49.7 240.0 %all-gather.16.cloned.1.call-start = ((), (), s32[]{:S(2)}) async-start(), calls=%async_computation.17 | async-start | bytes 5898240 | tf_op jit(solution)/shard_map/all_gather | solution.py:91
  76.4 12.0 copy-start.38
  76.4 12.2 copy-start.78
  147.9 6.8 copy-start.12
  147.9 6.8 copy-start.56
  147.9 6.8 copy-start.74
  285.8 9.2 copy-start.1
  285.8 9.2 copy-start.8
  285.9 9.2 copy-start.39
  285.9 9.2 copy-start.41
  285.9 9.2 copy-start.67
  295.9 42.8 %copy-start.9 = (bf16[384,1536]{1,0:T(8,128)(2,1)}, bf16[384,1536]{1,0:T(8,128)(2,1)S(1)}, u32[]{:S(2)}) copy-start(bf16[384,1536]{1,0:T(8,128)(2,1)S(1)} %multiply_convert_fusion.4) | copy-start | bytes 3538948
  296.5 11.7 copy-start.60
  297.1 11.2 copy-start.64
  297.3 11.0 copy-start.24
  332.8 135.3 %all-to-all-start.2 = ((bf16[2,8,120,1536]{3,2,0,1:T(8,128)(2,1)}), bf16[2,8,120,1536]{3,2,0,1:T(8,128)(2,1)}, u32[]{:S(2)}, u32[]{:S(2)}) async-start(bf16[2,8,120,1536]{3,2,0,1:T(8,128)(2,1)} %copy.152), calls=%async_computation.2 | async-start | bytes 11796480 | tf_op jit(solution)/shard_map/all_to_all | solution.py:235
  337.6 271.4 %all-gather.18.cloned.1.call-start = ((), (), s32[]{:S(2)}) async-start(), calls=%async_computation.18 | async-start | bytes 5898240 | tf_op jit(solution)/shard_map/all_gather | solution.py:95
  338.1 282.1 %all-gather.20.cloned.1.call-start = ((), (), s32[]{:S(2)}) async-start(), calls=%async_computation.19 | async-start | bytes 5898240 | tf_op jit(solution)/shard_map/all_gather | solution.py:96
  468.1 135.2 %all-to-all-start = ((bf16[2,8,120,1536]{3,2,0,1:T(8,128)(2,1)}), bf16[2,8,120,1536]{3,2,0,1:T(8,128)(2,1)}, u32[]{:S(2)}, u32[]{:S(2)}) async-start(bf16[2,8,120,1536]{3,2,0,1:T(8,128)(2,1)} %copy.146), calls=%async_computation | async-start | bytes 11796480 | tf_op jit(solution)/shard_map/all_to_all | solution.py:203
  472.8 158.8 %all-gather.22.cloned.1.call-start = ((), (), s32[]{:S(2)}) async-start(), calls=%async_computation.20 | async-start | bytes 5898240 | tf_op jit(solution)/shard_map/all_gather | solution.py:97
  631.6 13.1 copy-start.81
  644.6 13.2 copy-start.83
  652.7 135.6 %all-to-all-start.1 = ((bf16[2,8,120,1536]{3,2,0,1:T(8,128)(2,1)}), bf16[2,8,120,1536]{3,2,0,1:T(8,128)(2,1)}, u32[]{:S(2)}, u32[]{:S(2)}) async-start(bf16[2,8,120,1536]{3,2,0,1:T(8,128)(2,1)} %copy.148), calls=%async_computation.1 | async-start | bytes 11796480 | tf_op jit(solution)/shard_map/all_to_all | solution.py:216
  788.3 135.2 %all-to-all-start.3 = ((bf16[2,8,120,1536]{3,2,0,1:T(8,128)(2,1)}), bf16[2,8,120,1536]{3,2,0,1:T(8,128)(2,1)}, u32[]{:S(2)}, u32[]{:S(2)}) async-start(bf16[2,8,120,1536]{3,2,0,1:T(8,128)(2,1)} %copy.154), calls=%async_computation.3 | async-start | bytes 11796480 | tf_op jit(solution)/shard_map/all_to_all | solution.py:258
  793.0 383.8 %reduce-scatter.15.cloned.1.call-start = ((), (), s32[]{:S(2)}) async-start(), calls=%async_computation.21 | async-start | bytes 1769472 | tf_op jit(solution)/shard_map/reduce_scatter | solution.py:335
  813.3 9.7 copy-start.25
  823.0 13.0 copy-start.45
  823.0 13.0 copy-start.61
  823.0 13.0 copy-start.65
  953.2 10.8 copy-start.52
  953.2 10.8 copy-start.63
  953.2 14.8 copy-start.20
  964.0 9.0 slice-start
  993.9 6.6 copy-start.4
  1015.7 6.6 copy-start.4
  1037.5 6.6 copy-start.4
  1117.6 67.6 %reduce-scatter.17.cloned.1.call-start = ((), (), s32[]{:S(2)}) async-start(), calls=%async_computation.22 | async-start | bytes 1769472 | tf_op jit(solution)/shard_map/reduce_scatter | solution.py:338
  1122.0 121.0 %reduce-scatter.33.cloned.1.call-start = ((), (), s32[]{:S(2)}) async-start(), calls=%async_computation.30 | async-start | bytes 5898240
  1150.3 152.8 %reduce-scatter.27.cloned.1.call-start = ((), (), s32[]{:S(2)}) async-start(), calls=%async_computation.27 | async-start | bytes 5898240 | tf_op jit(solution)/shard_map/reduce_scatter | solution.py:413
  1159.9 203.2 %reduce-scatter.29.cloned.1.call-start = ((), (), s32[]{:S(2)}) async-start(), calls=%async_computation.28 | async-start | bytes 5898240 | tf_op jit(solution)/shard_map/reduce_scatter | solution.py:416
  1169.5 221.4 %reduce-scatter.31.cloned.1.call-start = ((), (), s32[]{:S(2)}) async-start(), calls=%async_computation.29 | async-start | bytes 491520
  1173.1 8.8 copy-start.57
  1173.1 8.8 copy-start.75
  1174.9 6.9 copy-start.13
  1176.7 243.1 %reduce-scatter.21.cloned.1.call-start = ((), (), s32[]{:S(2)}) async-start(), calls=%async_computation.24 | async-start | bytes 983040 | tf_op jit(solution)/shard_map/reduce_scatter | solution.py:390
  1183.4 265.2 %reduce-scatter.23.cloned.1.call-start = ((), (), s32[]{:S(2)}) async-start(), calls=%async_computation.25 | async-start | bytes 983040 | tf_op jit(solution)/shard_map/reduce_scatter | solution.py:393
  1187.7 320.9 %reduce-scatter.25.cloned.1.call-start = ((), (), s32[]{:S(2)}) async-start(), calls=%async_computation.26 | async-start | bytes 5898240 | tf_op jit(solution)/shard_map/reduce_scatter | solution.py:396
  1194.7 373.9 %reduce-scatter.19.cloned.1.call-start = ((), (), s32[]{:S(2)}) async-start(), calls=%async_computation.23 | async-start | bytes 5898240 | tf_op jit(solution)/shard_map/reduce_scatter | solution.py:387
  1201.7 441.2 %all-reduce.11.cloned.1.call-start = ((), (), s32[]{:S(2)}) async-start(), calls=%async_computation.31 | async-start | bytes 5505024 | tf_op jit(solution)/shard_map/psum | solution.py:406
  1306.0 59.9 %copy-start.30 = (bf16[384,12,128]{0,2,1:T(8,128)(2,1)S(1)}, bf16[384,12,128]{0,2,1:T(8,128)(2,1)}, u32[]{:S(2)}) copy-start(bf16[384,12,128]{0,2,1:T(8,128)(2,1)} %copy-done.29) | copy-start | bytes 3538948
  1371.7 196.9 %copy-start.16 = (bf16[1536,256]{1,0:T(8,128)(2,1)S(1)}, bf16[1536,256]{1,0:T(8,128)(2,1)}, u32[]{:S(2)}) copy-start(bf16[1536,256]{1,0:T(8,128)(2,1)} %copy-done.15) | copy-start | bytes 2359300
  1371.7 196.9 %copy-start.37 = (bf16[384,2,128]{2,1,0:T(2,128)(2,1)S(1)}, bf16[384,2,128]{2,1,0:T(2,128)(2,1)}, u32[]{:S(2)}) copy-start(bf16[384,2,128]{2,1,0:T(2,128)(2,1)} %copy-done.36) | copy-start | bytes 589828
  1570.9 46.0 %copy-start.71 = (f32[384]{0:T(512)S(1)}, f32[384]{0:T(512)}, u32[]{:S(2)}) copy-start(f32[384]{0:T(512)} %copy-done.70) | copy-start | bytes 4612
  (95 other events, 360.8 us)
Sparse Core Ops, SparseCore 0:
  37.2 25.3 all-gather.11
  64.8 24.5 all-gather.9
  91.3 56.5 all-gather.13
  149.6 57.0 all-gather.15
  339.9 57.5 all-gather.17
  399.2 57.0 all-gather.19
  475.5 57.3 all-gather.21
  1117.7 32.2 reduce-scatter.14
  1152.9 32.2 reduce-scatter.16
  1188.0 55.0 reduce-scatter.32
  1246.0 57.0 reduce-scatter.26
  1306.0 57.0 reduce-scatter.28
  1366.4 24.4 reduce-scatter.30
  1393.6 26.1 reduce-scatter.20
  1422.5 26.0 reduce-scatter.22
  1451.5 57.0 reduce-scatter.24
  1511.5 57.0 reduce-scatter.18
  1571.1 71.8 all-reduce.10
where the time goes:
time: 1670 us; the launch traced here: 1660 us
  waiting for transfers between devices  854 us (51%)
  matrix products  300 us (18%)
  local copies, waits for them, and re-layouts  266 us (16%)
  other arithmetic  111 us (7%)
  blocking collectives  86 us (5%)
  starting transfers between devices  20.4 us (1%)
    all_to_all x1, waiting for transfers between devices, body(): lax.all_to_all(outgoing, 'ctx', split_axis=1, concat_axis=1, tiled=True)  124 us
    all_to_all x1, waiting for transfers between devices, body(): lax.all_to_all(grad_outgoing, 'ctx', split_axis=1, concat_axis=1, tiled=T...  115 us
    all_to_all x1, waiting for transfers between devices, body(): lax.all_to_all(expert_out.reshape(local_experts, ctx_count, capacity, wid...  106 us
    all_to_all x1, waiting for transfers between devices, body(): lax.all_to_all(row_grad.reshape(local_experts, ctx_count, capacity, width...  86.7 us
    unnamed x20, waiting for transfers between devices  61.6 us
    reduce_scatter x1, waiting for transfers between devices, body(): lax.psum_scatter(dense_local[2].astype(jnp.bfloat16), 'fsdp', scatter_dim...  60 us
    reduce_scatter x1, waiting for transfers between devices, body(): lax.psum_scatter(dense_local[5].astype(jnp.bfloat16), 'fsdp', scatter_dim...  60 us
    reduce_scatter x1, waiting for transfers between devices, body(): lax.psum_scatter(up_local.astype(jnp.bfloat16), 'fsdp', scatter_dimension...  57.1 us
  transfers between devices with their start and end apart: 22, of which 15 were waited for; matrix products, arithmetic and copies ran while one was open for 24% of the time, Pallas kernels for 0%

commit v1 on v0

v1 whole, which is shorter than its diff:
```python
import functools

import jax
import jax.numpy as jnp
from jax import lax
from jax.experimental import pallas as pl
from jax.experimental.pallas import tpu as pltpu
from jax.sharding import PartitionSpec as P

QUERY_HEADS = 12
KVH = 2
HEAD_SIZE = 128

EPSILON = 1e-06
ROPE_BASE = 10000.0
MASKED = -1e30
LOG2E = 1.4426950408889634
LANES = 128
SLOT_STEP = 64
KEY_TILE = 512
VMEM_BYTES = 60 * 1024 * 1024
MESH = pl.DeviceIdType.MESH
F32 = jnp.float32
BF16 = jnp.bfloat16


def dot(left, right, contract):
    return lax.dot_general(left, right, (contract, ((), ())), preferred_element_type=F32)


NN = ((1,), (0,))
NT = ((1,), (1,))
TN = ((0,), (0,))


def rms_scale(value_rows, gain):
    return (
        value_rows
        * lax.rsqrt(jnp.mean(value_rows * value_rows, axis=-1, keepdims=True) + EPSILON)
        * gain
    )


def rotate(value_rows, cosine, sine):
    half_dim = value_rows.shape[-1] // 2
    first = value_rows[..., :half_dim]
    second = value_rows[..., half_dim:]
    return jnp.concatenate(
        [first * cosine - second * sine, second * cosine + first * sine], axis=-1
    )


def place():
    ctx = lax.axis_index("ctx")
    core = lax.rem(ctx, 2)
    return ctx, lax.axis_index("fsdp"), ctx // 2, core, ctx + 1 - 2 * core


def peers_of(me, fsdp):
    peers = []
    for shift in range(1, fsdp):
        peer = me
        for bit in range(fsdp.bit_length() - 1):
            if (shift >> bit) & 1:
                digit = lax.rem(me // (1 << bit), 2)
                peer = peer + (1 << bit) - (2 << bit) * digit
        peers.append(peer)
    return peers


def greet(chips, peers, line):
    ctx, me, chip, core, sibling = place()
    barrier = pltpu.get_barrier_semaphore()
    for peer in peers:
        pl.semaphore_signal(barrier, inc=1, device_id=(ctx, peer), device_id_type=MESH)
    pl.semaphore_signal(barrier, inc=1, device_id=(sibling, me), device_id_type=MESH)
    known = len(peers) + 1
    if not line:
        pl.semaphore_wait(barrier, known)
        return
    has_right = chip + 1 < chips
    has_left = chip >= 1

    @pl.when(has_right)
    def _():
        pl.semaphore_signal(barrier, inc=1, device_id=(ctx + 2, me), device_id_type=MESH)

    @pl.when(has_left)
    def _():
        pl.semaphore_signal(barrier, inc=1, device_id=(ctx - 2, me), device_id_type=MESH)

    @pl.when(has_right & has_left)
    def _():
        pl.semaphore_wait(barrier, known + 2)

    @pl.when(jnp.logical_not(has_right & has_left))
    def _():
        pl.semaphore_wait(barrier, known + 1)


def remote(src, dst, send_sem, recv_sem, device):
    return pltpu.make_async_remote_copy(
        src_ref=src,
        dst_ref=dst,
        send_sem=send_sem,
        recv_sem=recv_sem,
        device_id=device,
        device_id_type=MESH,
    )


class DenseGather:
    def __init__(self, ins, outs, sems, fsdp):
        local_sem, send_sem, recv_sem, pass_sem, took_sem = sems
        ctx, me, chip, core, sibling = place()
        self.sends, self.passes, self.locals = [], [], []
        for i in range(len(ins)):
            rows = ins[i].shape[0]
            half = rows // 2
            for j, peer in enumerate(peers_of(me, fsdp)):
                self.sends.append(
                    remote(
                        ins[i].at[pl.ds(core * half, half)],
                        outs[i].at[pl.ds(me * rows + core * half, half)],
                        send_sem.at[i, j],
                        recv_sem.at[i, j],
                        (ctx, peer),
                    )
                )
                got = outs[i].at[pl.ds(peer * rows + core * half, half)]
                self.passes.append(
                    remote(got, got, pass_sem.at[i, j], took_sem.at[i, j], (sibling, me))
                )
            self.locals.append(
                pltpu.make_async_copy(
                    ins[i], outs[i].at[pl.ds(me * rows, rows)], local_sem.at[i]
                )
            )

    def start(self):
        for copy in self.sends + self.locals:
            copy.start()

    def finish(self):
        for send, copy in zip(self.sends, self.passes):
            send.wait_recv()
            copy.start()
        for send in self.sends:
            send.wait_send()
        for copy in self.passes + self.locals:
            copy.wait()


def dense_sems(count, fsdp):
    return [pltpu.SemaphoreType.DMA((count,))] + [
        pltpu.SemaphoreType.DMA((count, fsdp - 1)) for unused in range(4)
    ]


class LineGather:
    def __init__(self, ins, outs, sems, chips):
        self.ins, self.outs, self.chips = ins, outs, chips
        self.sems = sems
        self.ctx, self.me, self.chip, core, self.sibling = place()
        self.count = len(ins)

    def to_right(self, i, step):
        outs, chips = self.outs, self.chips
        return remote(
            self.ins[i] if step == 0 else outs[i].at[0, chips - step],
            outs[i].at[0, chips - 1 - step],
            self.sems[1].at[i, step],
            self.sems[2].at[i, step],
            (self.ctx + 2, self.me),
        )

    def to_left(self, i, step):
        outs = self.outs
        return remote(
            self.ins[i] if step == 0 else outs[i].at[0, step],
            outs[i].at[0, step + 1],
            self.sems[3].at[i, step],
            self.sems[4].at[i, step],
            (self.ctx - 2, self.me),
        )

    def across(self, i, slot):
        return remote(
            self.ins[i] if slot == 0 else self.outs[i].at[0, slot],
            self.outs[i].at[1, slot],
            self.sems[5].at[i, slot],
            self.sems[6].at[i, slot],
            (self.sibling, self.me),
        )

    def local(self, i):
        return pltpu.make_async_copy(self.ins[i], self.outs[i].at[0, 0], self.sems[0].at[i])

    def run(self):
        chip, chips, count = self.chip, self.chips, self.count
        for step in range(chips - 1):

            @pl.when((chip + 1 < chips) & (chip >= step))
            def _():
                for i in range(count):
                    self.to_right(i, step).start()

            @pl.when((chip >= 1) & (chip + step < chips))
            def _():
                for i in range(count):
                    self.to_left(i, step).start()

            if step == 0:
                for i in range(count):
                    self.across(i, 0).start()
                    self.local(i).start()

            @pl.when(chip >= step + 1)
            def _():
                for i in range(count):
                    self.to_right(i, step).wait_recv()
                    self.across(i, chips - 1 - step).start()

            @pl.when(chip + step + 1 < chips)
            def _():
                for i in range(count):
                    self.to_left(i, step).wait_recv()
                    self.across(i, step + 1).start()

    def finish(self):
        chip, chips, count = self.chip, self.chips, self.count
        for step in range(chips - 1):

            @pl.when((chip + 1 < chips) & (chip >= step))
            def _():
                for i in range(count):
                    self.to_right(i, step).wait_send()

            @pl.when((chip >= 1) & (chip + step < chips))
            def _():
                for i in range(count):
                    self.to_left(i, step).wait_send()

        for slot in range(chips):
            for i in range(count):
                self.across(i, slot).wait()
        for i in range(count):
            self.local(i).wait()


def line_sems(count, chips):
    return (
        [pltpu.SemaphoreType.DMA((count,))]
        + [pltpu.SemaphoreType.DMA((count, chips - 1)) for unused in range(4)]
        + [pltpu.SemaphoreType.DMA((count, chips)) for unused in range(2)]
    )


def gather_kernel(dense, line, fsdp, chips, *refs):
    ins, outs, sems = refs[: dense + line], refs[dense + line : 2 * (dense + line)], None
    sems = refs[2 * (dense + line) :]
    ctx, me, chip, core, sibling = place()
    greet(chips, peers_of(me, fsdp) if dense else [], line > 0)
    if dense:
        first = DenseGather(ins[:dense], outs[:dense], sems[:5], fsdp)
        first.start()
    if line:
        second = LineGather(ins[dense:], outs[dense:], sems[-7:], chips)
        second.run()
    if dense:
        first.finish()
    if line:
        second.finish()


def gather(dense, line, fsdp, chips, collective_id):
    arrays = list(dense) + list(line)
    count = len(arrays)
    scratch = (dense_sems(len(dense), fsdp) if dense else []) + (
        line_sems(len(line), chips) if line else []
    )
    return pl.pallas_call(
        functools.partial(gather_kernel, len(dense), len(line), fsdp, chips),
        out_shape=[jax.ShapeDtypeStruct((fsdp * a.shape[0],) + a.shape[1:], a.dtype) for a in dense]
        + [jax.ShapeDtypeStruct((2, chips) + a.shape, a.dtype) for a in line],
        in_specs=[pl.BlockSpec(memory_space=pl.ANY)] * count,
        out_specs=[pl.BlockSpec(memory_space=pl.ANY)] * count,
        scratch_shapes=scratch,
        compiler_params=pltpu.CompilerParams(collective_id=collective_id, has_side_effects=True),
        name="gather",
    )(*arrays)


def add(*parts):
    total = parts[0].astype(F32)
    for part in parts[1:]:
        total = total + part.astype(F32)
    return total


def line_sum(chips, first, take, sends, gots, sems, done):
    ctx, me, chip, core, sibling = place()
    send_right, send_left = sends
    got_right, got_left = gots
    right_send, right_recv, left_send, left_recv = sems

    def right(step):
        return remote(
            send_right.at[step],
            got_right.at[step],
            right_send.at[step],
            right_recv.at[step],
            (ctx + 2, me),
        )

    def left(step):
        return remote(
            send_left.at[step],
            got_left.at[step],
            left_send.at[step],
            left_recv.at[step],
            (ctx - 2, me),
        )

    for step in range(chips - 1):
        far_right, far_left = chips - 1 - step, step + 1

        @pl.when(chip <= step)
        def _():
            take(far_right)
            if step == 0:
                send_right[step] = add(*first(far_right)).astype(BF16)
            else:

                @pl.when(chip == 0)
                def _():
                    send_right[step] = add(*first(far_right)).astype(BF16)

                @pl.when(chip >= 1)
                def _():
                    right(step - 1).wait_recv()
                    send_right[step] = add(*first(far_right), got_right[step - 1]).astype(BF16)

            right(step).start()

        @pl.when(chip >= chips - 1 - step)
        def _():
            take(far_left)
            if step == 0:
                send_left[step] = add(*first(far_left)).astype(BF16)
            else:

                @pl.when(chip == chips - 1)
                def _():
                    send_left[step] = add(*first(far_left)).astype(BF16)

                @pl.when(chip < chips - 1)
                def _():
                    left(step - 1).wait_recv()
                    send_left[step] = add(*first(far_left), got_left[step - 1]).astype(BF16)

            left(step).start()

    last = chips - 2
    take(0)

    @pl.when(chip == 0)
    def _():
        left(last).wait_recv()
        done(add(*first(0), got_left[last]))

    @pl.when(chip == chips - 1)
    def _():
        right(last).wait_recv()
        done(add(*first(0), got_right[last]))

    @pl.when((chip >= 1) & (chip < chips - 1))
    def _():
        left(last).wait_recv()
        right(last).wait_recv()
        done(add(*first(0), got_left[last], got_right[last]))

    def finish():
        for step in range(chips - 1):

            @pl.when(chip <= step)
            def _():
                right(step).wait_send()

            @pl.when(chip >= chips - 1 - step)
            def _():
                left(step).wait_send()

    return finish


def line_reduce_kernel(
    chips, mine_ref, other_ref, out_ref, pair, sr, sl, gr, gl, ps, pr, s0, s1, s2, s3
):
    ctx, me, chip, core, sibling = place()
    greet(chips, [], True)
    swaps = [
        remote(other_ref.at[r], pair.at[r], ps.at[r], pr.at[r], (sibling, me))
        for r in range(chips)
    ]
    order = []
    for step in range(chips - 1):
        for r in (chips - 1 - step, step + 1):
            if r not in order:
                order.append(r)
    for r in order + [0]:
        swaps[r].start()

    def done(total):
        out_ref[...] = total

    finish = line_sum(
        chips,
        lambda r: (mine_ref[r], pair[r]),
        lambda r: swaps[r].wait_recv(),
        (sr, sl),
        (gr, gl),
        (s0, s1, s2, s3),
        done,
    )
    finish()
    for swap in swaps:
        swap.wait_send()


def line_reduce_now(mine, other, chips, collective_id):
    unused, rows, width = mine.shape
    vmem = pl.BlockSpec(memory_space=pltpu.VMEM)
    return pl.pallas_call(
        functools.partial(line_reduce_kernel, chips),
        out_shape=jax.ShapeDtypeStruct((rows, width), F32),
        in_specs=[vmem, vmem],
        out_specs=vmem,
        scratch_shapes=[pltpu.VMEM((chips, rows, width), BF16)]
        + [pltpu.VMEM((chips - 1, rows, width), BF16) for unused in range(4)]
        + [pltpu.SemaphoreType.DMA((chips,)) for unused in range(2)]
        + [pltpu.SemaphoreType.DMA((chips - 1,)) for unused in range(4)],
        compiler_params=pltpu.CompilerParams(
            collective_id=collective_id, has_side_effects=True, vmem_limit_bytes=VMEM_BYTES
        ),
        name="line_reduce",
    )(mine, other)


def dense_reduce_kernel(
    fsdp,
    chips,
    local_ref,
    out_ref,
    pair,
    mine,
    cross,
    sums,
    sr,
    sl,
    gr,
    gl,
    spread,
    ps,
    pr,
    xs,
    xr,
    s0,
    s1,
    s2,
    s3,
    g0,
    g1,
    g2,
    g3,
    a0,
    a1,
):
    ctx, me, chip, core, sibling = place()
    peers = peers_of(me, fsdp)
    greet(chips, peers, True)
    cut = sums.shape[1] // chips
    owners = peers + [me]

    swaps = [
        remote(local_ref.at[owner, 1 - core], pair.at[j], ps.at[j], pr.at[j], (sibling, me))
        for j, owner in enumerate(owners)
    ]
    for swap in swaps:
        swap.start()

    crossings = []
    for j, owner in enumerate(owners):
        swaps[j].wait_recv()
        mine[j] = add(local_ref[owner, core], pair[j]).astype(BF16)
        if j < len(peers):
            copy = remote(mine.at[j], cross.at[j], xs.at[j], xr.at[j], (ctx, owner))
            copy.start()
            crossings.append(copy)
    for copy in crossings:
        copy.wait_recv()
    sums[...] = add(mine[len(peers)], *[cross[j] for j in range(len(peers))]).astype(BF16)

    def columns(r):
        owner = lax.rem(chip + r, chips)
        return pl.ds(pl.multiple_of(owner * cut, LANES), cut)

    def done(total):
        spread[0, 0] = total.astype(BF16)

    finish = line_sum(
        chips,
        lambda r: (sums[:, columns(r)],),
        lambda r: None,
        (sr, sl),
        (gr, gl),
        (s0, s1, s2, s3),
        done,
    )

    def to_right(step):
        return remote(
            spread.at[0, (chips - step) % chips],
            spread.at[0, chips - 1 - step],
            g0.at[step],
            g1.at[step],
            (ctx + 2, me),
        )

    def to_left(step):
        return remote(
            spread.at[0, step], spread.at[0, step + 1], g2.at[step], g3.at[step], (ctx - 2, me)
        )

    def across(slot):
        return remote(
            spread.at[0, slot], spread.at[1, slot], a0.at[slot], a1.at[slot], (sibling, me)
        )

    for step in range(chips - 1):

        @pl.when((chip + 1 < chips) & (chip >= step))
        def _():
            to_right(step).start()

        @pl.when((chip >= 1) & (chip + step < chips))
        def _():
            to_left(step).start()

        if step == 0:
            across(0).start()

        @pl.when(chip >= step + 1)
        def _():
            to_right(step).wait_recv()
            across(chips - 1 - step).start()

        @pl.when(chip + step + 1 < chips)
        def _():
            to_left(step).wait_recv()
            across(step + 1).start()

    for r in range(chips):
        out_ref[core, :, columns(r)] = spread[0, r]
    for r in range(chips):
        across(r).wait()
        out_ref[1 - core, :, columns(r)] = spread[1, r]
    for step in range(chips - 1):

        @pl.when((chip + 1 < chips) & (chip >= step))
        def _():
            to_right(step).wait_send()

        @pl.when((chip >= 1) & (chip + step < chips))
        def _():
            to_left(step).wait_send()

    finish()
    for copy in crossings + swaps:
        copy.wait_send()


def dense_reduce(local, fsdp, chips, collective_id):
    unused, unused_two, rows, width = local.shape
    cut = width // chips
    vmem = pl.BlockSpec(memory_space=pltpu.VMEM)
    return pl.pallas_call(
        functools.partial(dense_reduce_kernel, fsdp, chips),
        out_shape=jax.ShapeDtypeStruct((2, rows, width), BF16),
        in_specs=[vmem],
        out_specs=vmem,
        scratch_shapes=[
            pltpu.VMEM((fsdp, rows, width), BF16),
            pltpu.VMEM((fsdp, rows, width), BF16),
            pltpu.VMEM((fsdp - 1, rows, width), BF16),
            pltpu.VMEM((rows, width), BF16),
        ]
        + [pltpu.VMEM((chips - 1, rows, cut), BF16) for unused in range(4)]
        + [pltpu.VMEM((2, chips, rows, cut), BF16)]
        + [pltpu.SemaphoreType.DMA((fsdp,)) for unused in range(2)]
        + [pltpu.SemaphoreType.DMA((fsdp - 1,)) for unused in range(2)]
        + [pltpu.SemaphoreType.DMA((chips - 1,)) for unused in range(8)]
        + [pltpu.SemaphoreType.DMA((chips,)) for unused in range(2)],
        compiler_params=pltpu.CompilerParams(
            collective_id=collective_id, has_side_effects=True, vmem_limit_bytes=VMEM_BYTES
        ),
        name="dense_reduce",
    )(local)


def right_pairs(chips, least):
    return [(2 * z + k, 2 * z + 2 + k) for z in range(chips - 1) if least <= z for k in range(2)]


def left_pairs(chips, most):
    return [(2 * z + k, 2 * z - 2 + k) for z in range(1, chips) if z <= most for k in range(2)]


def swap_pairs(chips):
    return [(i, i ^ 1) for i in range(2 * chips)]


def after(value, *others):
    return lax.optimization_barrier((value,) + others)[0]


def line_gather_async(rows, chips, chip, ties):
    right, left = rows, rows
    got_right, got_left = [], []
    for step in range(chips - 1):
        if step >= 1:
            right = after(right, *ties[min(step, len(ties)) - 1])
            left = after(left, *ties[min(step, len(ties)) - 1])
        right = lax.ppermute(right, "ctx", right_pairs(chips, step))
        left = lax.ppermute(left, "ctx", left_pairs(chips, chips - 1 - step))
        got_right.append(right)
        got_left.append(left)
    slots = [rows]
    for r in range(1, chips):
        slots.append(jnp.where(chip + r < chips, got_left[r - 1], got_right[chips - 1 - r]))
    mine = jnp.stack(slots)
    return mine, lax.ppermute(mine, "ctx", swap_pairs(chips))


def line_reduce(mine, other, chips, ties):
    recv = lax.ppermute(other, "ctx", swap_pairs(chips))
    right = left = None
    for step in range(chips - 1):
        r_right, r_left = chips - 1 - step, step + 1
        parts_right, parts_left = [mine[r_right], recv[r_right]], [mine[r_left], recv[r_left]]
        if step > 0:
            parts_right.append(right)
            parts_left.append(left)
        send_right, send_left = add(*parts_right).astype(BF16), add(*parts_left).astype(BF16)
        tie = ties[min(step, len(ties) - 1)]
        if tie:
            send_right, send_left = after(send_right, *tie), after(send_left, *tie)
        right = lax.ppermute(
            send_right,
            "ctx",
            [(2 * z + k, 2 * z + 2 + k) for z in range(step + 1) for k in range(2)],
        )
        left = lax.ppermute(
            send_left,
            "ctx",
            [
                (2 * z + k, 2 * z - 2 + k)
                for z in range(chips - 1 - step, chips)
                for k in range(2)
            ],
        )
    return add(mine[0], recv[0], right, left)


def attention_kernel(
    scale, q_ref, k_ref, v_ref, oq_ref, pq_ref, ok_ref, out_ref, lse_ref, bias, scores
):
    keys = k_ref.shape[0]
    tiles = keys // KEY_TILE
    rows = q_ref.shape[0]

    @pl.when(pl.program_id(0) == 0)
    def _():
        def fill(t, carry):
            tile = pl.ds(pl.multiple_of(t * KEY_TILE, KEY_TILE), KEY_TILE)
            gap = oq_ref[...] - ok_ref[:, tile]
            bias[:, tile] = jnp.where((gap >= 0) & (gap <= pq_ref[...]), 0.0, MASKED)
            return carry

        lax.fori_loop(0, tiles, fill, 0)

    query = q_ref[...]

    def score(t, top):
        tile = pl.ds(pl.multiple_of(t * KEY_TILE, KEY_TILE), KEY_TILE)
        raw = dot(query, k_ref[tile, :], NT) * (scale * LOG2E) + bias[:, tile]
        scores[:, tile] = raw
        for part in range(KEY_TILE // LANES):
            top = jnp.maximum(top, raw[:, part * LANES : (part + 1) * LANES])
        return top

    top = lax.fori_loop(0, tiles, score, jnp.full((rows, LANES), MASKED, F32))
    top = jnp.max(top, axis=1, keepdims=True)

    def weigh(t, carry):
        total, acc = carry
        tile = pl.ds(pl.multiple_of(t * KEY_TILE, KEY_TILE), KEY_TILE)
        probs = jnp.exp2(scores[:, tile] - top)
        for part in range(KEY_TILE // LANES):
            total = total + probs[:, part * LANES : (part + 1) * LANES]
        acc = acc + dot(probs.astype(BF16), v_ref[tile, :], NN)
        return total, acc

    total, acc = lax.fori_loop(
        0, tiles, weigh, (jnp.zeros((rows, LANES), F32), jnp.zeros((rows, HEAD_SIZE), F32))
    )
    total = jnp.sum(total, axis=1, keepdims=True)
    out_ref[...] = (acc / total).astype(BF16)
    lse = jnp.broadcast_to(top + jnp.log2(total), (rows, LANES))
    lse_ref[0] = lse.T[:1, :]


def attention(queries, kv, order_mine, pos_mine, order_keys, group):
    rows = queries.shape[0]
    keys = kv.shape[0]
    per_group = QUERY_HEADS // KVH
    return pl.pallas_call(
        functools.partial(attention_kernel, HEAD_SIZE ** (-0.5)),
        grid=(per_group,),
        out_shape=[
            jax.ShapeDtypeStruct((rows, per_group * HEAD_SIZE), BF16),
            jax.ShapeDtypeStruct((per_group, 1, rows), F32),
        ],
        in_specs=[
            pl.BlockSpec((rows, HEAD_SIZE), lambda h: (0, group * per_group + h)),
            pl.BlockSpec((keys, HEAD_SIZE), lambda h: (0, group)),
            pl.BlockSpec((keys, HEAD_SIZE), lambda h: (0, KVH + group)),
            pl.BlockSpec((rows, 1), lambda h: (0, 0)),
            pl.BlockSpec((rows, 1), lambda h: (0, 0)),
            pl.BlockSpec((1, keys), lambda h: (0, 0)),
        ],
        out_specs=[
            pl.BlockSpec((rows, HEAD_SIZE), lambda h: (0, h)),
            pl.BlockSpec((1, 1, rows), lambda h: (h, 0, 0)),
        ],
        scratch_shapes=[pltpu.VMEM((rows, keys), F32), pltpu.VMEM((rows, keys), F32)],
        compiler_params=pltpu.CompilerParams(vmem_limit_bytes=VMEM_BYTES),
        cost_estimate=pl.CostEstimate(
            flops=4 * rows * keys * HEAD_SIZE * per_group,
            bytes_accessed=4 * rows * per_group * HEAD_SIZE + 4 * keys * HEAD_SIZE,
            transcendentals=rows * keys * per_group,
        ),
        name="attention",
    )(queries, kv, kv, order_mine[:, None], pos_mine[:, None], order_keys[None, :])


def attention_back_kernel(
    scale,
    per_group,
    q_ref,
    k_ref,
    v_ref,
    o_ref,
    do_ref,
    lse_ref,
    oq_ref,
    pq_ref,
    ok_ref,
    dq_ref,
    dk_ref,
    dv_ref,
    bias,
    dk_acc,
    dv_acc,
):
    keys = k_ref.shape[0]
    tiles = keys // KEY_TILE
    rows = q_ref.shape[0]
    head = pl.program_id(0)

    @pl.when(head == 0)
    def _():
        def fill(t, carry):
            tile = pl.ds(pl.multiple_of(t * KEY_TILE, KEY_TILE), KEY_TILE)
            gap = oq_ref[...] - ok_ref[tile, :]
            bias[tile, :] = jnp.where((gap >= 0) & (gap <= pq_ref[...]), 0.0, MASKED)
            return carry

        lax.fori_loop(0, tiles, fill, 0)

    @pl.when(lax.rem(head, per_group) == 0)
    def _():
        dk_acc[...] = jnp.zeros_like(dk_acc)
        dv_acc[...] = jnp.zeros_like(dv_acc)

    query = q_ref[...]
    grad = do_ref[...]
    lse = lse_ref[0]
    product = grad.astype(F32) * o_ref[...].astype(F32)
    delta = jnp.sum(product.T, axis=0, keepdims=True)

    def step(t, acc):
        tile = pl.ds(pl.multiple_of(t * KEY_TILE, KEY_TILE), KEY_TILE)
        key = k_ref[tile, :]
        raw = dot(key, query, NT) * (scale * LOG2E) + bias[tile, :]
        probs = jnp.exp2(raw - lse)
        prob_grad = dot(v_ref[tile, :], grad, NT)
        score_grad = (probs * (prob_grad - delta)).astype(BF16)
        dv_acc[tile, :] += dot(probs.astype(BF16), grad, NN)
        dk_acc[tile, :] += dot(score_grad, query, NN)
        return acc + dot(score_grad, key, TN)

    acc = lax.fori_loop(0, tiles, step, jnp.zeros((rows, HEAD_SIZE), F32))
    dq_ref[...] = acc * scale

    @pl.when(lax.rem(head, per_group) == per_group - 1)
    def _():
        dk_ref[...] = (dk_acc[...] * scale).astype(BF16)
        dv_ref[...] = dv_acc[...].astype(BF16)


def attention_back(
    queries, kv, attended, attended_grad, lse, order_mine, pos_mine, order_keys, group
):
    rows = queries.shape[0]
    keys = kv.shape[0]
    per_group = QUERY_HEADS // KVH
    head_rows = pl.BlockSpec((rows, HEAD_SIZE), lambda h: (0, group * per_group + h))
    group_rows = pl.BlockSpec((rows, HEAD_SIZE), lambda h: (0, h))
    return pl.pallas_call(
        functools.partial(attention_back_kernel, HEAD_SIZE ** (-0.5), per_group),
        grid=(per_group,),
        out_shape=[
            jax.ShapeDtypeStruct((rows, per_group * HEAD_SIZE), F32),
            jax.ShapeDtypeStruct((keys, HEAD_SIZE), BF16),
            jax.ShapeDtypeStruct((keys, HEAD_SIZE), BF16),
        ],
        in_specs=[
            head_rows,
            pl.BlockSpec((keys, HEAD_SIZE), lambda h: (0, group)),
            pl.BlockSpec((keys, HEAD_SIZE), lambda h: (0, KVH + group)),
            group_rows,
            head_rows,
            pl.BlockSpec((1, 1, rows), lambda h: (h, 0, 0)),
            pl.BlockSpec((1, rows), lambda h: (0, 0)),
            pl.BlockSpec((1, rows), lambda h: (0, 0)),
            pl.BlockSpec((keys, 1), lambda h: (0, 0)),
        ],
        out_specs=[
            group_rows,
            pl.BlockSpec((keys, HEAD_SIZE), lambda h: (0, 0)),
            pl.BlockSpec((keys, HEAD_SIZE), lambda h: (0, 0)),
        ],
        scratch_shapes=[
            pltpu.VMEM((keys, rows), F32),
            pltpu.VMEM((keys, HEAD_SIZE), F32),
            pltpu.VMEM((keys, HEAD_SIZE), F32),
        ],
        compiler_params=pltpu.CompilerParams(vmem_limit_bytes=VMEM_BYTES),
        cost_estimate=pl.CostEstimate(
            flops=10 * rows * keys * HEAD_SIZE * per_group,
            bytes_accessed=10 * rows * per_group * HEAD_SIZE + 8 * keys * HEAD_SIZE,
            transcendentals=rows * keys * per_group,
        ),
        name="attention_back",
    )(
        queries,
        kv,
        kv,
        attended,
        attended_grad,
        lse,
        order_mine[None, :],
        pos_mine[None, :],
        order_keys[:, None],
    )


def expert_kernel(
    capacity,
    local_experts,
    expert_count,
    first_ref,
    hidden_ref,
    grad_mine_ref,
    grad_other_ref,
    table_ref,
    weight_ref,
    gate_ref,
    up_ref,
    down_ref,
    out_mine,
    out_other,
    rows_mine,
    rows_other,
    save_x,
    save_pg,
    save_inner,
    save_da,
    save_db,
):
    tokens = hidden_ref.shape[2]
    slot_rows = save_x.shape[1] // 2
    first = first_ref[0]
    slot = lax.broadcasted_iota(jnp.int32, (slot_rows, tokens), 0).astype(F32) + 1.0
    slot = jnp.where(slot <= capacity, slot, -1.0)
    lane = lax.broadcasted_iota(jnp.int32, (2 * slot_rows, LANES), 1)
    picks = [[], []]
    outs = [[], []]
    backs = [[], []]
    for e in range(local_experts):
        rows_x, rows_g, rows_w = [], [], []
        for q in range(2):
            row = table_ref[q, 0, pl.ds(first + e, 1), :]
            hit = slot == row
            pick = jnp.where(hit, 1.0, 0.0).astype(BF16)
            weight = weight_ref[q, 0, pl.ds(first + e, 1), :]
            rows_w.append(jnp.sum(jnp.where(hit, weight, 0.0), axis=1, keepdims=True))
            rows_x.append(dot(pick, hidden_ref[q, 0], NN).astype(BF16))
            grad_rows = grad_mine_ref[0] if q == 0 else grad_other_ref[0]
            rows_g.append(dot(pick, grad_rows, NN))
            picks[q].append(pick)
        x = jnp.concatenate(rows_x, axis=0)
        g = jnp.concatenate(rows_g, axis=0)
        w = jnp.concatenate(rows_w, axis=0)
        pair_grad = (w * g).astype(BF16)
        gate_pre = dot(x, gate_ref[e], NN)
        up_pre = dot(x, up_ref[e], NN)
        sig = jax.nn.sigmoid(gate_pre)
        silu = gate_pre * sig
        inner = (silu * up_pre).astype(BF16)
        expert_out = dot(inner, down_ref[e], NN).astype(BF16).astype(F32)
        gate_grad = jnp.sum(expert_out * g, axis=1, keepdims=True)
        inner_grad = dot(pair_grad, down_ref[e], NT)
        da = (inner_grad * up_pre * sig * (1.0 + gate_pre * (1.0 - sig))).astype(BF16)
        db = (inner_grad * silu).astype(BF16)
        row_grad = (dot(da, gate_ref[e], NT) + dot(db, up_ref[e], NT)).astype(BF16)
        high = gate_grad.astype(BF16).astype(F32)
        extra = jnp.where(lane == first + e, high, 0.0) + jnp.where(
            lane == expert_count + first + e, gate_grad - high, 0.0
        )
        back = jnp.concatenate([row_grad, extra.astype(BF16)], axis=1)
        out_rows = (w * expert_out).astype(BF16)
        for q in range(2):
            part = slice(q * slot_rows, (q + 1) * slot_rows)
            outs[q].append(out_rows[part])
            backs[q].append(back[part])
        save_x[e] = x
        save_pg[e] = pair_grad
        save_inner[e] = inner
        save_da[e] = da
        save_db[e] = db
    for q in range(2):
        pick = jnp.concatenate(picks[q], axis=0)
        out_ref = out_mine if q == 0 else out_other
        rows_ref = rows_mine if q == 0 else rows_other
        out_ref[0] = dot(pick, jnp.concatenate(outs[q], axis=0), TN).astype(BF16)
        rows_ref[0] = dot(pick, jnp.concatenate(backs[q], axis=0), TN).astype(BF16)


def expert_rows_pass(
    first, hidden, grad_mine, grad_other, table, weights, gate, up, down, capacity, expert_count
):
    chips, tokens, width = grad_mine.shape
    local_experts, unused, hidden_units = gate.shape
    slots = 2 * SLOT_STEP * -(-capacity // SLOT_STEP)
    total = chips * slots
    once = pl.Buffered(1)

    def whole(shape):
        return pl.BlockSpec(shape, lambda r, s: (0,) * len(shape), pipeline_mode=once)

    def saved(columns):
        return pl.BlockSpec((local_experts, slots, columns), lambda r, s: (0, r, 0))

    chunk = pl.BlockSpec((1, tokens, width), lambda r, s: (r, 0, 0))
    wide = pl.BlockSpec((1, tokens, width + LANES), lambda r, s: (r, 0, 0))
    small = pl.BlockSpec((2, 1, expert_count, tokens), lambda r, s: (0, r, 0, 0))
    flops = 2 * total * width * hidden_units * local_experts * 6 + 8 * total * tokens * width
    return pl.pallas_call(
        functools.partial(expert_kernel, capacity, local_experts, expert_count),
        grid_spec=pltpu.PrefetchScalarGridSpec(
            num_scalar_prefetch=1,
            grid=(chips,),
            in_specs=[
                pl.BlockSpec((2, 1, tokens, width), lambda r, s: (0, r, 0, 0)),
                chunk,
                chunk,
                small,
                small,
                whole(gate.shape),
                whole(up.shape),
                whole(down.shape),
            ],
            out_specs=[
                chunk,
                chunk,
                wide,
                wide,
                saved(width),
                saved(width),
                saved(hidden_units),
                saved(hidden_units),
                saved(hidden_units),
            ],
        ),
        out_shape=[jax.ShapeDtypeStruct((chips, tokens, width), BF16)] * 2
        + [jax.ShapeDtypeStruct((chips, tokens, width + LANES), BF16)] * 2
        + [jax.ShapeDtypeStruct((local_experts, total, width), BF16)] * 2
        + [jax.ShapeDtypeStruct((local_experts, total, hidden_units), BF16)] * 3,
        compiler_params=pltpu.CompilerParams(vmem_limit_bytes=VMEM_BYTES),
        cost_estimate=pl.CostEstimate(
            flops=flops, bytes_accessed=80_000_000, transcendentals=total * hidden_units * 2
        ),
        name="expert_rows",
    )(first, hidden, grad_mine, grad_other, table, weights, gate, up, down)


def outer_kernel(per, split_left, left_ref, right_ref, out_ref):
    product = dot(left_ref[0], right_ref[0], TN).astype(BF16)
    axis = 0 if split_left else 1
    size = product.shape[axis] // per
    for i in range(per):
        out_ref[i, 0] = lax.slice_in_dim(product, i * size, (i + 1) * size, axis=axis)


def outer_products(left, right, fsdp, split_left):
    experts, total, m = left.shape
    n = right.shape[2]
    per = 1 if ((m if split_left else n) // fsdp) % LANES == 0 else 2
    if split_left:
        m = m // fsdp
    else:
        n = n // fsdp
    return pl.pallas_call(
        functools.partial(outer_kernel, per, split_left),
        grid=(experts, fsdp // per),
        out_shape=jax.ShapeDtypeStruct((fsdp, experts, m, n), BF16),
        in_specs=[
            pl.BlockSpec(
                (1, total, m * per if split_left else m),
                lambda e, f: (e, 0, f if split_left else 0),
            ),
            pl.BlockSpec(
                (1, total, n if split_left else n * per),
                lambda e, f: (e, 0, 0 if split_left else f),
            ),
        ],
        out_specs=pl.BlockSpec((per, 1, m, n), lambda e, f: (f, e, 0, 0)),
        compiler_params=pltpu.CompilerParams(vmem_limit_bytes=VMEM_BYTES),
        cost_estimate=pl.CostEstimate(
            flops=2 * total * m * n * experts * fsdp, bytes_accessed=14_000_000, transcendentals=0
        ),
        name="outer_products",
    )(left, right)


def body(
    tokens,
    grad_out,
    order,
    lengths,
    routes,
    gain_one,
    gain_two,
    w_query,
    w_key,
    w_value,
    w_out,
    w_router,
    w_gate,
    w_up,
    w_down,
):
    fsdp = lax.axis_size("fsdp")
    chips = lax.axis_size("ctx") // 2
    ctx_index = lax.axis_index("ctx")
    chip = ctx_index // 2
    core = lax.rem(ctx_index, 2)
    tok_rows = tokens.shape[1]
    width = tokens.shape[2]
    top_count = routes.shape[2]
    local_experts = w_gate.shape[0]
    expert_count = local_experts * chips * 2
    capacity = 5 * tok_rows * top_count // (4 * expert_count)
    kv_width = KVH * HEAD_SIZE
    shard = gain_one.shape[0]

    small = jnp.concatenate(
        [
            w_router,
            gain_one[:, None],
            gain_two[:, None],
            jnp.zeros((shard, LANES - expert_count - 2), BF16),
        ],
        axis=1,
    )
    qkv_shard = jnp.concatenate([w_query, w_key, w_value], axis=1)
    qkv_full, small_full = gather([qkv_shard, small], [], fsdp, chips, 0)

    qkv_full, w_gate, w_up, w_down = lax.optimization_barrier((qkv_full, w_gate, w_up, w_down))
    gate_full, up_full, down_full = (
        lax.all_gather(w_gate, "fsdp", axis=1, tiled=True),
        lax.all_gather(w_up, "fsdp", axis=1, tiled=True),
        lax.all_gather(w_down, "fsdp", axis=2, tiled=True),
    )
    router_full = small_full[:, :expert_count]
    gain_a = small_full[:, expert_count].astype(F32)
    gain_b = small_full[:, expert_count + 1].astype(F32)

    order_row = order[0]
    start_row = ctx_index * tok_rows
    order_mine = lax.dynamic_slice_in_dim(order_row, start_row, tok_rows)
    ends = jnp.cumsum(lengths[0])
    starts = ends - lengths[0]
    past = order_mine[:, None] >= ends[None, :]
    doc_start = jnp.max(jnp.where(past, ends[None, :], starts[:1]), axis=1)
    pos_mine = order_mine - doc_start
    by_chip = jnp.roll(order_row.reshape(chips, 2, tok_rows), -chip, axis=0)
    by_chip = jnp.where(core == 0, by_chip, by_chip[:, ::-1])
    order_keys = jnp.swapaxes(by_chip, 0, 1).reshape(-1)

    route_rows = routes[0]
    route_onehot = (route_rows[:, :, None] == jnp.arange(expert_count)[None, None, :]).astype(F32)
    routed = jnp.sum(route_onehot, axis=1)
    earlier = (order_mine[None, :] < order_mine[:, None]).astype(BF16)
    ranks = jnp.dot(earlier, routed.astype(BF16), preferred_element_type=F32)
    table = jnp.where(routed > 0, jnp.minimum(ranks, capacity) + 1.0, 0.0)

    half_dim = HEAD_SIZE // 2
    freqs = ROPE_BASE ** (-2.0 * jnp.arange(half_dim).astype(F32) / HEAD_SIZE)
    angles = pos_mine.astype(F32)[:, None] * freqs[None, :]
    cosine = jnp.cos(angles)[:, None, :]
    sine = jnp.sin(angles)[:, None, :]

    inputs = tokens[0].astype(F32)
    hidden_one = rms_scale(inputs, gain_a).astype(BF16)
    pre = jnp.dot(hidden_one, qkv_full, preferred_element_type=F32)
    turned = rotate(
        pre[:, : width + kv_width].reshape(tok_rows, QUERY_HEADS + KVH, HEAD_SIZE), cosine, sine
    )
    queries = turned[:, :QUERY_HEADS].astype(BF16).reshape(tok_rows, width)
    kv_mine = jnp.concatenate(
        [
            turned[:, QUERY_HEADS:].astype(BF16).reshape(tok_rows, kv_width),
            pre[:, width + kv_width :].astype(BF16),
        ],
        axis=1,
    )
    out_full, kv_all, table_all = gather([w_out], [kv_mine, table.T], fsdp, chips, 1)
    kv_all = kv_all.reshape(-1, 2 * kv_width)
    attended, lse = [], []
    for group in range(KVH):
        part, part_lse = attention(
            after(queries, *attended[-1:]), kv_all, order_mine, pos_mine, order_keys, group
        )
        attended.append(part)
        lse.append(part_lse)
    grad_mine, grad_other = line_gather_async(grad_out[0], chips, chip, [(kv_all,), attended[:1]])
    attended_parts, attended = attended, jnp.concatenate(attended, axis=1)
    middle = inputs + jnp.dot(attended, out_full, preferred_element_type=F32)
    hidden_two = rms_scale(middle, gain_b).astype(BF16)
    logits = jnp.dot(hidden_two, router_full, preferred_element_type=F32)
    chosen = jnp.where(routed > 0, logits, MASKED)
    gate_weights = jnp.where(routed > 0, jax.nn.softmax(chosen, axis=-1), 0.0)

    hidden_all, weights_all = gather([], [hidden_two, gate_weights.T], fsdp, chips, 2)
    first = (ctx_index * local_experts).astype(jnp.int32).reshape(1)
    (
        out_mine,
        out_other,
        rows_mine,
        rows_other,
        save_x,
        save_pg,
        save_inner,
        save_da,
        save_db,
    ) = expert_rows_pass(
        first,
        hidden_all,
        grad_mine,
        grad_other,
        table_all,
        weights_all,
        gate_full,
        up_full,
        down_full,
        capacity,
        expert_count,
    )
    gate_local = outer_products(save_x, save_da, fsdp, True)
    up_local = outer_products(save_x, save_db, fsdp, True)
    down_local = outer_products(save_inner, save_pg, fsdp, False)
    gate_grad_out, up_grad_out, down_grad_out = (
        lax.psum_scatter(part, "fsdp", scatter_dimension=0, tiled=True)[0].astype(F32)
        for part in (gate_local, up_local, down_local)
    )
    returned = line_reduce(
        rows_mine, rows_other, chips, [(gate_local,), (up_local,), (down_local,)]
    )

    out_grad = grad_out[0].astype(F32)
    extra = returned[:, width:]
    gate_grad = extra[:, :expert_count] + extra[:, expert_count : 2 * expert_count]
    logit_grad = (
        gate_weights * (gate_grad - jnp.sum(gate_weights * gate_grad, axis=-1, keepdims=True))
    ).astype(BF16)
    router_local = jnp.einsum("td,te->de", hidden_two, logit_grad, preferred_element_type=F32)
    hidden_two_grad = returned[:, :width] + jnp.einsum(
        "te,de->td", logit_grad, router_full, preferred_element_type=F32
    )
    unused_two, norm_two_back = jax.vjp(rms_scale, middle, gain_b)
    middle_part, gain_two_local = norm_two_back(hidden_two_grad)
    middle_grad = out_grad + middle_part
    branch_grad = middle_grad.astype(BF16)
    out_local = jnp.einsum("tc,td->cd", attended, branch_grad, preferred_element_type=F32)
    attended_grad = jnp.einsum(
        "td,cd->tc", branch_grad, out_full, preferred_element_type=F32
    ).astype(BF16)

    query_grad, kv_grads = [], [None] * (2 * KVH)
    for group in range(KVH):
        parts = attention_back(
            queries,
            kv_all,
            attended_parts[group],
            after(attended_grad, *query_grad[-1:]),
            lse[group],
            order_mine,
            pos_mine,
            order_keys,
            group,
        )
        query_grad.append(parts[0])
        kv_grads[group], kv_grads[KVH + group] = parts[1:]
    result = middle + line_reduce(
        after(out_mine, returned),
        after(out_other, returned),
        chips,
        [(branch_grad,), (attended_grad,), (query_grad[0],)],
    )
    kv_grads = jnp.concatenate(kv_grads, axis=1).reshape(2, chips, tok_rows, 2 * kv_width)
    kv_grad = line_reduce_now(kv_grads[0], kv_grads[1], chips, 3)
    turned_grad = rotate(
        jnp.concatenate(query_grad + [kv_grad[:, :kv_width]], axis=1).reshape(
            tok_rows, QUERY_HEADS + KVH, HEAD_SIZE
        ),
        cosine,
        -sine,
    ).reshape(tok_rows, width + kv_width)
    pre_grad = jnp.concatenate(
        [turned_grad.astype(BF16), kv_grad[:, kv_width:].astype(BF16)], axis=1
    )
    qkv_local = jnp.einsum("td,tc->dc", hidden_one, pre_grad, preferred_element_type=F32)
    hidden_one_grad = jnp.einsum("tc,dc->td", pre_grad, qkv_full, preferred_element_type=F32)
    unused_one, norm_one_back = jax.vjp(rms_scale, inputs, gain_a)
    input_part, gain_one_local = norm_one_back(hidden_one_grad)
    input_grad = (middle_grad + input_part).astype(BF16)

    first_local = jnp.concatenate([out_local, router_local, gain_two_local[:, None]], axis=1)
    first_grads = lax.psum(
        lax.psum_scatter(first_local.astype(BF16), "fsdp", scatter_dimension=0, tiled=True), "ctx"
    ).astype(F32)
    edge = width + 2 * kv_width
    extra_rows = jnp.pad(
        gain_one_local.reshape(fsdp, 1, 1, shard).astype(BF16),
        ((0, 0), (0, 1), (0, 15), (0, edge - shard)),
    )
    last_local = jnp.concatenate(
        [qkv_local.astype(BF16).reshape(fsdp, 2, shard // 2, edge), extra_rows], axis=2
    )
    last_grads = dense_reduce(last_local, fsdp, chips, 4)
    qkv_grads = last_grads[:, : shard // 2].reshape(shard, edge).astype(F32)
    return (
        result.astype(BF16)[None],
        input_grad[None],
        last_grads[0, shard // 2, :shard].astype(F32),
        first_grads[:, width + expert_count],
        qkv_grads[:, :width],
        qkv_grads[:, width : width + kv_width],
        qkv_grads[:, width + kv_width :],
        first_grads[:, :width],
        first_grads[:, width : width + expert_count],
        gate_grad_out,
        up_grad_out,
        down_grad_out,
    )


def solution(mesh):
    placed = (
        P("fsdp", "ctx", None),
        P("fsdp", "ctx", None),
        P("fsdp", None),
        P("fsdp", None),
        P("fsdp", "ctx", None),
        P("fsdp"),
        P("fsdp"),
        P("fsdp", None),
        P("fsdp", None),
        P("fsdp", None),
        P("fsdp", None),
        P("fsdp", None),
        P("ctx", "fsdp", None),
        P("ctx", "fsdp", None),
        P("ctx", None, "fsdp"),
    )
    return jax.shard_map(
        body,
        mesh=mesh,
        in_specs=placed,
        out_specs=(
            P("fsdp", "ctx", None),
            P("fsdp", "ctx", None),
            P("fsdp"),
            P("fsdp"),
            P("fsdp", None),
            P("fsdp", None),
            P("fsdp", None),
            P("fsdp", None),
            P("fsdp", None),
            P("ctx", "fsdp", None),
            P("ctx", "fsdp", None),
            P("ctx", None, "fsdp"),
        ),
        check_vma=False,
    )
```

time: 1670 us -> 1010 us (0.60)
  waiting for transfers between devices: 854 us -> 219 us
  Pallas kernels: 0 us -> 549 us
  matrix products: 300 us -> 33.8 us
  local copies, waits for them, and re-layouts: 266 us -> 60.8 us
  blocking collectives: 86 us -> 0 us
  other arithmetic: 111 us -> 82 us
  starting transfers between devices: 20.4 us -> 43.5 us
    pallas_call x0 -> x13, Pallas kernels: none -> 549 us  [the longest x3 200 us: gather(): pl.pallas_call(functools.partial(gather_kernel, len(dense), len(line), fs...]
    all_to_all x4 -> x0, waiting for transfers between devices: 432 us -> none  [the longest x1 124 us: body(): lax.all_to_all(outgoing, 'ctx', split_axis=1, concat_axis=1, tiled=True)]
    reduce_scatter x8 -> x0, waiting for transfers between devices: 288 us -> none  [the longest x1 60 us: body(): lax.psum_scatter(dense_local[2].astype(jnp.bfloat16), 'fsdp', scatter_dim...]
    dot_general x67 -> x10, matrix products: 300 us -> 33.8 us  [the longest x1 7.86 us: body(): jnp.einsum('tc,dc->td', pre_grad, qkv_full, preferred_element_type=F32)]
    ppermute x0 -> x21, waiting for transfers between devices: none -> 105 us  [the longest x6 76.4 us: line_reduce(): lax.ppermute(send_right, 'ctx', [(2 * z + k, 2 * z + 2 + k) for z in rang...]
    reduce_sum x13 -> x2, other arithmetic: 58.1 us -> 0.25 us  [the longest x1 0.23 us: body(): gate_weights = jnp.where(routed > 0, jax.nn.softmax(chosen, axis=-1), 0.0)]
    gather x4 -> x0, local copies, waits for them, and re-layouts: 51.6 us -> none  [the longest x1 16.2 us: body(): pair_pad[pair_table].reshape(local_experts, ctx_count, capacity, width)]
    all_gather x4 -> x0, waiting for transfers between devices: 50.3 us -> none  [the longest x1 50.3 us: body(): lax.all_gather(w_query, 'fsdp', axis=0, tiled=True)]
  transfers between devices with their start and end apart: 22 -> 29, of which waited for: 15 -> 8; matrix products, arithmetic and copies ran while one was open for 24% -> 15% of each run, Pallas kernels for 0% -> 42%
where the time goes in v1:
time: 1010 us; the launch traced here: 1000 us
  Pallas kernels  549 us (54%)
  waiting for transfers between devices  219 us (22%)
  other arithmetic  82 us (8%)
  local copies, waits for them, and re-layouts  60.8 us (6%)
  starting transfers between devices  43.5 us (4%)
  matrix products  33.8 us (3%)
  between operations  15.6 us (2%)
    pallas_call x3, Pallas kernels, gather(): pl.pallas_call(functools.partial(gather_kernel, len(dense), len(line), fs...  200 us
    pallas_call x1, Pallas kernels, dense_reduce(): pl.pallas_call(functools.partial(dense_reduce_kernel, fsdp, chips), out_s...  92.8 us
    ppermute x6, waiting for transfers between devices, line_reduce(): lax.ppermute(send_right, 'ctx', [(2 * z + k, 2 * z + 2 + k) for z in rang...  76.4 us
    pallas_call x2, Pallas kernels, attention_back(): pl.pallas_call(functools.partial(attention_back_kernel, HEAD_SIZE ** (-0....  62.8 us
    unnamed x12, waiting for transfers between devices  61 us
    pallas_call x1, Pallas kernels, expert_rows_pass(): pl.pallas_call(functools.partial(expert_kernel, capacity, local_experts,...  55 us
    psum x1, waiting for transfers between devices, body(): lax.psum(lax.psum_scatter(first_local.astype(BF16), 'fsdp', scatter_dimen...  52.8 us
    pallas_call x2, Pallas kernels, attention(): pl.pallas_call(functools.partial(attention_kernel, HEAD_SIZE ** (-0.5)),...  51.9 us
  transfers between devices with their start and end apart: 29, of which 8 were waited for; matrix products, arithmetic and copies ran while one was open for 15% of the time, Pallas kernels for 42%

profile of v1, /device:TPU:0, one launch (start us, length us, event | category | flops | bytes accessed | tf_op | source)
XLA Modules:
  0.0 1003.5 jit_solution(7124055240332561200)
XLA Ops:
  9.7 2.9 pad_maximum_fusion.3.refs_0_
  13.4 55.9 %gather.3 = (bf16[1536,2048]{1,0:T(8,128)(2,1)}, bf16[1536,128]{1,0:T(8,128)(2,1)}) custom-call(bf16[384,2048]{1,0:T(8,128)(2,1)} %pad_maximum_fusion.3.refs_0_, bf16[384,128]{1,0:T(8,128)(2,1)} %maximum_maximum_fusion.refs_1_), custom_call_target="tpu_custom_call" | custom-call | tf_op jit(solution)/shard_map/gather/pallas_call | solution.py:282
  70.1 4.5 collective-permute-start.1
  77.9 5.0 fusion.36
  84.6 1.8 slice.196
  86.4 2.2 copy.121
  94.0 54.4 %gather.4 = (bf16[1536,1536]{1,0:T(8,128)(2,1)}, bf16[2,4,384,512]{3,2,1,0:T(8,128)(2,1)}, f32[2,4,16,384]{3,2,1,0:T(8,128)}) custom-call(bf16[384,1536]{1,0:T(8,128)(2,1)} %refs_0_.1, bf16[384,512]{1,0:T(8,128)(2,1)} %pad_maximum_fusion.8.refs_1_, f32[16,384]{1,0:T(8,128)} %copy.125.refs_2_), custom_call_target="tpu_custom_call" | custom-call | tf_op jit(solution)/shard_map/gather/pallas_call | solution.py:282
  148.4 1.7 collective-permute-start.2
  156.8 26.1 %attention.2 = (bf16[384,768]{1,0:T(8,128)(2,1)}, f32[6,1,384]{2,1,0:T(1,128)}) custom-call(bf16[384,1536]{1,0:T(8,128)(2,1)} %copy.128.q_ref, bf16[3072,512]{1,0:T(8,128)(2,1)} %bitcast.150, bf16[3072,512]{1,0:T(8,128)(2,1)} %bitcast.151, s32[384,1]{1,0:T(8,128)} %copy.129.oq_ref, s32[384,1]{1,0:T(8,128)} %copy.130.pq_ref, ...), custom_call_target="tpu_custom_call" | custom-call | flops 3623878656 | bytes 2752512 | tf_op jit(solution)/shard_map/attention/pallas_call | solution.py:727
  189.0 27.6 %collective-permute-done.5 = bf16[384,1536]{1,0:T(8,128)(2,1)S(1)} collective-permute-done((bf16[384,1536]{1,0:T(8,128)(2,1)}, bf16[384,1536]{1,0:T(8,128)(2,1)S(1)}, u32[]{:S(2)}, u32[]{:S(2)}) %collective-permute-start.5) | collective-permute-done | bytes 1179680 | tf_op jit(solution)/shard_map/ppermute | solution.py:635
  216.7 3.6 pad_maximum_fusion.1.grad_mine_ref
  221.8 25.8 %attention.3 = (bf16[384,768]{1,0:T(8,128)(2,1)}, f32[6,1,384]{2,1,0:T(1,128)}) custom-call(bf16[384,1536]{1,0:T(8,128)(2,1)} %copy.131.q_ref, bf16[3072,512]{1,0:T(8,128)(2,1)} %bitcast.152, bf16[3072,512]{1,0:T(8,128)(2,1)} %bitcast.153, s32[384,1]{1,0:T(8,128)} %copy.129.oq_ref, s32[384,1]{1,0:T(8,128)} %copy.130.pq_ref, ...), custom_call_target="tpu_custom_call" | custom-call | flops 3623878656 | bytes 2752512 | tf_op jit(solution)/shard_map/attention/pallas_call | solution.py:727
  249.8 5.1 multiply_reduce_fusion.2
  260.5 89.5 %gather.5 = (bf16[2,4,384,1536]{3,2,1,0:T(8,128)(2,1)}, f32[2,4,16,384]{3,2,1,0:T(8,128)}) custom-call(bf16[384,1536]{1,0:T(8,128)(2,1)} %copy-done.2, f32[16,384]{1,0:T(8,128)} %copy.136.refs_1_), custom_call_target="tpu_custom_call" | custom-call | tf_op jit(solution)/shard_map/gather/pallas_call | solution.py:282
  350.1 55.0 %expert_rows.1 = (bf16[4,384,1536]{2,1,0:T(8,128)(2,1)}, bf16[4,384,1536]{2,1,0:T(8,128)(2,1)}, bf16[4,384,1664]{2,1,0:T(8,128)(2,1)}, bf16[4,384,1664]{2,1,0:T(...) custom-call(s32[1]{0:T(128)} %bitcast.14.first_ref, ...), custom_call_target="tpu_custom_call" | custom-call | flops 33822867456 | bytes 80000000 | tf_op jit(solution)/shard_map/expert_rows/pallas_call | solution.py:980
  405.2 12.2 %outer_products.5 = bf16[4,2,768,384]{3,2,1,0:T(8,128)(2,1)} custom-call(bf16[2,1024,768]{2,1,0:T(8,128)(2,1)} %get-tuple-element.88.left_ref, bf16[2,1024,1536]{2,1,0:T(8,128)(2,1)} %get-tuple-element.89.right_ref), custom_call_target="tpu_custom_call" | custom-call | flops 4831838208 | bytes 14000000 | tf_op jit(solution)/shard_map/outer_products/pallas_call | solution.py:1035
  417.4 11.4 %outer_products.4 = bf16[4,2,384,768]{3,2,1,0:T(8,128)(2,1)} custom-call(bf16[2,1024,1536]{2,1,0:T(8,128)(2,1)} %get-tuple-element.83.left_ref, bf16[2,1024,768]{2,1,0:T(8,128)(2,1)} %get-tuple-element.86.right_ref), custom_call_target="tpu_custom_call" | custom-call | flops 4831838208 | bytes 14000000 | tf_op jit(solution)/shard_map/outer_products/pallas_call | solution.py:1035
  429.7 11.7 %outer_products.3 = bf16[4,2,384,768]{3,2,1,0:T(8,128)(2,1)} custom-call(bf16[2,1024,1536]{2,1,0:T(8,128)(2,1)} %get-tuple-element.83.left_ref, bf16[2,1024,768]{2,1,0:T(8,128)(2,1)} %get-tuple-element.84.right_ref), custom_call_target="tpu_custom_call" | custom-call | flops 4831838208 | bytes 14000000 | tf_op jit(solution)/shard_map/outer_products/pallas_call | solution.py:1035
  441.5 3.1 bitcast_convert_fusion
  446.7 26.8 %collective-permute-done.8 = bf16[384,1664]{1,0:T(8,128)(2,1)S(1)} collective-permute-done((bf16[384,1664]{1,0:T(8,128)(2,1)S(1)}, bf16[384,1664]{1,0:T(8,128)(2,1)S(1)}, u32[]{:S(2)}, u32[]{:S(2)}) %collective-permute-start.8) | collective-permute-done | bytes 1277984 | tf_op jit(solution)/shard_map/ppermute | solution.py:658
  473.4 2.2 fusion.5
  475.6 4.6 collective-permute-start.9
  480.2 26.7 %collective-permute-done.9 = bf16[384,1664]{1,0:T(8,128)(2,1)S(1)} collective-permute-done((bf16[384,1664]{1,0:T(8,128)(2,1)S(1)}, bf16[384,1664]{1,0:T(8,128)(2,1)S(1)}, u32[]{:S(2)}, u32[]{:S(2)}) %collective-permute-start.9) | collective-permute-done | bytes 1277984 | tf_op jit(solution)/shard_map/ppermute | solution.py:658
  507.0 4.5 fusion.7
  512.2 5.9 collective-permute-start.10
  518.1 4.0 fusion.4
  523.5 3.3 broadcast_in_dim_reshape.10.ok_ref
  529.5 2.8 bitcast_convert_fusion.5
  532.3 3.0 reduce-scatter.17.cloned.1.call-done
  535.3 2.8 bitcast_convert_fusion.6
  538.2 57.1 %reduce-scatter.15.cloned.1.call-done = bf16[1,2,384,768]{3,2,1,0:T(8,128)(2,1)} async-done(((bf16[4,2,384,768]{3,2,1,0:T(8,128)(2,1)}), bf16[1,2,384,768]{3,2,1,0:T(8,128)(2,1)}) %reduce-scatter.15.cloned.1.call-update) | async-done | bytes 1179664
  595.3 2.8 bitcast_convert_fusion.7
  598.2 3.1 fusion.8
  604.4 2.0 fusion.54
  606.4 2.9 convolution_convert_fusion
  609.3 2.4 pad_maximum_fusion
  611.7 7.4 copy.148
  619.3 5.4 convolution_convert_fusion.2.do_ref
  624.7 31.7 %attention_back.2 = (f32[384,768]{1,0:T(8,128)}, bf16[3072,128]{1,0:T(8,128)(2,1)}, bf16[3072,128]{1,0:T(8,128)(2,1)}) custom-call(bf16[384,1536]{1,0:T(8,128)(2,1)} %copy.137.q_ref, bf16[3072,512]{1,0:T(8,128)(2,1)} %bitcast.154, bf16[3072,512]{1,0:T(8,128)(2,1)} %bitcast.155, bf16[384,768]{1,0:T(8,128)(2,1)} %get-tuple-element.66.o_ref, ...), custom_call_target="tpu_custom_call" | custom-call | flops 9059696640 | bytes 6094848 | tf_op jit(solution)/shard_map/attention_back/pallas_call | solution.py:830
  656.4 31.1 %attention_back.3 = (f32[384,768]{1,0:T(8,128)}, bf16[3072,128]{1,0:T(8,128)(2,1)}, bf16[3072,128]{1,0:T(8,128)(2,1)}) custom-call(bf16[384,1536]{1,0:T(8,128)(2,1)} %copy.137.q_ref, bf16[3072,512]{1,0:T(8,128)(2,1)} %bitcast.156, bf16[3072,512]{1,0:T(8,128)(2,1)} %bitcast.157, bf16[384,768]{1,0:T(8,128)(2,1)} %get-tuple-element.68.o_ref, ...), custom_call_target="tpu_custom_call" | custom-call | flops 9059696640 | bytes 6094848 | tf_op jit(solution)/shard_map/attention_back/pallas_call | solution.py:830
  687.5 4.1 bitcast_convert_fusion.2
  691.6 3.4 collective-permute-start.15
  696.3 1.7 collective-permute-start.18
  698.1 22.9 %collective-permute-done.15 = bf16[384,1536]{1,0:T(8,128)(2,1)S(1)} collective-permute-done((bf16[384,1536]{1,0:T(8,128)(2,1)S(1)}, bf16[384,1536]{1,0:T(8,128)(2,1)S(1)}, u32[]{:S(2)}, u32[]{:S(2)}) %collective-permute-start.15) | collective-permute-done | bytes 1179680 | tf_op jit(solution)/shard_map/ppermute | solution.py:658
  721.0 3.1 fusion.17
  724.0 5.4 collective-permute-start.16
  729.4 1.9 fusion.57
  731.3 51.6 %line_reduce.1 = f32[384,512]{1,0:T(8,128)} custom-call(bf16[4,384,512]{2,1,0:T(8,128)(2,1)} %bitcast.142, bf16[4,384,512]{2,1,0:T(8,128)(2,1)} %bitcast.141), custom_call_target="tpu_custom_call" | custom-call | tf_op jit(solution)/shard_map/line_reduce/pallas_call | solution.py:434
  785.6 3.0 pad_maximum_fusion.2
  788.6 3.4 copy.141
  792.8 2.1 subtract_convert_fusion
  795.2 5.9 fusion.19
  801.1 1.9 collective-permute-start.19
  803.1 7.9 fusion.10
  812.2 5.6 convolution_convert_fusion.1
  817.8 2.8 collective-permute-start.17
  820.6 3.4 fusion.16
  825.3 3.6 fusion.1.local_ref
  828.9 92.8 %dense_reduce.1 = bf16[2,208,2048]{2,1,0:T(8,128)(2,1)} custom-call(bf16[4,2,208,2048]{3,2,1,0:T(8,128)(2,1)} %fusion.1.local_ref), custom_call_target="tpu_custom_call" | custom-call | tf_op jit(solution)/shard_map/dense_reduce/pallas_call | solution.py:587
  927.8 2.5 copy.149
  930.3 6.0 fusion.24
  936.3 52.8 %all-reduce.6.cloned.1.call-done = bf16[384,1553]{0,1:T(8,128)(2,1)} async-done(((bf16[384,1553]{0,1:T(8,128)(2,1)}), bf16[384,1553]{0,1:T(8,128)(2,1)}) %all-reduce.6.cloned.1.call-update) | async-done | bytes 1192720 | tf_op jit(solution)/shard_map/psum | solution.py:1262
  989.1 2.8 slice.221
  991.9 3.1 copy.144
  (236 shorter events, 62.4 us)
Async XLA Ops:
  7.2 342.9 %all-gather.4.cloned.1.call-start = ((), (), s32[]{:S(2)}) async-start(), calls=%async_computation.4 | async-start | bytes 5898240 | tf_op jit(solution)/shard_map/all_gather | solution.py:1103
  12.6 63.3 %copy-start.53 = (s32[1,3]{1,0:T(1,128)S(1)}, s32[1,3]{1,0:T(1,128)}, u32[]{:S(2)}) copy-start(s32[1,3]{1,0:T(1,128)} %param.18) | copy-start | bytes 40
  13.4 64.1 %copy-start.10 = (bf16[1,384,1536]{2,1,0:T(8,128)(2,1)S(1)}, bf16[1,384,1536]{2,1,0:T(8,128)(2,1)}, u32[]{:S(2)}) copy-start(bf16[1,384,1536]{2,1,0:T(8,128)(2,1)} %param.15) | copy-start | bytes 3538948
  69.2 7.7 copy-start.12
  69.3 280.8 %all-gather.6.cloned.1.call-start = ((), (), s32[]{:S(2)}) async-start(), calls=%async_computation.5 | async-start | bytes 5898240 | tf_op jit(solution)/shard_map/all_gather | solution.py:1104
  70.0 280.1 %all-gather.8.cloned.1.call-start = ((), (), s32[]{:S(2)}) async-start(), calls=%async_computation.6 | async-start | bytes 5898240 | tf_op jit(solution)/shard_map/all_gather | solution.py:1105
  70.1 78.4 %collective-permute-start.1 = (bf16[384,1536]{1,0:T(8,128)(2,1)}, bf16[384,1536]{1,0:T(8,128)(2,1)}, u32[]{:S(2)}, u32[]{:S(2)}) collective-permute-start(bf16[384,1536]{1,0:T(8,128)(2,1)} %bitcast.16), channel_id=1, source_target_pairs={{0,8},{4,12},{8,16},{12,20},{16,24},{20,28},{1,9},{5,13},{9,17},{1... | collective-permute-start | bytes 3538952 | tf_op jit(solution)/shard_map/ppermute | solution.py:634
  74.6 76.9 %collective-permute-start = (bf16[384,1536]{1,0:T(8,128)(2,1)}, bf16[384,1536]{1,0:T(8,128)(2,1)}, u32[]{:S(2)}, u32[]{:S(2)}) collective-permute-start(bf16[384,1536]{1,0:T(8,128)(2,1)} %bitcast.16), channel_id=1, source_target_pairs={{8,0},{12,4},{16,8},{20,12},{24,16},{28,20},{9,1},{13,5},{17,9},{2... | collective-permute-start | bytes 3538952 | tf_op jit(solution)/shard_map/ppermute | solution.py:635
  76.8 6.1 copy-start.44
  76.8 79.2 %copy-start.41 = (s32[1,384]{1,0:T(1,128)}, s32[1,384]{1,0:T(1,128)S(1)}, u32[]{:S(2)}) copy-start(s32[1,384]{1,0:T(1,128)S(1)} %get-tuple-element.179.oq_ref) | copy-start | bytes 4612
  76.9 78.2 %copy-start.39 = (s32[384]{0:T(512)}, s32[384]{0:T(512)S(1)}, u32[]{:S(2)}) copy-start(s32[384]{0:T(512)S(1)} %select_reduce_fusion) | copy-start | bytes 4612
  77.5 5.4 copy-start.35
  77.8 5.1 copy-start.42
  77.8 5.0 copy-start.47
  84.6 4.0 copy-start.20
  89.9 2.3 copy-start.45
  90.8 59.9 %copy-start.46 = (s32[1,3072]{1,0:T(1,128)S(1)}, s32[1,3072]{1,0:T(1,128)}, u32[]{:S(2)}) copy-start(s32[1,3072]{1,0:T(1,128)} %param.17) | copy-start | bytes 36868
  90.8 62.0 %copy-start.9 = (bf16[384,14,64]{0,2,1:T(8,128)(2,1)S(1)}, bf16[384,14,64]{0,2,1:T(8,128)(2,1)}, u32[]{:S(2)}) copy-start(bf16[384,14,64]{0,2,1:T(8,128)(2,1)} %copy-done.8) | copy-start | bytes 2064388
  92.2 60.7 %copy-start.4 = (f32[384,16]{1,0:T(8,128)}, f32[384,16]{1,0:T(8,128)S(1)}, u32[]{:S(2)}) copy-start(f32[384,16]{1,0:T(8,128)S(1)} %copy.123) | copy-start | bytes 73732
  92.2 60.7 %copy-start.33 = (pred[384,16]{1,0:T(32,128)(4,1)}, pred[384,16]{1,0:T(32,128)(4,1)S(1)}, u32[]{:S(2)}) copy-start(pred[384,16]{1,0:T(32,128)(4,1)S(1)} %broadcast_compare_fusion) | copy-start | bytes 18436
  148.4 34.5 %collective-permute-start.2 = (bf16[384,1536]{1,0:T(8,128)(2,1)}, bf16[384,1536]{1,0:T(8,128)(2,1)}, u32[]{:S(2)}, u32[]{:S(2)}) collective-permute-start(bf16[384,1536]{1,0:T(8,128)(2,1)} %collective-permute-done.1), channel_id=1, source_target_pairs={{8,16},{12,20},{16,24},{20,28},{9,17},{13,21},{17,25},{21,29},{10,... | collective-permute-start | bytes 3538952 | tf_op jit(solution)/shard_map/ppermute | solution.py:634
  151.5 33.2 %collective-permute-start.4 = (bf16[384,1536]{1,0:T(8,128)(2,1)}, bf16[384,1536]{1,0:T(8,128)(2,1)}, u32[]{:S(2)}, u32[]{:S(2)}) collective-permute-start(bf16[384,1536]{1,0:T(8,128)(2,1)} %collective-permute-done), channel_id=1, source_target_pairs={{8,0},{12,4},{16,8},{20,12},{9,1},{13,5},{17,9},{21,13},{10,2},{14... | collective-permute-start | bytes 3538952 | tf_op jit(solution)/shard_map/ppermute | solution.py:635
  182.9 4.7 collective-permute-start.3
  183.7 345.8 %reduce-scatter.19.cloned.1.call-start = ((), (), s32[]{:S(2)}) async-start(), calls=%async_computation.11 | async-start | bytes 5898240
  184.7 31.9 %collective-permute-start.5 = (bf16[384,1536]{1,0:T(8,128)(2,1)}, bf16[384,1536]{1,0:T(8,128)(2,1)S(1)}, u32[]{:S(2)}, u32[]{:S(2)}) collective-permute-start(bf16[384,1536]{1,0:T(8,128)(2,1)} %collective-permute-done.4), channel_id=1, source_target_pairs={{8,0},{12,4},{9,1},{13,5},{10,2},{14,6},{11,3},{15,7}} | collective-permute-start | bytes 3538952 | tf_op jit(solution)/shard_map/ppermute | solution.py:635
  220.3 129.8 %collective-permute-start.6 = (bf16[4,384,1536]{2,1,0:T(8,128)(2,1)}, bf16[4,384,1536]{2,1,0:T(8,128)(2,1)}, u32[]{:S(2)}, u32[]{:S(2)}) collective-permute-start(bf16[4,384,1536]{2,1,0:T(8,128)(2,1)} %pad_maximum_fusion.1.grad_mine_ref), channel_id=1, source_target_pairs={{0,4},{4,0},{8,12},{12,8},{16,20},{20,16},{24,28},{28,24},{1,5},{5... | collective-permute-start | bytes 14155784 | tf_op jit(solution)/shard_map/ppermute | solution.py:642
  417.3 118.0 %reduce-scatter.17.cloned.1.call-start = ((), (), s32[]{:S(2)}) async-start(), calls=%async_computation.10 | async-start | bytes 5898240
  428.8 166.5 %reduce-scatter.15.cloned.1.call-start = ((), (), s32[]{:S(2)}) async-start(), calls=%async_computation.9 | async-start | bytes 5898240
  429.2 12.2 %collective-permute-start.7 = (bf16[4,384,1664]{2,1,0:T(8,128)(2,1)}, bf16[4,384,1664]{2,1,0:T(8,128)(2,1)}, u32[]{:S(2)}, u32[]{:S(2)}) collective-permute-start(bf16[4,384,1664]{2,1,0:T(8,128)(2,1)} %get-tuple-element.82), channel_id=1, source_target_pairs={{0,4},{4,0},{8,12},{12,8},{16,20},{20,16},{24,28},{28,24},{1,5},{5... | collective-permute-start | bytes 15335432 | tf_op jit(solution)/shard_map/ppermute | solution.py:646
  441.4 486.4 %reduce-scatter.13.cloned.1.call-start = ((), (), s32[]{:S(2)}) async-start(), calls=%async_computation.8 | async-start | bytes 6389760
  444.5 28.9 %collective-permute-start.8 = (bf16[384,1664]{1,0:T(8,128)(2,1)S(1)}, bf16[384,1664]{1,0:T(8,128)(2,1)S(1)}, u32[]{:S(2)}, u32[]{:S(2)}) collective-permute-start(bf16[384,1664]{1,0:T(8,128)(2,1)S(1)} %get-tuple-element.85), channel_id=1, source_target_pairs={{0,8},{4,12},{1,9},{5,13},{2,10},{6,14},{3,11},{7,15}} | collective-permute-start | bytes 3833864 | tf_op jit(solution)/shard_map/ppermute | solution.py:658
  445.9 34.3 %collective-permute-start.11 = (bf16[384,1664]{1,0:T(8,128)(2,1)S(1)}, bf16[384,1664]{1,0:T(8,128)(2,1)S(1)}, u32[]{:S(2)}, u32[]{:S(2)}) collective-permute-start(bf16[384,1664]{1,0:T(8,128)(2,1)S(1)} %get-tuple-element.91), channel_id=1, source_target_pairs={{24,16},{28,20},{25,17},{29,21},{26,18},{30,22},{27,19},{31,23}} | collective-permute-start | bytes 3833864 | tf_op jit(solution)/shard_map/ppermute | solution.py:663
  475.6 31.3 %collective-permute-start.9 = (bf16[384,1664]{1,0:T(8,128)(2,1)S(1)}, bf16[384,1664]{1,0:T(8,128)(2,1)S(1)}, u32[]{:S(2)}, u32[]{:S(2)}) collective-permute-start(bf16[384,1664]{1,0:T(8,128)(2,1)S(1)} %fusion.5), channel_id=1, source_target_pairs={{0,8},{4,12},{8,16},{12,20},{1,9},{5,13},{9,17},{13,21},{2,10},{6,... | collective-permute-start | bytes 3833864 | tf_op jit(solution)/shard_map/ppermute | solution.py:658
  511.5 6.7 collective-permute-start.12
  512.2 86.0 %collective-permute-start.10 = (bf16[384,1664]{1,0:T(8,128)(2,1)}, bf16[384,1664]{1,0:T(8,128)(2,1)}, u32[]{:S(2)}, u32[]{:S(2)}) collective-permute-start(bf16[384,1664]{1,0:T(8,128)(2,1)} %get-tuple-element.90), channel_id=1, source_target_pairs={{0,8},{4,12},{8,16},{12,20},{16,24},{20,28},{1,9},{5,13},{9,17},{1... | collective-permute-start | bytes 3833864 | tf_op jit(solution)/shard_map/ppermute | solution.py:658
  522.2 76.0 %collective-permute-start.13 = (bf16[384,1664]{1,0:T(8,128)(2,1)}, bf16[384,1664]{1,0:T(8,128)(2,1)}, u32[]{:S(2)}, u32[]{:S(2)}) collective-permute-start(bf16[384,1664]{1,0:T(8,128)(2,1)} %fusion.4), channel_id=1, source_target_pairs={{8,0},{12,4},{16,8},{20,12},{24,16},{28,20},{9,1},{13,5},{17,9},{2... | collective-permute-start | bytes 3833864 | tf_op jit(solution)/shard_map/ppermute | solution.py:663
  598.2 3.1 copy-start.6
  598.2 3.2 copy-start.16
  598.2 3.2 copy-start.38
  598.2 3.9 copy-start.14
  602.0 85.6 %collective-permute-start.14 = (bf16[4,384,1536]{2,1,0:T(8,128)(2,1)}, bf16[4,384,1536]{2,1,0:T(8,128)(2,1)}, u32[]{:S(2)}, u32[]{:S(2)}) collective-permute-start(bf16[4,384,1536]{2,1,0:T(8,128)(2,1)} %get-tuple-element.96), channel_id=1, source_target_pairs={{0,4},{4,0},{8,12},{12,8},{16,20},{20,16},{24,28},{28,24},{1,5},{5... | collective-permute-start | bytes 14155784 | tf_op jit(solution)/shard_map/ppermute | solution.py:646
  619.1 370.0 %all-reduce.6.cloned.1.call-start = ((), (), s32[]{:S(2)}) async-start(), calls=%async_computation.7 | async-start | bytes 2396160 | tf_op jit(solution)/shard_map/psum | solution.py:1262
  687.5 7.5 copy-start.23
  687.5 7.6 copy-start.25
  691.6 3.8 copy-start.22
  691.6 29.4 %collective-permute-start.15 = (bf16[384,1536]{1,0:T(8,128)(2,1)S(1)}, bf16[384,1536]{1,0:T(8,128)(2,1)S(1)}, u32[]{:S(2)}, u32[]{:S(2)}) collective-permute-start(bf16[384,1536]{1,0:T(8,128)(2,1)S(1)} %get-tuple-element.97), channel_id=1, source_target_pairs={{0,8},{4,12},{1,9},{5,13},{2,10},{6,14},{3,11},{7,15}} | collective-permute-start | bytes 3538952 | tf_op jit(solution)/shard_map/ppermute | solution.py:658
  696.3 98.9 %collective-permute-start.18 = (bf16[384,1536]{1,0:T(8,128)(2,1)}, bf16[384,1536]{1,0:T(8,128)(2,1)}, u32[]{:S(2)}, u32[]{:S(2)}) collective-permute-start(bf16[384,1536]{1,0:T(8,128)(2,1)} %get-tuple-element.102), channel_id=1, source_target_pairs={{24,16},{28,20},{25,17},{29,21},{26,18},{30,22},{27,19},{31,23}} | collective-permute-start | bytes 3538952 | tf_op jit(solution)/shard_map/ppermute | solution.py:663
  724.0 71.2 %collective-permute-start.16 = (bf16[384,1536]{1,0:T(8,128)(2,1)}, bf16[384,1536]{1,0:T(8,128)(2,1)}, u32[]{:S(2)}, u32[]{:S(2)}) collective-permute-start(bf16[384,1536]{1,0:T(8,128)(2,1)} %fusion.17), channel_id=1, source_target_pairs={{0,8},{4,12},{8,16},{12,20},{1,9},{5,13},{9,17},{13,21},{2,10},{6,... | collective-permute-start | bytes 3538952 | tf_op jit(solution)/shard_map/ppermute | solution.py:658
  731.3 54.3 %copy-start.19 = (f32[384,768]{1,0:T(8,128)S(1)}, f32[384,768]{1,0:T(8,128)}, u32[]{:S(2)}) copy-start(f32[384,768]{1,0:T(8,128)} %get-tuple-element.100) | copy-start | bytes 3538948
  788.6 3.4 copy-start.26
  788.6 4.2 copy-start.21
  788.6 4.2 copy-start.28
  795.1 7.9 copy-start.18
  795.1 7.9 copy-start.11
  795.1 7.9 copy-start.31
  795.2 7.9 copy-start.36
  795.2 7.9 copy-start.48
  801.1 19.5 %collective-permute-start.19 = (bf16[384,1536]{1,0:T(8,128)(2,1)}, bf16[384,1536]{1,0:T(8,128)(2,1)}, u32[]{:S(2)}, u32[]{:S(2)}) collective-permute-start(bf16[384,1536]{1,0:T(8,128)(2,1)} %get-tuple-element.103), channel_id=1, source_target_pairs={{16,8},{20,12},{24,16},{28,20},{17,9},{21,13},{25,17},{29,21},{18,... | collective-permute-start | bytes 3538952 | tf_op jit(solution)/shard_map/ppermute | solution.py:663
  817.8 7.5 copy-start.40
  817.8 112.5 %collective-permute-start.17 = (bf16[384,1536]{1,0:T(8,128)(2,1)}, bf16[384,1536]{1,0:T(8,128)(2,1)}, u32[]{:S(2)}, u32[]{:S(2)}) collective-permute-start(bf16[384,1536]{1,0:T(8,128)(2,1)} %get-tuple-element.101), channel_id=1, source_target_pairs={{0,8},{4,12},{8,16},{12,20},{16,24},{20,28},{1,9},{5,13},{9,17},{1... | collective-permute-start | bytes 3538952 | tf_op jit(solution)/shard_map/ppermute | solution.py:658
  824.0 106.3 %collective-permute-start.20 = (bf16[384,1536]{1,0:T(8,128)(2,1)}, bf16[384,1536]{1,0:T(8,128)(2,1)}, u32[]{:S(2)}, u32[]{:S(2)}) collective-permute-start(bf16[384,1536]{1,0:T(8,128)(2,1)} %fusion.16), channel_id=1, source_target_pairs={{8,0},{12,4},{16,8},{20,12},{24,16},{28,20},{9,1},{13,5},{17,9},{2... | collective-permute-start | bytes 3538952 | tf_op jit(solution)/shard_map/ppermute | solution.py:663
  923.6 2.7 copy-start.43
  923.6 2.7 copy-start.52
  991.9 3.1 copy-start.1
  (20 other events, 27.9 us)
Sparse Core Ops, SparseCore 0:
  69.4 78.5 all-gather.3
  149.8 57.5 all-gather.5
  209.2 56.9 all-gather.7
  417.5 57.8 reduce-scatter.18
  478.2 57.0 reduce-scatter.16
  538.2 57.0 reduce-scatter.14
  619.2 60.4 reduce-scatter.12
  930.4 58.6 all-reduce.5

commit v2 on v1

--- a/solution.py
+++ b/solution.py
@@ -17,6 +17,7 @@
 LOG2E = 1.4426950408889634
 LANES = 128
 SLOT_STEP = 64
+DENSE_PIECE = 1024
 KEY_TILE = 512
 VMEM_BYTES = 60 * 1024 * 1024
 MESH = pl.DeviceIdType.MESH
@@ -98,6 +99,22 @@
         pl.semaphore_wait(barrier, known + 1)
 
 
+class Bounce:
+    def __init__(self, src, dst, buffer, sem):
+        self.inward = pltpu.make_async_copy(src, buffer, sem)
+        self.outward = pltpu.make_async_copy(buffer, dst, sem)
+
+    def start(self):
+        self.inward.start()
+
+    def turn(self):
+        self.inward.wait()
+        self.outward.start()
+
+    def wait(self):
+        self.outward.wait()
+
+
 def remote(src, dst, send_sem, recv_sem, device):
     return pltpu.make_async_remote_copy(
         src_ref=src,
@@ -111,7 +128,7 @@
 
 class DenseGather:
     def __init__(self, ins, outs, sems, fsdp):
-        local_sem, send_sem, recv_sem, pass_sem, took_sem = sems
+        buffers, local_sem, send_sem, recv_sem, pass_sem, took_sem = sems
         ctx, me, chip, core, sibling = place()
         self.sends, self.passes, self.locals = [], [], []
         for i in range(len(ins)):
@@ -132,9 +149,7 @@
                     remote(got, got, pass_sem.at[i, j], took_sem.at[i, j], (sibling, me))
                 )
             self.locals.append(
-                pltpu.make_async_copy(
-                    ins[i], outs[i].at[pl.ds(me * rows, rows)], local_sem.at[i]
-                )
+                Bounce(ins[i], outs[i].at[pl.ds(me * rows, rows)], buffers[i], local_sem.at[i])
             )
 
     def start(self):
@@ -142,6 +157,8 @@
             copy.start()
 
     def finish(self):
+        for copy in self.locals:
+            copy.turn()
         for send, copy in zip(self.sends, self.passes):
             send.wait_recv()
             copy.start()
@@ -151,16 +168,19 @@
             copy.wait()
 
 
-def dense_sems(count, fsdp):
-    return [pltpu.SemaphoreType.DMA((count,))] + [
-        pltpu.SemaphoreType.DMA((count, fsdp - 1)) for unused in range(4)
-    ]
+def dense_scratch(arrays, fsdp):
+    count = len(arrays)
+    return (
+        [pltpu.VMEM(a.shape, a.dtype) for a in arrays]
+        + [pltpu.SemaphoreType.DMA((count,))]
+        + [pltpu.SemaphoreType.DMA((count, fsdp - 1)) for unused in range(4)]
+    )
 
 
 class LineGather:
     def __init__(self, ins, outs, sems, chips):
         self.ins, self.outs, self.chips = ins, outs, chips
-        self.sems = sems
+        self.buffers, self.sems = sems[:-7], sems[-7:]
         self.ctx, self.me, self.chip, core, self.sibling = place()
         self.count = len(ins)
 
@@ -194,99 +214,142 @@
         )
 
     def local(self, i):
-        return pltpu.make_async_copy(self.ins[i], self.outs[i].at[0, 0], self.sems[0].at[i])
-
-    def run(self):
+        return Bounce(self.ins[i], self.outs[i].at[0, 0], self.buffers[i], self.sems[0].at[i])
+
+    def send(self, step):
         chip, chips, count = self.chip, self.chips, self.count
-        for step in range(chips - 1):
-
-            @pl.when((chip + 1 < chips) & (chip >= step))
-            def _():
-                for i in range(count):
-                    self.to_right(i, step).start()
-
-            @pl.when((chip >= 1) & (chip + step < chips))
-            def _():
-                for i in range(count):
-                    self.to_left(i, step).start()
-
-            if step == 0:
-                for i in range(count):
-                    self.across(i, 0).start()
-                    self.local(i).start()
-
-            @pl.when(chip >= step + 1)
-            def _():
-                for i in range(count):
-                    self.to_right(i, step).wait_recv()
-                    self.across(i, chips - 1 - step).start()
-
-            @pl.when(chip + step + 1 < chips)
-            def _():
-                for i in range(count):
-                    self.to_left(i, step).wait_recv()
-                    self.across(i, step + 1).start()
-
-    def finish(self):
+
+        @pl.when((chip + 1 < chips) & (chip >= step))
+        def _():
+            for i in range(count):
+                self.to_right(i, step).start()
+
+        @pl.when((chip >= 1) & (chip + step < chips))
+        def _():
+            for i in range(count):
+                self.to_left(i, step).start()
+
+    def receive(self, step):
         chip, chips, count = self.chip, self.chips, self.count
-        for step in range(chips - 1):
-
-            @pl.when((chip + 1 < chips) & (chip >= step))
-            def _():
-                for i in range(count):
-                    self.to_right(i, step).wait_send()
-
-            @pl.when((chip >= 1) & (chip + step < chips))
-            def _():
-                for i in range(count):
-                    self.to_left(i, step).wait_send()
-
-        for slot in range(chips):
+
+        @pl.when(chip >= step + 1)
+        def _():
             for i in range(count):
-                self.across(i, slot).wait()
-        for i in range(count):
+                self.to_right(i, step).wait_recv()
+                self.across(i, chips - 1 - step).start()
+
+        @pl.when(chip + step + 1 < chips)
+        def _():
+            for i in range(count):
+                self.to_left(i, step).wait_recv()
+                self.across(i, step + 1).start()
+
+    def own(self):
+        for i in range(self.count):
+            self.across(i, 0).start()
+            self.local(i).start()
+
+    def turn_own(self):
+        for i in range(self.count):
+            self.local(i).turn()
+
+    def finish_own(self):
+        for i in range(self.count):
+            self.across(i, 0).wait()
             self.local(i).wait()
 
-
-def line_sems(count, chips):
+    def finish(self, step):
+        chip, chips, count = self.chip, self.chips, self.count
+
+        @pl.when((chip + 1 < chips) & (chip >= step))
+        def _():
+            for i in range(count):
+                self.to_right(i, step).wait_send()
+
+        @pl.when((chip >= 1) & (chip + step < chips))
+        def _():
+            for i in range(count):
+                self.to_left(i, step).wait_send()
+
+        @pl.when(chip >= step + 1)
+        def _():
+            for i in range(count):
+                self.across(i, chips - 1 - step).wait()
+
+        @pl.when(chip + step + 1 < chips)
+        def _():
+            for i in range(count):
+                self.across(i, step + 1).wait()
+
+
+def line_scratch(arrays, chips):
+    count = len(arrays)
     return (
-        [pltpu.SemaphoreType.DMA((count,))]
+        [pltpu.VMEM(a.shape, a.dtype) for a in arrays if a is not None]
+        + [pltpu.SemaphoreType.DMA((count,))]
         + [pltpu.SemaphoreType.DMA((count, chips - 1)) for unused in range(4)]
         + [pltpu.SemaphoreType.DMA((count, chips)) for unused in range(2)]
     )
 
 
-def gather_kernel(dense, line, fsdp, chips, *refs):
-    ins, outs, sems = refs[: dense + line], refs[dense + line : 2 * (dense + line)], None
-    sems = refs[2 * (dense + line) :]
+def gather_kernel(dense, line, resumed, steps, fsdp, chips, *refs):
+    count = dense + line + resumed
+    ins, outs, scratch = refs[:count], refs[count : 2 * count], refs[2 * count :]
     ctx, me, chip, core, sibling = place()
     greet(chips, peers_of(me, fsdp) if dense else [], line > 0)
+    split = dense + line
     if dense:
-        first = DenseGather(ins[:dense], outs[:dense], sems[:5], fsdp)
+        own, scratch = scratch[: dense + 5], scratch[dense + 5 :]
+        first = DenseGather(
+            ins[:dense], outs[:dense], (own[:dense],) + tuple(own[dense:]), fsdp
+        )
         first.start()
     if line:
-        second = LineGather(ins[dense:], outs[dense:], sems[-7:], chips)
-        second.run()
+        own, scratch = scratch[: line + 7], scratch[line + 7 :]
+        second = LineGather(ins[dense:split], outs[dense:split], own, chips)
+        for step in range(steps):
+            second.send(step)
+            if step == 0:
+                second.own()
+            second.receive(step)
+            if step == 0:
+                second.turn_own()
+    if resumed:
+        third = LineGather([None], outs[split:], scratch, chips)
+        third.send(chips - 2)
+        third.receive(chips - 2)
     if dense:
         first.finish()
     if line:
-        second.finish()
-
-
-def gather(dense, line, fsdp, chips, collective_id):
-    arrays = list(dense) + list(line)
+        second.finish_own()
+        for step in range(steps):
+            second.finish(step)
+    if resumed:
+        third.finish(chips - 2)
+
+
+def gather(dense, line, steps, fsdp, chips, collective_id, resumed=()):
+    arrays = list(dense) + list(line) + list(resumed)
     count = len(arrays)
-    scratch = (dense_sems(len(dense), fsdp) if dense else []) + (
-        line_sems(len(line), chips) if line else []
-    )
+    scratch = (dense_scratch(dense, fsdp) if dense else []) + (
+        line_scratch(line, chips) if line else []
+    )
+    if resumed:
+        scratch = scratch + line_scratch([None], chips)
     return pl.pallas_call(
-        functools.partial(gather_kernel, len(dense), len(line), fsdp, chips),
+        functools.partial(
+            gather_kernel, len(dense), len(line), len(resumed), steps, fsdp, chips
+        ),
         out_shape=[jax.ShapeDtypeStruct((fsdp * a.shape[0],) + a.shape[1:], a.dtype) for a in dense]
-        + [jax.ShapeDtypeStruct((2, chips) + a.shape, a.dtype) for a in line],
+        + [jax.ShapeDtypeStruct((2, chips) + a.shape, a.dtype) for a in line]
+        + [jax.ShapeDtypeStruct(a.shape, a.dtype) for a in resumed],
         in_specs=[pl.BlockSpec(memory_space=pl.ANY)] * count,
         out_specs=[pl.BlockSpec(memory_space=pl.ANY)] * count,
         scratch_shapes=scratch,
-        compiler_params=pltpu.CompilerParams(collective_id=collective_id, has_side_effects=True),
+        input_output_aliases={count - 1: count - 1} if resumed else {},
+        compiler_params=pltpu.CompilerParams(
+            collective_id=collective_id, has_side_effects=True, vmem_limit_bytes=VMEM_BYTES
+        ),
         name="gather",
     )(*arrays)
 
@@ -298,104 +361,107 @@
     return total
 
 
-def line_sum(chips, first, take, sends, gots, sems, done):
-    ctx, me, chip, core, sibling = place()
-    send_right, send_left = sends
-    got_right, got_left = gots
-    right_send, right_recv, left_send, left_recv = sems
-
-    def right(step):
+class LineSum:
+    def __init__(self, chips, held, keep, gots, sems):
+        self.chips, self.held, self.keep = chips, held, keep
+        self.got_right, self.got_left = gots
+        self.sems = sems
+        self.ctx, self.me, self.chip, core, sibling = place()
+
+    def right(self, step):
         return remote(
-            send_right.at[step],
-            got_right.at[step],
-            right_send.at[step],
-            right_recv.at[step],
-            (ctx + 2, me),
-        )
-
-    def left(step):
+            self.keep(self.chips - 1 - step),
+            self.got_right.at[step],
+            self.sems[0].at[step],
+            self.sems[1].at[step],
+            (self.ctx + 2, self.me),
+        )
+
+    def left(self, step):
         return remote(
-            send_left.at[step],
-            got_left.at[step],
-            left_send.at[step],
-            left_recv.at[step],
-            (ctx - 2, me),
-        )
-
-    for step in range(chips - 1):
+            self.keep(step + 1),
+            self.got_left.at[step],
+            self.sems[2].at[step],
+            self.sems[3].at[step],
+            (self.ctx - 2, self.me),
+        )
+
+    def step(self, step):
+        chip, chips = self.chip, self.chips
         far_right, far_left = chips - 1 - step, step + 1
 
         @pl.when(chip <= step)
         def _():
-            take(far_right)
+            parts = self.held(far_right)
             if step == 0:
-                send_right[step] = add(*first(far_right)).astype(BF16)
+                self.keep(far_right)[...] = add(*parts()).astype(BF16)
             else:
 
                 @pl.when(chip == 0)
                 def _():
-                    send_right[step] = add(*first(far_right)).astype(BF16)
+                    self.keep(far_right)[...] = add(*parts()).astype(BF16)
 
                 @pl.when(chip >= 1)
                 def _():
-                    right(step - 1).wait_recv()
-                    send_right[step] = add(*first(far_right), got_right[step - 1]).astype(BF16)
-
-            right(step).start()
+                    self.right(step - 1).wait_recv()
+                    total = add(*parts(), self.got_right[step - 1])
+                    self.keep(far_right)[...] = total.astype(BF16)
+
+            self.right(step).start()
 
         @pl.when(chip >= chips - 1 - step)
         def _():
-            take(far_left)
+            parts = self.held(far_left)
             if step == 0:
-                send_left[step] = add(*first(far_left)).astype(BF16)
+                self.keep(far_left)[...] = add(*parts()).astype(BF16)
             else:
 
                 @pl.when(chip == chips - 1)
                 def _():
-                    send_left[step] = add(*first(far_left)).astype(BF16)
+                    self.keep(far_left)[...] = add(*parts()).astype(BF16)
 
                 @pl.when(chip < chips - 1)
                 def _():
-                    left(step - 1).wait_recv()
-                    send_left[step] = add(*first(far_left), got_left[step - 1]).astype(BF16)
-
-            left(step).start()
-
-    last = chips - 2
-    take(0)
-
-    @pl.when(chip == 0)
-    def _():
-        left(last).wait_recv()
-        done(add(*first(0), got_left[last]))
-
-    @pl.when(chip == chips - 1)
-    def _():
-        right(last).wait_recv()
-        done(add(*first(0), got_right[last]))
-
-    @pl.when((chip >= 1) & (chip < chips - 1))
-    def _():
-        left(last).wait_recv()
-        right(last).wait_recv()
-        done(add(*first(0), got_left[last], got_right[last]))
-
-    def finish():
-        for step in range(chips - 1):
-
-            @pl.when(chip <= step)
+                    self.left(step - 1).wait_recv()
+                    total = add(*parts(), self.got_left[step - 1])
+                    self.keep(far_left)[...] = total.astype(BF16)
+
+            self.left(step).start()
+
+    def total(self, done):
+        chip, chips, last = self.chip, self.chips, self.chips - 2
+        parts = self.held(0)
+
+        @pl.when(chip == 0)
+        def _():
+            self.left(last).wait_recv()
+            done(add(*parts(), self.got_left[last]))
+
+        @pl.when(chip == chips - 1)
+        def _():
+            self.right(last).wait_recv()
+            done(add(*parts(), self.got_right[last]))
+
+        @pl.when((chip >= 1) & (chip < chips - 1))
+        def _():
+            self.left(last).wait_recv()
+            self.right(last).wait_recv()
+            done(add(*parts(), self.got_left[last], self.got_right[last]))
+
+    def finish(self):
+        for step in range(self.chips - 1):
+
+            @pl.when(self.chip <= step)
             def _():
-                right(step).wait_send()
-
-            @pl.when(chip >= chips - 1 - step)
+                self.right(step).wait_send()
+
+            @pl.when(self.chip >= self.chips - 1 - step)
             def _():
-                left(step).wait_send()
-
-    return finish
+                self.left(step).wait_send()
 
 
 def line_reduce_kernel(
-    chips, mine_ref, other_ref, out_ref, pair, sr, sl, gr, gl, ps, pr, s0, s1, s2, s3
+    chips, mine_ref, other_ref, out_ref, pair, gr, gl, ps, pr, s0, s1, s2, s3
 ):
     ctx, me, chip, core, sibling = place()
     greet(chips, [], True)
@@ -411,19 +477,19 @@
     for r in order + [0]:
         swaps[r].start()
 
+    def held(r):
+        swaps[r].wait_recv()
+        return lambda: (mine_ref[r], pair[r])
+
+    line = LineSum(chips, held, lambda r: pair.at[r], (gr, gl), (s0, s1, s2, s3))
+    for step in range(chips - 1):
+        line.step(step)
+
     def done(total):
         out_ref[...] = total
 
-    finish = line_sum(
-        chips,
-        lambda r: (mine_ref[r], pair[r]),
-        lambda r: swaps[r].wait_recv(),
-        (sr, sl),
-        (gr, gl),
-        (s0, s1, s2, s3),
-        done,
-    )
-    finish()
+    line.total(done)
+    line.finish()
     for swap in swaps:
         swap.wait_send()
 
@@ -437,7 +503,7 @@
         in_specs=[vmem, vmem],
         out_specs=vmem,
         scratch_shapes=[pltpu.VMEM((chips, rows, width), BF16)]
-        + [pltpu.VMEM((chips - 1, rows, width), BF16) for unused in range(4)]
+        + [pltpu.VMEM((chips - 1, rows, width), BF16) for unused in range(2)]
         + [pltpu.SemaphoreType.DMA((chips,)) for unused in range(2)]
         + [pltpu.SemaphoreType.DMA((chips - 1,)) for unused in range(4)],
         compiler_params=pltpu.CompilerParams(
@@ -447,229 +513,246 @@
     )(mine, other)
 
 
-def dense_reduce_kernel(
-    fsdp,
-    chips,
-    local_ref,
-    out_ref,
-    pair,
-    mine,
-    cross,
-    sums,
-    sr,
-    sl,
-    gr,
-    gl,
-    spread,
-    ps,
-    pr,
-    xs,
-    xr,
-    s0,
-    s1,
-    s2,
-    s3,
-    g0,
-    g1,
-    g2,
-    g3,
-    a0,
-    a1,
-):
+DENSE_BUFFERS = 6
+DENSE_SEMS = 14
+
+
+class DenseSum:
+    def __init__(self, local, out, buffers, sems, fsdp, chips):
+        self.local, self.out = local, out
+        self.pair, self.cross, self.sums, got_right, got_left, self.spread = buffers
+        self.sems = sems
+        self.chips = chips
+        self.ctx, self.me, self.chip, self.core, self.sibling = place()
+        self.owners = peers_of(self.me, fsdp) + [self.me]
+        self.cut = out.shape[2] // chips
+        self.line = LineSum(
+            chips,
+            lambda r: lambda: (self.sums[:, self.columns(r)],),
+            lambda r: self.keep_ref(r),
+            (got_right, got_left),
+            sems[4:8],
+        )
+
+    def keep_ref(self, r):
+        return self.sums.at[:, self.columns(r)]
+
+    def columns(self, r):
+        owner = lax.rem(self.chip + r, self.chips)
+        return pl.ds(pl.multiple_of(owner * self.cut, LANES), self.cut)
+
+    def swap(self, j):
+        return remote(
+            self.local.at[self.owners[j], 1 - self.core],
+            self.pair.at[j],
+            self.sems[0].at[j],
+            self.sems[1].at[j],
+            (self.sibling, self.me),
+        )
+
+    def crossing(self, j):
+        return remote(
+            self.pair.at[j],
+            self.cross.at[j],
+            self.sems[2].at[j],
+            self.sems[3].at[j],
+            (self.ctx, self.owners[j]),
+        )
+
+    def to_right(self, step):
+        return remote(
+            self.spread.at[0, (self.chips - step) % self.chips],
+            self.spread.at[0, self.chips - 1 - step],
+            self.sems[8].at[step],
+            self.sems[9].at[step],
+            (self.ctx + 2, self.me),
+        )
+
+    def to_left(self, step):
+        return remote(
+            self.spread.at[0, step],
+            self.spread.at[0, step + 1],
+            self.sems[10].at[step],
+            self.sems[11].at[step],
+            (self.ctx - 2, self.me),
+        )
+
+    def across(self, slot):
+        return remote(
+            self.spread.at[0, slot],
+            self.spread.at[1, slot],
+            self.sems[12].at[slot],
+            self.sems[13].at[slot],
+            (self.sibling, self.me),
+        )
+
+    def start(self):
+        for j in range(len(self.owners)):
+            self.swap(j).start()
+
+    def cross_over(self):
+        for j, owner in enumerate(self.owners):
+            self.swap(j).wait_recv()
+            self.pair[j] = add(self.local[owner, self.core], self.pair[j]).astype(BF16)
+            if j < len(self.owners) - 1:
+                self.crossing(j).start()
+
+    def stages(self):
+        chip, chips = self.chip, self.chips
+
+        def open_up():
+            for j in range(len(self.owners) - 1):
+                self.crossing(j).wait_recv()
+            self.sums[...] = add(
+                *[self.cross[j] for j in range(len(self.owners) - 1)],
+                self.pair[len(self.owners) - 1],
+            ).astype(BF16)
+            self.line.step(0)
+
+        def summed():
+            def done(total):
+                self.spread[0, 0] = total.astype(BF16)
+
+            self.line.total(done)
+            hand_on(0)
+
+        def hand_on(step):
+            @pl.when((chip + 1 < chips) & (chip >= step))
+            def _():
+                self.to_right(step).start()
+
+            @pl.when((chip >= 1) & (chip + step < chips))
+            def _():
+                self.to_left(step).start()
+
+            if step == 0:
+                self.across(0).start()
+
+        def take(step):
+            @pl.when(chip >= step + 1)
+            def _():
+                self.to_right(step).wait_recv()
+                self.across(chips - 1 - step).start()
+
+            @pl.when(chip + step + 1 < chips)
+            def _():
+                self.to_left(step).wait_recv()
+                self.across(step + 1).start()
+
+        def pass_on(step):
+            def run():
+                take(step - 1)
+                hand_on(step)
+
+            return run
+
+        def line_step(step):
+            return lambda: self.line.step(step)
+
+        return (
+            [open_up]
+            + [line_step(step) for step in range(1, chips - 1)]
+            + [summed]
+            + [pass_on(step) for step in range(1, chips - 1)]
+            + [lambda: take(chips - 2)]
+        )
+
+    def finish(self):
+        chip, chips = self.chip, self.chips
+        for r in range(chips):
+            self.out[self.core, :, self.columns(r)] = self.spread[0, r]
+        for r in range(chips):
+            self.across(r).wait()
+            self.out[1 - self.core, :, self.columns(r)] = self.spread[1, r]
+        for step in range(chips - 1):
+
+            @pl.when((chip + 1 < chips) & (chip >= step))
+            def _():
+                self.to_right(step).wait_send()
+
+            @pl.when((chip >= 1) & (chip + step < chips))
+            def _():
+                self.to_left(step).wait_send()
+
+        self.line.finish()
+        for j in range(len(self.owners) - 1):
+            self.crossing(j).wait_send()
+        for j in range(len(self.owners)):
+            self.swap(j).wait_send()
+
+
+def dense_reduce_kernel(fsdp, chips, cuts, *refs):
+    count = len(cuts)
+    arrays = max(cut[0] for cut in cuts) + 1
+    ins, outs, rest = refs[:arrays], refs[arrays : 2 * arrays], refs[2 * arrays :]
     ctx, me, chip, core, sibling = place()
-    peers = peers_of(me, fsdp)
-    greet(chips, peers, True)
-    cut = sums.shape[1] // chips
-    owners = peers + [me]
-
-    swaps = [
-        remote(local_ref.at[owner, 1 - core], pair.at[j], ps.at[j], pr.at[j], (sibling, me))
-        for j, owner in enumerate(owners)
-    ]
-    for swap in swaps:
-        swap.start()
-
-    crossings = []
-    for j, owner in enumerate(owners):
-        swaps[j].wait_recv()
-        mine[j] = add(local_ref[owner, core], pair[j]).astype(BF16)
-        if j < len(peers):
-            copy = remote(mine.at[j], cross.at[j], xs.at[j], xr.at[j], (ctx, owner))
-            copy.start()
-            crossings.append(copy)
-    for copy in crossings:
-        copy.wait_recv()
-    sums[...] = add(mine[len(peers)], *[cross[j] for j in range(len(peers))]).astype(BF16)
-
-    def columns(r):
-        owner = lax.rem(chip + r, chips)
-        return pl.ds(pl.multiple_of(owner * cut, LANES), cut)
-
-    def done(total):
-        spread[0, 0] = total.astype(BF16)
-
-    finish = line_sum(
-        chips,
-        lambda r: (sums[:, columns(r)],),
-        lambda r: None,
-        (sr, sl),
-        (gr, gl),
-        (s0, s1, s2, s3),
-        done,
-    )
-
-    def to_right(step):
-        return remote(
-            spread.at[0, (chips - step) % chips],
-            spread.at[0, chips - 1 - step],
-            g0.at[step],
-            g1.at[step],
-            (ctx + 2, me),
-        )
-
-    def to_left(step):
-        return remote(
-            spread.at[0, step], spread.at[0, step + 1], g2.at[step], g3.at[step], (ctx - 2, me)
-        )
-
-    def across(slot):
-        return remote(
-            spread.at[0, slot], spread.at[1, slot], a0.at[slot], a1.at[slot], (sibling, me)
-        )
-
-    for step in range(chips - 1):
-
-        @pl.when((chip + 1 < chips) & (chip >= step))
-        def _():
-            to_right(step).start()
-
-        @pl.when((chip >= 1) & (chip + step < chips))
-        def _():
-            to_left(step).start()
-
-        if step == 0:
-            across(0).start()
-
-        @pl.when(chip >= step + 1)
-        def _():
-            to_right(step).wait_recv()
-            across(chips - 1 - step).start()
-
-        @pl.when(chip + step + 1 < chips)
-        def _():
-            to_left(step).wait_recv()
-            across(step + 1).start()
-
-    for r in range(chips):
-        out_ref[core, :, columns(r)] = spread[0, r]
-    for r in range(chips):
-        across(r).wait()
-        out_ref[1 - core, :, columns(r)] = spread[1, r]
-    for step in range(chips - 1):
-
-        @pl.when((chip + 1 < chips) & (chip >= step))
-        def _():
-            to_right(step).wait_send()
-
-        @pl.when((chip >= 1) & (chip + step < chips))
-        def _():
-            to_left(step).wait_send()
-
-    finish()
-    for copy in crossings + swaps:
-        copy.wait_send()
-
-
-def dense_reduce(local, fsdp, chips, collective_id):
-    unused, unused_two, rows, width = local.shape
-    cut = width // chips
+    greet(chips, peers_of(me, fsdp), True)
+    sums = []
+    for i, (which, start, size) in enumerate(cuts):
+        buffers = rest[i * DENSE_BUFFERS : (i + 1) * DENSE_BUFFERS]
+        sems = rest[count * DENSE_BUFFERS + i * DENSE_SEMS :][:DENSE_SEMS]
+        sums.append(
+            DenseSum(
+                ins[which].at[:, :, :, pl.ds(start, size)],
+                outs[which].at[:, :, pl.ds(start, size)],
+                buffers,
+                sems,
+                fsdp,
+                chips,
+            )
+        )
+    for one in sums:
+        one.start()
+    for one in sums:
+        one.cross_over()
+    stages = [one.stages() for one in sums]
+    lag = chips - 1
+    for tick in range(len(stages[0]) + lag * (count - 1)):
+        for i in range(count):
+            if 0 <= tick - lag * i < len(stages[i]):
+                stages[i][tick - lag * i]()
+    for one in sums:
+        one.finish()
+
+
+def dense_reduce(arrays, piece, fsdp, chips, collective_id):
     vmem = pl.BlockSpec(memory_space=pltpu.VMEM)
-    return pl.pallas_call(
-        functools.partial(dense_reduce_kernel, fsdp, chips),
-        out_shape=jax.ShapeDtypeStruct((2, rows, width), BF16),
-        in_specs=[vmem],
-        out_specs=vmem,
-        scratch_shapes=[
-            pltpu.VMEM((fsdp, rows, width), BF16),
-            pltpu.VMEM((fsdp, rows, width), BF16),
-            pltpu.VMEM((fsdp - 1, rows, width), BF16),
-            pltpu.VMEM((rows, width), BF16),
-        ]
-        + [pltpu.VMEM((chips - 1, rows, cut), BF16) for unused in range(4)]
-        + [pltpu.VMEM((2, chips, rows, cut), BF16)]
-        + [pltpu.SemaphoreType.DMA((fsdp,)) for unused in range(2)]
+    cuts, buffers = [], []
+    for i, a in enumerate(arrays):
+        rows, width = a.shape[2:]
+        for start in range(0, width, piece):
+            size = min(piece, width - start)
+            cut = size // chips
+            cuts.append((i, start, size))
+            buffers += [
+                pltpu.VMEM((fsdp, rows, size), BF16),
+                pltpu.VMEM((fsdp - 1, rows, size), BF16),
+                pltpu.VMEM((rows, size), BF16),
+                pltpu.VMEM((chips - 1, rows, cut), BF16),
+                pltpu.VMEM((chips - 1, rows, cut), BF16),
+                pltpu.VMEM((2, chips, rows, cut), BF16),
+            ]
+    sems = (
+        [pltpu.SemaphoreType.DMA((fsdp,)) for unused in range(2)]
         + [pltpu.SemaphoreType.DMA((fsdp - 1,)) for unused in range(2)]
         + [pltpu.SemaphoreType.DMA((chips - 1,)) for unused in range(8)]
-        + [pltpu.SemaphoreType.DMA((chips,)) for unused in range(2)],
+        + [pltpu.SemaphoreType.DMA((chips,)) for unused in range(2)]
+    )
+    return pl.pallas_call(
+        functools.partial(dense_reduce_kernel, fsdp, chips, tuple(cuts)),
+        out_shape=[jax.ShapeDtypeStruct(a.shape[1:], BF16) for a in arrays],
+        in_specs=[vmem] * len(arrays),
+        out_specs=[vmem] * len(arrays),
+        scratch_shapes=buffers + sems * len(cuts),
         compiler_params=pltpu.CompilerParams(
             collective_id=collective_id, has_side_effects=True, vmem_limit_bytes=VMEM_BYTES
         ),
         name="dense_reduce",
-    )(local)
-
-
-def right_pairs(chips, least):
-    return [(2 * z + k, 2 * z + 2 + k) for z in range(chips - 1) if least <= z for k in range(2)]
-
-
-def left_pairs(chips, most):
-    return [(2 * z + k, 2 * z - 2 + k) for z in range(1, chips) if z <= most for k in range(2)]
-
-
-def swap_pairs(chips):
-    return [(i, i ^ 1) for i in range(2 * chips)]
+    )(*arrays)
 
 
 def after(value, *others):
     return lax.optimization_barrier((value,) + others)[0]
-
-
-def line_gather_async(rows, chips, chip, ties):
-    right, left = rows, rows
-    got_right, got_left = [], []
-    for step in range(chips - 1):
-        if step >= 1:
-            right = after(right, *ties[min(step, len(ties)) - 1])
-            left = after(left, *ties[min(step, len(ties)) - 1])
-        right = lax.ppermute(right, "ctx", right_pairs(chips, step))
-        left = lax.ppermute(left, "ctx", left_pairs(chips, chips - 1 - step))
-        got_right.append(right)
-        got_left.append(left)
-    slots = [rows]
-    for r in range(1, chips):
-        slots.append(jnp.where(chip + r < chips, got_left[r - 1], got_right[chips - 1 - r]))
-    mine = jnp.stack(slots)
-    return mine, lax.ppermute(mine, "ctx", swap_pairs(chips))
-
-
-def line_reduce(mine, other, chips, ties):
-    recv = lax.ppermute(other, "ctx", swap_pairs(chips))
-    right = left = None
-    for step in range(chips - 1):
-        r_right, r_left = chips - 1 - step, step + 1
-        parts_right, parts_left = [mine[r_right], recv[r_right]], [mine[r_left], recv[r_left]]
-        if step > 0:
-            parts_right.append(right)
-            parts_left.append(left)
-        send_right, send_left = add(*parts_right).astype(BF16), add(*parts_left).astype(BF16)
-        tie = ties[min(step, len(ties) - 1)]
-        if tie:
-            send_right, send_left = after(send_right, *tie), after(send_left, *tie)
-        right = lax.ppermute(
-            send_right,
-            "ctx",
-            [(2 * z + k, 2 * z + 2 + k) for z in range(step + 1) for k in range(2)],
-        )
-        left = lax.ppermute(
-            send_left,
-            "ctx",
-            [
-                (2 * z + k, 2 * z - 2 + k)
-                for z in range(chips - 1 - step, chips)
-                for k in range(2)
-            ],
-        )
-    return add(mine[0], recv[0], right, left)
 
 
 def attention_kernel(
@@ -880,17 +963,15 @@
     capacity,
     local_experts,
     expert_count,
-    first_ref,
+    place_ref,
     hidden_ref,
-    grad_mine_ref,
-    grad_other_ref,
+    grad_ref,
     table_ref,
     weight_ref,
     gate_ref,
     up_ref,
     down_ref,
-    out_mine,
-    out_other,
+    out_ref,
     rows_mine,
     rows_other,
     save_x,
@@ -901,7 +982,8 @@
 ):
     tokens = hidden_ref.shape[2]
     slot_rows = save_x.shape[1] // 2
-    first = first_ref[0]
+    core = place_ref[1]
+    first = place_ref[2]
     slot = lax.broadcasted_iota(jnp.int32, (slot_rows, tokens), 0).astype(F32) + 1.0
     slot = jnp.where(slot <= capacity, slot, -1.0)
     lane = lax.broadcasted_iota(jnp.int32, (2 * slot_rows, LANES), 1)
@@ -917,8 +999,7 @@
             weight = weight_ref[q, 0, pl.ds(first + e, 1), :]
             rows_w.append(jnp.sum(jnp.where(hit, weight, 0.0), axis=1, keepdims=True))
             rows_x.append(dot(pick, hidden_ref[q, 0], NN).astype(BF16))
-            grad_rows = grad_mine_ref[0] if q == 0 else grad_other_ref[0]
-            rows_g.append(dot(pick, grad_rows, NN))
+            rows_g.append(dot(pick, grad_ref[q, 0], NN))
             picks[q].append(pick)
         x = jnp.concatenate(rows_x, axis=0)
         g = jnp.concatenate(rows_g, axis=0)
@@ -952,16 +1033,17 @@
         save_db[e] = db
     for q in range(2):
         pick = jnp.concatenate(picks[q], axis=0)
-        out_ref = out_mine if q == 0 else out_other
         rows_ref = rows_mine if q == 0 else rows_other
-        out_ref[0] = dot(pick, jnp.concatenate(outs[q], axis=0), TN).astype(BF16)
+        out_ref[0, core if q == 0 else 1 - core] = dot(
+            pick, jnp.concatenate(outs[q], axis=0), TN
+        ).astype(BF16)
         rows_ref[0] = dot(pick, jnp.concatenate(backs[q], axis=0), TN).astype(BF16)
 
 
 def expert_rows_pass(
-    first, hidden, grad_mine, grad_other, table, weights, gate, up, down, capacity, expert_count
+    where, hidden, grad, table, weights, gate, up, down, capacity, expert_count
 ):
-    chips, tokens, width = grad_mine.shape
+    unused, chips, tokens, width = grad.shape
     local_experts, unused, hidden_units = gate.shape
     slots = 2 * SLOT_STEP * -(-capacity // SLOT_STEP)
     total = chips * slots
@@ -973,7 +1055,10 @@
     def saved(columns):
         return pl.BlockSpec((local_experts, slots, columns), lambda r, s: (0, r, 0))
 
-    chunk = pl.BlockSpec((1, tokens, width), lambda r, s: (r, 0, 0))
+    chunk = pl.BlockSpec((2, 1, tokens, width), lambda r, s: (0, r, 0, 0))
+    placed = pl.BlockSpec(
+        (1, 2, tokens, width), lambda r, s: (lax.rem(s[0] + r, chips), 0, 0, 0)
+    )
     wide = pl.BlockSpec((1, tokens, width + LANES), lambda r, s: (r, 0, 0))
     small = pl.BlockSpec((2, 1, expert_count, tokens), lambda r, s: (0, r, 0, 0))
     flops = 2 * total * width * hidden_units * local_experts * 6 + 8 * total * tokens * width
@@ -983,7 +1068,6 @@
             num_scalar_prefetch=1,
             grid=(chips,),
             in_specs=[
-                pl.BlockSpec((2, 1, tokens, width), lambda r, s: (0, r, 0, 0)),
                 chunk,
                 chunk,
                 small,
@@ -993,8 +1077,7 @@
                 whole(down.shape),
             ],
             out_specs=[
-                chunk,
-                chunk,
+                placed,
                 wide,
                 wide,
                 saved(width),
@@ -1004,7 +1087,7 @@
                 saved(hidden_units),
             ],
         ),
-        out_shape=[jax.ShapeDtypeStruct((chips, tokens, width), BF16)] * 2
+        out_shape=[jax.ShapeDtypeStruct((chips, 2, tokens, width), BF16)]
         + [jax.ShapeDtypeStruct((chips, tokens, width + LANES), BF16)] * 2
         + [jax.ShapeDtypeStruct((local_experts, total, width), BF16)] * 2
         + [jax.ShapeDtypeStruct((local_experts, total, hidden_units), BF16)] * 3,
@@ -1013,7 +1096,7 @@
             flops=flops, bytes_accessed=80_000_000, transcendentals=total * hidden_units * 2
         ),
         name="expert_rows",
-    )(first, hidden, grad_mine, grad_other, table, weights, gate, up, down)
+    )(where, hidden, grad, table, weights, gate, up, down)
 
 
 def outer_kernel(per, split_left, left_ref, right_ref, out_ref):
@@ -1096,7 +1179,9 @@
         axis=1,
     )
     qkv_shard = jnp.concatenate([w_query, w_key, w_value], axis=1)
-    qkv_full, small_full = gather([qkv_shard, small], [], fsdp, chips, 0)
+    qkv_full, small_full, grad_all = gather(
+        [qkv_shard, small], [grad_out[0]], chips - 2, fsdp, chips, 0
+    )
 
     qkv_full, w_gate, w_up, w_down = lax.optimization_barrier((qkv_full, w_gate, w_up, w_down))
     gate_full, up_full, down_full = (
@@ -1147,7 +1232,9 @@
         ],
         axis=1,
     )
-    out_full, kv_all, table_all = gather([w_out], [kv_mine, table.T], fsdp, chips, 1)
+    out_full, kv_all, table_all, grad_all = gather(
+        [w_out], [kv_mine, table.T], chips - 1, fsdp, chips, 1, [grad_all]
+    )
     kv_all = kv_all.reshape(-1, 2 * kv_width)
     attended, lse = [], []
     for group in range(KVH):
@@ -1156,7 +1243,6 @@
         )
         attended.append(part)
         lse.append(part_lse)
-    grad_mine, grad_other = line_gather_async(grad_out[0], chips, chip, [(kv_all,), attended[:1]])
     attended_parts, attended = attended, jnp.concatenate(attended, axis=1)
     middle = inputs + jnp.dot(attended, out_full, preferred_element_type=F32)
     hidden_two = rms_scale(middle, gain_b).astype(BF16)
@@ -1164,11 +1250,10 @@
     chosen = jnp.where(routed > 0, logits, MASKED)
     gate_weights = jnp.where(routed > 0, jax.nn.softmax(chosen, axis=-1), 0.0)
 
-    hidden_all, weights_all = gather([], [hidden_two, gate_weights.T], fsdp, chips, 2)
-    first = (ctx_index * local_experts).astype(jnp.int32).reshape(1)
+    hidden_all, weights_all = gather([], [hidden_two, gate_weights.T], chips - 1, fsdp, chips, 2)
+    where = jnp.stack([chip, core, ctx_index * local_experts]).astype(jnp.int32)
     (
-        out_mine,
-        out_other,
+        out_rows,
         rows_mine,
         rows_other,
         save_x,
@@ -1177,10 +1262,9 @@
         save_da,
         save_db,
     ) = expert_rows_pass(
-        first,
+        where,
         hidden_all,
-        grad_mine,
-        grad_other,
+        grad_all,
         table_all,
         weights_all,
         gate_full,
@@ -1192,13 +1276,19 @@
     gate_local = outer_products(save_x, save_da, fsdp, True)
     up_local = outer_products(save_x, save_db, fsdp, True)
     down_local = outer_products(save_inner, save_pg, fsdp, False)
-    gate_grad_out, up_grad_out, down_grad_out = (
-        lax.psum_scatter(part, "fsdp", scatter_dimension=0, tiled=True)[0].astype(F32)
+    returned = line_reduce_now(
+        after(rows_mine, gate_local, up_local, down_local), rows_other, chips, 5
+    )
+    out_sum = lax.psum_scatter(
+        after(out_rows, returned).reshape(2 * chips, tok_rows, width),
+        "ctx",
+        scatter_dimension=0,
+        tiled=True,
+    )
+    expert_grads = [
+        lax.psum_scatter(part, "fsdp", scatter_dimension=0, tiled=True)
         for part in (gate_local, up_local, down_local)
-    )
-    returned = line_reduce(
-        rows_mine, rows_other, chips, [(gate_local,), (up_local,), (down_local,)]
-    )
+    ]
 
     out_grad = grad_out[0].astype(F32)
     extra = returned[:, width:]
@@ -1234,12 +1324,6 @@
         )
         query_grad.append(parts[0])
         kv_grads[group], kv_grads[KVH + group] = parts[1:]
-    result = middle + line_reduce(
-        after(out_mine, returned),
-        after(out_other, returned),
-        chips,
-        [(branch_grad,), (attended_grad,), (query_grad[0],)],
-    )
     kv_grads = jnp.concatenate(kv_grads, axis=1).reshape(2, chips, tok_rows, 2 * kv_width)
     kv_grad = line_reduce_now(kv_grads[0], kv_grads[1], chips, 3)
     turned_grad = rotate(
@@ -1258,30 +1342,49 @@
     input_part, gain_one_local = norm_one_back(hidden_one_grad)
     input_grad = (middle_grad + input_part).astype(BF16)
 
-    first_local = jnp.concatenate([out_local, router_local, gain_two_local[:, None]], axis=1)
-    first_grads = lax.psum(
-        lax.psum_scatter(first_local.astype(BF16), "fsdp", scatter_dimension=0, tiled=True), "ctx"
-    ).astype(F32)
+    def halves(local):
+        local = local.astype(BF16).reshape(fsdp, 2, shard // 2, local.shape[1])
+        pad = -local.shape[3] % (LANES * chips)
+        return jnp.pad(local, ((0, 0), (0, 0), (0, 0), (0, pad))) if pad else local
+
+    span = shard * expert_count // 16
+    wide = LANES * chips * -(-max(span, shard) // (LANES * chips))
+    small_local = jnp.stack(
+        [
+            jnp.pad(
+                router_local.astype(BF16).reshape(fsdp, 16, span),
+                ((0, 0), (0, 0), (0, wide - span)),
+            ),
+            jnp.pad(
+                jnp.stack(
+                    [gain_one_local.reshape(fsdp, shard), gain_two_local.reshape(fsdp, shard)],
+                    axis=1,
+                ).astype(BF16),
+                ((0, 0), (0, 14), (0, wide - shard)),
+            ),
+        ],
+        axis=1,
+    )
+    qkv_sum, out_proj_sum, small_sum = dense_reduce(
+        [halves(qkv_local), halves(out_local), small_local], DENSE_PIECE, fsdp, chips, 4
+    )
     edge = width + 2 * kv_width
-    extra_rows = jnp.pad(
-        gain_one_local.reshape(fsdp, 1, 1, shard).astype(BF16),
-        ((0, 0), (0, 1), (0, 15), (0, edge - shard)),
-    )
-    last_local = jnp.concatenate(
-        [qkv_local.astype(BF16).reshape(fsdp, 2, shard // 2, edge), extra_rows], axis=2
-    )
-    last_grads = dense_reduce(last_local, fsdp, chips, 4)
-    qkv_grads = last_grads[:, : shard // 2].reshape(shard, edge).astype(F32)
+    qkv_grads = qkv_sum.reshape(shard, -1)
+    out_proj_grad = out_proj_sum.reshape(shard, -1)[:, :width]
+    gate_grad_out, up_grad_out, down_grad_out = (
+        after(part, pre_grad)[0].astype(F32) for part in expert_grads
+    )
+    result = middle + after(out_sum, pre_grad)[0].astype(F32)
     return (
         result.astype(BF16)[None],
         input_grad[None],
-        last_grads[0, shard // 2, :shard].astype(F32),
-        first_grads[:, width + expert_count],
-        qkv_grads[:, :width],
-        qkv_grads[:, width : width + kv_width],
-        qkv_grads[:, width + kv_width :],
-        first_grads[:, :width],
-        first_grads[:, width : width + expert_count],
+        small_sum[1, 0, :shard].astype(F32),
+        small_sum[1, 1, :shard].astype(F32),
+        qkv_grads[:, :width].astype(F32),
+        qkv_grads[:, width : width + kv_width].astype(F32),
+        qkv_grads[:, width + kv_width : edge].astype(F32),
+        out_proj_grad.astype(F32),
+        small_sum[0, :, :span].reshape(shard, expert_count).astype(F32),
         gate_grad_out,
         up_grad_out,
         down_grad_out,

time: 1010 us -> 865 us (0.86)
  waiting for transfers between devices: 219 us -> 1.47 us
  Pallas kernels: 549 us -> 692 us
  other arithmetic: 82 us -> 44.4 us
  starting transfers between devices: 43.5 us -> 11.6 us
    pallas_call x1 -> x2, Pallas kernels: 51.6 us -> 160 us  [line_reduce_now(): pl.pallas_call(functools.partial(line_reduce_kernel, chips), out_shape=ja...]
    ppermute x21 -> x0, waiting for transfers between devices: 105 us -> none  [the longest x6 76.4 us: line_reduce(): lax.ppermute(send_right, 'ctx', [(2 * z + k, 2 * z + 2 + k) for z in rang...]
    unnamed x12 -> x7, waiting for transfers between devices: 61 us -> 1.46 us
    psum x1 -> x0, waiting for transfers between devices: 52.8 us -> none  [body(): lax.psum(lax.psum_scatter(first_local.astype(BF16), 'fsdp', scatter_dimen...]
    ppermute x21 -> x0, starting transfers between devices: 42.6 us -> none  [the longest x6 23.4 us: line_reduce(): lax.ppermute(send_right, 'ctx', [(2 * z + k, 2 * z + 2 + k) for z in rang...]
    pallas_call x4, Pallas kernels: 292 us -> 326 us  [the longest x3 217 us: gather(): pl.pallas_call(functools.partial(gather_kernel, len(dense), len(line), le...]
    convert_element_type x15 -> x7, other arithmetic: 42 us -> 15 us  [the longest x2 5.57 us: body(): after(part, pre_grad)[0].astype(F32)]
    unnamed x4 -> x3, starting transfers between devices: 0.57 us -> 11.4 us
  transfers between devices with their start and end apart: 29 -> 7, of which waited for: 8 -> 0; matrix products, arithmetic and copies ran while one was open for 15% -> 14% of each run, Pallas kernels for 42% -> 65%
where the time goes in v2:
time: 865 us; the launch traced here: 856 us
  Pallas kernels  692 us (80%)
  local copies, waits for them, and re-layouts  50.9 us (6%)
  other arithmetic  44.4 us (5%)
  matrix products  40.3 us (5%)
  between operations  15.3 us (2%)
  starting transfers between devices  11.6 us (1%)
    pallas_call x3, Pallas kernels, gather(): pl.pallas_call(functools.partial(gather_kernel, len(dense), len(line), le...  217 us
    pallas_call x2, Pallas kernels, line_reduce_now(): pl.pallas_call(functools.partial(line_reduce_kernel, chips), out_shape=ja...  160 us
    pallas_call x1, Pallas kernels, dense_reduce(): pl.pallas_call(functools.partial(dense_reduce_kernel, fsdp, chips, tuple(...  109 us
    pallas_call x2, Pallas kernels, attention_back(): pl.pallas_call(functools.partial(attention_back_kernel, HEAD_SIZE ** (-0....  62.3 us
    pallas_call x1, Pallas kernels, expert_rows_pass(): pl.pallas_call(functools.partial(expert_kernel, capacity, local_experts,...  56.1 us
    pallas_call x2, Pallas kernels, attention(): pl.pallas_call(functools.partial(attention_kernel, HEAD_SIZE ** (-0.5)),...  51.6 us
    pallas_call x3, Pallas kernels, outer_products(): pl.pallas_call(functools.partial(outer_kernel, per, split_left), grid=(ex...  35.6 us
  transfers between devices with their start and end apart: 7, of which 0 were waited for; matrix products, arithmetic and copies ran while one was open for 14% of the time, Pallas kernels for 65%

profile of v2, /device:TPU:0, one launch (start us, length us, event | category | flops | bytes accessed | tf_op | source)
XLA Modules:
  0.0 855.7 jit_solution(7147800982558424408)
XLA Ops:
  9.7 2.9 pad_maximum_fusion.1.refs_0_
  13.4 65.3 %gather.3 = (bf16[1536,2048]{1,0:T(8,128)(2,1)}, bf16[1536,128]{1,0:T(8,128)(2,1)}, bf16[2,4,384,1536]{3,2,1,0:T(8,128)(2,1)}) custom-call(bf16[384,2048]{1,0:T(8,128)(2,1)} %pad_maximum_fusion.1.refs_0_, bf16[384,128]{1,0:T(8,128)(2,1)} %maximum_maximum_fusion.refs_1_, bf16[384,1536]{1,0:T(8,128)(2,1)} %bitcast.95), custom_call_target="tpu_custom_call" | custom-call | tf_op jit(solution)/shard_map/gather/pallas_call | solution.py:339
  81.7 4.8 fusion.21
  87.6 2.2 copy.129
  90.0 1.1 fusion.38
  91.1 2.2 multiply_subtract_fusion
  97.0 1.5 copy.136.q_ref
  100.8 65.3 %gather.4 = (bf16[1536,1536]{1,0:T(8,128)(2,1)}, bf16[2,4,384,512]{3,2,1,0:T(8,128)(2,1)}, f32[2,4,16,384]{3,2,1,0:T(8,128)}, bf16[2,4,384,1536]{3,2,1,0:T(8,128)(2,1)}) custom-call(bf16[384,1536]{1,0:T(8,128)(2,1)} %refs_0_.1, bf16[384,512]{1,0:T(8,128)(2,1)} %pad_maximum_fusion.4.refs_1_, ...), custom_call_target="tpu_custom_call", output_to_operand_aliasing={{3}: (3, {})} | custom-call | tf_op jit(solution)/shard_map/gather/pallas_call | solution.py:339
  166.2 25.8 %attention.2 = (bf16[384,768]{1,0:T(8,128)(2,1)}, f32[6,1,384]{2,1,0:T(1,128)}) custom-call(bf16[384,1536]{1,0:T(8,128)(2,1)} %copy.136.q_ref, bf16[3072,512]{1,0:T(8,128)(2,1)} %bitcast.108, bf16[3072,512]{1,0:T(8,128)(2,1)} %bitcast.109, s32[384,1]{1,0:T(8,128)} %copy.137.oq_ref, s32[384,1]{1,0:T(8,128)} %copy.138.pq_ref, ...), custom_call_target="tpu_custom_call" | custom-call | flops 3623878656 | bytes 2752512 | tf_op jit(solution)/shard_map/attention/pallas_call | solution.py:810
  192.0 1.4 copy.139.q_ref
  193.5 25.8 %attention.3 = (bf16[384,768]{1,0:T(8,128)(2,1)}, f32[6,1,384]{2,1,0:T(1,128)}) custom-call(bf16[384,1536]{1,0:T(8,128)(2,1)} %copy.139.q_ref, bf16[3072,512]{1,0:T(8,128)(2,1)} %bitcast.110, bf16[3072,512]{1,0:T(8,128)(2,1)} %bitcast.111, s32[384,1]{1,0:T(8,128)} %copy.137.oq_ref, s32[384,1]{1,0:T(8,128)} %copy.138.pq_ref, ...), custom_call_target="tpu_custom_call" | custom-call | flops 3623878656 | bytes 2752512 | tf_op jit(solution)/shard_map/attention/pallas_call | solution.py:810
  219.3 1.1 constant_dynamic-update-slice_fusion
  220.4 1.0 copy-done.23
  221.4 5.7 multiply_reduce_fusion.2
  227.5 1.0 copy-done
  230.3 0.9 fusion.28
  231.2 1.6 copy.144.refs_1_
  232.8 86.8 %gather.5 = (bf16[2,4,384,1536]{3,2,1,0:T(8,128)(2,1)}, f32[2,4,16,384]{3,2,1,0:T(8,128)}) custom-call(bf16[384,1536]{1,0:T(8,128)(2,1)} %copy-done, f32[16,384]{1,0:T(8,128)} %copy.144.refs_1_), custom_call_target="tpu_custom_call" | custom-call | tf_op jit(solution)/shard_map/gather/pallas_call | solution.py:339
  320.2 56.1 %expert_rows.1 = (bf16[4,2,384,1536]{3,2,1,0:T(8,128)(2,1)}, bf16[4,384,1664]{2,1,0:T(8,128)(2,1)}, bf16[4,384,1664]{2,1,0:T(8,128)(2,1)}, bf16[2,1024,1536]{2,1...) custom-call(s32[3]{0:T(128)} %pad_add_fusion.place_ref, ...), custom_call_target="tpu_custom_call" | custom-call | flops 33822867456 | bytes 80000000 | tf_op jit(solution)/shard_map/expert_rows/pallas_call | solution.py:1065
  376.3 12.1 %outer_products.5 = bf16[4,2,768,384]{3,2,1,0:T(8,128)(2,1)} custom-call(bf16[2,1024,768]{2,1,0:T(8,128)(2,1)} %get-tuple-element.75.left_ref, bf16[2,1024,1536]{2,1,0:T(8,128)(2,1)} %get-tuple-element.76.right_ref), custom_call_target="tpu_custom_call" | custom-call | flops 4831838208 | bytes 14000000 | tf_op jit(solution)/shard_map/outer_products/pallas_call | solution.py:1118
  388.5 12.0 %outer_products.3 = bf16[4,2,384,768]{3,2,1,0:T(8,128)(2,1)} custom-call(bf16[2,1024,1536]{2,1,0:T(8,128)(2,1)} %get-tuple-element.72.left_ref, bf16[2,1024,768]{2,1,0:T(8,128)(2,1)} %get-tuple-element.73.right_ref), custom_call_target="tpu_custom_call" | custom-call | flops 4831838208 | bytes 14000000 | tf_op jit(solution)/shard_map/outer_products/pallas_call | solution.py:1118
  400.5 11.3 %reduce-scatter.15.cloned.1.call-start = ((), (), s32[]{:S(2)}) async-start(), calls=%async_computation.9 | async-start | bytes 5898240
  411.8 11.5 %outer_products.4 = bf16[4,2,384,768]{3,2,1,0:T(8,128)(2,1)} custom-call(bf16[2,1024,1536]{2,1,0:T(8,128)(2,1)} %get-tuple-element.72.left_ref, bf16[2,1024,768]{2,1,0:T(8,128)(2,1)} %get-tuple-element.74.right_ref), custom_call_target="tpu_custom_call" | custom-call | flops 4831838208 | bytes 14000000 | tf_op jit(solution)/shard_map/outer_products/pallas_call | solution.py:1118
  423.4 99.5 %line_reduce.2 = f32[384,1664]{1,0:T(8,128)} custom-call(bf16[4,384,1664]{2,1,0:T(8,128)(2,1)} %get-tuple-element.77.mine_ref, bf16[4,384,1664]{2,1,0:T(8,128)(2,1)} %get-tuple-element.78.other_ref), custom_call_target="tpu_custom_call" | custom-call | tf_op jit(solution)/shard_map/line_reduce/pallas_call | solution.py:500
  522.9 3.3 broadcast_in_dim_reshape.10.ok_ref
  526.2 1.4 copy.145.q_ref
  527.7 1.2 reshape_subtract_fusion.pq_ref
  528.9 1.6 multiply_reduce_fusion.3
  530.5 1.5 multiply_convert_fusion.1
  532.1 3.4 multiply_reduce_fusion
  536.6 3.0 convolution_convert_fusion.2.do_ref
  539.7 30.9 %attention_back.2 = (f32[384,768]{1,0:T(8,128)}, bf16[3072,128]{1,0:T(8,128)(2,1)}, bf16[3072,128]{1,0:T(8,128)(2,1)}) custom-call(bf16[384,1536]{1,0:T(8,128)(2,1)} %copy.145.q_ref, bf16[3072,512]{1,0:T(8,128)(2,1)} %bitcast.112, bf16[3072,512]{1,0:T(8,128)(2,1)} %bitcast.113, bf16[384,768]{1,0:T(8,128)(2,1)} %get-tuple-element.59.o_ref, ...), custom_call_target="tpu_custom_call" | custom-call | flops 9059696640 | bytes 6094848 | tf_op jit(solution)/shard_map/attention_back/pallas_call | solution.py:913
  570.6 2.1 constant_dynamic-update-slice_fusion.5
  572.7 31.3 %attention_back.3 = (f32[384,768]{1,0:T(8,128)}, bf16[3072,128]{1,0:T(8,128)(2,1)}, bf16[3072,128]{1,0:T(8,128)(2,1)}) custom-call(bf16[384,1536]{1,0:T(8,128)(2,1)} %copy.145.q_ref, bf16[3072,512]{1,0:T(8,128)(2,1)} %bitcast.114, bf16[3072,512]{1,0:T(8,128)(2,1)} %bitcast.115, bf16[384,768]{1,0:T(8,128)(2,1)} %get-tuple-element.61.o_ref, ...), custom_call_target="tpu_custom_call" | custom-call | flops 9059696640 | bytes 6094848 | tf_op jit(solution)/shard_map/attention_back/pallas_call | solution.py:913
  604.1 2.2 constant_dynamic-update-slice_fusion.4
  606.3 1.0 constant_dynamic-update-slice_fusion.3
  607.4 1.0 constant_dynamic-update-slice_fusion.2
  608.4 3.8 fusion.46
  612.2 60.7 %line_reduce.3 = f32[384,512]{1,0:T(8,128)} custom-call(bf16[4,384,512]{2,1,0:T(8,128)(2,1)} %bitcast.94, bf16[4,384,512]{2,1,0:T(8,128)(2,1)} %bitcast.93), custom_call_target="tpu_custom_call" | custom-call | tf_op jit(solution)/shard_map/line_reduce/pallas_call | solution.py:500
  672.9 1.0 slice.102
  673.9 1.7 slice.158
  675.6 3.0 pad_maximum_fusion
  678.6 3.5 copy.149
  682.1 1.7 copy.150
  683.8 1.8 convolution_convert_fusion.3
  685.6 1.0 copy.151
  686.7 0.9 reshape.275
  687.6 2.3 subtract_convert_fusion
  690.0 1.5 copy-done.6
  691.6 7.8 fusion.3
  700.2 1.3 stack_reshape.11
  702.9 7.0 convolution_convert_fusion
  710.0 5.8 convolution_convert_fusion.1
  715.8 108.5 %dense_reduce.1 = (bf16[2,192,2048]{2,1,0:T(8,128)(2,1)}, bf16[2,192,1536]{2,1,0:T(8,128)(2,1)}, bf16[2,16,512]{2,1,0:T(8,128)(2,1)}) custom-call(bf16[4,2,192,2048]{3,2,1,0:T(8,128)(2,1)} %bitcast.92, bf16[4,2,192,1536]{3,2,1,0:T(8,128)(2,1)} %bitcast.96, bf16[4,2,16,512]{3,2,1,0:T(8,128)(2,1)} %pad_maximum_fusion.5.refs_2_), custom_call_target="tpu_custom_call" | custom-call | tf_op jit(solution)/shard_map/dense_reduce/pallas_call | solution.py:741
  824.3 1.3 slice_convert_fusion.5
  825.6 1.5 reshape.284
  827.2 1.6 copy.154
  828.8 1.4 convert_reduce_fusion.3
  830.9 2.1 slice_convert_fusion.3
  832.9 3.0 slice_convert_fusion
  835.9 1.8 bitcast_convert_fusion.3
  837.7 3.0 bitcast_convert_fusion
  840.7 2.6 bitcast_convert_fusion.1
  843.3 5.1 fusion.10
  (164 shorter events, 20.6 us)
Async XLA Ops:
  7.2 313.0 %all-gather.4.cloned.1.call-start = ((), (), s32[]{:S(2)}) async-start(), calls=%async_computation.4 | async-start | bytes 5898240 | tf_op jit(solution)/shard_map/all_gather | solution.py:1188
  78.7 1.6 copy-start.8
  78.7 2.1 copy-start.5
  78.8 241.4 %all-gather.6.cloned.1.call-start = ((), (), s32[]{:S(2)}) async-start(), calls=%async_computation.5 | async-start | bytes 5898240 | tf_op jit(solution)/shard_map/all_gather | solution.py:1189
  79.5 240.7 %all-gather.8.cloned.1.call-start = ((), (), s32[]{:S(2)}) async-start(), calls=%async_computation.6 | async-start | bytes 5898240 | tf_op jit(solution)/shard_map/all_gather | solution.py:1190
  80.2 757.4 %reduce-scatter.17.cloned.1.call-start = ((), (), s32[]{:S(2)}) async-start(), calls=%async_computation.10 | async-start | bytes 5898240
  81.2 0.6 copy-start.35
  81.2 0.6 copy-start.38
  86.5 0.9 copy-start.45
  87.6 2.2 copy-start.37
  89.9 9.4 %copy-start.34 = (s32[1,384]{1,0:T(1,128)}, s32[1,384]{1,0:T(1,128)S(1)}, u32[]{:S(2)}) copy-start(s32[1,384]{1,0:T(1,128)S(1)} %get-tuple-element.165.oq_ref) | copy-start | bytes 4612
  90.0 8.4 copy-start.31
  91.1 2.3 copy-start.17
  91.1 2.4 copy-start.44
  93.7 3.3 copy-start.3
  93.7 3.2 copy-start.27
  96.0 0.9 copy-start.26
  96.8 3.3 copy-start.21
  192.0 1.4 copy-start.22
  220.4 1.0 copy-start.23
  227.2 1.9 copy-start.42
  227.2 1.3 copy-start.9
  227.2 1.3 copy-start.28
  227.2 1.9 copy-start.32
  227.2 1.9 copy-start.4
  227.5 1.0 copy-start
  229.1 0.7 copy-start.10
  229.1 0.7 copy-start.29
  229.8 0.6 copy-start.30
  388.4 449.2 %reduce-scatter.13.cloned.1.call-start = ((), (), s32[]{:S(2)}) async-start(), calls=%async_computation.8 | async-start | bytes 5898240
  400.5 437.2 %reduce-scatter.15.cloned.1.call-start = ((), (), s32[]{:S(2)}) async-start(), calls=%async_computation.9 | async-start | bytes 5898240
  423.3 420.0 %reduce-scatter.11.cloned.1.call-start = ((), (), s32[]{:S(2)}) async-start(), calls=%async_computation.7 | async-start | bytes 10616832 | tf_op jit(solution)/shard_map/reduce_scatter | solution.py:1282
  532.0 3.5 copy-start.18
  532.1 3.5 copy-start.43
  532.1 3.5 copy-start.7
  532.1 3.5 copy-start.33
  532.1 4.1 slice-start
  535.6 1.1 slice-start.1
  536.6 3.0 copy-start.2
  572.7 33.6 %copy-start.19 = (bf16[3072,128]{1,0:T(8,128)(2,1)S(1)}, bf16[3072,128]{1,0:T(8,128)(2,1)}, u32[]{:S(2)}) copy-start(bf16[3072,128]{1,0:T(8,128)(2,1)} %get-tuple-element.87) | copy-start | bytes 2359300
  604.1 3.3 copy-start.20
  612.2 63.4 %copy-start.16 = (f32[384,768]{1,0:T(8,128)S(1)}, f32[384,768]{1,0:T(8,128)}, u32[]{:S(2)}) copy-start(f32[384,768]{1,0:T(8,128)} %get-tuple-element.81) | copy-start | bytes 3538948
  678.6 5.2 copy-start.1
  689.8 1.7 copy-start.6
  689.8 1.8 copy-start.24
  689.8 1.8 copy-start.39
  690.0 9.4 %copy-start.11 = (bf16[384,14,128]{0,2,1:T(8,128)(2,1)}, bf16[384,14,128]{0,2,1:T(8,128)(2,1)S(1)}, u32[]{:S(2)}) copy-start(bf16[384,14,128]{0,2,1:T(8,128)(2,1)S(1)} %pad_maximum_fusion.3) | copy-start | bytes 4128772
  702.9 7.0 copy-start.12
  702.9 7.0 copy-start.25
  702.9 7.0 copy-start.40
  715.8 114.4 %copy-start.36 = (f32[384]{0:T(512)S(1)}, f32[384]{0:T(512)}, u32[]{:S(2)}) copy-start(f32[384]{0:T(512)} %copy-done.35) | copy-start | bytes 4612
  830.9 5.0 copy-start.15
  837.7 3.0 copy-start.13
  837.7 3.0 copy-start.14
  840.7 2.6 copy-start.41
Sparse Core Ops, SparseCore 0:
  78.9 76.1 all-gather.3
  156.9 56.0 all-gather.5
  214.8 56.9 all-gather.7
  388.6 56.0 reduce-scatter.16
  447.5 57.0 reduce-scatter.12
  507.4 57.1 reduce-scatter.14
  566.9 124.7 reduce-scatter.10

commit v3 on v2

--- a/solution.py
+++ b/solution.py
@@ -18,8 +18,10 @@
 LANES = 128
 SLOT_STEP = 64
 DENSE_PIECE = 1024
+LINE_TASK = 4
 KEY_TILE = 512
-VMEM_BYTES = 60 * 1024 * 1024
+VMEM_BYTES = 56 * 1024 * 1024
+EXPERT_VMEM_BYTES = 119 * 512 * 1024
 MESH = pl.DeviceIdType.MESH
 F32 = jnp.float32
 BF16 = jnp.bfloat16
@@ -361,26 +363,54 @@
     return total
 
 
+def add_into(target, parts):
+    rows = target.shape[0]
+    tile = 32 if rows % 32 == 0 else 16
+
+    def some(t, carry):
+        part = pl.ds(pl.multiple_of(t * tile, tile), tile)
+        target[part, :] = add(*[ref[part, :] for ref in parts]).astype(target.dtype)
+        return carry
+
+    lax.fori_loop(0, rows // tile, some, 0)
+
+
 class LineSum:
-    def __init__(self, chips, held, keep, gots, sems):
-        self.chips, self.held, self.keep = chips, held, keep
-        self.got_right, self.got_left = gots
+    def __init__(self, chips, held, keep, got, sems):
+        self.chips, self.held, self.keep, self.got = chips, held, keep, got
         self.sems = sems
         self.ctx, self.me, self.chip, core, sibling = place()
 
     def right(self, step):
         return remote(
             self.keep(self.chips - 1 - step),
-            self.got_right.at[step],
+            self.got.at[step - self.chip],
             self.sems[0].at[step],
             self.sems[1].at[step],
             (self.ctx + 2, self.me),
         )
 
+    def from_left(self, step):
+        slot = step + 1 - self.chip
+        pltpu.make_async_remote_copy(
+            src_ref=self.keep(self.chips - 1 - step),
+            dst_ref=self.got.at[slot],
+            send_sem=self.sems[0].at[step],
+            recv_sem=self.sems[1].at[step],
+            device_id=(self.ctx - 2, self.me),
+            device_id_type=MESH,
+        ).wait_recv()
+        return self.got.at[slot]
+
+    def from_right(self, step):
+        slot = step + 2
+        self.left(step).wait_recv()
+        return self.got.at[slot]
+
     def left(self, step):
         return remote(
             self.keep(step + 1),
-            self.got_left.at[step],
+            self.got.at[step + 2],
             self.sems[2].at[step],
             self.sems[3].at[step],
             (self.ctx - 2, self.me),
@@ -394,18 +424,16 @@
         def _():
             parts = self.held(far_right)
             if step == 0:
-                self.keep(far_right)[...] = add(*parts()).astype(BF16)
+                add_into(self.keep(far_right), parts())
             else:
 
                 @pl.when(chip == 0)
                 def _():
-                    self.keep(far_right)[...] = add(*parts()).astype(BF16)
+                    add_into(self.keep(far_right), parts())
 
                 @pl.when(chip >= 1)
                 def _():
-                    self.right(step - 1).wait_recv()
-                    total = add(*parts(), self.got_right[step - 1])
-                    self.keep(far_right)[...] = total.astype(BF16)
+                    add_into(self.keep(far_right), [self.from_left(step - 1)] + parts())
 
             self.right(step).start()
 
@@ -413,40 +441,34 @@
         def _():
             parts = self.held(far_left)
             if step == 0:
-                self.keep(far_left)[...] = add(*parts()).astype(BF16)
+                add_into(self.keep(far_left), parts())
             else:
 
                 @pl.when(chip == chips - 1)
                 def _():
-                    self.keep(far_left)[...] = add(*parts()).astype(BF16)
+                    add_into(self.keep(far_left), parts())
 
                 @pl.when(chip < chips - 1)
                 def _():
-                    self.left(step - 1).wait_recv()
-                    total = add(*parts(), self.got_left[step - 1])
-                    self.keep(far_left)[...] = total.astype(BF16)
+                    add_into(self.keep(far_left), [self.from_right(step - 1)] + parts())
 
             self.left(step).start()
 
-    def total(self, done):
+    def total(self, target):
         chip, chips, last = self.chip, self.chips, self.chips - 2
         parts = self.held(0)
 
         @pl.when(chip == 0)
         def _():
-            self.left(last).wait_recv()
-            done(add(*parts(), self.got_left[last]))
+            add_into(target, [self.from_right(last)] + parts())
 
         @pl.when(chip == chips - 1)
         def _():
-            self.right(last).wait_recv()
-            done(add(*parts(), self.got_right[last]))
+            add_into(target, [self.from_left(last)] + parts())
 
         @pl.when((chip >= 1) & (chip < chips - 1))
         def _():
-            self.left(last).wait_recv()
-            self.right(last).wait_recv()
-            done(add(*parts(), self.got_left[last], self.got_right[last]))
+            add_into(target, [self.from_right(last), self.from_left(last)] + parts())
 
     def finish(self):
         for step in range(self.chips - 1):
@@ -461,7 +483,7 @@
 
 
 def line_reduce_kernel(
-    chips, mine_ref, other_ref, out_ref, pair, gr, gl, ps, pr, s0, s1, s2, s3
+    chips, mine_ref, other_ref, out_ref, pair, got, ps, pr, s0, s1, s2, s3
 ):
     ctx, me, chip, core, sibling = place()
     greet(chips, [], True)
@@ -479,16 +501,12 @@
 
     def held(r):
         swaps[r].wait_recv()
-        return lambda: (mine_ref[r], pair[r])
-
-    line = LineSum(chips, held, lambda r: pair.at[r], (gr, gl), (s0, s1, s2, s3))
+        return lambda: [mine_ref.at[r], pair.at[r]]
+
+    line = LineSum(chips, held, lambda r: pair.at[r], got, (s0, s1, s2, s3))
     for step in range(chips - 1):
         line.step(step)
-
-    def done(total):
-        out_ref[...] = total
-
-    line.total(done)
+    line.total(out_ref)
     line.finish()
     for swap in swaps:
         swap.wait_send()
@@ -503,7 +521,7 @@
         in_specs=[vmem, vmem],
         out_specs=vmem,
         scratch_shapes=[pltpu.VMEM((chips, rows, width), BF16)]
-        + [pltpu.VMEM((chips - 1, rows, width), BF16) for unused in range(2)]
+        + [pltpu.VMEM((chips + 1, rows, width), BF16)]
         + [pltpu.SemaphoreType.DMA((chips,)) for unused in range(2)]
         + [pltpu.SemaphoreType.DMA((chips - 1,)) for unused in range(4)],
         compiler_params=pltpu.CompilerParams(
@@ -513,14 +531,14 @@
     )(mine, other)
 
 
-DENSE_BUFFERS = 6
+DENSE_BUFFERS = 5
 DENSE_SEMS = 14
 
 
 class DenseSum:
     def __init__(self, local, out, buffers, sems, fsdp, chips):
         self.local, self.out = local, out
-        self.pair, self.cross, self.sums, got_right, got_left, self.spread = buffers
+        self.pair, self.cross, self.sums, got, self.spread = buffers
         self.sems = sems
         self.chips = chips
         self.ctx, self.me, self.chip, self.core, self.sibling = place()
@@ -528,9 +546,9 @@
         self.cut = out.shape[2] // chips
         self.line = LineSum(
             chips,
-            lambda r: lambda: (self.sums[:, self.columns(r)],),
+            lambda r: lambda: [self.keep_ref(r)],
             lambda r: self.keep_ref(r),
-            (got_right, got_left),
+            got,
             sems[4:8],
         )
 
@@ -593,7 +611,7 @@
     def cross_over(self):
         for j, owner in enumerate(self.owners):
             self.swap(j).wait_recv()
-            self.pair[j] = add(self.local[owner, self.core], self.pair[j]).astype(BF16)
+            add_into(self.pair.at[j], [self.local.at[owner, self.core], self.pair.at[j]])
             if j < len(self.owners) - 1:
                 self.crossing(j).start()
 
@@ -603,17 +621,15 @@
         def open_up():
             for j in range(len(self.owners) - 1):
                 self.crossing(j).wait_recv()
-            self.sums[...] = add(
-                *[self.cross[j] for j in range(len(self.owners) - 1)],
-                self.pair[len(self.owners) - 1],
-            ).astype(BF16)
+            add_into(
+                self.sums,
+                [self.cross.at[j] for j in range(len(self.owners) - 1)]
+                + [self.pair.at[len(self.owners) - 1]],
+            )
             self.line.step(0)
 
         def summed():
-            def done(total):
-                self.spread[0, 0] = total.astype(BF16)
-
-            self.line.total(done)
+            self.line.total(self.spread.at[0, 0])
             hand_on(0)
 
         def hand_on(step):
@@ -728,8 +744,7 @@
                 pltpu.VMEM((fsdp, rows, size), BF16),
                 pltpu.VMEM((fsdp - 1, rows, size), BF16),
                 pltpu.VMEM((rows, size), BF16),
-                pltpu.VMEM((chips - 1, rows, cut), BF16),
-                pltpu.VMEM((chips - 1, rows, cut), BF16),
+                pltpu.VMEM((chips + 1, rows, cut), BF16),
                 pltpu.VMEM((2, chips, rows, cut), BF16),
             ]
     sems = (
@@ -959,11 +974,27 @@
     )
 
 
-def expert_kernel(
+def chunk_order(chip, i, chips):
+    right_half = lax.div(2 * chip, chips)
+    near = chip + right_half * (chips - 1 - 2 * chip)
+    alone = chips - 1 - 2 * near
+    paired = lax.div(i - alone + chips, chips)
+    turn = (i - alone) * paired
+    odd = lax.rem(turn, 2)
+    pair = lax.div(turn, 2)
+    distance = (1 - paired) * (chips - 1 - near - i) + paired * (
+        (1 - odd) * (near - pair) + odd * (chips - near + pair)
+    )
+    return lax.rem(distance + right_half * (chips - 2 * distance), chips)
+
+
+def experts_kernel(
     capacity,
     local_experts,
     expert_count,
-    place_ref,
+    chips,
+    fsdp,
+    per,
     hidden_ref,
     grad_ref,
     table_ref,
@@ -971,171 +1002,404 @@
     gate_ref,
     up_ref,
     down_ref,
+    returned_ref,
     out_ref,
-    rows_mine,
-    rows_other,
-    save_x,
-    save_pg,
-    save_inner,
-    save_da,
-    save_db,
+    gate_grad_ref,
+    up_grad_ref,
+    down_grad_ref,
+    x_ref,
+    pg_ref,
+    inner_ref,
+    da_ref,
+    db_ref,
+    gate_v,
+    up_v,
+    down_v,
+    hidden_v,
+    grad_v,
+    out_v,
+    x_v,
+    pg_v,
+    g_v,
+    inner_v,
+    da_v,
+    db_v,
+    mine_v,
+    other_v,
+    pair,
+    got,
+    stage_tall,
+    weight_sem,
+    load_sem,
+    out_sem,
+    save_sem,
+    swap_send,
+    swap_recv,
+    right_send,
+    right_recv,
+    left_send,
+    left_recv,
+    stage_sem,
 ):
-    tokens = hidden_ref.shape[2]
-    slot_rows = save_x.shape[1] // 2
-    core = place_ref[1]
-    first = place_ref[2]
+    ctx, me, chip, core, sibling = place()
+    tokens = hidden_v.shape[1]
+    width = hidden_v.shape[2]
+    slots = x_v.shape[1]
+    slot_rows = slots // 2
+    units = inner_v.shape[2]
+    total_rows = x_ref.shape[1]
+    first = ctx * local_experts
+
+    weights_in = [
+        pltpu.make_async_copy(src, dst, weight_sem.at[k])
+        for k, (src, dst) in enumerate(
+            ((gate_ref, gate_v), (up_ref, up_v), (down_ref, down_v))
+        )
+    ]
+
+    def load(i):
+        r = chunk_order(chip, i, chips)
+        return [
+            pltpu.make_async_copy(hidden_ref.at[:, r], hidden_v, load_sem.at[0]),
+            pltpu.make_async_copy(grad_ref.at[:, r], grad_v, load_sem.at[1]),
+        ]
+
+    def saves(i):
+        rows = pl.ds(i * slots, slots)
+        return [
+            pltpu.make_async_copy(src, dst.at[:, rows], save_sem.at[k])
+            for k, (src, dst) in enumerate(
+                ((x_v, x_ref), (pg_v, pg_ref), (inner_v, inner_ref), (da_v, da_ref), (db_v, db_ref))
+            )
+        ]
+
+    def out_copy(i):
+        owner = lax.rem(chip + chunk_order(chip, i, chips), chips)
+        return pltpu.make_async_copy(out_v, out_ref.at[owner], out_sem)
+
+    def swap(i):
+        r = chunk_order(chip, i, chips)
+        return remote(
+            other_v.at[lax.rem(i, 2)],
+            pair.at[r],
+            swap_send.at[r],
+            swap_recv.at[r],
+            (sibling, me),
+        )
+
+    def join(i):
+        r = chunk_order(chip, i, chips)
+        swap(i).wait_recv()
+        add_into(pair.at[r], [pair.at[r], mine_v.at[lax.rem(i, 2)]])
+
+    line = LineSum(
+        chips,
+        lambda r: lambda: [pair.at[r]],
+        lambda r: pair.at[r],
+        got,
+        (right_send, right_recv, left_send, left_recv),
+    )
+
+    for copy in load(0) + weights_in:
+        copy.start()
+    greet(chips, [], True)
+
     slot = lax.broadcasted_iota(jnp.int32, (slot_rows, tokens), 0).astype(F32) + 1.0
     slot = jnp.where(slot <= capacity, slot, -1.0)
-    lane = lax.broadcasted_iota(jnp.int32, (2 * slot_rows, LANES), 1)
-    picks = [[], []]
-    outs = [[], []]
-    backs = [[], []]
+    lane = lax.broadcasted_iota(jnp.int32, (slots, LANES), 1)
+
+    def chunk(i, carry):
+        r = chunk_order(chip, i, chips)
+        for copy in load(i):
+            copy.wait()
+
+        @pl.when(i >= 1)
+        def _():
+            for copy in saves(i - 1):
+                copy.wait()
+
+        picks = [[], []]
+        weight_rows = []
+        for e in range(local_experts):
+            rows_w = []
+            for q in range(2):
+                hit = slot == table_ref[q, r, pl.ds(first + e, 1), :]
+                pick = jnp.where(hit, 1.0, 0.0).astype(BF16)
+                weight = weight_ref[q, r, pl.ds(first + e, 1), :]
+                w = jnp.sum(jnp.where(hit, weight, 0.0), axis=1, keepdims=True)
+                rows = pl.ds(q * slot_rows, slot_rows)
+                x_v[e, rows, :] = dot(pick, hidden_v[q], NN).astype(BF16)
+                g = dot(pick, grad_v[q], NN)
+                g_v[e, rows, :] = g.astype(BF16)
+                pg_v[e, rows, :] = (w * g).astype(BF16)
+                picks[q].append(pick)
+                rows_w.append(w)
+            weight_rows.append(jnp.concatenate(rows_w, axis=0))
+
+        @pl.when(i + 1 < chips)
+        def _():
+            for copy in load(i + 1):
+                copy.start()
+
+        @pl.when(i == 0)
+        def _():
+            for copy in weights_in:
+                copy.wait()
+
+        outs = [[], []]
+        backs = [[], []]
+        for e in range(local_experts):
+            x = x_v[e]
+            pair_grad = pg_v[e]
+            w = weight_rows[e]
+            gate = gate_v[e * width : (e + 1) * width, :]
+            up = up_v[e * width : (e + 1) * width, :]
+            down = down_v[e * units : (e + 1) * units, :]
+            gate_pre = dot(x, gate, NN)
+            up_pre = dot(x, up, NN)
+            sig = jax.nn.sigmoid(gate_pre)
+            silu = gate_pre * sig
+            inner = (silu * up_pre).astype(BF16)
+            inner_v[e] = inner
+            expert_out = dot(inner, down, NN).astype(BF16).astype(F32)
+            gate_grad = jnp.sum(expert_out * g_v[e].astype(F32), axis=1, keepdims=True)
+            inner_grad = dot(pair_grad, down, NT)
+            da = (inner_grad * up_pre * sig * (1.0 + gate_pre * (1.0 - sig))).astype(BF16)
+            db = (inner_grad * silu).astype(BF16)
+            da_v[e] = da
+            db_v[e] = db
+            row_grad = (dot(da, gate, NT) + dot(db, up, NT)).astype(BF16)
+            high = gate_grad.astype(BF16).astype(F32)
+            extra = jnp.where(lane == first + e, high, 0.0) + jnp.where(
+                lane == expert_count + first + e, gate_grad - high, 0.0
+            )
+            back = jnp.concatenate([row_grad, extra.astype(BF16)], axis=1)
+            out_rows = (w * expert_out).astype(BF16)
+            for q in range(2):
+                part = slice(q * slot_rows, (q + 1) * slot_rows)
+                outs[q].append(out_rows[part])
+                backs[q].append(back[part])
+
+        for copy in saves(i):
+            copy.start()
+
+        @pl.when(i >= 1)
+        def _():
+            out_copy(i - 1).wait()
+
+        @pl.when(i >= 2)
+        def _():
+            swap(i - 2).wait_send()
+
+        for q in range(2):
+            pick = jnp.concatenate(picks[q], axis=0)
+            held = other_v if q else mine_v
+            held[lax.rem(i, 2)] = dot(pick, jnp.concatenate(backs[q], axis=0), TN).astype(BF16)
+            if q:
+                swap(i).start()
+        for q in range(2):
+            pick = jnp.concatenate(picks[q], axis=0)
+            out_v[1 - core if q else core] = dot(
+                pick, jnp.concatenate(outs[q], axis=0), TN
+            ).astype(BF16)
+        out_copy(i).start()
+
+        @pl.when(i == 0)
+        def _():
+            join(0)
+            line.step(0)
+
+        @pl.when(i >= 2)
+        def _():
+            join(i - 1)
+
+        for step in range(1, chips - 1):
+            if 2 * step < chips:
+
+                @pl.when(i == 2 * step)
+                def _():
+                    line.step(step)
+
+        return carry
+
+    lax.fori_loop(0, chips, chunk, 0)
+    join(chips - 1)
+    for copy in saves(chips - 1):
+        copy.wait()
+    out_copy(chips - 1).wait()
+    for i in range(max(0, chips - 2), chips):
+        swap(i).wait_send()
+
+    shard = width // fsdp
+    blocks = fsdp // per
+    block = per * shard
+
+    def fetch(copies):
+        copies = [
+            pltpu.make_async_copy(src, dst, save_sem.at[k])
+            for k, (src, dst) in enumerate(copies)
+        ]
+        for copy in copies:
+            copy.start()
+        for copy in copies:
+            copy.wait()
+
+    def products(e, staged, target, product):
+        def write(f):
+            return [
+                pltpu.make_async_copy(
+                    staged(lax.rem(f, 2), p),
+                    target.at[f * per + p, e],
+                    stage_sem.at[lax.rem(f, 2), p],
+                )
+                for p in range(per)
+            ]
+
+        def one(f, carry):
+            @pl.when(f >= 2)
+            def _():
+                for copy in write(f - 2):
+                    copy.wait()
+
+            product(f)
+            for copy in write(f):
+                copy.start()
+            return carry
+
+        lax.fori_loop(0, blocks, one, 0)
+        for f in range(max(0, blocks - 2), blocks):
+            for copy in write(f):
+                copy.wait()
+
+    def stage_wide(slot, p):
+        return hidden_v.at[slot, pl.ds(p * shard, shard), pl.ds(0, units)]
+
+    def wide(e, held, target):
+        def product(f):
+            columns = pl.ds(pl.multiple_of(f * block, LANES), block)
+            value = dot(
+                down_v[:total_rows, columns],
+                held[e * total_rows : (e + 1) * total_rows, :],
+                TN,
+            ).astype(BF16)
+            for p in range(per):
+                stage_wide(lax.rem(f, 2), p)[...] = value[p * shard : (p + 1) * shard, :]
+
+        products(e, stage_wide, target, product)
+
+    def tall(e, target):
+        def product(f):
+            columns = pl.ds(pl.multiple_of(f * block, LANES), block)
+            value = dot(
+                gate_v[e * total_rows : (e + 1) * total_rows, :],
+                down_v[:total_rows, columns],
+                TN,
+            ).astype(BF16)
+            for p in range(per):
+                stage_tall[lax.rem(f, 2), p] = value[:, p * shard : (p + 1) * shard]
+
+        products(e, lambda slot, p: stage_tall.at[slot, p], target, product)
+
+    work = []
     for e in range(local_experts):
-        rows_x, rows_g, rows_w = [], [], []
-        for q in range(2):
-            row = table_ref[q, 0, pl.ds(first + e, 1), :]
-            hit = slot == row
-            pick = jnp.where(hit, 1.0, 0.0).astype(BF16)
-            weight = weight_ref[q, 0, pl.ds(first + e, 1), :]
-            rows_w.append(jnp.sum(jnp.where(hit, weight, 0.0), axis=1, keepdims=True))
-            rows_x.append(dot(pick, hidden_ref[q, 0], NN).astype(BF16))
-            rows_g.append(dot(pick, grad_ref[q, 0], NN))
-            picks[q].append(pick)
-        x = jnp.concatenate(rows_x, axis=0)
-        g = jnp.concatenate(rows_g, axis=0)
-        w = jnp.concatenate(rows_w, axis=0)
-        pair_grad = (w * g).astype(BF16)
-        gate_pre = dot(x, gate_ref[e], NN)
-        up_pre = dot(x, up_ref[e], NN)
-        sig = jax.nn.sigmoid(gate_pre)
-        silu = gate_pre * sig
-        inner = (silu * up_pre).astype(BF16)
-        expert_out = dot(inner, down_ref[e], NN).astype(BF16).astype(F32)
-        gate_grad = jnp.sum(expert_out * g, axis=1, keepdims=True)
-        inner_grad = dot(pair_grad, down_ref[e], NT)
-        da = (inner_grad * up_pre * sig * (1.0 + gate_pre * (1.0 - sig))).astype(BF16)
-        db = (inner_grad * silu).astype(BF16)
-        row_grad = (dot(da, gate_ref[e], NT) + dot(db, up_ref[e], NT)).astype(BF16)
-        high = gate_grad.astype(BF16).astype(F32)
-        extra = jnp.where(lane == first + e, high, 0.0) + jnp.where(
-            lane == expert_count + first + e, gate_grad - high, 0.0
-        )
-        back = jnp.concatenate([row_grad, extra.astype(BF16)], axis=1)
-        out_rows = (w * expert_out).astype(BF16)
-        for q in range(2):
-            part = slice(q * slot_rows, (q + 1) * slot_rows)
-            outs[q].append(out_rows[part])
-            backs[q].append(back[part])
-        save_x[e] = x
-        save_pg[e] = pair_grad
-        save_inner[e] = inner
-        save_da[e] = da
-        save_db[e] = db
-    for q in range(2):
-        pick = jnp.concatenate(picks[q], axis=0)
-        rows_ref = rows_mine if q == 0 else rows_other
-        out_ref[0, core if q == 0 else 1 - core] = dot(
-            pick, jnp.concatenate(outs[q], axis=0), TN
-        ).astype(BF16)
-        rows_ref[0] = dot(pick, jnp.concatenate(backs[q], axis=0), TN).astype(BF16)
-
-
-def expert_rows_pass(
-    where, hidden, grad, table, weights, gate, up, down, capacity, expert_count
+        copies = [(x_ref.at[e], down_v.at[:total_rows])]
+        if e == 0:
+            for k in range(local_experts):
+                held = pl.ds(k * total_rows, total_rows)
+                copies += [(da_ref.at[k], gate_v.at[held]), (db_ref.at[k], up_v.at[held])]
+        work.append(lambda copies=copies: fetch(copies))
+        work.append(lambda e=e: wide(e, gate_v, gate_grad_ref))
+        work.append(lambda e=e: wide(e, up_v, up_grad_ref))
+    for e in range(local_experts):
+        copies = [(pg_ref.at[e], down_v.at[:total_rows])]
+        if e == 0:
+            for k in range(local_experts):
+                copies.append((inner_ref.at[k], gate_v.at[pl.ds(k * total_rows, total_rows)]))
+        work.append(lambda copies=copies: fetch(copies))
+        work.append(lambda e=e: tall(e, down_grad_ref))
+    late = [step for step in range(1, chips - 1) if 2 * step >= chips]
+    for n, task in enumerate(work):
+        task()
+        if n == LINE_TASK or (n > LINE_TASK and late):
+            if late:
+                line.step(late.pop(0))
+    for step in late:
+        line.step(step)
+
+    line.total(returned_ref)
+    line.finish()
+
+
+def experts_pass(
+    hidden, grad, table, weights, gate, up, down, capacity, expert_count, fsdp, collective_id
 ):
     unused, chips, tokens, width = grad.shape
-    local_experts, unused, hidden_units = gate.shape
+    local_experts, unused, units = gate.shape
     slots = 2 * SLOT_STEP * -(-capacity // SLOT_STEP)
     total = chips * slots
-    once = pl.Buffered(1)
-
-    def whole(shape):
-        return pl.BlockSpec(shape, lambda r, s: (0,) * len(shape), pipeline_mode=once)
-
-    def saved(columns):
-        return pl.BlockSpec((local_experts, slots, columns), lambda r, s: (0, r, 0))
-
-    chunk = pl.BlockSpec((2, 1, tokens, width), lambda r, s: (0, r, 0, 0))
-    placed = pl.BlockSpec(
-        (1, 2, tokens, width), lambda r, s: (lax.rem(s[0] + r, chips), 0, 0, 0)
-    )
-    wide = pl.BlockSpec((1, tokens, width + LANES), lambda r, s: (r, 0, 0))
-    small = pl.BlockSpec((2, 1, expert_count, tokens), lambda r, s: (0, r, 0, 0))
-    flops = 2 * total * width * hidden_units * local_experts * 6 + 8 * total * tokens * width
-    return pl.pallas_call(
-        functools.partial(expert_kernel, capacity, local_experts, expert_count),
-        grid_spec=pltpu.PrefetchScalarGridSpec(
-            num_scalar_prefetch=1,
-            grid=(chips,),
-            in_specs=[
-                chunk,
-                chunk,
-                small,
-                small,
-                whole(gate.shape),
-                whole(up.shape),
-                whole(down.shape),
-            ],
-            out_specs=[
-                placed,
-                wide,
-                wide,
-                saved(width),
-                saved(width),
-                saved(hidden_units),
-                saved(hidden_units),
-                saved(hidden_units),
-            ],
+    shard = width // fsdp
+    per = 1 if shard % LANES == 0 else 2
+    wide = width + LANES
+    anywhere = pl.BlockSpec(memory_space=pl.ANY)
+    vmem = pl.BlockSpec(memory_space=pltpu.VMEM)
+    flops = 2 * total * width * units * local_experts * 9 + 8 * total * tokens * width
+    saved = [(local_experts, total, width)] * 2 + [(local_experts, total, units)] * 3
+    held = [(local_experts, slots, width)] * 3 + [(local_experts, slots, units)] * 3
+    outs = pl.pallas_call(
+        functools.partial(
+            experts_kernel, capacity, local_experts, expert_count, chips, fsdp, per
         ),
-        out_shape=[jax.ShapeDtypeStruct((chips, 2, tokens, width), BF16)]
-        + [jax.ShapeDtypeStruct((chips, tokens, width + LANES), BF16)] * 2
-        + [jax.ShapeDtypeStruct((local_experts, total, width), BF16)] * 2
-        + [jax.ShapeDtypeStruct((local_experts, total, hidden_units), BF16)] * 3,
-        compiler_params=pltpu.CompilerParams(vmem_limit_bytes=VMEM_BYTES),
+        out_shape=[
+            jax.ShapeDtypeStruct((tokens, wide), BF16),
+            jax.ShapeDtypeStruct((chips, 2, tokens, width), BF16),
+            jax.ShapeDtypeStruct((fsdp, local_experts, shard, units), BF16),
+            jax.ShapeDtypeStruct((fsdp, local_experts, shard, units), BF16),
+            jax.ShapeDtypeStruct((fsdp, local_experts, units, shard), BF16),
+        ]
+        + [jax.ShapeDtypeStruct(shape, BF16) for shape in saved],
+        in_specs=[anywhere, anywhere, vmem, vmem, anywhere, anywhere, anywhere],
+        out_specs=[vmem] + [anywhere] * 9,
+        scratch_shapes=[
+            pltpu.VMEM((local_experts * width, units), BF16),
+            pltpu.VMEM((local_experts * width, units), BF16),
+            pltpu.VMEM((local_experts * units, width), BF16),
+            pltpu.VMEM((2, tokens, width), BF16),
+            pltpu.VMEM((2, tokens, width), BF16),
+            pltpu.VMEM((2, tokens, width), BF16),
+        ]
+        + [pltpu.VMEM(shape, BF16) for shape in held]
+        + [
+            pltpu.VMEM((2, tokens, wide), BF16),
+            pltpu.VMEM((2, tokens, wide), BF16),
+            pltpu.VMEM((chips, tokens, wide), BF16),
+            pltpu.VMEM((chips + 1, tokens, wide), BF16),
+            pltpu.VMEM((2, per, units, shard), BF16),
+            pltpu.SemaphoreType.DMA((3,)),
+            pltpu.SemaphoreType.DMA((2,)),
+            pltpu.SemaphoreType.DMA,
+            pltpu.SemaphoreType.DMA((5,)),
+            pltpu.SemaphoreType.DMA((chips,)),
+            pltpu.SemaphoreType.DMA((chips,)),
+        ]
+        + [pltpu.SemaphoreType.DMA((chips - 1,)) for unused in range(4)]
+        + [pltpu.SemaphoreType.DMA((2, per))],
+        compiler_params=pltpu.CompilerParams(
+            collective_id=collective_id, has_side_effects=True, vmem_limit_bytes=EXPERT_VMEM_BYTES
+        ),
         cost_estimate=pl.CostEstimate(
-            flops=flops, bytes_accessed=80_000_000, transcendentals=total * hidden_units * 2
+            flops=flops, bytes_accessed=100_000_000, transcendentals=total * units * 2
         ),
-        name="expert_rows",
-    )(where, hidden, grad, table, weights, gate, up, down)
-
-
-def outer_kernel(per, split_left, left_ref, right_ref, out_ref):
-    product = dot(left_ref[0], right_ref[0], TN).astype(BF16)
-    axis = 0 if split_left else 1
-    size = product.shape[axis] // per
-    for i in range(per):
-        out_ref[i, 0] = lax.slice_in_dim(product, i * size, (i + 1) * size, axis=axis)
-
-
-def outer_products(left, right, fsdp, split_left):
-    experts, total, m = left.shape
-    n = right.shape[2]
-    per = 1 if ((m if split_left else n) // fsdp) % LANES == 0 else 2
-    if split_left:
-        m = m // fsdp
-    else:
-        n = n // fsdp
-    return pl.pallas_call(
-        functools.partial(outer_kernel, per, split_left),
-        grid=(experts, fsdp // per),
-        out_shape=jax.ShapeDtypeStruct((fsdp, experts, m, n), BF16),
-        in_specs=[
-            pl.BlockSpec(
-                (1, total, m * per if split_left else m),
-                lambda e, f: (e, 0, f if split_left else 0),
-            ),
-            pl.BlockSpec(
-                (1, total, n if split_left else n * per),
-                lambda e, f: (e, 0, 0 if split_left else f),
-            ),
-        ],
-        out_specs=pl.BlockSpec((per, 1, m, n), lambda e, f: (f, e, 0, 0)),
-        compiler_params=pltpu.CompilerParams(vmem_limit_bytes=VMEM_BYTES),
-        cost_estimate=pl.CostEstimate(
-            flops=2 * total * m * n * experts * fsdp, bytes_accessed=14_000_000, transcendentals=0
-        ),
-        name="outer_products",
-    )(left, right)
+        name="experts",
+    )(
+        hidden,
+        grad,
+        table,
+        weights,
+        gate.reshape(local_experts * width, units),
+        up.reshape(local_experts * width, units),
+        down.reshape(local_experts * units, width),
+    )
+    return outs[:5]
 
 
 def body(
@@ -1251,18 +1515,7 @@
     gate_weights = jnp.where(routed > 0, jax.nn.softmax(chosen, axis=-1), 0.0)
 
     hidden_all, weights_all = gather([], [hidden_two, gate_weights.T], chips - 1, fsdp, chips, 2)
-    where = jnp.stack([chip, core, ctx_index * local_experts]).astype(jnp.int32)
-    (
-        out_rows,
-        rows_mine,
-        rows_other,
-        save_x,
-        save_pg,
-        save_inner,
-        save_da,
-        save_db,
-    ) = expert_rows_pass(
-        where,
+    returned, out_rows, gate_local, up_local, down_local = experts_pass(
         hidden_all,
         grad_all,
         table_all,
@@ -1272,15 +1525,11 @@
         down_full,
         capacity,
         expert_count,
-    )
-    gate_local = outer_products(save_x, save_da, fsdp, True)
-    up_local = outer_products(save_x, save_db, fsdp, True)
-    down_local = outer_products(save_inner, save_pg, fsdp, False)
-    returned = line_reduce_now(
-        after(rows_mine, gate_local, up_local, down_local), rows_other, chips, 5
+        fsdp,
+        5,
     )
     out_sum = lax.psum_scatter(
-        after(out_rows, returned).reshape(2 * chips, tok_rows, width),
+        out_rows.reshape(2 * chips, tok_rows, width),
         "ctx",
         scatter_dimension=0,
         tiled=True,
@@ -1291,6 +1540,7 @@
     ]
 
     out_grad = grad_out[0].astype(F32)
+    returned = returned.astype(F32)
     extra = returned[:, width:]
     gate_grad = extra[:, :expert_count] + extra[:, expert_count : 2 * expert_count]
     logit_grad = (

time: 865 us -> 792 us (0.916)
  Pallas kernels: 692 us -> 637 us
  starting transfers between devices: 11.6 us -> 0.27 us
    pallas_call x2 -> x1, Pallas kernels: 160 us -> 36.3 us  [line_reduce_now(): pl.pallas_call(functools.partial(line_reduce_kernel, chips), out_shape=ja...]
    pallas_call x1, Pallas kernels: 109 us -> 153 us  [dense_reduce(): pl.pallas_call(functools.partial(dense_reduce_kernel, fsdp, chips, tuple(...]
    pallas_call x4 -> x1, Pallas kernels: 91.7 us -> 117 us  [experts_pass(): pl.pallas_call(functools.partial(experts_kernel, capacity, local_experts,...]
    unnamed x3, starting transfers between devices: 11.4 us -> 0.12 us
  transfers between devices with their start and end apart: 7 -> 7, of which waited for: 0 -> 0; matrix products, arithmetic and copies ran while one was open for 14% -> 14% of each run, Pallas kernels for 65% -> 58%
where the time goes in v3:
time: 792 us; the launch traced here: 782 us
  Pallas kernels  637 us (80%)
  local copies, waits for them, and re-layouts  46.1 us (6%)
  other arithmetic  41.7 us (5%)
  matrix products  38.1 us (5%)
  between operations  15.4 us (2%)
    pallas_call x3, Pallas kernels, gather(): pl.pallas_call(functools.partial(gather_kernel, len(dense), len(line), le...  217 us
    pallas_call x1, Pallas kernels, dense_reduce(): pl.pallas_call(functools.partial(dense_reduce_kernel, fsdp, chips, tuple(...  153 us
    pallas_call x1, Pallas kernels, experts_pass(): pl.pallas_call(functools.partial(experts_kernel, capacity, local_experts,...  117 us
    pallas_call x2, Pallas kernels, attention_back(): pl.pallas_call(functools.partial(attention_back_kernel, HEAD_SIZE ** (-0....  62.2 us
    pallas_call x2, Pallas kernels, attention(): pl.pallas_call(functools.partial(attention_kernel, HEAD_SIZE ** (-0.5)),...  51.7 us
    pallas_call x1, Pallas kernels, line_reduce_now(): pl.pallas_call(functools.partial(line_reduce_kernel, chips), out_shape=ja...  36.3 us
  transfers between devices with their start and end apart: 7, of which 0 were waited for; matrix products, arithmetic and copies ran while one was open for 14% of the time, Pallas kernels for 58%

profile of v3, /device:TPU:0, one launch (start us, length us, event | category | flops | bytes accessed | tf_op | source)
XLA Modules:
  0.0 781.5 jit_solution(9048444006967469739)
XLA Ops:
  7.2 0.8 broadcast_in_dim.46
  8.0 0.8 broadcast_in_dim.47
  8.8 0.8 copy.126
  9.7 2.9 pad_maximum_fusion.1.refs_0_
  12.6 0.8 maximum_maximum_fusion.refs_1_
  13.4 65.3 %gather.3 = (bf16[1536,2048]{1,0:T(8,128)(2,1)}, bf16[1536,128]{1,0:T(8,128)(2,1)}, bf16[2,4,384,1536]{3,2,1,0:T(8,128)(2,1)}) custom-call(bf16[384,2048]{1,0:T(8,128)(2,1)} %pad_maximum_fusion.1.refs_0_, bf16[384,128]{1,0:T(8,128)(2,1)} %maximum_maximum_fusion.refs_1_, bf16[384,1536]{1,0:T(8,128)(2,1)} %bitcast.95), custom_call_target="tpu_custom_call" | custom-call | tf_op jit(solution)/shard_map/gather/pallas_call | solution.py:341
  81.8 4.8 fusion.21
  89.6 2.2 copy.129
  92.0 1.1 fusion.38
  93.1 2.2 multiply_subtract_fusion
  97.0 1.5 copy.136.q_ref
  98.5 0.8 copy.138.pq_ref
  99.3 0.8 copy.137.oq_ref
  100.1 0.8 pad_maximum_fusion.4.refs_1_
  100.9 65.4 %gather.4 = (bf16[1536,1536]{1,0:T(8,128)(2,1)}, bf16[2,4,384,512]{3,2,1,0:T(8,128)(2,1)}, f32[2,4,16,384]{3,2,1,0:T(8,128)}, bf16[2,4,384,1536]{3,2,1,0:T(8,128)(2,1)}) custom-call(bf16[384,1536]{1,0:T(8,128)(2,1)} %refs_0_.1, bf16[384,512]{1,0:T(8,128)(2,1)} %pad_maximum_fusion.4.refs_1_, ...), custom_call_target="tpu_custom_call", output_to_operand_aliasing={{3}: (3, {})} | custom-call | tf_op jit(solution)/shard_map/gather/pallas_call | solution.py:341
  166.3 25.8 %attention.2 = (bf16[384,768]{1,0:T(8,128)(2,1)}, f32[6,1,384]{2,1,0:T(1,128)}) custom-call(bf16[384,1536]{1,0:T(8,128)(2,1)} %copy.136.q_ref, bf16[3072,512]{1,0:T(8,128)(2,1)} %bitcast.111, bf16[3072,512]{1,0:T(8,128)(2,1)} %bitcast.112, s32[384,1]{1,0:T(8,128)} %copy.137.oq_ref, s32[384,1]{1,0:T(8,128)} %copy.138.pq_ref, ...), custom_call_target="tpu_custom_call" | custom-call | flops 3623878656 | bytes 2752512 | tf_op jit(solution)/shard_map/attention/pallas_call | solution.py:825
  192.1 1.4 copy.139.q_ref
  193.6 25.9 %attention.3 = (bf16[384,768]{1,0:T(8,128)(2,1)}, f32[6,1,384]{2,1,0:T(1,128)}) custom-call(bf16[384,1536]{1,0:T(8,128)(2,1)} %copy.139.q_ref, bf16[3072,512]{1,0:T(8,128)(2,1)} %bitcast.113, bf16[3072,512]{1,0:T(8,128)(2,1)} %bitcast.114, s32[384,1]{1,0:T(8,128)} %copy.137.oq_ref, s32[384,1]{1,0:T(8,128)} %copy.138.pq_ref, ...), custom_call_target="tpu_custom_call" | custom-call | flops 3623878656 | bytes 2752512 | tf_op jit(solution)/shard_map/attention/pallas_call | solution.py:825
  219.5 1.1 constant_dynamic-update-slice_fusion
  220.6 5.4 multiply_reduce_fusion.2
  226.9 1.0 copy-done
  229.7 0.9 fusion.28
  230.6 1.6 copy.144.refs_1_
  232.2 86.5 %gather.5 = (bf16[2,4,384,1536]{3,2,1,0:T(8,128)(2,1)}, f32[2,4,16,384]{3,2,1,0:T(8,128)}) custom-call(bf16[384,1536]{1,0:T(8,128)(2,1)} %copy-done, f32[16,384]{1,0:T(8,128)} %copy.144.refs_1_), custom_call_target="tpu_custom_call" | custom-call | tf_op jit(solution)/shard_map/gather/pallas_call | solution.py:341
  318.8 116.8 %experts.1 = (bf16[384,1664]{1,0:T(8,128)(2,1)}, bf16[4,2,384,1536]{3,2,1,0:T(8,128)(2,1)}, bf16[4,2,384,768]{3,2,1,0:T(8,128)(2,1)}, bf16[4,2,384,768]{3,2,1,0:...) custom-call(bf16[2,4,384,1536]{3,2,1,0:T(8,128)(2,1)} %get-tuple-ele, ...), custom_call_target="tpu_custom_call" | custom-call | flops 48318382080 | bytes 100000000 | tf_op jit(solution)/shard_map/experts/pallas_call | solution.py:1348
  437.6 3.3 broadcast_in_dim_reshape.10.ok_ref
  440.9 1.4 copy.145.q_ref
  442.3 1.3 reshape_subtract_fusion.pq_ref
  443.6 1.5 convert_element_type.166
  445.9 1.4 multiply_reduce_fusion
  447.9 0.8 slice-done
  449.0 3.0 convolution_convert_fusion.2.do_ref
  452.0 31.2 %attention_back.2 = (f32[384,768]{1,0:T(8,128)}, bf16[3072,128]{1,0:T(8,128)(2,1)}, bf16[3072,128]{1,0:T(8,128)(2,1)}) custom-call(bf16[384,1536]{1,0:T(8,128)(2,1)} %copy.145.q_ref, bf16[3072,512]{1,0:T(8,128)(2,1)} %bitcast.115, bf16[3072,512]{1,0:T(8,128)(2,1)} %bitcast.116, bf16[384,768]{1,0:T(8,128)(2,1)} %get-tuple-element.54.o_ref, ...), custom_call_target="tpu_custom_call" | custom-call | flops 9059696640 | bytes 6094848 | tf_op jit(solution)/shard_map/attention_back/pallas_call | solution.py:928
  483.2 1.3 constant_dynamic-update-slice_fusion.5
  484.5 31.0 %attention_back.3 = (f32[384,768]{1,0:T(8,128)}, bf16[3072,128]{1,0:T(8,128)(2,1)}, bf16[3072,128]{1,0:T(8,128)(2,1)}) custom-call(bf16[384,1536]{1,0:T(8,128)(2,1)} %copy.145.q_ref, bf16[3072,512]{1,0:T(8,128)(2,1)} %bitcast.117, bf16[3072,512]{1,0:T(8,128)(2,1)} %bitcast.118, bf16[384,768]{1,0:T(8,128)(2,1)} %get-tuple-element.56.o_ref, ...), custom_call_target="tpu_custom_call" | custom-call | flops 9059696640 | bytes 6094848 | tf_op jit(solution)/shard_map/attention_back/pallas_call | solution.py:928
  515.6 1.4 constant_dynamic-update-slice_fusion.4
  517.4 1.9 fusion.46
  519.3 36.3 %line_reduce.1 = f32[384,512]{1,0:T(8,128)} custom-call(bf16[4,384,512]{2,1,0:T(8,128)(2,1)} %bitcast.94, bf16[4,384,512]{2,1,0:T(8,128)(2,1)} %bitcast.93), custom_call_target="tpu_custom_call" | custom-call | tf_op jit(solution)/shard_map/line_reduce/pallas_call | solution.py:518
  555.5 1.0 slice.102
  556.6 1.7 slice.161
  558.3 1.7 pad_maximum_fusion
  560.0 3.7 copy.149
  563.7 1.7 copy.150
  565.4 1.8 convolution_convert_fusion.3
  567.2 1.0 copy.151
  568.3 0.9 reshape.287
  569.2 2.4 subtract_convert_fusion
  571.8 1.5 copy-done.8
  573.4 8.0 %fusion.3 = (bf16[1536]{0:T(1024)(128)(2,1)}, f32[384]{0:T(512)}, f32[384,1536]{1,0:T(8,128)}) fusion(bf16[1,384,1536]{2,1,0:T(8,128)(2,1)S(1)} %copy-done.8, f32[384]{0:T(512)S(1)} %copy-done.46, f32[1536]{0:T(1024)S(1)} %get-tuple-element.151, bf16[1536,2048]{1,0:T(8,128)(2,1)} %get-tuple-element.51, bf16[384,256]{0,1:T(8,128)(2,1)S(1)} %copy-done.29, ...), kind=kOutput, calls=%fused_computation.16 | convolution fusion | flops 2423191552 | bytes 11415552 | tf_op jit(solution)/shard_map/tc,dc->td/dot_general | solution.py:1590
  582.0 1.3 stack_reshape.11
  583.3 0.8 fusion.37
  584.8 7.0 convolution_convert_fusion
  591.8 5.8 convolution_convert_fusion.1
  597.7 152.5 %dense_reduce.1 = (bf16[2,192,2048]{2,1,0:T(8,128)(2,1)}, bf16[2,192,1536]{2,1,0:T(8,128)(2,1)}, bf16[2,16,512]{2,1,0:T(8,128)(2,1)}) custom-call(bf16[4,2,192,2048]{3,2,1,0:T(8,128)(2,1)} %bitcast.92, bf16[4,2,192,1536]{3,2,1,0:T(8,128)(2,1)} %bitcast.96, bf16[4,2,16,512]{3,2,1,0:T(8,128)(2,1)} %pad_maximum_fusion.5.refs_2_), custom_call_target="tpu_custom_call" | custom-call | tf_op jit(solution)/shard_map/dense_reduce/pallas_call | solution.py:756
  750.2 1.3 slice_convert_fusion.5
  751.5 1.5 reshape.296
  753.1 1.6 copy.154
  754.7 1.4 convert_reduce_fusion.3
  756.8 2.1 slice_convert_fusion.3
  758.8 3.0 slice_convert_fusion
  761.8 1.8 bitcast_convert_fusion.3
  763.6 3.0 bitcast_convert_fusion
  766.6 2.6 bitcast_convert_fusion.1
  769.2 5.1 fusion.10
  (174 shorter events, 16.8 us)
Async XLA Ops:
  7.2 311.6 %all-gather.4.cloned.1.call-start = ((), (), s32[]{:S(2)}) async-start(), calls=%async_computation.4 | async-start | bytes 5898240 | tf_op jit(solution)/shard_map/all_gather | solution.py:1452
  78.7 1.6 copy-start.10
  78.7 2.1 copy-start.6
  78.8 240.0 %all-gather.6.cloned.1.call-start = ((), (), s32[]{:S(2)}) async-start(), calls=%async_computation.5 | async-start | bytes 5898240 | tf_op jit(solution)/shard_map/all_gather | solution.py:1453
  79.5 239.3 %all-gather.8.cloned.1.call-start = ((), (), s32[]{:S(2)}) async-start(), calls=%async_computation.6 | async-start | bytes 5898240 | tf_op jit(solution)/shard_map/all_gather | solution.py:1454
  80.2 683.3 %reduce-scatter.17.cloned.1.call-start = ((), (), s32[]{:S(2)}) async-start(), calls=%async_computation.10 | async-start | bytes 5898240
  81.2 0.6 copy-start.42
  81.2 0.6 copy-start.45
  86.6 1.5 copy-start.44
  86.6 2.8 copy-start.52
  88.8 3.0 copy-start.31
  91.8 7.5 copy-start.41
  92.0 6.5 copy-start.38
  93.1 2.3 copy-start.22
  93.1 2.4 copy-start.51
  95.6 1.4 copy-start.3
  95.7 1.3 copy-start.32
  96.8 3.3 copy-start.26
  192.1 1.5 copy-start.27
  193.6 27.0 %copy-start.7 = (bf16[1,384,1536]{2,1,0:T(8,128)(2,1)S(1)}, bf16[1,384,1536]{2,1,0:T(8,128)(2,1)}, u32[]{:S(2)}) copy-start(bf16[1,384,1536]{2,1,0:T(8,128)(2,1)} %param.15) | copy-start | bytes 3538948
  220.6 5.4 copy-start.28
  226.0 2.5 copy-start.49
  226.0 1.9 copy-start.11
  226.0 1.9 copy-start.33
  226.1 0.6 copy-start.39
  226.6 1.9 copy-start.4
  226.9 1.0 copy-start
  228.5 0.7 copy-start.13
  228.5 0.7 copy-start.34
  229.2 0.6 copy-start.36
  435.7 327.9 %reduce-scatter.13.cloned.1.call-start = ((), (), s32[]{:S(2)}) async-start(), calls=%async_computation.8 | async-start | bytes 5898240
  436.3 327.3 %reduce-scatter.15.cloned.1.call-start = ((), (), s32[]{:S(2)}) async-start(), calls=%async_computation.9 | async-start | bytes 5898240
  436.8 332.3 %reduce-scatter.11.cloned.1.call-start = ((), (), s32[]{:S(2)}) async-start(), calls=%async_computation.7 | async-start | bytes 10616832 | tf_op jit(solution)/shard_map/reduce_scatter | solution.py:1531
  442.3 2.8 copy-start.5
  442.3 2.8 copy-start.14
  442.3 2.8 copy-start.35
  442.3 2.8 copy-start.37
  443.6 2.2 copy-start.12
  443.6 2.2 copy-start.40
  445.8 1.5 copy-start.23
  445.8 1.5 copy-start.50
  445.8 1.5 copy-start.9
  445.8 2.9 slice-start
  447.3 1.7 slice-start.1
  449.0 3.0 copy-start.2
  484.5 32.5 %copy-start.24 = (bf16[3072,128]{1,0:T(8,128)(2,1)S(1)}, bf16[3072,128]{1,0:T(8,128)(2,1)}, u32[]{:S(2)}) copy-start(bf16[3072,128]{1,0:T(8,128)(2,1)} %get-tuple-element.74) | copy-start | bytes 2359300
  515.6 1.6 copy-start.25
  519.2 39.0 %copy-start.20 = (f32[384,768]{1,0:T(8,128)S(1)}, f32[384,768]{1,0:T(8,128)}, u32[]{:S(2)}) copy-start(f32[384,768]{1,0:T(8,128)} %get-tuple-element.68) | copy-start | bytes 3538948
  519.2 39.0 %copy-start.21 = (f32[384,768]{1,0:T(8,128)S(1)}, f32[384,768]{1,0:T(8,128)}, u32[]{:S(2)}) copy-start(f32[384,768]{1,0:T(8,128)} %get-tuple-element.71) | copy-start | bytes 3538948
  560.0 5.4 copy-start.1
  571.6 1.7 copy-start.8
  571.6 1.8 copy-start.29
  571.6 1.8 copy-start.46
  571.8 9.6 %copy-start.15 = (bf16[384,14,128]{0,2,1:T(8,128)(2,1)}, bf16[384,14,128]{0,2,1:T(8,128)(2,1)S(1)}, u32[]{:S(2)}) copy-start(bf16[384,14,128]{0,2,1:T(8,128)(2,1)S(1)} %pad_maximum_fusion.3) | copy-start | bytes 4128772
  584.8 7.0 copy-start.16
  584.8 7.0 copy-start.30
  584.8 7.0 copy-start.47
  597.7 158.4 %copy-start.43 = (f32[384]{0:T(512)S(1)}, f32[384]{0:T(512)}, u32[]{:S(2)}) copy-start(f32[384]{0:T(512)} %copy-done.42) | copy-start | bytes 4612
  756.8 5.0 copy-start.19
  763.6 3.0 copy-start.17
  763.6 3.0 copy-start.18
  766.6 2.6 copy-start.48
Sparse Core Ops, SparseCore 0:
  78.9 76.2 all-gather.3
  157.0 56.0 all-gather.5
  214.9 56.9 all-gather.7
  435.8 55.0 reduce-scatter.16
  493.7 57.0 reduce-scatter.12
  553.7 58.4 reduce-scatter.14
  614.5 132.1 reduce-scatter.10

commit v4 on v3

--- a/solution.py
+++ b/solution.py
@@ -22,6 +22,7 @@
 KEY_TILE = 512
 VMEM_BYTES = 56 * 1024 * 1024
 EXPERT_VMEM_BYTES = 119 * 512 * 1024
+BACK_VMEM_BYTES = 61 * 1024 * 1024
 MESH = pl.DeviceIdType.MESH
 F32 = jnp.float32
 BF16 = jnp.bfloat16
@@ -470,8 +471,8 @@
         def _():
             add_into(target, [self.from_right(last), self.from_left(last)] + parts())
 
-    def finish(self):
-        for step in range(self.chips - 1):
+    def finish(self, steps=None):
+        for step in range(self.chips - 1 if steps is None else steps):
 
             @pl.when(self.chip <= step)
             def _():
@@ -480,55 +481,6 @@
             @pl.when(self.chip >= self.chips - 1 - step)
             def _():
                 self.left(step).wait_send()
-
-
-def line_reduce_kernel(
-    chips, mine_ref, other_ref, out_ref, pair, got, ps, pr, s0, s1, s2, s3
-):
-    ctx, me, chip, core, sibling = place()
-    greet(chips, [], True)
-    swaps = [
-        remote(other_ref.at[r], pair.at[r], ps.at[r], pr.at[r], (sibling, me))
-        for r in range(chips)
-    ]
-    order = []
-    for step in range(chips - 1):
-        for r in (chips - 1 - step, step + 1):
-            if r not in order:
-                order.append(r)
-    for r in order + [0]:
-        swaps[r].start()
-
-    def held(r):
-        swaps[r].wait_recv()
-        return lambda: [mine_ref.at[r], pair.at[r]]
-
-    line = LineSum(chips, held, lambda r: pair.at[r], got, (s0, s1, s2, s3))
-    for step in range(chips - 1):
-        line.step(step)
-    line.total(out_ref)
-    line.finish()
-    for swap in swaps:
-        swap.wait_send()
-
-
-def line_reduce_now(mine, other, chips, collective_id):
-    unused, rows, width = mine.shape
-    vmem = pl.BlockSpec(memory_space=pltpu.VMEM)
-    return pl.pallas_call(
-        functools.partial(line_reduce_kernel, chips),
-        out_shape=jax.ShapeDtypeStruct((rows, width), F32),
-        in_specs=[vmem, vmem],
-        out_specs=vmem,
-        scratch_shapes=[pltpu.VMEM((chips, rows, width), BF16)]
-        + [pltpu.VMEM((chips + 1, rows, width), BF16)]
-        + [pltpu.SemaphoreType.DMA((chips,)) for unused in range(2)]
-        + [pltpu.SemaphoreType.DMA((chips - 1,)) for unused in range(4)],
-        compiler_params=pltpu.CompilerParams(
-            collective_id=collective_id, has_side_effects=True, vmem_limit_bytes=VMEM_BYTES
-        ),
-        name="line_reduce",
-    )(mine, other)
 
 
 DENSE_BUFFERS = 5
@@ -700,9 +652,25 @@
 def dense_reduce_kernel(fsdp, chips, cuts, *refs):
     count = len(cuts)
     arrays = max(cut[0] for cut in cuts) + 1
-    ins, outs, rest = refs[:arrays], refs[arrays : 2 * arrays], refs[2 * arrays :]
+    ins, refs = refs[:arrays], refs[arrays:]
+    own_ref, right_ref, left_ref = refs[:3]
+    outs, total_ref, refs = refs[3 : 3 + arrays], refs[3 + arrays], refs[4 + arrays :]
+    from_left, from_right, r_send, r_recv, l_send, l_recv = refs[:6]
+    rest = refs[6:]
     ctx, me, chip, core, sibling = place()
     greet(chips, peers_of(me, fsdp), True)
+
+    to_right = remote(right_ref, from_left, r_send, r_recv, (ctx + 2, me))
+    to_left = remote(left_ref, from_right, l_send, l_recv, (ctx - 2, me))
+
+    @pl.when(chip + 1 < chips)
+    def _():
+        to_right.start()
+
+    @pl.when(chip >= 1)
+    def _():
+        to_left.start()
+
     sums = []
     for i, (which, start, size) in enumerate(cuts):
         buffers = rest[i * DENSE_BUFFERS : (i + 1) * DENSE_BUFFERS]
@@ -727,11 +695,39 @@
         for i in range(count):
             if 0 <= tick - lag * i < len(stages[i]):
                 stages[i][tick - lag * i]()
+    @pl.when(chip >= 1)
+    def _():
+        to_right.wait_recv()
+
+    @pl.when(chip + 1 < chips)
+    def _():
+        to_left.wait_recv()
+
+    @pl.when(chip == 0)
+    def _():
+        add_into(total_ref, [from_right, own_ref])
+
+    @pl.when(chip == chips - 1)
+    def _():
+        add_into(total_ref, [from_left, own_ref])
+
+    @pl.when((chip >= 1) & (chip + 1 < chips))
+    def _():
+        add_into(total_ref, [from_left, from_right, own_ref])
+
     for one in sums:
         one.finish()
 
-
-def dense_reduce(arrays, piece, fsdp, chips, collective_id):
+    @pl.when(chip + 1 < chips)
+    def _():
+        to_right.wait_send()
+
+    @pl.when(chip >= 1)
+    def _():
+        to_left.wait_send()
+
+
+def dense_reduce(arrays, own, right, left, piece, fsdp, chips, collective_id):
     vmem = pl.BlockSpec(memory_space=pltpu.VMEM)
     cuts, buffers = [], []
     for i, a in enumerate(arrays):
@@ -755,15 +751,20 @@
     )
     return pl.pallas_call(
         functools.partial(dense_reduce_kernel, fsdp, chips, tuple(cuts)),
-        out_shape=[jax.ShapeDtypeStruct(a.shape[1:], BF16) for a in arrays],
-        in_specs=[vmem] * len(arrays),
-        out_specs=[vmem] * len(arrays),
-        scratch_shapes=buffers + sems * len(cuts),
+        out_shape=[jax.ShapeDtypeStruct(a.shape[1:], BF16) for a in arrays]
+        + [jax.ShapeDtypeStruct(own.shape, F32)],
+        in_specs=[vmem] * len(arrays) + [vmem, pl.BlockSpec(memory_space=pl.ANY)]
+        + [pl.BlockSpec(memory_space=pl.ANY)],
+        out_specs=[vmem] * (len(arrays) + 1),
+        scratch_shapes=[pltpu.VMEM(own.shape, BF16)] * 2
+        + [pltpu.SemaphoreType.DMA] * 4
+        + buffers
+        + sems * len(cuts),
         compiler_params=pltpu.CompilerParams(
             collective_id=collective_id, has_side_effects=True, vmem_limit_bytes=VMEM_BYTES
         ),
         name="dense_reduce",
-    )(*arrays)
+    )(*arrays, own, right, left)
 
 
 def after(value, *others):
@@ -854,7 +855,7 @@
 
 def attention_back_kernel(
     scale,
-    per_group,
+    chips,
     q_ref,
     k_ref,
     v_ref,
@@ -864,20 +865,112 @@
     oq_ref,
     pq_ref,
     ok_ref,
+    mine_ref,
+    other_ref,
     dq_ref,
-    dk_ref,
-    dv_ref,
+    kv_ref,
+    own_ref,
+    right_ref,
+    left_ref,
     bias,
     dk_acc,
     dv_acc,
+    mine_v,
+    pair,
+    got,
+    kv_v,
+    kv_pair,
+    kv_got,
+    load_sem,
+    store_sem,
+    swap_send,
+    swap_recv,
+    r_send,
+    r_recv,
+    l_send,
+    l_recv,
+    kv_swap_send,
+    kv_swap_recv,
+    kr_send,
+    kr_recv,
+    kl_send,
+    kl_recv,
 ):
+    ctx, me, chip, core, sibling = place()
     keys = k_ref.shape[0]
     tiles = keys // KEY_TILE
     rows = q_ref.shape[0]
+    per_group = QUERY_HEADS // KVH
     head = pl.program_id(0)
+
+    order = []
+    for step in range(chips - 1):
+        for r in (chips - 1 - step, step + 1):
+            if r not in order:
+                order.append(r)
+    order.append(0)
+    swaps = [
+        remote(other_ref.at[r], pair.at[r], swap_send.at[r], swap_recv.at[r], (sibling, me))
+        for r in range(chips)
+    ]
+    loads = [
+        pltpu.make_async_copy(mine_ref.at[r], mine_v.at[j % 2], load_sem.at[j % 2])
+        for j, r in enumerate(order)
+    ]
+    line = LineSum(
+        chips,
+        lambda r: lambda: [pair.at[r]],
+        lambda r: pair.at[r],
+        got,
+        (r_send, r_recv, l_send, l_recv),
+    )
+
+    def join(j):
+        loads[j].wait()
+        swaps[order[j]].wait_recv()
+        add_into(pair.at[order[j]], [pair.at[order[j]], mine_v.at[j % 2]])
+        if j + 2 < chips:
+            loads[j + 2].start()
+
+    def kv_swap(group, r):
+        return remote(
+            kv_v.at[group, 1, r],
+            kv_pair.at[group, r],
+            kv_swap_send.at[group, r],
+            kv_swap_recv.at[group, r],
+            (sibling, me),
+        )
+
+    def kv_line(group):
+        def held(r):
+            kv_swap(group, r).wait_recv()
+            return lambda: [kv_v.at[group, 0, r], kv_pair.at[group, r]]
+
+        return LineSum(
+            chips,
+            held,
+            lambda r: kv_pair.at[group, r],
+            kv_got.at[group],
+            tuple(sem.at[group] for sem in (kr_send, kr_recv, kl_send, kl_recv)),
+        )
+
+    def kv_start(group):
+        for q in range(2):
+            for r in range(chips):
+                part = pl.ds((q * chips + r) * rows, rows)
+                kv_v[group, q, r, :, :HEAD_SIZE] = (dk_acc[part, :] * scale).astype(BF16)
+                kv_v[group, q, r, :, HEAD_SIZE:] = dv_acc[part, :].astype(BF16)
+        for r in order:
+            kv_swap(group, r).start()
 
     @pl.when(head == 0)
     def _():
+        greet(chips, [], True)
+        for r in order:
+            swaps[r].start()
+        for copy in loads[:2]:
+            copy.start()
+
         def fill(t, carry):
             tile = pl.ds(pl.multiple_of(t * KEY_TILE, KEY_TILE), KEY_TILE)
             gap = oq_ref[...] - ok_ref[tile, :]
@@ -911,54 +1004,124 @@
     acc = lax.fori_loop(0, tiles, step, jnp.zeros((rows, HEAD_SIZE), F32))
     dq_ref[...] = acc * scale
 
-    @pl.when(lax.rem(head, per_group) == per_group - 1)
+    last = QUERY_HEADS - 1
+    stride = max(1, last // (chips - 2))
+    early = {per_group + 2 * s: s for s in range(chips - 1) if per_group + 2 * s < last}
+    for h in range(QUERY_HEADS):
+
+        @pl.when(head == h)
+        def _():
+            if h == 0:
+                for j in range(chips):
+                    join(j)
+            for s in range(chips - 2):
+                if h == s * stride:
+                    line.step(s)
+            if h % per_group == per_group - 1:
+                kv_start(h // per_group)
+            if h in early:
+                kv_line(0).step(early[h])
+
+    @pl.when(head == last)
     def _():
-        dk_ref[...] = (dk_acc[...] * scale).astype(BF16)
-        dv_ref[...] = dv_acc[...].astype(BF16)
+        def store(k, r, target):
+            return pltpu.make_async_copy(pair.at[r], target, store_sem.at[k])
+
+        @pl.when((chip >= 1) & (chip + 1 < chips))
+        def _():
+            add_into(pair.at[1], [pair.at[1], line.from_left(chips - 3)])
+            add_into(pair.at[chips - 1], [pair.at[chips - 1], line.from_right(chips - 3)])
+
+        for copy in (
+            store(0, 0, own_ref),
+            store(1, 1, right_ref),
+            store(2, chips - 1, left_ref),
+        ):
+            copy.start()
+        for group in range(KVH):
+            one = kv_line(group)
+            for s in range(chips - 1):
+                if group > 0 or s not in early.values():
+                    one.step(s)
+            one.total(kv_ref.at[group])
+        for group in range(KVH):
+            kv_line(group).finish()
+            for r in range(chips):
+                kv_swap(group, r).wait_send()
+        line.finish(chips - 2)
+        for swap in swaps:
+            swap.wait_send()
+        for copy in (
+            store(0, 0, own_ref),
+            store(1, 1, right_ref),
+            store(2, chips - 1, left_ref),
+        ):
+            copy.wait()
 
 
 def attention_back(
-    queries, kv, attended, attended_grad, lse, order_mine, pos_mine, order_keys, group
+    queries, kv, attended, attended_grad, lse, order_mine, pos_mine, order_keys, mine, other,
+    collective_id
 ):
     rows = queries.shape[0]
     keys = kv.shape[0]
+    chips, unused, width = mine.shape
     per_group = QUERY_HEADS // KVH
-    head_rows = pl.BlockSpec((rows, HEAD_SIZE), lambda h: (0, group * per_group + h))
-    group_rows = pl.BlockSpec((rows, HEAD_SIZE), lambda h: (0, h))
+    head_rows = pl.BlockSpec((rows, HEAD_SIZE), lambda h: (0, h))
+    anywhere = pl.BlockSpec(memory_space=pl.ANY)
     return pl.pallas_call(
-        functools.partial(attention_back_kernel, HEAD_SIZE ** (-0.5), per_group),
-        grid=(per_group,),
+        functools.partial(attention_back_kernel, HEAD_SIZE ** (-0.5), chips),
+        grid=(QUERY_HEADS,),
         out_shape=[
-            jax.ShapeDtypeStruct((rows, per_group * HEAD_SIZE), F32),
-            jax.ShapeDtypeStruct((keys, HEAD_SIZE), BF16),
-            jax.ShapeDtypeStruct((keys, HEAD_SIZE), BF16),
-        ],
+            jax.ShapeDtypeStruct(queries.shape, F32),
+            jax.ShapeDtypeStruct((KVH, rows, 2 * HEAD_SIZE), F32),
+        ]
+        + [jax.ShapeDtypeStruct((rows, width), BF16)] * 3,
         in_specs=[
             head_rows,
-            pl.BlockSpec((keys, HEAD_SIZE), lambda h: (0, group)),
-            pl.BlockSpec((keys, HEAD_SIZE), lambda h: (0, KVH + group)),
-            group_rows,
+            pl.BlockSpec((keys, HEAD_SIZE), lambda h: (0, h // per_group)),
+            pl.BlockSpec((keys, HEAD_SIZE), lambda h: (0, KVH + h // per_group)),
+            head_rows,
             head_rows,
             pl.BlockSpec((1, 1, rows), lambda h: (h, 0, 0)),
             pl.BlockSpec((1, rows), lambda h: (0, 0)),
             pl.BlockSpec((1, rows), lambda h: (0, 0)),
             pl.BlockSpec((keys, 1), lambda h: (0, 0)),
+            anywhere,
+            anywhere,
         ],
         out_specs=[
-            group_rows,
-            pl.BlockSpec((keys, HEAD_SIZE), lambda h: (0, 0)),
-            pl.BlockSpec((keys, HEAD_SIZE), lambda h: (0, 0)),
+            head_rows,
+            pl.BlockSpec((KVH, rows, 2 * HEAD_SIZE), lambda h: (0, 0, 0)),
+            anywhere,
+            anywhere,
+            anywhere,
         ],
         scratch_shapes=[
             pltpu.VMEM((keys, rows), F32),
             pltpu.VMEM((keys, HEAD_SIZE), F32),
             pltpu.VMEM((keys, HEAD_SIZE), F32),
-        ],
-        compiler_params=pltpu.CompilerParams(vmem_limit_bytes=VMEM_BYTES),
+            pltpu.VMEM((2, rows, width), BF16),
+            pltpu.VMEM((chips, rows, width), BF16),
+            pltpu.VMEM((chips + 1, rows, width), BF16),
+            pltpu.VMEM((KVH, 2, chips, rows, 2 * HEAD_SIZE), BF16),
+            pltpu.VMEM((KVH, chips, rows, 2 * HEAD_SIZE), BF16),
+            pltpu.VMEM((KVH, chips + 1, rows, 2 * HEAD_SIZE), BF16),
+            pltpu.SemaphoreType.DMA((2,)),
+            pltpu.SemaphoreType.DMA((3,)),
+            pltpu.SemaphoreType.DMA((chips,)),
+            pltpu.SemaphoreType.DMA((chips,)),
+        ]
+        + [pltpu.SemaphoreType.DMA((chips - 1,)) for unused in range(4)]
+        + [pltpu.SemaphoreType.DMA((KVH, chips)) for unused in range(2)]
+        + [pltpu.SemaphoreType.DMA((KVH, chips - 1)) for unused in range(4)],
+        compiler_params=pltpu.CompilerParams(
+            collective_id=collective_id, has_side_effects=True, vmem_limit_bytes=BACK_VMEM_BYTES
+        ),
         cost_estimate=pl.CostEstimate(
-            flops=10 * rows * keys * HEAD_SIZE * per_group,
-            bytes_accessed=10 * rows * per_group * HEAD_SIZE + 8 * keys * HEAD_SIZE,
-            transcendentals=rows * keys * per_group,
+            flops=10 * rows * keys * HEAD_SIZE * QUERY_HEADS,
+            bytes_accessed=10 * rows * QUERY_HEADS * HEAD_SIZE + 8 * keys * KVH * HEAD_SIZE,
+            transcendentals=rows * keys * QUERY_HEADS,
         ),
         name="attention_back",
     )(
@@ -971,6 +1134,8 @@
         order_mine[None, :],
         pos_mine[None, :],
         order_keys[:, None],
+        mine,
+        other,
     )
 
 
@@ -1003,7 +1168,8 @@
     up_ref,
     down_ref,
     returned_ref,
-    out_ref,
+    out_mine_ref,
+    out_other_ref,
     gate_grad_ref,
     up_grad_ref,
     down_grad_ref,
@@ -1073,9 +1239,12 @@
             )
         ]
 
-    def out_copy(i):
-        owner = lax.rem(chip + chunk_order(chip, i, chips), chips)
-        return pltpu.make_async_copy(out_v, out_ref.at[owner], out_sem)
+    def out_copies(i):
+        r = chunk_order(chip, i, chips)
+        return [
+            pltpu.make_async_copy(out_v.at[0], out_mine_ref.at[r], out_sem.at[0]),
+            pltpu.make_async_copy(out_v.at[1], out_other_ref.at[r], out_sem.at[1]),
+        ]
 
     def swap(i):
         r = chunk_order(chip, i, chips)
@@ -1185,7 +1354,8 @@
 
         @pl.when(i >= 1)
         def _():
-            out_copy(i - 1).wait()
+            for copy in out_copies(i - 1):
+                copy.wait()
 
         @pl.when(i >= 2)
         def _():
@@ -1199,10 +1369,9 @@
                 swap(i).start()
         for q in range(2):
             pick = jnp.concatenate(picks[q], axis=0)
-            out_v[1 - core if q else core] = dot(
-                pick, jnp.concatenate(outs[q], axis=0), TN
-            ).astype(BF16)
-        out_copy(i).start()
+            out_v[q] = dot(pick, jnp.concatenate(outs[q], axis=0), TN).astype(BF16)
+        for copy in out_copies(i):
+            copy.start()
 
         @pl.when(i == 0)
         def _():
@@ -1226,7 +1395,8 @@
     join(chips - 1)
     for copy in saves(chips - 1):
         copy.wait()
-    out_copy(chips - 1).wait()
+    for copy in out_copies(chips - 1):
+        copy.wait()
     for i in range(max(0, chips - 2), chips):
         swap(i).wait_send()
 
@@ -1351,14 +1521,15 @@
         ),
         out_shape=[
             jax.ShapeDtypeStruct((tokens, wide), BF16),
-            jax.ShapeDtypeStruct((chips, 2, tokens, width), BF16),
+            jax.ShapeDtypeStruct((chips, tokens, width), BF16),
+            jax.ShapeDtypeStruct((chips, tokens, width), BF16),
             jax.ShapeDtypeStruct((fsdp, local_experts, shard, units), BF16),
             jax.ShapeDtypeStruct((fsdp, local_experts, shard, units), BF16),
             jax.ShapeDtypeStruct((fsdp, local_experts, units, shard), BF16),
         ]
         + [jax.ShapeDtypeStruct(shape, BF16) for shape in saved],
         in_specs=[anywhere, anywhere, vmem, vmem, anywhere, anywhere, anywhere],
-        out_specs=[vmem] + [anywhere] * 9,
+        out_specs=[vmem] + [anywhere] * 10,
         scratch_shapes=[
             pltpu.VMEM((local_experts * width, units), BF16),
             pltpu.VMEM((local_experts * width, units), BF16),
@@ -1376,7 +1547,7 @@
             pltpu.VMEM((2, per, units, shard), BF16),
             pltpu.SemaphoreType.DMA((3,)),
             pltpu.SemaphoreType.DMA((2,)),
-            pltpu.SemaphoreType.DMA,
+            pltpu.SemaphoreType.DMA((2,)),
             pltpu.SemaphoreType.DMA((5,)),
             pltpu.SemaphoreType.DMA((chips,)),
             pltpu.SemaphoreType.DMA((chips,)),
@@ -1399,7 +1570,7 @@
         up.reshape(local_experts * width, units),
         down.reshape(local_experts * units, width),
     )
-    return outs[:5]
+    return outs[:6]
 
 
 def body(
@@ -1515,7 +1686,7 @@
     gate_weights = jnp.where(routed > 0, jax.nn.softmax(chosen, axis=-1), 0.0)
 
     hidden_all, weights_all = gather([], [hidden_two, gate_weights.T], chips - 1, fsdp, chips, 2)
-    returned, out_rows, gate_local, up_local, down_local = experts_pass(
+    returned, out_mine, out_other, gate_local, up_local, down_local = experts_pass(
         hidden_all,
         grad_all,
         table_all,
@@ -1528,12 +1699,6 @@
         fsdp,
         5,
     )
-    out_sum = lax.psum_scatter(
-        out_rows.reshape(2 * chips, tok_rows, width),
-        "ctx",
-        scatter_dimension=0,
-        tiled=True,
-    )
     expert_grads = [
         lax.psum_scatter(part, "fsdp", scatter_dimension=0, tiled=True)
         for part in (gate_local, up_local, down_local)
@@ -1559,32 +1724,30 @@
         "td,cd->tc", branch_grad, out_full, preferred_element_type=F32
     ).astype(BF16)
 
-    query_grad, kv_grads = [], [None] * (2 * KVH)
-    for group in range(KVH):
-        parts = attention_back(
-            queries,
-            kv_all,
-            attended_parts[group],
-            after(attended_grad, *query_grad[-1:]),
-            lse[group],
-            order_mine,
-            pos_mine,
-            order_keys,
-            group,
-        )
-        query_grad.append(parts[0])
-        kv_grads[group], kv_grads[KVH + group] = parts[1:]
-    kv_grads = jnp.concatenate(kv_grads, axis=1).reshape(2, chips, tok_rows, 2 * kv_width)
-    kv_grad = line_reduce_now(kv_grads[0], kv_grads[1], chips, 3)
+    query_grad, kv_grad, out_own, out_right, out_left = attention_back(
+        queries,
+        kv_all,
+        attended,
+        attended_grad,
+        jnp.concatenate(lse, axis=0),
+        order_mine,
+        pos_mine,
+        order_keys,
+        out_mine,
+        out_other,
+        3,
+    )
+    key_grad = [kv_grad[group, :, :HEAD_SIZE] for group in range(KVH)]
+    value_grad = [kv_grad[group, :, HEAD_SIZE:] for group in range(KVH)]
     turned_grad = rotate(
-        jnp.concatenate(query_grad + [kv_grad[:, :kv_width]], axis=1).reshape(
+        jnp.concatenate([query_grad] + key_grad, axis=1).reshape(
             tok_rows, QUERY_HEADS + KVH, HEAD_SIZE
         ),
         cosine,
         -sine,
     ).reshape(tok_rows, width + kv_width)
     pre_grad = jnp.concatenate(
-        [turned_grad.astype(BF16), kv_grad[:, kv_width:].astype(BF16)], axis=1
+        [turned_grad.astype(BF16)] + [part.astype(BF16) for part in value_grad], axis=1
     )
     qkv_local = jnp.einsum("td,tc->dc", hidden_one, pre_grad, preferred_element_type=F32)
     hidden_one_grad = jnp.einsum("tc,dc->td", pre_grad, qkv_full, preferred_element_type=F32)
@@ -1615,8 +1778,15 @@
         ],
         axis=1,
     )
-    qkv_sum, out_proj_sum, small_sum = dense_reduce(
-        [halves(qkv_local), halves(out_local), small_local], DENSE_PIECE, fsdp, chips, 4
+    qkv_sum, out_proj_sum, small_sum, out_sum = dense_reduce(
+        [halves(qkv_local), halves(out_local), small_local],
+        out_own,
+        out_right,
+        out_left,
+        DENSE_PIECE,
+        fsdp,
+        chips,
+        4,
     )
     edge = width + 2 * kv_width
     qkv_grads = qkv_sum.reshape(shard, -1)
@@ -1624,7 +1794,7 @@
     gate_grad_out, up_grad_out, down_grad_out = (
         after(part, pre_grad)[0].astype(F32) for part in expert_grads
     )
-    result = middle + after(out_sum, pre_grad)[0].astype(F32)
+    result = middle + out_sum
     return (
         result.astype(BF16)[None],
         input_grad[None],

time: 792 us -> 745 us (0.941)
  Pallas kernels: 637 us -> 602 us
  local copies, waits for them, and re-layouts: 46.1 us -> 31.8 us
    pallas_call x2 -> x1, Pallas kernels: 62.2 us -> 103 us  [attention_back(): pl.pallas_call(functools.partial(attention_back_kernel, HEAD_SIZE ** (-0....]
    pallas_call x1, Pallas kernels: 153 us -> 113 us  [dense_reduce(): pl.pallas_call(functools.partial(dense_reduce_kernel, fsdp, chips, tuple(...]
    pallas_call x1 -> x0, Pallas kernels: 36.3 us -> none  [line_reduce_now(): pl.pallas_call(functools.partial(line_reduce_kernel, chips), out_shape=ja...]
  transfers between devices with their start and end apart: 7 -> 6, of which waited for: 0 -> 0; matrix products, arithmetic and copies ran while one was open for 14% -> 14% of each run, Pallas kernels for 58% -> 57%
where the time goes in v4:
time: 745 us; the launch traced here: 735 us
  Pallas kernels  602 us (81%)
  other arithmetic  42.8 us (6%)
  matrix products  40.8 us (5%)
  local copies, waits for them, and re-layouts  31.8 us (4%)
  between operations  15.2 us (2%)
    pallas_call x3, Pallas kernels, gather(): pl.pallas_call(functools.partial(gather_kernel, len(dense), len(line), le...  217 us
    pallas_call x1, Pallas kernels, experts_pass(): pl.pallas_call(functools.partial(experts_kernel, capacity, local_experts,...  117 us
    pallas_call x1, Pallas kernels, dense_reduce(): pl.pallas_call(functools.partial(dense_reduce_kernel, fsdp, chips, tuple(...  113 us
    pallas_call x1, Pallas kernels, attention_back(): pl.pallas_call(functools.partial(attention_back_kernel, HEAD_SIZE ** (-0....  103 us
    pallas_call x2, Pallas kernels, attention(): pl.pallas_call(functools.partial(attention_kernel, HEAD_SIZE ** (-0.5)),...  51.6 us
  transfers between devices with their start and end apart: 6, of which 0 were waited for; matrix products, arithmetic and copies ran while one was open for 14% of the time, Pallas kernels for 57%

profile of v4, /device:TPU:0, one launch (start us, length us, event | category | flops | bytes accessed | tf_op | source)
XLA Modules:
  0.0 735.2 jit_solution(18379932819609301010)
XLA Ops:
  7.2 0.8 broadcast_in_dim.46
  8.0 0.8 broadcast_in_dim.47
  8.8 0.8 copy.123
  9.7 2.9 pad_maximum_fusion.1.refs_0_
  12.6 0.8 maximum_maximum_fusion.refs_1_
  13.4 65.3 %gather.3 = (bf16[1536,2048]{1,0:T(8,128)(2,1)}, bf16[1536,128]{1,0:T(8,128)(2,1)}, bf16[2,4,384,1536]{3,2,1,0:T(8,128)(2,1)}) custom-call(bf16[384,2048]{1,0:T(8,128)(2,1)} %pad_maximum_fusion.1.refs_0_, bf16[384,128]{1,0:T(8,128)(2,1)} %maximum_maximum_fusion.refs_1_, bf16[384,1536]{1,0:T(8,128)(2,1)} %bitcast.95), custom_call_target="tpu_custom_call" | custom-call | tf_op jit(solution)/shard_map/gather/pallas_call | solution.py:342
  78.8 0.7 all-gather.6.cloned.1.call-update
  79.6 0.7 all-gather.8.cloned.1.call-update
  81.2 4.8 fusion.20
  86.2 0.7 slice.162
  87.1 2.2 copy.126
  89.5 1.1 fusion.37
  90.6 2.2 multiply_subtract_fusion
  92.8 0.8 copy.153
  94.1 0.7 copy.130.refs_2_
  95.3 0.7 reduce.12
  96.1 0.6 broadcast_in_dim_reshape.7.ok_ref
  97.0 1.5 copy.133.q_ref
  98.5 0.8 copy.135.pq_ref
  99.3 0.8 copy.134.oq_ref
  100.2 0.8 pad_maximum_fusion.4.refs_1_
  101.0 65.3 %gather.4 = (bf16[1536,1536]{1,0:T(8,128)(2,1)}, bf16[2,4,384,512]{3,2,1,0:T(8,128)(2,1)}, f32[2,4,16,384]{3,2,1,0:T(8,128)}, bf16[2,4,384,1536]{3,2,1,0:T(8,128)(2,1)}) custom-call(bf16[384,1536]{1,0:T(8,128)(2,1)} %refs_0_.1, bf16[384,512]{1,0:T(8,128)(2,1)} %pad_maximum_fusion.4.refs_1_, ...), custom_call_target="tpu_custom_call", output_to_operand_aliasing={{3}: (3, {})} | custom-call | tf_op jit(solution)/shard_map/gather/pallas_call | solution.py:342
  166.3 25.8 %attention.2 = (bf16[384,768]{1,0:T(8,128)(2,1)}, f32[6,1,384]{2,1,0:T(1,128)}) custom-call(bf16[384,1536]{1,0:T(8,128)(2,1)} %copy.133.q_ref, bf16[3072,512]{1,0:T(8,128)(2,1)} %bitcast.108, bf16[3072,512]{1,0:T(8,128)(2,1)} %bitcast.109, s32[384,1]{1,0:T(8,128)} %copy.134.oq_ref, s32[384,1]{1,0:T(8,128)} %copy.135.pq_ref, ...), custom_call_target="tpu_custom_call" | custom-call | flops 3623878656 | bytes 2752512 | tf_op jit(solution)/shard_map/attention/pallas_call | solution.py:826
  192.1 1.5 copy.136.q_ref
  193.6 25.9 %attention.3 = (bf16[384,768]{1,0:T(8,128)(2,1)}, f32[6,1,384]{2,1,0:T(1,128)}) custom-call(bf16[384,1536]{1,0:T(8,128)(2,1)} %copy.136.q_ref, bf16[3072,512]{1,0:T(8,128)(2,1)} %bitcast.110, bf16[3072,512]{1,0:T(8,128)(2,1)} %bitcast.111, s32[384,1]{1,0:T(8,128)} %copy.134.oq_ref, s32[384,1]{1,0:T(8,128)} %copy.135.pq_ref, ...), custom_call_target="tpu_custom_call" | custom-call | flops 3623878656 | bytes 2752512 | tf_op jit(solution)/shard_map/attention/pallas_call | solution.py:826
  219.5 1.1 constant_dynamic-update-slice_fusion.o_ref
  220.6 5.4 multiply_reduce_fusion.2
  226.3 1.0 copy-done.1
  228.3 0.7 copy.141.refs_1_
  229.0 86.5 %gather.5 = (bf16[2,4,384,1536]{3,2,1,0:T(8,128)(2,1)}, f32[2,4,16,384]{3,2,1,0:T(8,128)}) custom-call(bf16[384,1536]{1,0:T(8,128)(2,1)} %copy-done.1, f32[16,384]{1,0:T(8,128)} %copy.141.refs_1_), custom_call_target="tpu_custom_call" | custom-call | tf_op jit(solution)/shard_map/gather/pallas_call | solution.py:342
  315.6 116.8 %experts.1 = (bf16[384,1664]{1,0:T(8,128)(2,1)}, bf16[4,384,1536]{2,1,0:T(8,128)(2,1)}, bf16[4,384,1536]{2,1,0:T(8,128)(2,1)}, bf16[4,2,384,768]{3,2,1,0:T(8,128...) custom-call(bf16[2,4,384,1536]{3,2,1,0:T(8,128)(2,1)} %get-tuple-ele, ...), custom_call_target="tpu_custom_call" | custom-call | flops 48318382080 | bytes 100000000 | tf_op jit(solution)/shard_map/experts/pallas_call | solution.py:1518
  433.2 2.6 broadcast_in_dim_reshape.9.ok_ref
  435.8 2.4 copy.142.q_ref
  438.1 0.6 pad_maximum_fusion.6.lse_ref
  439.3 1.5 convert_element_type.167
  441.4 0.9 multiply_reduce_fusion
  442.7 2.0 fusion.4
  444.8 6.3 convolution_convert_fusion.2.do_ref
  451.0 103.2 %attention_back.1 = (f32[384,1536]{1,0:T(8,128)}, f32[2,384,256]{2,1,0:T(8,128)}, bf16[384,1536]{1,0:T(8,128)(2,1)}, bf16[384,1536]{1,0:T(8,128)(2,1)}, bf16[384,1536]{1,0:T(8,128)(2,1)}) custom-call(bf16[384,1536]{1,0:T(8,128)(2,1)} %copy.142.q_ref, bf16[3072,512]{1,0:T(8,128)(2,1)} %bitcast.112, bf16[3072,512]{1,0:T(8,128)(2,1)} %bitcast.113, ...), custom_call_target="tpu_custom_call" | custom-call | flops 18119393280 | bytes 12189696 | tf_op jit(solution)/shard_map/attention_back/pallas_call | solution.py:1072
  554.3 1.2 convert.39
  555.4 1.1 slice_bitcast_fusion.1
  556.5 4.0 pad_maximum_fusion
  560.5 3.6 copy.144
  564.5 1.6 convolution_convert_fusion.3
  566.6 2.4 subtract_convert_fusion
  569.2 1.5 copy-done.6
  570.7 7.2 fusion.8
  577.9 0.7 pad_maximum_fusion.5.refs_2_
  578.6 7.1 convolution_convert_fusion
  585.8 6.7 convolution_convert_fusion.1
  592.5 113.4 %dense_reduce.1 = (bf16[2,192,2048]{2,1,0:T(8,128)(2,1)}, bf16[2,192,1536]{2,1,0:T(8,128)(2,1)}, bf16[2,16,512]{2,1,0:T(8,128)(2,1)}, f32[384,1536]{1,0:T(8,128)}) custom-call(bf16[4,2,192,2048]{3,2,1,0:T(8,128)(2,1)} %bitcast.93, bf16[4,2,192,1536]{3,2,1,0:T(8,128)(2,1)} %bitcast.94, bf16[4,2,16,512]{3,2,1,0:T(8,128)(2,1)} %pad_maximum_fusion.5.refs_2_, ...), custom_call_target="tpu_custom_call" | custom-call | tf_op jit(solution)/shard_map/dense_reduce/pallas_call | solution.py:752
  705.9 0.7 slice_convert_fusion.4
  706.7 0.7 copy.150
  707.4 1.4 convert_reduce_fusion.3
  708.8 2.1 slice_convert_fusion.2
  710.9 3.0 slice_convert_fusion
  713.8 1.8 bitcast_convert_fusion.3
  715.6 0.7 copy-done.11
  716.3 1.4 fusion.9
  717.7 0.7 copy-done.2
  718.7 0.8 copy-done.10
  719.5 1.7 fusion.10
  721.1 2.9 bitcast_convert_fusion
  724.1 3.8 bitcast_convert_fusion.1
  (129 shorter events, 8.1 us)
Async XLA Ops:
  7.2 308.4 %all-gather.4.cloned.1.call-start = ((), (), s32[]{:S(2)}) async-start(), calls=%async_computation.3 | async-start | bytes 5898240 | tf_op jit(solution)/shard_map/all_gather | solution.py:1623
  78.7 1.6 copy-start.9
  78.7 2.1 copy-start.4
  78.8 236.8 %all-gather.6.cloned.1.call-start = ((), (), s32[]{:S(2)}) async-start(), calls=%async_computation.4 | async-start | bytes 5898240 | tf_op jit(solution)/shard_map/all_gather | solution.py:1624
  79.5 236.1 %all-gather.8.cloned.1.call-start = ((), (), s32[]{:S(2)}) async-start(), calls=%async_computation.5 | async-start | bytes 5898240 | tf_op jit(solution)/shard_map/all_gather | solution.py:1625
  80.2 640.9 %reduce-scatter.14.cloned.1.call-start = ((), (), s32[]{:S(2)}) async-start(), calls=%async_computation.8 | async-start | bytes 5898240
  81.2 4.8 copy-start.27
  81.2 4.8 copy-start.32
  86.0 0.9 copy-start.35
  87.1 2.2 copy-start.29
  89.3 10.0 %copy-start.25 = (s32[1,384]{1,0:T(1,128)}, s32[1,384]{1,0:T(1,128)S(1)}, u32[]{:S(2)}) copy-start(s32[1,384]{1,0:T(1,128)S(1)} %get-tuple-element.153.oq_ref) | copy-start | bytes 4612
  90.6 3.0 copy-start.34
  93.8 2.3 copy-start.23
  96.9 3.3 copy-start.18
  97.0 95.1 %copy-start = (bf16[384,12,128]{0,2,1:T(8,128)(2,1)}, bf16[384,12,128]{0,2,1:T(8,128)(2,1)S(1)}, u32[]{:S(2)}) copy-start(bf16[384,12,128]{0,2,1:T(8,128)(2,1)S(1)} %slice.114) | copy-start | bytes 3538948
  97.0 3.2 copy-start.19
  192.1 1.5 copy-start.20
  193.6 27.0 %copy-start.5 = (bf16[1,384,1536]{2,1,0:T(8,128)(2,1)S(1)}, bf16[1,384,1536]{2,1,0:T(8,128)(2,1)}, u32[]{:S(2)}) copy-start(bf16[1,384,1536]{2,1,0:T(8,128)(2,1)} %param.15) | copy-start | bytes 3538948
  220.6 5.4 copy-start.22
  226.0 1.3 copy-start.24
  226.3 1.0 copy-start.1
  432.5 288.6 %reduce-scatter.10.cloned.1.call-start = ((), (), s32[]{:S(2)}) async-start(), calls=%async_computation.6 | async-start | bytes 5898240
  433.1 5.1 copy-start.30
  433.1 5.1 copy-start.31
  433.1 5.7 copy-start.26
  433.1 290.9 %reduce-scatter.12.cloned.1.call-start = ((), (), s32[]{:S(2)}) async-start(), calls=%async_computation.7 | async-start | bytes 5898240
  441.4 0.9 copy-start.16
  441.4 1.3 copy-start.3
  560.5 3.9 copy-start.17
  564.2 2.4 copy-start.21
  569.0 1.7 copy-start.6
  569.0 1.7 copy-start.33
  569.1 8.7 %copy-start.12 = (bf16[384,14,128]{0,2,1:T(8,128)(2,1)}, bf16[384,14,128]{0,2,1:T(8,128)(2,1)S(1)}, u32[]{:S(2)}) copy-start(bf16[384,14,128]{0,2,1:T(8,128)(2,1)S(1)} %pad_maximum_fusion.3) | copy-start | bytes 4128772
  578.6 7.2 copy-start.7
  578.6 7.2 copy-start.13
  592.5 116.3 %copy-start.28 = (f32[384]{0:T(512)S(1)}, f32[384]{0:T(512)}, u32[]{:S(2)}) copy-start(f32[384]{0:T(512)} %copy-done.27) | copy-start | bytes 4612
  708.8 5.0 copy-start.15
  713.8 2.5 copy-start.11
  716.3 2.1 copy-start.2
  716.3 2.4 copy-start.8
  716.3 3.2 copy-start.10
  721.1 2.9 copy-start.14
Sparse Core Ops, SparseCore 0:
  78.9 76.2 all-gather.3
  157.0 56.0 all-gather.5
  214.9 56.9 all-gather.7
  432.6 55.0 reduce-scatter.13
  490.6 57.0 reduce-scatter.9
  550.5 61.6 reduce-scatter.11

commit v5 on v4

--- a/solution.py
+++ b/solution.py
@@ -23,6 +23,7 @@
 VMEM_BYTES = 56 * 1024 * 1024
 EXPERT_VMEM_BYTES = 119 * 512 * 1024
 BACK_VMEM_BYTES = 61 * 1024 * 1024
+FRONT_VMEM_BYTES = 40 * 1024 * 1024
 MESH = pl.DeviceIdType.MESH
 F32 = jnp.float32
 BF16 = jnp.bfloat16
@@ -260,6 +261,34 @@
         for i in range(self.count):
             self.across(i, 0).wait()
             self.local(i).wait()
+
+    def arrived(self, slot):
+        for i in range(self.count):
+            remote(
+                self.outs[i].at[0, slot],
+                self.outs[i].at[1, slot],
+                self.sems[5].at[i, slot],
+                self.sems[6].at[i, slot],
+                (self.sibling, self.me),
+            ).wait_recv()
+
+    def sent(self):
+        chip, chips, count = self.chip, self.chips, self.count
+        for step in range(chips - 1):
+
+            @pl.when((chip + 1 < chips) & (chip >= step))
+            def _():
+                for i in range(count):
+                    self.to_right(i, step).wait_send()
+
+            @pl.when((chip >= 1) & (chip + step < chips))
+            def _():
+                for i in range(count):
+                    self.to_left(i, step).wait_send()
+
+        for slot in range(chips):
+            for i in range(count):
+                self.across(i, slot).wait_send()
 
     def finish(self, step):
         chip, chips, count = self.chip, self.chips, self.count
@@ -771,86 +800,348 @@
     return lax.optimization_barrier((value,) + others)[0]
 
 
-def attention_kernel(
-    scale, q_ref, k_ref, v_ref, oq_ref, pq_ref, ok_ref, out_ref, lse_ref, bias, scores
+def chunk_order(chip, i, chips):
+    right_half = lax.div(2 * chip, chips)
+    near = chip + right_half * (chips - 1 - 2 * chip)
+    alone = chips - 1 - 2 * near
+    paired = lax.div(i - alone + chips, chips)
+    turn = (i - alone) * paired
+    odd = lax.rem(turn, 2)
+    pair = lax.div(turn, 2)
+    distance = (1 - paired) * (chips - 1 - near - i) + paired * (
+        (1 - odd) * (near - pair) + odd * (chips - near + pair)
+    )
+    return lax.rem(distance + right_half * (chips - 2 * distance), chips)
+
+
+def front_kernel(
+    scale,
+    chips,
+    expert_count,
+    tokens_ref,
+    gain_a_ref,
+    gain_b_ref,
+    small_ref,
+    cos_ref,
+    sin_ref,
+    oq_ref,
+    pq_ref,
+    ok_ref,
+    routed_ref,
+    table_ref,
+    qkv_ref,
+    wo_ref,
+    passed_ref,
+    q_ref,
+    normed_ref,
+    kv_ref,
+    table_all_ref,
+    attended_ref,
+    lse_ref,
+    middle_ref,
+    gate_ref,
+    weights_ref,
+    hidden_all_ref,
+    grad_ref,
+    qkv_v,
+    wo_v,
+    hidden_v,
+    bias,
+    top,
+    total,
+    acc,
+    load_sem,
+    own_sem,
+    *line_sems,
 ):
-    keys = k_ref.shape[0]
-    tiles = keys // KEY_TILE
-    rows = q_ref.shape[0]
-
-    @pl.when(pl.program_id(0) == 0)
-    def _():
-        def fill(t, carry):
-            tile = pl.ds(pl.multiple_of(t * KEY_TILE, KEY_TILE), KEY_TILE)
-            gap = oq_ref[...] - ok_ref[:, tile]
-            bias[:, tile] = jnp.where((gap >= 0) & (gap <= pq_ref[...]), 0.0, MASKED)
+    ctx, me, chip, core, sibling = place()
+    rows = tokens_ref.shape[0]
+    width = tokens_ref.shape[1]
+    half = rows // 2
+    kv_width = KVH * HEAD_SIZE
+    per_group = QUERY_HEADS // KVH
+    parts = [pl.ds(0, half), pl.ds(half, half)]
+    loads = [
+        pltpu.make_async_copy(src, dst, load_sem.at[k])
+        for k, (src, dst) in enumerate(((qkv_ref, qkv_v), (wo_ref, wo_v)))
+    ]
+    for copy in loads:
+        copy.start()
+    greet(chips, [], True)
+    kv_line = LineGather(
+        [kv_ref.at[0, 0], table_all_ref.at[0, 0]], [kv_ref, table_all_ref], line_sems[:7], chips
+    )
+    grad_line = LineGather([None], [grad_ref], line_sems[7:14], chips)
+    hidden_lines = [
+        LineGather(
+            [hidden_v.at[parts[0]]], [hidden_all_ref.at[:, :, parts[0]]], line_sems[14:21], chips
+        ),
+        LineGather(
+            [hidden_v.at[parts[1]], weights_ref.at[0, 0]],
+            [hidden_all_ref.at[:, :, parts[1]], weights_ref],
+            line_sems[21:28],
+            chips,
+        ),
+    ]
+
+    def normed(value, gain):
+        return value * lax.rsqrt(jnp.mean(value * value, axis=-1, keepdims=True) + EPSILON) * gain
+
+    table_all_ref[0, 0] = table_ref[...]
+    for part in parts:
+        normed_ref[part, :] = normed(
+            tokens_ref[part, :].astype(F32), gain_a_ref[...]
+        ).astype(BF16)
+    loads[0].wait()
+    for part in parts:
+        rows_one = normed_ref[part, :]
+        cosine, sine = cos_ref[part, :], sin_ref[part, :]
+        for h in range(KVH):
+            columns = slice(width + h * HEAD_SIZE, width + (h + 1) * HEAD_SIZE)
+            value = dot(rows_one, qkv_v[:, columns], NN)
+            value = value * cosine + pltpu.roll(value, HEAD_SIZE // 2, 1) * sine
+            kv_ref[0, 0, part, h * HEAD_SIZE : (h + 1) * HEAD_SIZE] = value.astype(BF16)
+        kv_ref[0, 0, part, kv_width:] = dot(
+            rows_one, qkv_v[:, width + kv_width :], NN
+        ).astype(BF16)
+    kv_line.send(0)
+    for i in range(2):
+        kv_line.across(i, 0).start()
+    for part in parts:
+        rows_one = normed_ref[part, :]
+        cosine, sine = cos_ref[part, :], sin_ref[part, :]
+        for h in range(0, QUERY_HEADS, 2):
+            pre = dot(rows_one, qkv_v[:, h * HEAD_SIZE : (h + 2) * HEAD_SIZE], NN)
+            for k in range(2):
+                value = pre[:, k * HEAD_SIZE : (k + 1) * HEAD_SIZE]
+                value = value * cosine + pltpu.roll(value, HEAD_SIZE // 2, 1) * sine
+                q_ref[part, (h + k) * HEAD_SIZE : (h + k + 1) * HEAD_SIZE] = value.astype(BF16)
+
+    def turn(index, r):
+        part = parts[index]
+        for q in range(2):
+            gap = oq_ref[part, :] - ok_ref[q * chips + r]
+            bias[:, q * rows : (q + 1) * rows] = jnp.where(
+                (gap >= 0) & (gap <= pq_ref[part, :]), 0.0, MASKED
+            )
+
+        def one(h, carry):
+            group = lax.div(h, per_group)
+            columns = pl.ds(pl.multiple_of(h * HEAD_SIZE, HEAD_SIZE), HEAD_SIZE)
+            key_columns = pl.ds(pl.multiple_of(group * HEAD_SIZE, HEAD_SIZE), HEAD_SIZE)
+            value_columns = pl.ds(
+                pl.multiple_of(kv_width + group * HEAD_SIZE, HEAD_SIZE), HEAD_SIZE
+            )
+            query = q_ref[part, columns]
+            scores = []
+            peak = top[h, part, :]
+            for q in range(2):
+                raw = dot(query, kv_ref[q, r, :, key_columns], NT) * (scale * LOG2E)
+                raw = raw + bias[:, q * rows : (q + 1) * rows]
+                scores.append(raw)
+            best = scores[0][:, :LANES]
+            for q in range(2):
+                for k in range(rows // LANES):
+                    best = jnp.maximum(best, scores[q][:, k * LANES : (k + 1) * LANES])
+            new = jnp.maximum(peak, jnp.max(best, axis=1, keepdims=True))
+            fade = jnp.exp2(peak - new)
+            wide = jnp.concatenate([new] * (rows // LANES), axis=1)
+            mass = total[h] * fade
+            out = acc[:, columns] * fade
+            for q in range(2):
+                probs = jnp.exp2(scores[q] - wide)
+                for k in range(rows // LANES):
+                    mass = mass + probs[:, k * LANES : (k + 1) * LANES]
+                out = out + dot(probs.astype(BF16), kv_ref[q, r, :, value_columns], NN)
+            top[h, part, :] = new
+            total[h] = mass
+            acc[:, columns] = out
             return carry
 
-        lax.fori_loop(0, tiles, fill, 0)
-
-    query = q_ref[...]
-
-    def score(t, top):
-        tile = pl.ds(pl.multiple_of(t * KEY_TILE, KEY_TILE), KEY_TILE)
-        raw = dot(query, k_ref[tile, :], NT) * (scale * LOG2E) + bias[:, tile]
-        scores[:, tile] = raw
-        for part in range(KEY_TILE // LANES):
-            top = jnp.maximum(top, raw[:, part * LANES : (part + 1) * LANES])
-        return top
-
-    top = lax.fori_loop(0, tiles, score, jnp.full((rows, LANES), MASKED, F32))
-    top = jnp.max(top, axis=1, keepdims=True)
-
-    def weigh(t, carry):
-        total, acc = carry
-        tile = pl.ds(pl.multiple_of(t * KEY_TILE, KEY_TILE), KEY_TILE)
-        probs = jnp.exp2(scores[:, tile] - top)
-        for part in range(KEY_TILE // LANES):
-            total = total + probs[:, part * LANES : (part + 1) * LANES]
-        acc = acc + dot(probs.astype(BF16), v_ref[tile, :], NN)
-        return total, acc
-
-    total, acc = lax.fori_loop(
-        0, tiles, weigh, (jnp.zeros((rows, LANES), F32), jnp.zeros((rows, HEAD_SIZE), F32))
-    )
-    total = jnp.sum(total, axis=1, keepdims=True)
-    out_ref[...] = (acc / total).astype(BF16)
-    lse = jnp.broadcast_to(top + jnp.log2(total), (rows, LANES))
-    lse_ref[0] = lse.T[:1, :]
-
-
-def attention(queries, kv, order_mine, pos_mine, order_keys, group):
-    rows = queries.shape[0]
-    keys = kv.shape[0]
-    per_group = QUERY_HEADS // KVH
+        lax.fori_loop(0, QUERY_HEADS, one, 0)
+
+    def begin(index):
+        top[:, parts[index], :] = jnp.full((QUERY_HEADS, half, LANES), MASKED, F32)
+        total[...] = jnp.zeros_like(total)
+        acc[...] = jnp.zeros_like(acc)
+
+    def end(index):
+        part = parts[index]
+        for h in range(QUERY_HEADS):
+            columns = slice(h * HEAD_SIZE, (h + 1) * HEAD_SIZE)
+            mass = jnp.sum(total[h], axis=1, keepdims=True)
+            attended_ref[part, columns] = (acc[:, columns] / mass).astype(BF16)
+            top[h, part, :] = top[h, part, :] + jnp.log2(mass)
+        if index == 0:
+            loads[1].wait()
+        middle = tokens_ref[part, :].astype(F32) + dot(attended_ref[part, :], wo_v[...], NN)
+        middle_ref[part, :] = middle
+        rows_two = normed(middle, gain_b_ref[...]).astype(BF16)
+        hidden_v[part, :] = rows_two
+        routed = routed_ref[part, :] > 0.0
+        logits = jnp.where(routed, dot(rows_two, small_ref[...], NN), MASKED)
+        power = jnp.exp(logits - jnp.max(logits, axis=1, keepdims=True))
+        power = jnp.where(routed, power, 0.0)
+        gate_ref[part, :] = power / jnp.sum(power, axis=1, keepdims=True)
+        if index == 1:
+            weights_ref[0, 0] = gate_ref[...].T[:expert_count, :]
+        line = hidden_lines[index]
+        line.send(0)
+        for i in range(line.count):
+            line.across(i, 0).start()
+        own(index).start()
+
+    def own(index):
+        return pltpu.make_async_copy(
+            hidden_v.at[parts[index]],
+            hidden_all_ref.at[0, 0, parts[index]],
+            own_sem.at[index],
+        )
+
+    begin(0)
+
+    def first_turn(t, carry):
+        for k in range(1, chips):
+
+            @pl.when(t == k)
+            def _():
+                kv_line.receive(k - 1)
+                if k < chips - 1:
+                    kv_line.send(k)
+                else:
+                    grad_line.send(chips - 2)
+
+        r = chunk_order(chip, chips - 1 - t, chips)
+        kv_line.arrived(r)
+        turn(0, r)
+        return carry
+
+    lax.fori_loop(0, chips, first_turn, 0)
+    end(0)
+    begin(1)
+    early = [step for step in range(chips - 1) if 2 * step + 2 < chips]
+
+    def second_turn(t, carry):
+        for step in early:
+
+            @pl.when(t == 2 * step + 2)
+            def _():
+                hidden_lines[0].receive(step)
+                if step + 1 < chips - 1:
+                    hidden_lines[0].send(step + 1)
+
+        turn(1, t)
+        return carry
+
+    lax.fori_loop(0, chips, second_turn, 0)
+    grad_line.receive(chips - 2)
+    late = [step for step in range(chips - 1) if step not in early]
+    for step in late[:1]:
+        hidden_lines[0].receive(step)
+        if step + 1 < chips - 1:
+            hidden_lines[0].send(step + 1)
+    end(1)
+    for h in range(QUERY_HEADS):
+        lse_ref[h] = top[h].T[:1, :]
+    for step in late[1:]:
+        hidden_lines[0].receive(step)
+        if step + 1 < chips - 1:
+            hidden_lines[0].send(step + 1)
+    for step in range(chips - 1):
+        hidden_lines[1].receive(step)
+        if step + 1 < chips - 1:
+            hidden_lines[1].send(step + 1)
+    for line in hidden_lines:
+        for slot in range(chips):
+            line.arrived(slot)
+        line.sent()
+    kv_line.sent()
+    grad_line.finish(chips - 2)
+    for index in range(2):
+        own(index).wait()
+
+
+def front(
+    tokens,
+    gain_a,
+    gain_b,
+    small,
+    cosine,
+    sine,
+    order_mine,
+    pos_mine,
+    order_keys,
+    routed,
+    table,
+    qkv,
+    w_out,
+    grad_all,
+    chips,
+    collective_id,
+):
+    rows, width = tokens.shape
+    expert_count = table.shape[0]
+    kv_width = KVH * HEAD_SIZE
+    vmem = pl.BlockSpec(memory_space=pltpu.VMEM)
+    anywhere = pl.BlockSpec(memory_space=pl.ANY)
+    shapes = [
+        ((rows, width), BF16),
+        ((rows, width), BF16),
+        ((2, chips, rows, 2 * kv_width), BF16),
+        ((2, chips, expert_count, rows), F32),
+        ((rows, width), BF16),
+        ((QUERY_HEADS, 1, rows), F32),
+        ((rows, width), F32),
+        ((rows, LANES), F32),
+        ((2, chips, expert_count, rows), F32),
+        ((2, chips, rows, width), BF16),
+        (grad_all.shape, BF16),
+    ]
+    flops = 4 * rows * (2 * chips * rows) * width + 2 * rows * width * (2 * width + 2 * kv_width)
     return pl.pallas_call(
-        functools.partial(attention_kernel, HEAD_SIZE ** (-0.5)),
-        grid=(per_group,),
-        out_shape=[
-            jax.ShapeDtypeStruct((rows, per_group * HEAD_SIZE), BF16),
-            jax.ShapeDtypeStruct((per_group, 1, rows), F32),
-        ],
-        in_specs=[
-            pl.BlockSpec((rows, HEAD_SIZE), lambda h: (0, group * per_group + h)),
-            pl.BlockSpec((keys, HEAD_SIZE), lambda h: (0, group)),
-            pl.BlockSpec((keys, HEAD_SIZE), lambda h: (0, KVH + group)),
-            pl.BlockSpec((rows, 1), lambda h: (0, 0)),
-            pl.BlockSpec((rows, 1), lambda h: (0, 0)),
-            pl.BlockSpec((1, keys), lambda h: (0, 0)),
-        ],
-        out_specs=[
-            pl.BlockSpec((rows, HEAD_SIZE), lambda h: (0, h)),
-            pl.BlockSpec((1, 1, rows), lambda h: (h, 0, 0)),
-        ],
-        scratch_shapes=[pltpu.VMEM((rows, keys), F32), pltpu.VMEM((rows, keys), F32)],
-        compiler_params=pltpu.CompilerParams(vmem_limit_bytes=VMEM_BYTES),
+        functools.partial(front_kernel, HEAD_SIZE ** (-0.5), chips, expert_count),
+        out_shape=[jax.ShapeDtypeStruct(shape, kind) for shape, kind in shapes],
+        in_specs=[vmem] * 11 + [anywhere] * 3,
+        out_specs=[vmem] * 9 + [anywhere] * 2,
+        scratch_shapes=[
+            pltpu.VMEM(qkv.shape, BF16),
+            pltpu.VMEM(w_out.shape, BF16),
+            pltpu.VMEM((rows, width), BF16),
+            pltpu.VMEM((rows // 2, 2 * rows), F32),
+            pltpu.VMEM((QUERY_HEADS, rows, LANES), F32),
+            pltpu.VMEM((QUERY_HEADS, rows // 2, LANES), F32),
+            pltpu.VMEM((rows // 2, width), F32),
+            pltpu.SemaphoreType.DMA((2,)),
+            pltpu.SemaphoreType.DMA((2,)),
+        ]
+        + line_scratch([None] * 2, chips)
+        + line_scratch([None], chips)
+        + line_scratch([None], chips)
+        + line_scratch([None] * 2, chips),
+        input_output_aliases={13: 10},
+        compiler_params=pltpu.CompilerParams(
+            collective_id=collective_id, has_side_effects=True, vmem_limit_bytes=FRONT_VMEM_BYTES
+        ),
         cost_estimate=pl.CostEstimate(
-            flops=4 * rows * keys * HEAD_SIZE * per_group,
-            bytes_accessed=4 * rows * per_group * HEAD_SIZE + 4 * keys * HEAD_SIZE,
-            transcendentals=rows * keys * per_group,
+            flops=flops, bytes_accessed=40_000_000, transcendentals=rows * rows * chips * 24
         ),
-        name="attention",
-    )(queries, kv, kv, order_mine[:, None], pos_mine[:, None], order_keys[None, :])
+        name="front",
+    )(
+        tokens,
+        gain_a[None, :],
+        gain_b[None, :],
+        small,
+        cosine,
+        sine,
+        order_mine[:, None],
+        pos_mine[:, None],
+        order_keys.reshape(2 * chips, 1, rows),
+        routed,
+        table,
+        qkv,
+        w_out,
+        grad_all,
+    )
 
 
 def attention_back_kernel(
@@ -1139,20 +1430,6 @@
     )
 
 
-def chunk_order(chip, i, chips):
-    right_half = lax.div(2 * chip, chips)
-    near = chip + right_half * (chips - 1 - 2 * chip)
-    alone = chips - 1 - 2 * near
-    paired = lax.div(i - alone + chips, chips)
-    turn = (i - alone) * paired
-    odd = lax.rem(turn, 2)
-    pair = lax.div(turn, 2)
-    distance = (1 - paired) * (chips - 1 - near - i) + paired * (
-        (1 - odd) * (near - pair) + odd * (chips - near + pair)
-    )
-    return lax.rem(distance + right_half * (chips - 2 * distance), chips)
-
-
 def experts_kernel(
     capacity,
     local_experts,
@@ -1614,8 +1891,8 @@
         axis=1,
     )
     qkv_shard = jnp.concatenate([w_query, w_key, w_value], axis=1)
-    qkv_full, small_full, grad_all = gather(
-        [qkv_shard, small], [grad_out[0]], chips - 2, fsdp, chips, 0
+    qkv_full, small_full, out_full, grad_all = gather(
+        [qkv_shard, small, w_out], [grad_out[0]], chips - 2, fsdp, chips, 0
     )
 
     qkv_full, w_gate, w_up, w_down = lax.optimization_barrier((qkv_full, w_gate, w_up, w_down))
@@ -1650,42 +1927,45 @@
     half_dim = HEAD_SIZE // 2
     freqs = ROPE_BASE ** (-2.0 * jnp.arange(half_dim).astype(F32) / HEAD_SIZE)
     angles = pos_mine.astype(F32)[:, None] * freqs[None, :]
-    cosine = jnp.cos(angles)[:, None, :]
-    sine = jnp.sin(angles)[:, None, :]
+    cosine = jnp.cos(angles)
+    sine = jnp.sin(angles)
 
     inputs = tokens[0].astype(F32)
-    hidden_one = rms_scale(inputs, gain_a).astype(BF16)
-    pre = jnp.dot(hidden_one, qkv_full, preferred_element_type=F32)
-    turned = rotate(
-        pre[:, : width + kv_width].reshape(tok_rows, QUERY_HEADS + KVH, HEAD_SIZE), cosine, sine
-    )
-    queries = turned[:, :QUERY_HEADS].astype(BF16).reshape(tok_rows, width)
-    kv_mine = jnp.concatenate(
-        [
-            turned[:, QUERY_HEADS:].astype(BF16).reshape(tok_rows, kv_width),
-            pre[:, width + kv_width :].astype(BF16),
-        ],
-        axis=1,
-    )
-    out_full, kv_all, table_all, grad_all = gather(
-        [w_out], [kv_mine, table.T], chips - 1, fsdp, chips, 1, [grad_all]
+    (
+        queries,
+        hidden_one,
+        kv_all,
+        table_all,
+        attended,
+        lse,
+        middle,
+        gate_weights,
+        weights_all,
+        hidden_all,
+        grad_all,
+    ) = front(
+        tokens[0],
+        gain_a,
+        gain_b,
+        small_full,
+        jnp.concatenate([cosine, cosine], axis=1),
+        jnp.concatenate([-sine, sine], axis=1),
+        order_mine,
+        pos_mine,
+        order_keys,
+        jnp.pad(routed, ((0, 0), (0, LANES - expert_count))),
+        table.T,
+        qkv_full,
+        out_full,
+        grad_all,
+        chips,
+        1,
     )
     kv_all = kv_all.reshape(-1, 2 * kv_width)
-    attended, lse = [], []
-    for group in range(KVH):
-        part, part_lse = attention(
-            after(queries, *attended[-1:]), kv_all, order_mine, pos_mine, order_keys, group
-        )
-        attended.append(part)
-        lse.append(part_lse)
-    attended_parts, attended = attended, jnp.concatenate(attended, axis=1)
-    middle = inputs + jnp.dot(attended, out_full, preferred_element_type=F32)
-    hidden_two = rms_scale(middle, gain_b).astype(BF16)
-    logits = jnp.dot(hidden_two, router_full, preferred_element_type=F32)
-    chosen = jnp.where(routed > 0, logits, MASKED)
-    gate_weights = jnp.where(routed > 0, jax.nn.softmax(chosen, axis=-1), 0.0)
-
-    hidden_all, weights_all = gather([], [hidden_two, gate_weights.T], chips - 1, fsdp, chips, 2)
+    gate_weights = gate_weights[:, :expert_count]
+    hidden_two = hidden_all[0, 0]
+    cosine, sine = cosine[:, None, :], sine[:, None, :]
+
     returned, out_mine, out_other, gate_local, up_local, down_local = experts_pass(
         hidden_all,
         grad_all,
@@ -1729,7 +2009,7 @@
         kv_all,
         attended,
         attended_grad,
-        jnp.concatenate(lse, axis=0),
+        lse,
         order_mine,
         pos_mine,
         order_keys,

time: 745 us -> 684 us (0.918)
  Pallas kernels: 602 us -> 550 us
  waiting for transfers between devices: 2.02 us -> 19.6 us
  matrix products: 40.8 us -> 30.4 us
    pallas_call x3 -> x1, Pallas kernels: 217 us -> 69.9 us  [gather(): pl.pallas_call(functools.partial(gather_kernel, len(dense), len(line), le...]
    pallas_call x2 -> x1, Pallas kernels: 51.6 us -> 144 us  [front(): pl.pallas_call(functools.partial(front_kernel, HEAD_SIZE ** (-0.5), chips...]
    all_gather x1, waiting for transfers between devices: 0.02 us -> 17.6 us  [body(): lax.all_gather(w_down, 'fsdp', axis=2, tiled=True)]
    dot_general x3 -> x0, matrix products: 10.8 us -> none  [the longest x1 5.41 us: body(): middle = inputs + jnp.dot(attended, out_full, preferred_element_type=F32)]
  transfers between devices with their start and end apart: 6 -> 6, of which waited for: 0 -> 1; matrix products, arithmetic and copies ran while one was open for 14% -> 11% of each run, Pallas kernels for 57% -> 54%
where the time goes in v5:
time: 684 us; the launch traced here: 679 us
  Pallas kernels  550 us (80%)
  other arithmetic  38.1 us (6%)
  matrix products  30.4 us (4%)
  local copies, waits for them, and re-layouts  25.6 us (4%)
  waiting for transfers between devices  19.6 us (3%)
  between operations  14.9 us (2%)
    pallas_call x1, Pallas kernels, front(): pl.pallas_call(functools.partial(front_kernel, HEAD_SIZE ** (-0.5), chips...  144 us
    pallas_call x1, Pallas kernels, dense_reduce(): pl.pallas_call(functools.partial(dense_reduce_kernel, fsdp, chips, tuple(...  117 us
    pallas_call x1, Pallas kernels, experts_pass(): pl.pallas_call(functools.partial(experts_kernel, capacity, local_experts,...  117 us
    pallas_call x1, Pallas kernels, attention_back(): pl.pallas_call(functools.partial(attention_back_kernel, HEAD_SIZE ** (-0....  104 us
    pallas_call x1, Pallas kernels, gather(): pl.pallas_call(functools.partial(gather_kernel, len(dense), len(line), le...  69.9 us
    all_gather x1, waiting for transfers between devices, body(): lax.all_gather(w_down, 'fsdp', axis=2, tiled=True)  17.6 us
    unnamed x61, local copies, waits for them, and re-layouts  14.6 us
  transfers between devices with their start and end apart: 6, of which 1 were waited for; matrix products, arithmetic and copies ran while one was open for 11% of the time, Pallas kernels for 54%

profile of v5, /device:TPU:0, one launch (start us, length us, event | category | flops | bytes accessed | tf_op | source)
XLA Modules:
  0.0 679.2 jit_solution(2550920447660712135)
XLA Ops:
  7.2 0.8 broadcast_in_dim.38
  8.0 0.8 broadcast_in_dim.39
  8.8 0.8 copy.94
  9.7 2.9 pad_maximum_fusion.1.refs_0_
  12.6 0.8 maximum_maximum_fusion.refs_1_
  13.4 69.9 %gather.1 = (bf16[1536,2048]{1,0:T(8,128)(2,1)}, bf16[1536,128]{1,0:T(8,128)(2,1)}, bf16[1536,1536]{1,0:T(8,128)(2,1)}, bf16[2,4,384,1536]{3,2,1,0:T(8,128)(2,1)}) custom-call(bf16[384,2048]{1,0:T(8,128)(2,1)} %pad_maximum_fusion.1.refs_0_, bf16[384,128]{1,0:T(8,128)(2,1)} %maximum_maximum_fusion.refs_1_, bf16[384,1536]{1,0:T(8,128)(2,1)} %refs_2_.1, ...), custom_call_target="tpu_custom_call" | custom-call | tf_op jit(solution)/shard_map/gather/pallas_call | solution.py:371
  83.4 0.7 all-gather.6.cloned.1.call-update
  84.1 0.7 all-gather.8.cloned.1.call-update
  84.9 0.5 broadcast.155
  85.4 0.7 reduce.14
  86.8 0.5 convert_reduce_fusion
  87.6 0.8 fusion.26
  88.4 0.7 copy-done.16
  89.2 0.3 fusion.12.table_ref
  89.6 1.4 copy-done
  91.0 143.8 %front.1 = (bf16[384,1536]{1,0:T(8,128)(2,1)S(1)}, bf16[384,1536]{1,0:T(8,128)(2,1)S(1)}, bf16[2,4,384,512]{3,2,1,0:T(8,128)(2,1)S(1)}, f32[2,4,16,384]{3,2,1,0:...) custom-call(bf16[384,1536]{1,0:T(8,128)(2,1)S(1)} %bitcast.68, ...), custom_call_target="tpu_custom_call", output_to_operand_aliasing={{10}: (13, {})} | custom-call | flops 11475615744 | bytes 40000000 | tf_op jit(solution)/shard_map/front/pallas_call | solution.py:1101
  234.8 1.6 copy-done.4
  236.4 1.0 copy-done.5
  237.4 1.0 copy-done.6
  238.4 1.0 copy-done.8
  239.5 0.7 copy-done.9
  240.1 0.7 copy-done.10
  240.8 17.6 %all-gather.8.cloned.1.call-done = bf16[2,768,1536]{2,1,0:T(8,128)(2,1)} async-done(((bf16[2,768,384]{2,1,0:T(8,128)(2,1)}), bf16[2,768,1536]{2,1,0:T(8,128)(2,1)}) %all-gather.8.cloned.1.call-update) | async-done | bytes 4718608 | tf_op jit(solution)/shard_map/all_gather | solution.py:1902
  258.5 116.5 %experts.1 = (bf16[384,1664]{1,0:T(8,128)(2,1)}, bf16[4,384,1536]{2,1,0:T(8,128)(2,1)}, bf16[4,384,1536]{2,1,0:T(8,128)(2,1)}, bf16[4,2,384,768]{3,2,1,0:T(8,128...) custom-call(bf16[2,4,384,1536]{3,2,1,0:T(8,128)(2,1)} %get-tuple-ele, ...), custom_call_target="tpu_custom_call" | custom-call | flops 48318382080 | bytes 100000000 | tf_op jit(solution)/shard_map/experts/pallas_call | solution.py:1795
  375.1 0.5 reduce-scatter.12.cloned.1.call-update
  375.6 2.6 broadcast_in_dim_reshape.4.ok_ref
  378.5 1.7 fusion.3
  380.2 0.2 multiply_reduce_fusion.2
  380.4 0.6 reshape_subtract_fusion.pq_ref
  381.2 0.2 multiply_reduce_fusion.3
  381.4 0.2 multiply_convert_fusion
  381.6 0.9 multiply_reduce_fusion
  382.5 0.4 copy-done.13
  382.9 2.0 fusion
  384.9 6.1 convolution_convert_fusion.2.do_ref
  391.0 103.7 %attention_back.1 = (f32[384,1536]{1,0:T(8,128)}, f32[2,384,256]{2,1,0:T(8,128)}, bf16[384,1536]{1,0:T(8,128)(2,1)}, bf16[384,1536]{1,0:T(8,128)(2,1)}, bf16[384,1536]{1,0:T(8,128)(2,1)}) custom-call(bf16[384,1536]{1,0:T(8,128)(2,1)} %copy-done.8, bf16[3072,512]{1,0:T(8,128)(2,1)} %bitcast.69, bf16[3072,512]{1,0:T(8,128)(2,1)} %bitcast.70, ...), custom_call_target="tpu_custom_call" | custom-call | flops 18119393280 | bytes 12189696 | tf_op jit(solution)/shard_map/attention_back/pallas_call | solution.py:1363
  494.7 1.2 convert.31
  495.9 1.1 slice_bitcast_fusion.1
  496.9 3.4 pad_maximum_fusion
  500.3 4.0 copy.104
  504.6 1.6 convolution_convert_fusion.3
  506.1 0.2 copy.109
  506.4 0.3 reshape.256
  506.7 2.2 subtract_convert_fusion
  509.1 1.6 copy-done.1
  510.6 7.4 %fusion.6 = (f32[384]{0:T(512)S(1)}, bf16[1536]{0:T(1024)(128)(2,1)S(1)}, f32[384,1536]{1,0:T(8,128)}) fusion(f32[1536]{0:T(1024)S(1)} %get-tuple-element.151, bf16[1,384,1536]{2,1,0:T(8,128)(2,1)S(1)} %copy-done.1, f32[384]{0:T(512)S(1)} %fusion.31, bf16[1536,2048]{1,0:T(8,128)(2,1)} %get-tuple-element.51.qkv_ref, bf16[384,128]{0,1:T(8,128)(2,1)S(1)} %copy.108, ...), kind=kOutput, calls=%fused_computation.17 | convolution fusion | flops 2424764416 | bytes 11415552 | tf_op jit(solution)/shard_map/tc,dc->td/dot_general | solution.py:2033
  518.1 0.7 pad_maximum_fusion.6.refs_2_
  518.8 7.1 %convolution_convert_fusion = bf16[1536,1536]{1,0:T(8,128)(2,1)} fusion(bf16[384,1536]{1,0:T(8,128)(2,1)} %copy-done.5, f32[384,1536]{1,0:T(8,128)} %fusion), kind=kOutput, calls=%fused_computation | convolution fusion | flops 1814888448 | bytes 8257536 | tf_op jit(solution)/shard_map/tc,td->cd/dot_general | solution.py:2002
  525.9 7.0 %convolution_convert_fusion.1 = bf16[1536,2048]{1,0:T(8,128)(2,1)} fusion(bf16[384,1536]{1,0:T(8,128)(2,1)S(1)} %copy-done.7, bf16[384,128]{0,1:T(8,128)(2,1)S(1)} %copy.108, bf16[384,128]{0,1:T(8,128)(2,1)S(1)} %copy.107, bf16[384,1792]{0,1:T(8,128)(2,1)S(1)} %bitcast.78), kind=kOutput, calls=%fused_computation.1 | convolution fusion | flops 2423783424 | bytes 9043968 | tf_op jit(solution)/shard_map/td,tc->dc/dot_general | solution.py:2032
  532.9 116.6 %dense_reduce.1 = (bf16[2,192,2048]{2,1,0:T(8,128)(2,1)}, bf16[2,192,1536]{2,1,0:T(8,128)(2,1)}, bf16[2,16,512]{2,1,0:T(8,128)(2,1)}, f32[384,1536]{1,0:T(8,128)}) custom-call(bf16[4,2,192,2048]{3,2,1,0:T(8,128)(2,1)} %bitcast.72, bf16[4,2,192,1536]{3,2,1,0:T(8,128)(2,1)} %bitcast.73, bf16[4,2,16,512]{3,2,1,0:T(8,128)(2,1)} %pad_maximum_fusion.6.refs_2_, ...), custom_call_target="tpu_custom_call" | custom-call | tf_op jit(solution)/shard_map/dense_reduce/pallas_call | solution.py:781
  649.5 0.7 slice_convert_fusion.3
  650.4 0.7 copy.112
  651.1 1.4 convert_reduce_fusion.3
  652.5 2.1 slice_convert_fusion.1
  654.5 3.0 slice_convert_fusion
  657.5 1.8 bitcast_convert_fusion.3
  659.3 0.7 copy-done.15
  660.0 1.4 fusion.7
  661.4 1.0 copy-done.12
  662.4 0.7 copy-done.14
  663.1 1.7 fusion.8
  664.8 2.9 bitcast_convert_fusion
  667.7 1.6 bitcast_convert_fusion.1
  669.3 2.8 bitcast_convert_fusion.2
  (97 shorter events, 2.5 us)
Async XLA Ops:
  7.2 233.6 %all-gather.4.cloned.1.call-start = ((), (), s32[]{:S(2)}) async-start(), calls=%async_computation.3 | async-start | bytes 5898240 | tf_op jit(solution)/shard_map/all_gather | solution.py:1900
  83.2 2.2 copy-start.26
  83.2 2.9 copy-start.28
  83.3 3.6 copy-start.3
  83.3 4.1 copy-start.27
  83.3 157.5 %all-gather.6.cloned.1.call-start = ((), (), s32[]{:S(2)}) async-start(), calls=%async_computation.4 | async-start | bytes 5898240 | tf_op jit(solution)/shard_map/all_gather | solution.py:1901
  84.1 174.4 %all-gather.8.cloned.1.call-start = ((), (), s32[]{:S(2)}) async-start(), calls=%async_computation.5 | async-start | bytes 5898240 | tf_op jit(solution)/shard_map/all_gather | solution.py:1902
  84.8 580.0 %reduce-scatter.14.cloned.1.call-start = ((), (), s32[]{:S(2)}) async-start(), calls=%async_computation.8 | async-start | bytes 5898240
  86.4 294.0 %copy-start.25 = (s32[1,384]{1,0:T(1,128)}, s32[1,384]{1,0:T(1,128)S(1)}, u32[]{:S(2)}) copy-start(s32[1,384]{1,0:T(1,128)S(1)} %get-tuple-element.155.oq_ref) | copy-start | bytes 4612
  88.4 0.7 copy-start.16
  88.4 1.1 copy-start.18
  89.6 1.4 copy-start
  234.8 1.6 copy-start.4
  236.4 1.0 copy-start.5
  237.4 1.0 copy-start.6
  238.4 1.0 copy-start.8
  239.5 0.7 copy-start.9
  240.1 0.7 copy-start.10
  240.8 134.2 %copy-start.11 = (f32[12,1,384]{2,1,0:T(1,128)}, f32[12,1,384]{2,1,0:T(1,128)S(1)}, u32[]{:S(2)}) copy-start(f32[12,1,384]{2,1,0:T(1,128)S(1)} %get-tuple-element.68.lse_ref) | copy-start | bytes 55300
  375.0 289.8 %reduce-scatter.12.cloned.1.call-start = ((), (), s32[]{:S(2)}) async-start(), calls=%async_computation.7 | async-start | bytes 5898240
  375.0 3.2 copy-start.19
  375.1 3.3 copy-start.17
  375.6 293.7 %reduce-scatter.10.cloned.1.call-start = ((), (), s32[]{:S(2)}) async-start(), calls=%async_computation.6 | async-start | bytes 5898240
  378.5 2.5 copy-start.22
  381.6 1.3 copy-start.13
  508.9 1.7 copy-start.1
  509.1 9.0 %copy-start.20 = (bf16[384,14,128]{0,2,1:T(8,128)(2,1)}, bf16[384,14,128]{0,2,1:T(8,128)(2,1)S(1)}, u32[]{:S(2)}) copy-start(bf16[384,14,128]{0,2,1:T(8,128)(2,1)S(1)} %pad_maximum_fusion.3) | copy-start | bytes 4128772
  518.8 7.1 %copy-start.7 = (bf16[384,1536]{1,0:T(8,128)(2,1)S(1)}, bf16[384,1536]{1,0:T(8,128)(2,1)}, u32[]{:S(2)}) copy-start(bf16[384,1536]{1,0:T(8,128)(2,1)} %copy-done.6) | copy-start | bytes 3538948
  518.8 7.1 %copy-start.21 = (bf16[384,14,128]{0,2,1:T(8,128)(2,1)S(1)}, bf16[384,14,128]{0,2,1:T(8,128)(2,1)}, u32[]{:S(2)}) copy-start(bf16[384,14,128]{0,2,1:T(8,128)(2,1)} %copy-done.20) | copy-start | bytes 4128772
  652.4 5.0 copy-start.24
  657.5 2.5 copy-start.15
  659.9 1.4 copy-start.2
  659.9 2.5 copy-start.12
  660.0 3.2 copy-start.14
  664.8 2.9 copy-start.23
Sparse Core Ops, SparseCore 0:
  83.4 57.2 all-gather.3
  142.6 57.0 all-gather.5
  201.5 56.9 all-gather.7
  375.1 56.7 reduce-scatter.13
  434.7 57.0 reduce-scatter.11
  494.7 62.8 reduce-scatter.9

commit v6 on v5

--- a/solution.py
+++ b/solution.py
@@ -43,15 +43,6 @@
         value_rows
         * lax.rsqrt(jnp.mean(value_rows * value_rows, axis=-1, keepdims=True) + EPSILON)
         * gain
-    )
-
-
-def rotate(value_rows, cosine, sine):
-    half_dim = value_rows.shape[-1] // 2
-    first = value_rows[..., :half_dim]
-    second = value_rows[..., half_dim:]
-    return jnp.concatenate(
-        [first * cosine - second * sine, second * cosine + first * sine], axis=-1
     )
 
 
@@ -179,6 +170,29 @@
         + [pltpu.SemaphoreType.DMA((count,))]
         + [pltpu.SemaphoreType.DMA((count, fsdp - 1)) for unused in range(4)]
     )
+
+
+class ShardGather:
+    def __init__(self, ref, out, buffer, sems, fsdp):
+        own_sem, send_sem, recv_sem = sems
+        ctx, me, chip, core, sibling = place()
+        rows = ref.shape[1]
+        mine = out.at[:, pl.ds(me * rows, rows)]
+        self.sends = [
+            remote(ref, mine, send_sem.at[j], recv_sem.at[j], (ctx, peer))
+            for j, peer in enumerate(peers_of(me, fsdp))
+        ]
+        self.own = Bounce(ref, mine, buffer, own_sem)
+
+    def start(self):
+        for copy in self.sends + [self.own]:
+            copy.start()
+
+    def finish(self):
+        self.own.turn()
+        for copy in self.sends:
+            copy.wait()
+        self.own.wait()
 
 
 class LineGather:
@@ -817,6 +831,7 @@
 def front_kernel(
     scale,
     chips,
+    fsdp,
     expert_count,
     tokens_ref,
     gain_a_ref,
@@ -831,6 +846,7 @@
     table_ref,
     qkv_ref,
     wo_ref,
+    gate_w_ref,
     passed_ref,
     q_ref,
     normed_ref,
@@ -842,9 +858,11 @@
     gate_ref,
     weights_ref,
     hidden_all_ref,
+    gate_full_ref,
     grad_ref,
     qkv_v,
     wo_v,
+    gate_v,
     hidden_v,
     bias,
     top,
@@ -852,6 +870,9 @@
     acc,
     load_sem,
     own_sem,
+    gate_own,
+    gate_send,
+    gate_recv,
     *line_sems,
 ):
     ctx, me, chip, core, sibling = place()
@@ -867,7 +888,11 @@
     ]
     for copy in loads:
         copy.start()
-    greet(chips, [], True)
+    greet(chips, peers_of(me, fsdp), True)
+    gate_gather = ShardGather(
+        gate_w_ref, gate_full_ref, gate_v, (gate_own, gate_send, gate_recv), fsdp
+    )
+    gate_gather.start()
     kv_line = LineGather(
         [kv_ref.at[0, 0], table_all_ref.at[0, 0]], [kv_ref, table_all_ref], line_sems[:7], chips
     )
@@ -1056,6 +1081,7 @@
             line.arrived(slot)
         line.sent()
     kv_line.sent()
+    gate_gather.finish()
     grad_line.finish(chips - 2)
     for index in range(2):
         own(index).wait()
@@ -1075,8 +1101,10 @@
     table,
     qkv,
     w_out,
+    w_gate,
     grad_all,
     chips,
+    fsdp,
     collective_id,
 ):
     rows, width = tokens.shape
@@ -1095,17 +1123,19 @@
         ((rows, LANES), F32),
         ((2, chips, expert_count, rows), F32),
         ((2, chips, rows, width), BF16),
+        ((w_gate.shape[0], width, w_gate.shape[2]), BF16),
         (grad_all.shape, BF16),
     ]
     flops = 4 * rows * (2 * chips * rows) * width + 2 * rows * width * (2 * width + 2 * kv_width)
     return pl.pallas_call(
-        functools.partial(front_kernel, HEAD_SIZE ** (-0.5), chips, expert_count),
+        functools.partial(front_kernel, HEAD_SIZE ** (-0.5), chips, fsdp, expert_count),
         out_shape=[jax.ShapeDtypeStruct(shape, kind) for shape, kind in shapes],
-        in_specs=[vmem] * 11 + [anywhere] * 3,
-        out_specs=[vmem] * 9 + [anywhere] * 2,
+        in_specs=[vmem] * 11 + [anywhere] * 4,
+        out_specs=[vmem] * 9 + [anywhere] * 3,
         scratch_shapes=[
             pltpu.VMEM(qkv.shape, BF16),
             pltpu.VMEM(w_out.shape, BF16),
+            pltpu.VMEM(w_gate.shape, BF16),
             pltpu.VMEM((rows, width), BF16),
             pltpu.VMEM((rows // 2, 2 * rows), F32),
             pltpu.VMEM((QUERY_HEADS, rows, LANES), F32),
@@ -1113,12 +1143,15 @@
             pltpu.VMEM((rows // 2, width), F32),
             pltpu.SemaphoreType.DMA((2,)),
             pltpu.SemaphoreType.DMA((2,)),
+            pltpu.SemaphoreType.DMA,
+            pltpu.SemaphoreType.DMA((fsdp - 1,)),
+            pltpu.SemaphoreType.DMA((fsdp - 1,)),
         ]
         + line_scratch([None] * 2, chips)
         + line_scratch([None], chips)
         + line_scratch([None], chips)
         + line_scratch([None] * 2, chips),
-        input_output_aliases={13: 10},
+        input_output_aliases={14: 11},
         compiler_params=pltpu.CompilerParams(
             collective_id=collective_id, has_side_effects=True, vmem_limit_bytes=FRONT_VMEM_BYTES
         ),
@@ -1140,6 +1173,7 @@
         table,
         qkv,
         w_out,
+        w_gate,
         grad_all,
     )
 
@@ -1156,6 +1190,8 @@
     oq_ref,
     pq_ref,
     ok_ref,
+    cos_ref,
+    sin_ref,
     mine_ref,
     other_ref,
     dq_ref,
@@ -1166,6 +1202,7 @@
     bias,
     dk_acc,
     dv_acc,
+    kv_total,
     mine_v,
     pair,
     got,
@@ -1204,8 +1241,9 @@
         remote(other_ref.at[r], pair.at[r], swap_send.at[r], swap_recv.at[r], (sibling, me))
         for r in range(chips)
     ]
+    slots = mine_v.shape[0]
     loads = [
-        pltpu.make_async_copy(mine_ref.at[r], mine_v.at[j % 2], load_sem.at[j % 2])
+        pltpu.make_async_copy(mine_ref.at[r], mine_v.at[j % slots], load_sem.at[j % slots])
         for j, r in enumerate(order)
     ]
     line = LineSum(
@@ -1219,9 +1257,9 @@
     def join(j):
         loads[j].wait()
         swaps[order[j]].wait_recv()
-        add_into(pair.at[order[j]], [pair.at[order[j]], mine_v.at[j % 2]])
-        if j + 2 < chips:
-            loads[j + 2].start()
+        add_into(pair.at[order[j]], [pair.at[order[j]], mine_v.at[j % slots]])
+        if j + slots < chips:
+            loads[j + slots].start()
 
     def kv_swap(group, r):
         return remote(
@@ -1259,7 +1297,7 @@
         greet(chips, [], True)
         for r in order:
             swaps[r].start()
-        for copy in loads[:2]:
+        for copy in loads[:slots]:
             copy.start()
 
         def fill(t, carry):
@@ -1293,7 +1331,11 @@
         return acc + dot(score_grad, key, TN)
 
     acc = lax.fori_loop(0, tiles, step, jnp.zeros((rows, HEAD_SIZE), F32))
-    dq_ref[...] = acc * scale
+    def turn_back(value):
+        back = value * cos_ref[...] - pltpu.roll(value, HEAD_SIZE // 2, 1) * sin_ref[...]
+        return back.astype(BF16)
+
+    dq_ref[...] = turn_back(acc * scale)
 
     last = QUERY_HEADS - 1
     stride = max(1, last // (chips - 2))
@@ -1334,7 +1376,13 @@
             for s in range(chips - 1):
                 if group > 0 or s not in early.values():
                     one.step(s)
-            one.total(kv_ref.at[group])
+            one.total(kv_total)
+            kv_ref[:, group * HEAD_SIZE : (group + 1) * HEAD_SIZE] = turn_back(
+                kv_total[:, :HEAD_SIZE]
+            )
+            kv_ref[:, (KVH + group) * HEAD_SIZE : (KVH + group + 1) * HEAD_SIZE] = kv_total[
+                :, HEAD_SIZE:
+            ].astype(BF16)
         for group in range(KVH):
             kv_line(group).finish()
             for r in range(chips):
@@ -1351,8 +1399,19 @@
 
 
 def attention_back(
-    queries, kv, attended, attended_grad, lse, order_mine, pos_mine, order_keys, mine, other,
-    collective_id
+    queries,
+    kv,
+    attended,
+    attended_grad,
+    lse,
+    order_mine,
+    pos_mine,
+    order_keys,
+    cosine,
+    sine,
+    mine,
+    other,
+    collective_id,
 ):
     rows = queries.shape[0]
     keys = kv.shape[0]
@@ -1364,8 +1423,8 @@
         functools.partial(attention_back_kernel, HEAD_SIZE ** (-0.5), chips),
         grid=(QUERY_HEADS,),
         out_shape=[
-            jax.ShapeDtypeStruct(queries.shape, F32),
-            jax.ShapeDtypeStruct((KVH, rows, 2 * HEAD_SIZE), F32),
+            jax.ShapeDtypeStruct(queries.shape, BF16),
+            jax.ShapeDtypeStruct((rows, 2 * KVH * HEAD_SIZE), BF16),
         ]
         + [jax.ShapeDtypeStruct((rows, width), BF16)] * 3,
         in_specs=[
@@ -1378,12 +1437,14 @@
             pl.BlockSpec((1, rows), lambda h: (0, 0)),
             pl.BlockSpec((1, rows), lambda h: (0, 0)),
             pl.BlockSpec((keys, 1), lambda h: (0, 0)),
+            pl.BlockSpec((rows, HEAD_SIZE), lambda h: (0, 0)),
+            pl.BlockSpec((rows, HEAD_SIZE), lambda h: (0, 0)),
             anywhere,
             anywhere,
         ],
         out_specs=[
             head_rows,
-            pl.BlockSpec((KVH, rows, 2 * HEAD_SIZE), lambda h: (0, 0, 0)),
+            pl.BlockSpec((rows, 2 * KVH * HEAD_SIZE), lambda h: (0, 0)),
             anywhere,
             anywhere,
             anywhere,
@@ -1392,7 +1453,8 @@
             pltpu.VMEM((keys, rows), F32),
             pltpu.VMEM((keys, HEAD_SIZE), F32),
             pltpu.VMEM((keys, HEAD_SIZE), F32),
-            pltpu.VMEM((2, rows, width), BF16),
+            pltpu.VMEM((rows, 2 * HEAD_SIZE), F32),
+            pltpu.VMEM((2 if chips <= 4 else 1, rows, width), BF16),
             pltpu.VMEM((chips, rows, width), BF16),
             pltpu.VMEM((chips + 1, rows, width), BF16),
             pltpu.VMEM((KVH, 2, chips, rows, 2 * HEAD_SIZE), BF16),
@@ -1425,6 +1487,8 @@
         order_mine[None, :],
         pos_mine[None, :],
         order_keys[:, None],
+        cosine,
+        sine,
         mine,
         other,
     )
@@ -1895,9 +1959,8 @@
         [qkv_shard, small, w_out], [grad_out[0]], chips - 2, fsdp, chips, 0
     )
 
-    qkv_full, w_gate, w_up, w_down = lax.optimization_barrier((qkv_full, w_gate, w_up, w_down))
-    gate_full, up_full, down_full = (
-        lax.all_gather(w_gate, "fsdp", axis=1, tiled=True),
+    qkv_full, w_up, w_down = lax.optimization_barrier((qkv_full, w_up, w_down))
+    up_full, down_full = (
         lax.all_gather(w_up, "fsdp", axis=1, tiled=True),
         lax.all_gather(w_down, "fsdp", axis=2, tiled=True),
     )
@@ -1927,8 +1990,8 @@
     half_dim = HEAD_SIZE // 2
     freqs = ROPE_BASE ** (-2.0 * jnp.arange(half_dim).astype(F32) / HEAD_SIZE)
     angles = pos_mine.astype(F32)[:, None] * freqs[None, :]
-    cosine = jnp.cos(angles)
-    sine = jnp.sin(angles)
+    cosine = jnp.concatenate([jnp.cos(angles), jnp.cos(angles)], axis=1)
+    sine = jnp.concatenate([-jnp.sin(angles), jnp.sin(angles)], axis=1)
 
     inputs = tokens[0].astype(F32)
     (
@@ -1942,14 +2005,15 @@
         gate_weights,
         weights_all,
         hidden_all,
+        gate_full,
         grad_all,
     ) = front(
         tokens[0],
         gain_a,
         gain_b,
         small_full,
-        jnp.concatenate([cosine, cosine], axis=1),
-        jnp.concatenate([-sine, sine], axis=1),
+        cosine,
+        sine,
         order_mine,
         pos_mine,
         order_keys,
@@ -1957,14 +2021,15 @@
         table.T,
         qkv_full,
         out_full,
+        w_gate,
         grad_all,
         chips,
+        fsdp,
         1,
     )
     kv_all = kv_all.reshape(-1, 2 * kv_width)
     gate_weights = gate_weights[:, :expert_count]
     hidden_two = hidden_all[0, 0]
-    cosine, sine = cosine[:, None, :], sine[:, None, :]
 
     returned, out_mine, out_other, gate_local, up_local, down_local = experts_pass(
         hidden_all,
@@ -2013,22 +2078,13 @@
         order_mine,
         pos_mine,
         order_keys,
+        cosine,
+        sine,
         out_mine,
         out_other,
         3,
     )
-    key_grad = [kv_grad[group, :, :HEAD_SIZE] for group in range(KVH)]
-    value_grad = [kv_grad[group, :, HEAD_SIZE:] for group in range(KVH)]
-    turned_grad = rotate(
-        jnp.concatenate([query_grad] + key_grad, axis=1).reshape(
-            tok_rows, QUERY_HEADS + KVH, HEAD_SIZE
-        ),
-        cosine,
-        -sine,
-    ).reshape(tok_rows, width + kv_width)
-    pre_grad = jnp.concatenate(
-        [turned_grad.astype(BF16)] + [part.astype(BF16) for part in value_grad], axis=1
-    )
+    pre_grad = jnp.concatenate([query_grad, kv_grad], axis=1)
     qkv_local = jnp.einsum("td,tc->dc", hidden_one, pre_grad, preferred_element_type=F32)
     hidden_one_grad = jnp.einsum("tc,dc->td", pre_grad, qkv_full, preferred_element_type=F32)
     unused_one, norm_one_back = jax.vjp(rms_scale, inputs, gain_a)

time: 684 us -> 662 us (0.968)
  waiting for transfers between devices: 19.6 us -> 1.28 us
  Pallas kernels: 550 us -> 558 us
    all_gather x1, waiting for transfers between devices: 17.6 us -> 0.01 us  [body(): lax.all_gather(w_down, 'fsdp', axis=2, tiled=True)]
    unnamed x61 -> x62, local copies, waits for them, and re-layouts: 14.6 us -> 16 us
  transfers between devices with their start and end apart: 6 -> 5, of which waited for: 1 -> 0; matrix products, arithmetic and copies ran while one was open for 11% -> 10% of each run, Pallas kernels for 54% -> 56%
where the time goes in v6:
time: 662 us; the launch traced here: 658 us
  Pallas kernels  558 us (84%)
  other arithmetic  32 us (5%)
  matrix products  30.9 us (5%)
  local copies, waits for them, and re-layouts  21.5 us (3%)
  between operations  14.4 us (2%)
    pallas_call x1, Pallas kernels, front(): pl.pallas_call(functools.partial(front_kernel, HEAD_SIZE ** (-0.5), chips...  145 us
    pallas_call x1, Pallas kernels, dense_reduce(): pl.pallas_call(functools.partial(dense_reduce_kernel, fsdp, chips, tuple(...  123 us
    pallas_call x1, Pallas kernels, experts_pass(): pl.pallas_call(functools.partial(experts_kernel, capacity, local_experts,...  117 us
    pallas_call x1, Pallas kernels, attention_back(): pl.pallas_call(functools.partial(attention_back_kernel, HEAD_SIZE ** (-0....  103 us
    pallas_call x1, Pallas kernels, gather(): pl.pallas_call(functools.partial(gather_kernel, len(dense), len(line), le...  69.9 us
    unnamed x62, local copies, waits for them, and re-layouts  16 us
  transfers between devices with their start and end apart: 5, of which 0 were waited for; matrix products, arithmetic and copies ran while one was open for 10% of the time, Pallas kernels for 56%

profile of v6, /device:TPU:0, one launch (start us, length us, event | category | flops | bytes accessed | tf_op | source)
XLA Modules:
  0.0 657.8 jit_solution(402104611479469475)
XLA Ops:
  7.2 0.8 broadcast_in_dim.38
  8.0 0.8 broadcast_in_dim.39
  8.8 0.8 copy.79
  9.7 2.9 pad_maximum_fusion.refs_0_
  12.6 0.8 maximum_maximum_fusion.refs_1_
  13.4 69.9 %gather.1 = (bf16[1536,2048]{1,0:T(8,128)(2,1)}, bf16[1536,128]{1,0:T(8,128)(2,1)}, bf16[1536,1536]{1,0:T(8,128)(2,1)}, bf16[2,4,384,1536]{3,2,1,0:T(8,128)(2,1)}) custom-call(bf16[384,2048]{1,0:T(8,128)(2,1)} %pad_maximum_fusion.refs_0_, bf16[384,128]{1,0:T(8,128)(2,1)} %maximum_maximum_fusion.refs_1_, bf16[384,1536]{1,0:T(8,128)(2,1)} %refs_2_.1, ...), custom_call_target="tpu_custom_call" | custom-call | tf_op jit(solution)/shard_map/gather/pallas_call | solution.py:385
  83.3 0.7 all-gather.5.cloned.1.call-update
  84.1 0.5 broadcast.125
  84.6 0.7 reduce.14
  85.4 0.2 reduce-window.8
  85.8 0.1 copy.86.pq_ref
  85.9 0.1 copy.85.oq_ref
  86.1 0.5 convert_reduce_fusion
  86.9 0.8 fusion.26
  87.6 0.2 pad_maximum_fusion.1
  87.8 0.3 fusion.12.table_ref
  88.1 0.4 copy-done.4
  88.5 1.3 copy-done
  89.8 1.4 copy-done.6
  91.2 144.7 %front.1 = (bf16[384,1536]{1,0:T(8,128)(2,1)S(1)}, bf16[384,1536]{1,0:T(8,128)(2,1)S(1)}, bf16[2,4,384,512]{3,2,1,0:T(8,128)(2,1)S(1)}, f32[2,4,16,384]{3,2,1,0:...) custom-call(bf16[384,1536]{1,0:T(8,128)(2,1)S(1)} %bitcast.60, ...), custom_call_target="tpu_custom_call", output_to_operand_aliasing={{11}: (14, {})} | custom-call | flops 11475615744 | bytes 40000000 | tf_op jit(solution)/shard_map/front/pallas_call | solution.py:1130
  235.9 0.7 copy-done.5
  236.6 1.7 copy-done.7
  238.2 1.0 copy-done.8
  239.2 1.0 copy-done.9
  240.2 1.0 copy-done.11
  241.3 0.7 copy-done.12
  241.9 0.7 copy-done.13
  242.6 117.2 %experts.1 = (bf16[384,1664]{1,0:T(8,128)(2,1)}, bf16[4,384,1536]{2,1,0:T(8,128)(2,1)}, bf16[4,384,1536]{2,1,0:T(8,128)(2,1)}, bf16[4,2,384,768]{3,2,1,0:T(8,128...) custom-call(bf16[2,4,384,1536]{3,2,1,0:T(8,128)(2,1)} %get-tuple-ele, ...), custom_call_target="tpu_custom_call" | custom-call | flops 48318382080 | bytes 100000000 | tf_op jit(solution)/shard_map/experts/pallas_call | solution.py:1859
  359.9 0.5 reduce-scatter.12.cloned.1.call-update
  360.4 2.6 broadcast_in_dim_reshape.4.ok_ref
  363.1 1.7 fusion.3
  364.7 0.2 multiply_reduce_fusion.2
  365.0 0.6 reshape_subtract_fusion.pq_ref
  365.6 0.2 convert_element_type.159
  365.7 0.2 multiply_reduce_fusion.3
  366.0 0.2 multiply_convert_fusion
  366.1 1.6 convolution_convert_fusion.3
  367.7 2.3 multiply_reduce_fusion
  370.0 0.2 copy.88
  370.3 0.3 reshape.199
  370.5 2.8 fusion
  373.3 6.6 convolution_convert_fusion.2.do_ref
  379.9 103.0 %attention_back.1 = (bf16[384,1536]{1,0:T(8,128)(2,1)}, bf16[384,512]{1,0:T(8,128)(2,1)}, bf16[384,1536]{1,0:T(8,128)(2,1)}, bf16[384,1536]{1,0:T(8,128)(2,1)}, bf16[384,1536]{1,0:T(8,128)(2,1)}) custom-call(bf16[384,1536]{1,0:T(8,128)(2,1)} %copy-done.11, bf16[3072,512]{1,0:T(8,128)(2,1)} %bitcast.61, bf16[3072,512]{1,0:T(8,128)(2,1)} %bitcast.62, ...), custom_call_target="tpu_custom_call" | custom-call | flops 18119393280 | bytes 12189696 | tf_op jit(solution)/shard_map/attention_back/pallas_call | solution.py:1422
  482.9 1.5 constant_dynamic-update-slice_fusion.1
  484.5 0.1 copy-done.1
  484.6 7.8 %fusion.6 = (f32[384]{0:T(512)S(1)}, bf16[1536]{0:T(1024)(128)(2,1)S(1)}, f32[384,1536]{1,0:T(8,128)}) fusion(f32[1536]{0:T(1024)S(1)} %get-tuple-element.151, bf16[1,384,1536]{2,1,0:T(8,128)(2,1)S(1)} %copy-done.1, f32[384]{0:T(512)S(1)} %fusion.31, bf16[384,2048]{1,0:T(8,128)(2,1)S(1)} %constant_dynamic-update-slice_fusion, ...), kind=kOutput, calls=%fused_computation.16 | convolution fusion | flops 2420045824 | bytes 11415552 | tf_op jit(solution)/shard_map/tc,dc->td/dot_general | solution.py:2089
  492.5 0.7 pad_maximum_fusion.3.refs_2_
  493.1 7.0 %convolution_convert_fusion = bf16[1536,1536]{1,0:T(8,128)(2,1)} fusion(bf16[384,1536]{1,0:T(8,128)(2,1)} %copy-done.8, f32[384,1536]{1,0:T(8,128)} %copy-done.15), kind=kOutput, calls=%fused_computation | convolution fusion | flops 1814888448 | bytes 8257536 | tf_op jit(solution)/shard_map/tc,td->cd/dot_general | solution.py:2067
  500.2 5.4 convolution_convert_fusion.1
  505.6 122.9 %dense_reduce.1 = (bf16[2,192,2048]{2,1,0:T(8,128)(2,1)}, bf16[2,192,1536]{2,1,0:T(8,128)(2,1)}, bf16[2,16,512]{2,1,0:T(8,128)(2,1)}, f32[384,1536]{1,0:T(8,128)}) custom-call(bf16[4,2,192,2048]{3,2,1,0:T(8,128)(2,1)} %bitcast.63, bf16[4,2,192,1536]{3,2,1,0:T(8,128)(2,1)} %bitcast.64, bf16[4,2,16,512]{3,2,1,0:T(8,128)(2,1)} %pad_maximum_fusion.3.refs_2_, ...), custom_call_target="tpu_custom_call" | custom-call | tf_op jit(solution)/shard_map/dense_reduce/pallas_call | solution.py:795
  628.5 0.7 slice_convert_fusion.3
  629.3 0.7 copy.91
  630.0 1.4 convert_reduce_fusion.3
  631.4 2.1 slice_convert_fusion.1
  633.4 3.0 slice_convert_fusion
  636.4 1.8 bitcast_convert_fusion.3
  638.2 0.7 copy-done.18
  638.9 1.4 fusion.7
  640.3 1.0 copy-done.16
  641.3 0.7 copy-done.17
  642.0 1.6 fusion.8
  643.7 2.9 bitcast_convert_fusion
  646.6 1.6 bitcast_convert_fusion.1
  648.2 2.8 bitcast_convert_fusion.2
  (85 shorter events, 1.1 us)
Async XLA Ops:
  7.2 235.4 %all-gather.3.cloned.1.call-start = ((), (), s32[]{:S(2)}) async-start(), calls=%async_computation.3 | async-start | bytes 5898240 | tf_op jit(solution)/shard_map/all_gather | solution.py:1964
  13.4 71.3 %copy-start.26 = (s32[1,3072]{1,0:T(1,128)S(1)}, s32[1,3072]{1,0:T(1,128)}, u32[]{:S(2)}) copy-start(s32[1,3072]{1,0:T(1,128)} %param.17) | copy-start | bytes 36868
  13.4 72.1 %copy-start.28 = (s32[1,3]{1,0:T(1,128)S(1)}, s32[1,3]{1,0:T(1,128)}, u32[]{:S(2)}) copy-start(s32[1,3]{1,0:T(1,128)} %param.18) | copy-start | bytes 40
  83.2 2.8 copy-start.3
  83.2 3.4 copy-start.27
  83.3 159.3 %all-gather.5.cloned.1.call-start = ((), (), s32[]{:S(2)}) async-start(), calls=%async_computation.4 | async-start | bytes 5898240 | tf_op jit(solution)/shard_map/all_gather | solution.py:1965
  84.0 559.7 %reduce-scatter.14.cloned.1.call-start = ((), (), s32[]{:S(2)}) async-start(), calls=%async_computation.7 | async-start | bytes 5898240
  85.6 279.3 %copy-start.25 = (s32[1,384]{1,0:T(1,128)}, s32[1,384]{1,0:T(1,128)S(1)}, u32[]{:S(2)}) copy-start(s32[1,384]{1,0:T(1,128)S(1)} %get-tuple-element.155.oq_ref) | copy-start | bytes 4612
  87.8 0.7 copy-start.4
  88.5 1.3 copy-start
  89.8 1.4 copy-start.6
  235.9 0.7 copy-start.5
  236.6 1.7 copy-start.7
  238.2 1.0 copy-start.8
  239.2 1.0 copy-start.9
  240.2 1.0 copy-start.11
  241.3 0.7 copy-start.12
  241.9 0.7 copy-start.13
  242.6 117.2 %copy-start.14 = (f32[12,1,384]{2,1,0:T(1,128)}, f32[12,1,384]{2,1,0:T(1,128)S(1)}, u32[]{:S(2)}) copy-start(f32[12,1,384]{2,1,0:T(1,128)S(1)} %get-tuple-element.68.lse_ref) | copy-start | bytes 55300
  359.8 283.9 %reduce-scatter.12.cloned.1.call-start = ((), (), s32[]{:S(2)}) async-start(), calls=%async_computation.6 | async-start | bytes 5898240
  360.4 287.8 %reduce-scatter.10.cloned.1.call-start = ((), (), s32[]{:S(2)}) async-start(), calls=%async_computation.5 | async-start | bytes 5898240
  363.1 2.5 copy-start.19
  373.3 6.6 copy-start.15
  482.9 1.6 copy-start.24
  482.9 1.7 copy-start.1
  484.6 7.8 %copy-start.22 = (bf16[384,2048]{1,0:T(8,128)(2,1)}, bf16[384,2048]{1,0:T(8,128)(2,1)S(1)}, u32[]{:S(2)}) copy-start(bf16[384,2048]{1,0:T(8,128)(2,1)S(1)} %constant_dynamic-update-slice_fusion) | copy-start | bytes 4718596
  493.1 7.0 %copy-start.10 = (bf16[384,1536]{1,0:T(8,128)(2,1)S(1)}, bf16[384,1536]{1,0:T(8,128)(2,1)}, u32[]{:S(2)}) copy-start(bf16[384,1536]{1,0:T(8,128)(2,1)} %copy-done.9) | copy-start | bytes 3538948
  493.1 7.0 %copy-start.23 = (bf16[384,2048]{1,0:T(8,128)(2,1)S(1)}, bf16[384,2048]{1,0:T(8,128)(2,1)}, u32[]{:S(2)}) copy-start(bf16[384,2048]{1,0:T(8,128)(2,1)} %copy-done.22) | copy-start | bytes 4718596
  631.4 5.0 copy-start.21
  636.4 2.5 copy-start.18
  638.9 1.4 copy-start.2
  638.9 2.5 copy-start.16
  638.9 3.2 copy-start.17
  643.7 2.9 copy-start.20
Sparse Core Ops, SparseCore 0:
  83.4 95.2 all-gather.2
  180.5 61.4 all-gather.4
  359.9 55.7 reduce-scatter.13
  418.6 57.0 reduce-scatter.11
  478.5 79.1 reduce-scatter.9

commit v7 on v6

--- a/solution.py
+++ b/solution.py
@@ -531,8 +531,8 @@
 
 
 class DenseSum:
-    def __init__(self, local, out, buffers, sems, fsdp, chips):
-        self.local, self.out = local, out
+    def __init__(self, local, held, out, buffers, sems, fsdp, chips):
+        self.local, self.held, self.out = local, held, out
         self.pair, self.cross, self.sums, got, self.spread = buffers
         self.sems = sems
         self.chips = chips
@@ -606,7 +606,7 @@
     def cross_over(self):
         for j, owner in enumerate(self.owners):
             self.swap(j).wait_recv()
-            add_into(self.pair.at[j], [self.local.at[owner, self.core], self.pair.at[j]])
+            add_into(self.pair.at[j], [self.held(j, owner), self.pair.at[j]])
             if j < len(self.owners) - 1:
                 self.crossing(j).start()
 
@@ -718,9 +718,11 @@
     for i, (which, start, size) in enumerate(cuts):
         buffers = rest[i * DENSE_BUFFERS : (i + 1) * DENSE_BUFFERS]
         sems = rest[count * DENSE_BUFFERS + i * DENSE_SEMS :][:DENSE_SEMS]
+        local = ins[which].at[:, :, :, pl.ds(start, size)]
         sums.append(
             DenseSum(
-                ins[which].at[:, :, :, pl.ds(start, size)],
+                local,
+                lambda j, owner, local=local: local.at[owner, core],
                 outs[which].at[:, :, pl.ds(start, size)],
                 buffers,
                 sems,
@@ -770,6 +772,26 @@
         to_left.wait_send()
 
 
+def dense_buffers(rows, size, fsdp, chips):
+    cut = size // chips
+    return [
+        pltpu.VMEM((fsdp, rows, size), BF16),
+        pltpu.VMEM((fsdp - 1, rows, size), BF16),
+        pltpu.VMEM((rows, size), BF16),
+        pltpu.VMEM((chips + 1, rows, cut), BF16),
+        pltpu.VMEM((2, chips, rows, cut), BF16),
+    ]
+
+
+def dense_sems(fsdp, chips):
+    return (
+        [pltpu.SemaphoreType.DMA((fsdp,)) for unused in range(2)]
+        + [pltpu.SemaphoreType.DMA((fsdp - 1,)) for unused in range(2)]
+        + [pltpu.SemaphoreType.DMA((chips - 1,)) for unused in range(8)]
+        + [pltpu.SemaphoreType.DMA((chips,)) for unused in range(2)]
+    )
+
+
 def dense_reduce(arrays, own, right, left, piece, fsdp, chips, collective_id):
     vmem = pl.BlockSpec(memory_space=pltpu.VMEM)
     cuts, buffers = [], []
@@ -777,21 +799,9 @@
         rows, width = a.shape[2:]
         for start in range(0, width, piece):
             size = min(piece, width - start)
-            cut = size // chips
             cuts.append((i, start, size))
-            buffers += [
-                pltpu.VMEM((fsdp, rows, size), BF16),
-                pltpu.VMEM((fsdp - 1, rows, size), BF16),
-                pltpu.VMEM((rows, size), BF16),
-                pltpu.VMEM((chips + 1, rows, cut), BF16),
-                pltpu.VMEM((2, chips, rows, cut), BF16),
-            ]
-    sems = (
-        [pltpu.SemaphoreType.DMA((fsdp,)) for unused in range(2)]
-        + [pltpu.SemaphoreType.DMA((fsdp - 1,)) for unused in range(2)]
-        + [pltpu.SemaphoreType.DMA((chips - 1,)) for unused in range(8)]
-        + [pltpu.SemaphoreType.DMA((chips,)) for unused in range(2)]
-    )
+            buffers += dense_buffers(rows, size, fsdp, chips)
+    sems = dense_sems(fsdp, chips)
     return pl.pallas_call(
         functools.partial(dense_reduce_kernel, fsdp, chips, tuple(cuts)),
         out_shape=[jax.ShapeDtypeStruct(a.shape[1:], BF16) for a in arrays]
@@ -1181,6 +1191,8 @@
 def attention_back_kernel(
     scale,
     chips,
+    fsdp,
+    early_dense,
     q_ref,
     k_ref,
     v_ref,
@@ -1194,11 +1206,13 @@
     sin_ref,
     mine_ref,
     other_ref,
+    dense_ref,
     dq_ref,
     kv_ref,
     own_ref,
     right_ref,
     left_ref,
+    dense_out_ref,
     bias,
     dk_acc,
     dv_acc,
@@ -1223,6 +1237,7 @@
     kr_recv,
     kl_send,
     kl_recv,
+    *dense_refs,
 ):
     ctx, me, chip, core, sibling = place()
     keys = k_ref.shape[0]
@@ -1261,6 +1276,25 @@
         if j + slots < chips:
             loads[j + slots].start()
 
+    if early_dense:
+        dense_v, dense_load = dense_refs[:2]
+        buffers = dense_refs[2 : 2 + DENSE_BUFFERS]
+        dense = DenseSum(
+            dense_ref,
+            lambda j, owner: dense_v.at[j],
+            dense_out_ref,
+            buffers,
+            dense_refs[2 + DENSE_BUFFERS :],
+            fsdp,
+            chips,
+        )
+        dense_loads = [
+            pltpu.make_async_copy(dense_ref.at[owner, core], dense_v.at[j], dense_load.at[j])
+            for j, owner in enumerate(dense.owners)
+        ]
+        stages = dense.stages()
+        at_head = {QUERY_HEADS - 1 - len(stages) // 2 + k: k for k in range(len(stages) // 2)}
+
     def kv_swap(group, r):
         return remote(
             kv_v.at[group, 1, r],
@@ -1294,7 +1328,11 @@
 
     @pl.when(head == 0)
     def _():
-        greet(chips, [], True)
+        greet(chips, peers_of(me, fsdp) if early_dense else [], True)
+        if early_dense:
+            for copy in dense_loads:
+                copy.start()
+            dense.start()
         for r in order:
             swaps[r].start()
         for copy in loads[:slots]:
@@ -1347,6 +1385,12 @@
             if h == 0:
                 for j in range(chips):
                     join(j)
+            if early_dense and h == 1:
+                for copy in dense_loads:
+                    copy.wait()
+                dense.cross_over()
+            if early_dense and h in at_head:
+                stages[at_head[h]]()
             for s in range(chips - 2):
                 if h == s * stride:
                     line.step(s)
@@ -1371,11 +1415,14 @@
             store(2, chips - 1, left_ref),
         ):
             copy.start()
+        rest = stages[len(stages) // 2 :] if early_dense else []
         for group in range(KVH):
             one = kv_line(group)
             for s in range(chips - 1):
                 if group > 0 or s not in early.values():
                     one.step(s)
+                    if rest:
+                        rest.pop(0)()
             one.total(kv_total)
             kv_ref[:, group * HEAD_SIZE : (group + 1) * HEAD_SIZE] = turn_back(
                 kv_total[:, :HEAD_SIZE]
@@ -1383,6 +1430,10 @@
             kv_ref[:, (KVH + group) * HEAD_SIZE : (KVH + group + 1) * HEAD_SIZE] = kv_total[
                 :, HEAD_SIZE:
             ].astype(BF16)
+        for stage in rest:
+            stage()
+        if early_dense:
+            dense.finish()
         for group in range(KVH):
             kv_line(group).finish()
             for r in range(chips):
@@ -1411,6 +1462,9 @@
     sine,
     mine,
     other,
+    dense,
+    fsdp,
+    early_dense,
     collective_id,
 ):
     rows = queries.shape[0]
@@ -1420,13 +1474,16 @@
     head_rows = pl.BlockSpec((rows, HEAD_SIZE), lambda h: (0, h))
     anywhere = pl.BlockSpec(memory_space=pl.ANY)
     return pl.pallas_call(
-        functools.partial(attention_back_kernel, HEAD_SIZE ** (-0.5), chips),
+        functools.partial(
+            attention_back_kernel, HEAD_SIZE ** (-0.5), chips, fsdp, early_dense
+        ),
         grid=(QUERY_HEADS,),
         out_shape=[
             jax.ShapeDtypeStruct(queries.shape, BF16),
             jax.ShapeDtypeStruct((rows, 2 * KVH * HEAD_SIZE), BF16),
         ]
-        + [jax.ShapeDtypeStruct((rows, width), BF16)] * 3,
+        + [jax.ShapeDtypeStruct((rows, width), BF16)] * 3
+        + [jax.ShapeDtypeStruct(dense.shape[1:], BF16)],
         in_specs=[
             head_rows,
             pl.BlockSpec((keys, HEAD_SIZE), lambda h: (0, h // per_group)),
@@ -1441,6 +1498,7 @@
             pl.BlockSpec((rows, HEAD_SIZE), lambda h: (0, 0)),
             anywhere,
             anywhere,
+            anywhere,
         ],
         out_specs=[
             head_rows,
@@ -1448,6 +1506,7 @@
             anywhere,
             anywhere,
             anywhere,
+            pl.BlockSpec(dense.shape[1:], lambda h: (0, 0, 0)) if early_dense else anywhere,
         ],
         scratch_shapes=[
             pltpu.VMEM((keys, rows), F32),
@@ -1467,7 +1526,17 @@
         ]
         + [pltpu.SemaphoreType.DMA((chips - 1,)) for unused in range(4)]
         + [pltpu.SemaphoreType.DMA((KVH, chips)) for unused in range(2)]
-        + [pltpu.SemaphoreType.DMA((KVH, chips - 1)) for unused in range(4)],
+        + [pltpu.SemaphoreType.DMA((KVH, chips - 1)) for unused in range(4)]
+        + (
+            [
+                pltpu.VMEM((fsdp,) + dense.shape[2:], BF16),
+                pltpu.SemaphoreType.DMA((fsdp,)),
+            ]
+            + dense_buffers(dense.shape[2], dense.shape[3], fsdp, chips)
+            + dense_sems(fsdp, chips)
+            if early_dense
+            else []
+        ),
         compiler_params=pltpu.CompilerParams(
             collective_id=collective_id, has_side_effects=True, vmem_limit_bytes=BACK_VMEM_BYTES
         ),
@@ -1491,6 +1560,7 @@
         sine,
         mine,
         other,
+        dense,
     )
 
 
@@ -1512,6 +1582,7 @@
     out_mine_ref,
     out_other_ref,
     gate_grad_ref,
+    gate_got_ref,
     up_grad_ref,
     down_grad_ref,
     x_ref,
@@ -1547,8 +1618,12 @@
     left_send,
     left_recv,
     stage_sem,
+    tile_own,
+    tile_send,
+    tile_recv,
 ):
     ctx, me, chip, core, sibling = place()
+    peers = peers_of(me, fsdp)
     tokens = hidden_v.shape[1]
     width = hidden_v.shape[2]
     slots = x_v.shape[1]
@@ -1612,7 +1687,7 @@
 
     for copy in load(0) + weights_in:
         copy.start()
-    greet(chips, [], True)
+    greet(chips, peers if per == 1 else [], True)
 
     slot = lax.broadcasted_iota(jnp.int32, (slot_rows, tokens), 0).astype(F32) + 1.0
     slot = jnp.where(slot <= capacity, slot, -1.0)
@@ -1785,7 +1860,7 @@
     def stage_wide(slot, p):
         return hidden_v.at[slot, pl.ds(p * shard, shard), pl.ds(0, units)]
 
-    def wide(e, held, target):
+    def wide(e, held, staged, target):
         def product(f):
             columns = pl.ds(pl.multiple_of(f * block, LANES), block)
             value = dot(
@@ -1794,9 +1869,9 @@
                 TN,
             ).astype(BF16)
             for p in range(per):
-                stage_wide(lax.rem(f, 2), p)[...] = value[p * shard : (p + 1) * shard, :]
-
-        products(e, stage_wide, target, product)
+                staged(lax.rem(f, 2), p)[...] = value[p * shard : (p + 1) * shard, :]
+
+        products(e, staged, target, product)
 
     def tall(e, target):
         def product(f):
@@ -1811,16 +1886,53 @@
 
         products(e, lambda slot, p: stage_tall.at[slot, p], target, product)
 
-    work = []
-    for e in range(local_experts):
+    def tile(e, j):
+        held = (hidden_v, grad_v)[e]
+        return held.at[j // 2, pl.ds(0, shard), pl.ds((j % 2) * units, units)]
+
+    def tile_copy(e, j):
+        if j == len(peers):
+            return pltpu.make_async_copy(tile(e, j), gate_grad_ref.at[e], tile_own.at[e])
+        return remote(
+            tile(e, j),
+            gate_got_ref.at[j, e],
+            tile_send.at[e, j],
+            tile_recv.at[e, j],
+            (ctx, peers[j]),
+        )
+
+    def gate_tiles(e):
+        for j, owner in enumerate(peers + [me]):
+            columns = pl.ds(pl.multiple_of(owner * shard, LANES), shard)
+            tile(e, j)[...] = dot(
+                down_v[:total_rows, columns],
+                gate_v[e * total_rows : (e + 1) * total_rows, :],
+                TN,
+            ).astype(BF16)
+            tile_copy(e, j).start()
+
+    def fetch_x(e):
         copies = [(x_ref.at[e], down_v.at[:total_rows])]
         if e == 0:
             for k in range(local_experts):
                 held = pl.ds(k * total_rows, total_rows)
                 copies += [(da_ref.at[k], gate_v.at[held]), (db_ref.at[k], up_v.at[held])]
-        work.append(lambda copies=copies: fetch(copies))
-        work.append(lambda e=e: wide(e, gate_v, gate_grad_ref))
-        work.append(lambda e=e: wide(e, up_v, up_grad_ref))
+        return lambda: fetch(copies)
+
+    def stage_up(slot, p):
+        return out_v.at[slot, pl.ds(p * shard, shard), pl.ds(0, units)]
+
+    work = []
+    for e in range(local_experts):
+        work.append(fetch_x(e))
+        if per == 1:
+            work.append(lambda e=e: gate_tiles(e))
+        else:
+            work.append(lambda e=e: wide(e, gate_v, stage_wide, gate_grad_ref))
+        if e > 0:
+            work.append(lambda e=e: wide(e, up_v, stage_up, up_grad_ref))
+    work.append(lambda: fetch([(x_ref.at[0], down_v.at[:total_rows])]))
+    work.append(lambda: wide(0, up_v, stage_up, up_grad_ref))
     for e in range(local_experts):
         copies = [(pg_ref.at[e], down_v.at[:total_rows])]
         if e == 0:
@@ -1839,6 +1951,10 @@
 
     line.total(returned_ref)
     line.finish()
+    if per == 1:
+        for e in range(local_experts):
+            for j in range(fsdp):
+                tile_copy(e, j).wait()
 
 
 def experts_pass(
@@ -1864,13 +1980,16 @@
             jax.ShapeDtypeStruct((tokens, wide), BF16),
             jax.ShapeDtypeStruct((chips, tokens, width), BF16),
             jax.ShapeDtypeStruct((chips, tokens, width), BF16),
-            jax.ShapeDtypeStruct((fsdp, local_experts, shard, units), BF16),
+            jax.ShapeDtypeStruct(
+                ((fsdp,) if per > 1 else ()) + (local_experts, shard, units), BF16
+            ),
+            jax.ShapeDtypeStruct((fsdp - 1, local_experts, shard, units), BF16),
             jax.ShapeDtypeStruct((fsdp, local_experts, shard, units), BF16),
             jax.ShapeDtypeStruct((fsdp, local_experts, units, shard), BF16),
         ]
         + [jax.ShapeDtypeStruct(shape, BF16) for shape in saved],
         in_specs=[anywhere, anywhere, vmem, vmem, anywhere, anywhere, anywhere],
-        out_specs=[vmem] + [anywhere] * 10,
+        out_specs=[vmem] + [anywhere] * 11,
         scratch_shapes=[
             pltpu.VMEM((local_experts * width, units), BF16),
             pltpu.VMEM((local_experts * width, units), BF16),
@@ -1894,7 +2013,8 @@
             pltpu.SemaphoreType.DMA((chips,)),
         ]
         + [pltpu.SemaphoreType.DMA((chips - 1,)) for unused in range(4)]
-        + [pltpu.SemaphoreType.DMA((2, per))],
+        + [pltpu.SemaphoreType.DMA((2, per)), pltpu.SemaphoreType.DMA((local_experts,))]
+        + [pltpu.SemaphoreType.DMA((local_experts, fsdp - 1)) for unused in range(2)],
         compiler_params=pltpu.CompilerParams(
             collective_id=collective_id, has_side_effects=True, vmem_limit_bytes=EXPERT_VMEM_BYTES
         ),
@@ -1911,7 +2031,7 @@
         up.reshape(local_experts * width, units),
         down.reshape(local_experts * units, width),
     )
-    return outs[:6]
+    return outs[:7]
 
 
 def body(
@@ -2031,7 +2151,7 @@
     gate_weights = gate_weights[:, :expert_count]
     hidden_two = hidden_all[0, 0]
 
-    returned, out_mine, out_other, gate_local, up_local, down_local = experts_pass(
+    returned, out_mine, out_other, gate_local, gate_got, up_local, down_local = experts_pass(
         hidden_all,
         grad_all,
         table_all,
@@ -2044,10 +2164,13 @@
         fsdp,
         5,
     )
-    expert_grads = [
+    direct = gate_local.ndim == 3
+    if not direct:
+        gate_local = lax.psum_scatter(gate_local, "fsdp", scatter_dimension=0, tiled=True)[0]
+    up_sum, down_sum = (
         lax.psum_scatter(part, "fsdp", scatter_dimension=0, tiled=True)
-        for part in (gate_local, up_local, down_local)
-    ]
+        for part in (up_local, down_local)
+    )
 
     out_grad = grad_out[0].astype(F32)
     returned = returned.astype(F32)
@@ -2069,7 +2192,13 @@
         "td,cd->tc", branch_grad, out_full, preferred_element_type=F32
     ).astype(BF16)
 
-    query_grad, kv_grad, out_own, out_right, out_left = attention_back(
+    def halves(local):
+        local = local.astype(BF16).reshape(fsdp, 2, shard // 2, local.shape[1])
+        pad = -local.shape[3] % (LANES * chips)
+        return jnp.pad(local, ((0, 0), (0, 0), (0, 0), (0, pad))) if pad else local
+
+    early_dense = chips <= 4
+    query_grad, kv_grad, out_own, out_right, out_left, out_proj_sum = attention_back(
         queries,
         kv_all,
         attended,
@@ -2082,6 +2211,9 @@
         sine,
         out_mine,
         out_other,
+        halves(out_local),
+        fsdp,
+        early_dense,
         3,
     )
     pre_grad = jnp.concatenate([query_grad, kv_grad], axis=1)
@@ -2090,11 +2222,6 @@
     unused_one, norm_one_back = jax.vjp(rms_scale, inputs, gain_a)
     input_part, gain_one_local = norm_one_back(hidden_one_grad)
     input_grad = (middle_grad + input_part).astype(BF16)
-
-    def halves(local):
-        local = local.astype(BF16).reshape(fsdp, 2, shard // 2, local.shape[1])
-        pad = -local.shape[3] % (LANES * chips)
-        return jnp.pad(local, ((0, 0), (0, 0), (0, 0), (0, pad))) if pad else local
 
     span = shard * expert_count // 16
     wide = LANES * chips * -(-max(span, shard) // (LANES * chips))
@@ -2114,8 +2241,8 @@
         ],
         axis=1,
     )
-    qkv_sum, out_proj_sum, small_sum, out_sum = dense_reduce(
-        [halves(qkv_local), halves(out_local), small_local],
+    *sums, out_sum = dense_reduce(
+        [halves(qkv_local), small_local] + ([] if early_dense else [halves(out_local)]),
         out_own,
         out_right,
         out_left,
@@ -2124,12 +2251,20 @@
         chips,
         4,
     )
+    qkv_sum, small_sum = sums[:2]
+    if not early_dense:
+        out_proj_sum = sums[2]
     edge = width + 2 * kv_width
     qkv_grads = qkv_sum.reshape(shard, -1)
     out_proj_grad = out_proj_sum.reshape(shard, -1)[:, :width]
-    gate_grad_out, up_grad_out, down_grad_out = (
-        after(part, pre_grad)[0].astype(F32) for part in expert_grads
-    )
+    up_grad_out, down_grad_out = (
+        after(part, pre_grad)[0].astype(F32) for part in (up_sum, down_sum)
+    )
+    if direct:
+        gate_local, gate_got = lax.optimization_barrier((gate_local, gate_got, pre_grad))[:2]
+        gate_grad_out = add(gate_local, *[gate_got[j] for j in range(fsdp - 1)])
+    else:
+        gate_grad_out = after(gate_local, pre_grad).astype(F32)
     result = middle + out_sum
     return (
         result.astype(BF16)[None],

time: 662 us -> 644 us (0.973)
  Pallas kernels: 558 us -> 541 us
    pallas_call x1, Pallas kernels: 123 us -> 81.1 us  [dense_reduce(): pl.pallas_call(functools.partial(dense_reduce_kernel, fsdp, chips, tuple(...]
    pallas_call x1, Pallas kernels: 103 us -> 124 us  [attention_back(): pl.pallas_call(functools.partial(attention_back_kernel, HEAD_SIZE ** (-0....]
  transfers between devices with their start and end apart: 5 -> 4, of which waited for: 0 -> 0; matrix products, arithmetic and copies ran while one was open for 10% -> 10% of each run, Pallas kernels for 56% -> 55%
where the time goes in v7:
time: 644 us; the launch traced here: 640 us
  Pallas kernels  541 us (84%)
  other arithmetic  33.3 us (5%)
  matrix products  27.5 us (4%)
  local copies, waits for them, and re-layouts  22.6 us (4%)
  between operations  14.5 us (2%)
    pallas_call x1, Pallas kernels, front(): pl.pallas_call(functools.partial(front_kernel, HEAD_SIZE ** (-0.5), chips...  145 us
    pallas_call x1, Pallas kernels, attention_back(): pl.pallas_call(functools.partial(attention_back_kernel, HEAD_SIZE ** (-0....  124 us
    pallas_call x1, Pallas kernels, experts_pass(): pl.pallas_call(functools.partial(experts_kernel, capacity, local_experts,...  121 us
    pallas_call x1, Pallas kernels, dense_reduce(): pl.pallas_call(functools.partial(dense_reduce_kernel, fsdp, chips, tuple(...  81.1 us
    pallas_call x1, Pallas kernels, gather(): pl.pallas_call(functools.partial(gather_kernel, len(dense), len(line), le...  69.9 us
    unnamed x62, local copies, waits for them, and re-layouts  17.1 us
  transfers between devices with their start and end apart: 4, of which 0 were waited for; matrix products, arithmetic and copies ran while one was open for 10% of the time, Pallas kernels for 55%

profile of v7, /device:TPU:0, one launch (start us, length us, event | category | flops | bytes accessed | tf_op | source)
XLA Modules:
  0.0 639.5 jit_solution(9100177674300064697)
XLA Ops:
  7.2 0.8 broadcast_in_dim.38
  8.0 0.8 broadcast_in_dim.39
  8.8 0.8 copy.79
  9.7 2.9 pad_maximum_fusion.refs_0_
  12.6 0.8 maximum_maximum_fusion.refs_1_
  13.4 69.9 %gather.1 = (bf16[1536,2048]{1,0:T(8,128)(2,1)}, bf16[1536,128]{1,0:T(8,128)(2,1)}, bf16[1536,1536]{1,0:T(8,128)(2,1)}, bf16[2,4,384,1536]{3,2,1,0:T(8,128)(2,1)}) custom-call(bf16[384,2048]{1,0:T(8,128)(2,1)} %pad_maximum_fusion.refs_0_, bf16[384,128]{1,0:T(8,128)(2,1)} %maximum_maximum_fusion.refs_1_, bf16[384,1536]{1,0:T(8,128)(2,1)} %refs_2_.1, ...), custom_call_target="tpu_custom_call" | custom-call | tf_op jit(solution)/shard_map/gather/pallas_call | solution.py:385
  83.3 0.7 all-gather.5.cloned.1.call-update
  84.1 0.5 broadcast.125
  84.6 0.7 reduce.14
  85.4 0.2 reduce-window.8
  85.8 0.1 copy.86.pq_ref
  85.9 0.1 copy.85.oq_ref
  86.1 0.5 convert_reduce_fusion
  86.7 0.1 copy.84
  86.9 0.8 fusion.26
  87.6 0.2 pad_maximum_fusion.1
  87.8 0.3 fusion.12.table_ref
  88.1 0.4 copy-done.3
  88.5 1.3 copy-done
  89.8 1.4 copy-done.5
  91.2 144.7 %front.1 = (bf16[384,1536]{1,0:T(8,128)(2,1)S(1)}, bf16[384,1536]{1,0:T(8,128)(2,1)S(1)}, bf16[2,4,384,512]{3,2,1,0:T(8,128)(2,1)S(1)}, f32[2,4,16,384]{3,2,1,0:...) custom-call(bf16[384,1536]{1,0:T(8,128)(2,1)S(1)} %bitcast.66, ...), custom_call_target="tpu_custom_call", output_to_operand_aliasing={{11}: (14, {})} | custom-call | flops 11475615744 | bytes 40000000 | tf_op jit(solution)/shard_map/front/pallas_call | solution.py:1140
  235.9 0.7 copy-done.4
  236.6 1.8 copy-done.6
  238.4 1.0 copy-done.7
  239.4 1.0 copy-done.9
  240.4 1.0 copy-done.10
  241.4 0.7 copy-done.11
  242.1 0.7 copy-done.12
  242.8 121.4 %experts.1 = (bf16[384,1664]{1,0:T(8,128)(2,1)}, bf16[4,384,1536]{2,1,0:T(8,128)(2,1)}, bf16[4,384,1536]{2,1,0:T(8,128)(2,1)}, bf16[2,384,768]{2,1,0:T(8,128)(2,...) custom-call(bf16[2,4,384,1536]{3,2,1,0:T(8,128)(2,1)} %get-tuple-ele, ...), custom_call_target="tpu_custom_call" | custom-call | flops 48318382080 | bytes 100000000 | tf_op jit(solution)/shard_map/experts/pallas_call | solution.py:1975
  364.2 2.6 broadcast_in_dim_reshape.4.ok_ref
  366.8 1.7 fusion.3
  368.5 0.2 multiply_reduce_fusion.2
  368.7 0.6 reshape_subtract_fusion.pq_ref
  369.3 0.2 convert_element_type.174
  369.5 0.2 multiply_reduce_fusion.3
  369.7 0.2 multiply_convert_fusion
  369.9 2.3 multiply_reduce_fusion
  372.2 2.7 fusion
  375.0 4.6 convolution_convert_fusion.1
  379.6 3.0 convolution_convert_fusion.2.do_ref
  382.6 123.8 %attention_back.1 = (bf16[384,1536]{1,0:T(8,128)(2,1)}, bf16[384,512]{1,0:T(8,128)(2,1)}, bf16[384,1536]{1,0:T(8,128)(2,1)}, bf16[384,1536]{1,0:T(8,128)(2,1)}, ...) custom-call(bf16[384,1536]{1,0:T(8,128)(2,1)} %copy-done.10, bf16[3072,512]{1,0:T(8,128)(2,1)} %bitcast.67, ...), custom_call_target="tpu_custom_call" | custom-call | flops 18119393280 | bytes 12189696 | tf_op jit(solution)/shard_map/attention_back/pallas_call | solution.py:1476
  506.4 1.5 constant_dynamic-update-slice_fusion.1
  508.0 1.1 copy-done.21
  509.2 1.6 convolution_convert_fusion.3
  510.7 0.2 copy.88
  511.0 0.3 reshape.203
  511.2 7.8 %fusion.6 = (f32[384]{0:T(512)S(1)}, bf16[1536]{0:T(1024)(128)(2,1)S(1)}, f32[384,1536]{1,0:T(8,128)}) fusion(f32[1536]{0:T(1024)S(1)} %get-tuple-element.155, bf16[1,384,1536]{2,1,0:T(8,128)(2,1)} %param.15, f32[384]{0:T(512)S(1)} %fusion.31, bf16[384,2048]{1,0:T(8,128)(2,1)} %copy-done.21, bf16[1536,2048]{1,0:T(8,128)(2,1)} %get-tuple-element.53.qkv_ref), kind=kOutput, calls=%fused_computation.16 | convolution fusion | flops 2420045824 | bytes 11415552 | tf_op jit(solution)/shard_map/tc,dc->td/dot_general | solution.py:2221
  519.1 0.7 pad_maximum_fusion.3.refs_1_
  519.8 7.9 %convolution_convert_fusion = bf16[1536,2048]{1,0:T(8,128)(2,1)} fusion(bf16[384,1536]{1,0:T(8,128)(2,1)} %copy-done.9, bf16[384,2048]{1,0:T(8,128)(2,1)} %copy-done.21), kind=kOutput, calls=%fused_computation | convolution fusion | flops 2419064832 | bytes 9043968 | tf_op jit(solution)/shard_map/td,tc->dc/dot_general | solution.py:2220
  527.7 81.1 %dense_reduce.1 = (bf16[2,192,2048]{2,1,0:T(8,128)(2,1)}, bf16[2,16,512]{2,1,0:T(8,128)(2,1)}, f32[384,1536]{1,0:T(8,128)}) custom-call(bf16[4,2,192,2048]{3,2,1,0:T(8,128)(2,1)} %bitcast.69, bf16[4,2,16,512]{3,2,1,0:T(8,128)(2,1)} %pad_maximum_fusion.3.refs_1_, bf16[384,1536]{1,0:T(8,128)(2,1)} %get-tuple-element.75.refs_2_, ...), custom_call_target="tpu_custom_call" | custom-call | tf_op jit(solution)/shard_map/dense_reduce/pallas_call | solution.py:805
  608.8 0.7 slice_convert_fusion.3
  609.6 0.7 copy.91
  610.3 1.4 convert_reduce_fusion.3
  611.7 2.0 slice_convert_fusion.1
  613.7 4.4 convert_add_fusion
  618.1 1.7 slice_convert_fusion
  619.8 1.8 bitcast_convert_fusion.2
  621.5 0.7 copy-done.17
  622.2 1.4 fusion.7
  623.6 1.0 copy-done.15
  624.7 0.7 copy-done.16
  625.4 1.6 fusion.8
  627.0 2.8 bitcast_convert_fusion
  629.9 2.8 bitcast_convert_fusion.1
  (83 shorter events, 0.9 us)
Async XLA Ops:
  7.2 235.6 %all-gather.3.cloned.1.call-start = ((), (), s32[]{:S(2)}) async-start(), calls=%async_computation.2 | async-start | bytes 5898240 | tf_op jit(solution)/shard_map/all_gather | solution.py:2084
  13.4 71.3 %copy-start.24 = (s32[1,3072]{1,0:T(1,128)S(1)}, s32[1,3072]{1,0:T(1,128)}, u32[]{:S(2)}) copy-start(s32[1,3072]{1,0:T(1,128)} %param.17) | copy-start | bytes 36868
  13.4 72.1 %copy-start.26 = (s32[1,3]{1,0:T(1,128)S(1)}, s32[1,3]{1,0:T(1,128)}, u32[]{:S(2)}) copy-start(s32[1,3]{1,0:T(1,128)} %param.18) | copy-start | bytes 40
  83.2 2.8 copy-start.2
  83.2 3.4 copy-start.25
  83.3 159.5 %all-gather.5.cloned.1.call-start = ((), (), s32[]{:S(2)}) async-start(), calls=%async_computation.3 | async-start | bytes 5898240 | tf_op jit(solution)/shard_map/all_gather | solution.py:2085
  84.0 543.0 %reduce-scatter.9.cloned.1.call-start = ((), (), s32[]{:S(2)}) async-start(), calls=%async_computation.5 | async-start | bytes 5898240
  85.6 283.1 %copy-start.23 = (s32[1,384]{1,0:T(1,128)}, s32[1,384]{1,0:T(1,128)S(1)}, u32[]{:S(2)}) copy-start(s32[1,384]{1,0:T(1,128)S(1)} %get-tuple-element.159.oq_ref) | copy-start | bytes 4612
  87.8 0.7 copy-start.3
  88.5 1.3 copy-start
  89.8 1.4 copy-start.5
  235.9 0.7 copy-start.4
  236.6 1.8 copy-start.6
  238.4 1.0 copy-start.7
  239.4 1.0 copy-start.9
  240.4 1.0 copy-start.10
  241.4 0.7 copy-start.11
  242.1 0.7 copy-start.12
  242.8 121.4 %copy-start.13 = (f32[12,1,384]{2,1,0:T(1,128)}, f32[12,1,384]{2,1,0:T(1,128)S(1)}, u32[]{:S(2)}) copy-start(f32[12,1,384]{2,1,0:T(1,128)S(1)} %get-tuple-element.70.lse_ref) | copy-start | bytes 55300
  364.2 265.7 %reduce-scatter.7.cloned.1.call-start = ((), (), s32[]{:S(2)}) async-start(), calls=%async_computation.4 | async-start | bytes 5898240
  366.8 2.5 copy-start.19
  372.2 2.8 copy-start.8
  372.2 7.4 %slice-start = ((s8[4718592]{0:T(1024)(128)(4,1)}), s8[4194304]{0:T(1024)(128)(4,1)S(1)}, s32[]{:S(2)}) async-start(s8[4718592]{0:T(1024)(128)(4,1)} %bitcast.77), calls=%async_computation.6 | async-start | bytes 8388608
  375.0 4.6 copy-start.14
  375.0 4.6 slice-start.1
  506.4 1.5 copy-start.22
  508.0 1.1 copy-start.21
  613.7 4.4 copy-start.18
  618.1 1.7 copy-start.20
  619.8 2.5 copy-start.17
  622.2 1.4 copy-start.1
  622.2 2.5 copy-start.15
  622.2 3.2 copy-start.16
Sparse Core Ops, SparseCore 0:
  83.4 95.2 all-gather.2
  180.5 61.5 all-gather.4
  364.3 74.3 reduce-scatter.8
  441.5 65.5 reduce-scatter.6

commit v8 on v7

--- a/solution.py
+++ b/solution.py
@@ -23,7 +23,7 @@
 VMEM_BYTES = 56 * 1024 * 1024
 EXPERT_VMEM_BYTES = 119 * 512 * 1024
 BACK_VMEM_BYTES = 61 * 1024 * 1024
-FRONT_VMEM_BYTES = 40 * 1024 * 1024
+FRONT_VMEM_BYTES = 50 * 1024 * 1024
 MESH = pl.DeviceIdType.MESH
 F32 = jnp.float32
 BF16 = jnp.bfloat16
@@ -121,26 +121,77 @@
     )
 
 
+class Spread:
+    def __init__(self, block, place_of, size, sems, fsdp):
+        send_sem, recv_sem, on_send, on_recv = sems
+        ctx, me, chip, core, sibling = place()
+        self.peers = peers_of(me, fsdp)
+        self.square = fsdp == 4
+        near = self.peers[:2] if self.square else self.peers
+        self.sends = [
+            remote(block, place_of(me, 0, size), send_sem.at[j], recv_sem.at[j], (ctx, peer))
+            for j, peer in enumerate(near)
+        ]
+        self.on, self.last = [], []
+        if self.square:
+            half = size // 2
+            across_x, across_y, far = self.peers
+            for k, (owner, target) in enumerate(((across_x, across_y), (across_y, across_x))):
+                part = place_of(owner, k * half, half)
+                self.on.append(remote(part, part, on_send.at[k], on_recv.at[k], (ctx, target)))
+                part = place_of(far, k * half, half)
+                self.last.append(remote(part, part, on_send.at[k], on_recv.at[k], (ctx, target)))
+
+    def start(self):
+        for copy in self.sends:
+            copy.start()
+
+    def hand_on(self, also=lambda j: None):
+        for j, copy in enumerate(self.sends):
+            copy.wait_recv()
+            if self.square:
+                self.on[j].start()
+            also(j)
+
+    def finish(self, also=lambda j: None):
+        for copy in self.last:
+            copy.wait_recv()
+        if self.square:
+            also(2)
+        for copy in self.sends + self.on:
+            copy.wait_send()
+
+
+def spread_sems(fsdp):
+    return [pltpu.SemaphoreType.DMA((fsdp - 1,)) for unused in range(4)]
+
+
 class DenseGather:
     def __init__(self, ins, outs, sems, fsdp):
-        buffers, local_sem, send_sem, recv_sem, pass_sem, took_sem = sems
+        buffers, local_sem, pass_sem, took_sem, spread_refs = sems
         ctx, me, chip, core, sibling = place()
-        self.sends, self.passes, self.locals = [], [], []
+        peers = peers_of(me, fsdp)
+        self.spreads, self.passes, self.locals = [], [], []
         for i in range(len(ins)):
             rows = ins[i].shape[0]
             half = rows // 2
-            for j, peer in enumerate(peers_of(me, fsdp)):
-                self.sends.append(
-                    remote(
-                        ins[i].at[pl.ds(core * half, half)],
-                        outs[i].at[pl.ds(me * rows + core * half, half)],
-                        send_sem.at[i, j],
-                        recv_sem.at[i, j],
-                        (ctx, peer),
-                    )
+
+            def place_of(owner, begin, size, i=i, rows=rows, half=half):
+                return outs[i].at[pl.ds(owner * rows + core * half + begin, size)]
+
+            self.spreads.append(
+                Spread(
+                    ins[i].at[pl.ds(core * half, half)],
+                    place_of,
+                    half,
+                    spread_refs[4 * i : 4 * i + 4],
+                    fsdp,
                 )
-                got = outs[i].at[pl.ds(peer * rows + core * half, half)]
-                self.passes.append(
+            )
+            self.passes.append([])
+            for j, peer in enumerate(peers):
+                got = place_of(peer, 0, half)
+                self.passes[i].append(
                     remote(got, got, pass_sem.at[i, j], took_sem.at[i, j], (sibling, me))
                 )
             self.locals.append(
@@ -148,18 +199,24 @@
             )
 
     def start(self):
-        for copy in self.sends + self.locals:
+        for spread in self.spreads:
+            spread.start()
+        for copy in self.locals:
             copy.start()
 
-    def finish(self):
+    def hand_on(self):
         for copy in self.locals:
             copy.turn()
-        for send, copy in zip(self.sends, self.passes):
-            send.wait_recv()
-            copy.start()
-        for send in self.sends:
-            send.wait_send()
-        for copy in self.passes + self.locals:
+        for i, spread in enumerate(self.spreads):
+            spread.hand_on(lambda j, i=i: self.passes[i][j].start())
+
+    def finish(self):
+        for i, spread in enumerate(self.spreads):
+            spread.finish(lambda j, i=i: self.passes[i][j].start())
+        for passes in self.passes:
+            for copy in passes:
+                copy.wait()
+        for copy in self.locals:
             copy.wait()
 
 
@@ -168,30 +225,32 @@
     return (
         [pltpu.VMEM(a.shape, a.dtype) for a in arrays]
         + [pltpu.SemaphoreType.DMA((count,))]
-        + [pltpu.SemaphoreType.DMA((count, fsdp - 1)) for unused in range(4)]
+        + [pltpu.SemaphoreType.DMA((count, fsdp - 1)) for unused in range(2)]
+        + spread_sems(fsdp) * count
     )
 
 
 class ShardGather:
     def __init__(self, ref, out, buffer, sems, fsdp):
-        own_sem, send_sem, recv_sem = sems
         ctx, me, chip, core, sibling = place()
         rows = ref.shape[1]
-        mine = out.at[:, pl.ds(me * rows, rows)]
-        self.sends = [
-            remote(ref, mine, send_sem.at[j], recv_sem.at[j], (ctx, peer))
-            for j, peer in enumerate(peers_of(me, fsdp))
-        ]
-        self.own = Bounce(ref, mine, buffer, own_sem)
+
+        def place_of(owner, begin, size):
+            return out.at[:, pl.ds(owner * rows + begin, size)]
+
+        self.spread = Spread(ref, place_of, rows, sems[1:], fsdp)
+        self.own = Bounce(ref, place_of(me, 0, rows), buffer, sems[0])
 
     def start(self):
-        for copy in self.sends + [self.own]:
-            copy.start()
+        self.spread.start()
+        self.own.start()
+
+    def hand_on(self):
+        self.spread.hand_on()
+        self.own.turn()
 
     def finish(self):
-        self.own.turn()
-        for copy in self.sends:
-            copy.wait()
+        self.spread.finish()
         self.own.wait()
 
 
@@ -345,9 +404,12 @@
     greet(chips, peers_of(me, fsdp) if dense else [], line > 0)
     split = dense + line
     if dense:
-        own, scratch = scratch[: dense + 5], scratch[dense + 5 :]
+        own, scratch = scratch[: 5 * dense + 3], scratch[5 * dense + 3 :]
         first = DenseGather(
-            ins[:dense], outs[:dense], (own[:dense],) + tuple(own[dense:]), fsdp
+            ins[:dense],
+            outs[:dense],
+            (own[:dense],) + tuple(own[dense : dense + 3]) + (own[dense + 3 :],),
+            fsdp,
         )
         first.start()
     if line:
@@ -357,6 +419,8 @@
             second.send(step)
             if step == 0:
                 second.own()
+            if step == steps - 1 and dense:
+                first.hand_on()
             second.receive(step)
             if step == 0:
                 second.turn_own()
@@ -858,18 +922,23 @@
     wo_ref,
     gate_w_ref,
     passed_ref,
+    table_all_ref,
+    lse_ref,
+    gate_ref,
+    weights_ref,
+    q_hbm,
+    normed_hbm,
+    kv_hbm,
+    attended_hbm,
+    middle_hbm,
+    hidden_all_ref,
+    gate_full_ref,
+    grad_ref,
     q_ref,
     normed_ref,
     kv_ref,
-    table_all_ref,
     attended_ref,
-    lse_ref,
     middle_ref,
-    gate_ref,
-    weights_ref,
-    hidden_all_ref,
-    gate_full_ref,
-    grad_ref,
     qkv_v,
     wo_v,
     gate_v,
@@ -881,8 +950,11 @@
     load_sem,
     own_sem,
     gate_own,
-    gate_send,
-    gate_recv,
+    gate_s0,
+    gate_s1,
+    gate_s2,
+    gate_s3,
+    keep_sem,
     *line_sems,
 ):
     ctx, me, chip, core, sibling = place()
@@ -900,7 +972,11 @@
         copy.start()
     greet(chips, peers_of(me, fsdp), True)
     gate_gather = ShardGather(
-        gate_w_ref, gate_full_ref, gate_v, (gate_own, gate_send, gate_recv), fsdp
+        gate_w_ref,
+        gate_full_ref,
+        gate_v,
+        (gate_own, gate_s0, gate_s1, gate_s2, gate_s3),
+        fsdp,
     )
     gate_gather.start()
     kv_line = LineGather(
@@ -1026,6 +1102,9 @@
             line.across(i, 0).start()
         own(index).start()
 
+    def keep(k, src, dst):
+        return pltpu.make_async_copy(src, dst, keep_sem.at[k])
+
     def own(index):
         return pltpu.make_async_copy(
             hidden_v.at[parts[index]],
@@ -1034,6 +1113,8 @@
         )
 
     begin(0)
+    keep(0, q_ref, q_hbm).start()
+    keep(1, normed_ref, normed_hbm).start()
 
     def first_turn(t, carry):
         for k in range(1, chips):
@@ -1054,6 +1135,8 @@
     lax.fori_loop(0, chips, first_turn, 0)
     end(0)
     begin(1)
+    gate_gather.hand_on()
+    keep(2, kv_ref, kv_hbm).start()
     early = [step for step in range(chips - 1) if 2 * step + 2 < chips]
 
     def second_turn(t, carry):
@@ -1076,6 +1159,8 @@
         if step + 1 < chips - 1:
             hidden_lines[0].send(step + 1)
     end(1)
+    keep(3, attended_ref, attended_hbm).start()
+    keep(4, middle_ref, middle_hbm).start()
     for h in range(QUERY_HEADS):
         lse_ref[h] = top[h].T[:1, :]
     for step in late[1:]:
@@ -1095,6 +1180,16 @@
     grad_line.finish(chips - 2)
     for index in range(2):
         own(index).wait()
+    for k, (src, dst) in enumerate(
+        (
+            (q_ref, q_hbm),
+            (normed_ref, normed_hbm),
+            (kv_ref, kv_hbm),
+            (attended_ref, attended_hbm),
+            (middle_ref, middle_hbm),
+        )
+    ):
+        keep(k, src, dst).wait()
 
 
 def front(
@@ -1123,15 +1218,19 @@
     vmem = pl.BlockSpec(memory_space=pltpu.VMEM)
     anywhere = pl.BlockSpec(memory_space=pl.ANY)
     shapes = [
+        ((2, chips, expert_count, rows), F32),
+        ((QUERY_HEADS, 1, rows), F32),
+        ((rows, LANES), F32),
+        ((2, chips, expert_count, rows), F32),
+    ]
+    kept = [
         ((rows, width), BF16),
         ((rows, width), BF16),
         ((2, chips, rows, 2 * kv_width), BF16),
-        ((2, chips, expert_count, rows), F32),
         ((rows, width), BF16),
-        ((QUERY_HEADS, 1, rows), F32),
         ((rows, width), F32),
-        ((rows, LANES), F32),
-        ((2, chips, expert_count, rows), F32),
+    ]
+    gathered = [
         ((2, chips, rows, width), BF16),
         ((w_gate.shape[0], width, w_gate.shape[2]), BF16),
         (grad_all.shape, BF16),
@@ -1139,10 +1238,13 @@
     flops = 4 * rows * (2 * chips * rows) * width + 2 * rows * width * (2 * width + 2 * kv_width)
     return pl.pallas_call(
         functools.partial(front_kernel, HEAD_SIZE ** (-0.5), chips, fsdp, expert_count),
-        out_shape=[jax.ShapeDtypeStruct(shape, kind) for shape, kind in shapes],
+        out_shape=[
+            jax.ShapeDtypeStruct(shape, kind) for shape, kind in shapes + kept + gathered
+        ],
         in_specs=[vmem] * 11 + [anywhere] * 4,
-        out_specs=[vmem] * 9 + [anywhere] * 3,
-        scratch_shapes=[
+        out_specs=[vmem] * 4 + [anywhere] * 8,
+        scratch_shapes=[pltpu.VMEM(shape, kind) for shape, kind in kept]
+        + [
             pltpu.VMEM(qkv.shape, BF16),
             pltpu.VMEM(w_out.shape, BF16),
             pltpu.VMEM(w_gate.shape, BF16),
@@ -1154,9 +1256,9 @@
             pltpu.SemaphoreType.DMA((2,)),
             pltpu.SemaphoreType.DMA((2,)),
             pltpu.SemaphoreType.DMA,
-            pltpu.SemaphoreType.DMA((fsdp - 1,)),
-            pltpu.SemaphoreType.DMA((fsdp - 1,)),
         ]
+        + spread_sems(fsdp)
+        + [pltpu.SemaphoreType.DMA((5,))]
         + line_scratch([None] * 2, chips)
         + line_scratch([None], chips)
         + line_scratch([None], chips)
@@ -1340,7 +1442,8 @@
 
         def fill(t, carry):
             tile = pl.ds(pl.multiple_of(t * KEY_TILE, KEY_TILE), KEY_TILE)
-            gap = oq_ref[...] - ok_ref[tile, :]
+            key_order = jnp.broadcast_to(ok_ref[:, tile], (8, KEY_TILE)).T[:, :1]
+            gap = oq_ref[...] - key_order
             bias[tile, :] = jnp.where((gap >= 0) & (gap <= pq_ref[...]), 0.0, MASKED)
             return carry
 
@@ -1383,7 +1486,10 @@
         @pl.when(head == h)
         def _():
             if h == 0:
-                for j in range(chips):
+                for j in range(min(2, chips)):
+                    join(j)
+            if h == 1:
+                for j in range(2, chips):
                     join(j)
             if early_dense and h == 1:
                 for copy in dense_loads:
@@ -1392,7 +1498,7 @@
             if early_dense and h in at_head:
                 stages[at_head[h]]()
             for s in range(chips - 2):
-                if h == s * stride:
+                if h == (s * stride if s == 0 else max(1, s * stride)):
                     line.step(s)
             if h % per_group == per_group - 1:
                 kv_start(h // per_group)
@@ -1493,7 +1599,7 @@
             pl.BlockSpec((1, 1, rows), lambda h: (h, 0, 0)),
             pl.BlockSpec((1, rows), lambda h: (0, 0)),
             pl.BlockSpec((1, rows), lambda h: (0, 0)),
-            pl.BlockSpec((keys, 1), lambda h: (0, 0)),
+            pl.BlockSpec((1, keys), lambda h: (0, 0)),
             pl.BlockSpec((rows, HEAD_SIZE), lambda h: (0, 0)),
             pl.BlockSpec((rows, HEAD_SIZE), lambda h: (0, 0)),
             anywhere,
@@ -1555,7 +1661,7 @@
         lse,
         order_mine[None, :],
         pos_mine[None, :],
-        order_keys[:, None],
+        order_keys[None, :],
         cosine,
         sine,
         mine,
@@ -1983,7 +2089,9 @@
             jax.ShapeDtypeStruct(
                 ((fsdp,) if per > 1 else ()) + (local_experts, shard, units), BF16
             ),
-            jax.ShapeDtypeStruct((fsdp - 1, local_experts, shard, units), BF16),
+            jax.ShapeDtypeStruct(
+                (fsdp - 1 if per == 1 else 1, local_experts, shard, units), BF16
+            ),
             jax.ShapeDtypeStruct((fsdp, local_experts, shard, units), BF16),
             jax.ShapeDtypeStruct((fsdp, local_experts, units, shard), BF16),
         ]
@@ -2115,15 +2223,15 @@
 
     inputs = tokens[0].astype(F32)
     (
+        table_all,
+        lse,
+        gate_weights,
+        weights_all,
         queries,
         hidden_one,
         kv_all,
-        table_all,
         attended,
-        lse,
         middle,
-        gate_weights,
-        weights_all,
         hidden_all,
         gate_full,
         grad_all,

time: 644 us -> 623 us (0.967)
  Pallas kernels: 541 us -> 530 us
  local copies, waits for them, and re-layouts: 22.6 us -> 13.7 us
    unnamed x62 -> x54, local copies, waits for them, and re-layouts: 17.1 us -> 10.2 us
  transfers between devices with their start and end apart: 4 -> 4, of which waited for: 0 -> 0; matrix products, arithmetic and copies ran while one was open for 10% -> 10% of each run, Pallas kernels for 55% -> 56%
where the time goes in v8:
time: 623 us; the launch traced here: 620 us
  Pallas kernels  530 us (85%)
  other arithmetic  33.3 us (5%)
  matrix products  27.5 us (4%)
  between operations  14.5 us (2%)
  local copies, waits for them, and re-layouts  13.7 us (2%)
    pallas_call x1, Pallas kernels, front(): pl.pallas_call(functools.partial(front_kernel, HEAD_SIZE ** (-0.5), chips...  145 us
    pallas_call x1, Pallas kernels, experts_pass(): pl.pallas_call(functools.partial(experts_kernel, capacity, local_experts,...  120 us
    pallas_call x1, Pallas kernels, attention_back(): pl.pallas_call(functools.partial(attention_back_kernel, HEAD_SIZE ** (-0....  119 us
    pallas_call x1, Pallas kernels, dense_reduce(): pl.pallas_call(functools.partial(dense_reduce_kernel, fsdp, chips, tuple(...  81.7 us
    pallas_call x1, Pallas kernels, gather(): pl.pallas_call(functools.partial(gather_kernel, len(dense), len(line), le...  64.1 us
  transfers between devices with their start and end apart: 4, of which 0 were waited for; matrix products, arithmetic and copies ran while one was open for 10% of the time, Pallas kernels for 56%

profile of v8, /device:TPU:0, one launch (start us, length us, event | category | flops | bytes accessed | tf_op | source)
XLA Modules:
  0.0 619.5 jit_solution(9395642118974740013)
XLA Ops:
  7.2 0.8 broadcast_in_dim.38
  8.0 0.8 broadcast_in_dim.39
  8.8 0.8 copy.76
  9.7 0.1 pad.28.clone
  9.7 2.9 pad_maximum_fusion.refs_0_
  12.6 0.8 maximum_maximum_fusion.refs_1_
  13.4 64.1 %gather.1 = (bf16[1536,2048]{1,0:T(8,128)(2,1)}, bf16[1536,128]{1,0:T(8,128)(2,1)}, bf16[1536,1536]{1,0:T(8,128)(2,1)}, bf16[2,4,384,1536]{3,2,1,0:T(8,128)(2,1)}) custom-call(bf16[384,2048]{1,0:T(8,128)(2,1)} %pad_maximum_fusion.refs_0_, bf16[384,128]{1,0:T(8,128)(2,1)} %maximum_maximum_fusion.refs_1_, bf16[384,1536]{1,0:T(8,128)(2,1)} %refs_2_.1, ...), custom_call_target="tpu_custom_call" | custom-call | tf_op jit(solution)/shard_map/gather/pallas_call | solution.py:449
  77.5 0.0 all-gather.5.cloned.1.call-start
  77.5 0.7 all-gather.5.cloned.1.call-update
  78.3 0.5 broadcast.125
  78.8 0.7 reduce.14
  79.6 0.2 reduce-window.8
  79.9 0.1 select_reduce_fusion
  80.0 0.1 copy.83.pq_ref
  80.1 0.2 copy.82.oq_ref
  80.3 0.5 convert_reduce_fusion
  80.9 0.1 copy.81
  81.1 0.8 fusion.26
  81.8 0.2 pad_maximum_fusion.1
  82.0 0.3 fusion.12.table_ref
  82.3 144.8 %front.1 = (f32[2,4,16,384]{3,2,1,0:T(8,128)S(1)}, f32[12,1,384]{2,1,0:T(1,128)S(1)}, f32[384,128]{1,0:T(8,128)S(1)}, f32[2,4,16,384]{3,2,1,0:T(8,128)S(1)}, bf1...) custom-call(bf16[384,1536]{1,0:T(8,128)(2,1)} %bitcast.68, ...), custom_call_target="tpu_custom_call", output_to_operand_aliasing={{11}: (14, {})} | custom-call | flops 11475615744 | bytes 40000000 | tf_op jit(solution)/shard_map/front/pallas_call | solution.py:1239
  227.2 1.0 copy-done.3
  228.2 0.7 copy-done.4
  228.9 0.7 copy-done.5
  229.6 0.6 copy-done.6
  230.2 120.4 %experts.1 = (bf16[384,1664]{1,0:T(8,128)(2,1)}, bf16[4,384,1536]{2,1,0:T(8,128)(2,1)}, bf16[4,384,1536]{2,1,0:T(8,128)(2,1)}, bf16[2,384,768]{2,1,0:T(8,128)(2,...) custom-call(bf16[2,4,384,1536]{3,2,1,0:T(8,128)(2,1)} %get-tuple-ele, ...), custom_call_target="tpu_custom_call" | custom-call | flops 48318382080 | bytes 100000000 | tf_op jit(solution)/shard_map/experts/pallas_call | solution.py:2081
  350.7 0.0 reduce-scatter.7.cloned.1.call-start
  350.7 0.6 broadcast_in_dim_reshape.3.ok_ref
  351.3 1.7 fusion.3
  353.0 0.2 multiply_reduce_fusion.2
  353.2 0.6 reshape_subtract_fusion.pq_ref
  353.8 0.2 convert_element_type.174
  354.0 0.2 multiply_reduce_fusion.3
  354.2 0.2 multiply_convert_fusion
  354.4 2.3 multiply_reduce_fusion
  356.7 2.7 fusion
  359.5 4.6 convolution_convert_fusion.1
  364.1 3.0 convolution_convert_fusion.2.do_ref
  367.1 118.6 %attention_back.1 = (bf16[384,1536]{1,0:T(8,128)(2,1)}, bf16[384,512]{1,0:T(8,128)(2,1)}, bf16[384,1536]{1,0:T(8,128)(2,1)}, bf16[384,1536]{1,0:T(8,128)(2,1)}, ...) custom-call(bf16[384,1536]{1,0:T(8,128)(2,1)} %copy-done.3, bf16[3072,512]{1,0:T(8,128)(2,1)} %bitcast.82, ...), custom_call_target="tpu_custom_call" | custom-call | flops 18119393280 | bytes 12189696 | tf_op jit(solution)/shard_map/attention_back/pallas_call | solution.py:1582
  485.8 1.5 constant_dynamic-update-slice_fusion.1
  487.3 1.1 copy-done.16
  488.5 1.6 convolution_convert_fusion.3
  490.1 0.2 copy.84
  490.3 0.3 reshape.203
  490.6 7.8 %fusion.6 = (f32[384]{0:T(512)S(1)}, bf16[1536]{0:T(1024)(128)(2,1)S(1)}, f32[384,1536]{1,0:T(8,128)}) fusion(f32[1536]{0:T(1024)S(1)} %get-tuple-element.155, bf16[1,384,1536]{2,1,0:T(8,128)(2,1)} %param.15, f32[384]{0:T(512)S(1)} %fusion.31, bf16[384,2048]{1,0:T(8,128)(2,1)} %copy-done.16, bf16[1536,2048]{1,0:T(8,128)(2,1)} %get-tuple-element.53.qkv_ref), kind=kOutput, calls=%fused_computation.16 | convolution fusion | flops 2420045824 | bytes 11415552 | tf_op jit(solution)/shard_map/tc,dc->td/dot_general | solution.py:2329
  498.5 0.7 pad_maximum_fusion.3.refs_1_
  499.2 7.9 %convolution_convert_fusion = bf16[1536,2048]{1,0:T(8,128)(2,1)} fusion(bf16[384,1536]{1,0:T(8,128)(2,1)} %get-tuple-element.57, bf16[384,2048]{1,0:T(8,128)(2,1)} %copy-done.16), kind=kOutput, calls=%fused_computation | convolution fusion | flops 2419064832 | bytes 9043968 | tf_op jit(solution)/shard_map/td,tc->dc/dot_general | solution.py:2328
  507.1 81.7 %dense_reduce.1 = (bf16[2,192,2048]{2,1,0:T(8,128)(2,1)}, bf16[2,16,512]{2,1,0:T(8,128)(2,1)}, f32[384,1536]{1,0:T(8,128)}) custom-call(bf16[4,2,192,2048]{3,2,1,0:T(8,128)(2,1)} %bitcast.66, bf16[4,2,16,512]{3,2,1,0:T(8,128)(2,1)} %pad_maximum_fusion.3.refs_1_, bf16[384,1536]{1,0:T(8,128)(2,1)} %get-tuple-element.75.refs_2_, ...), custom_call_target="tpu_custom_call" | custom-call | tf_op jit(solution)/shard_map/dense_reduce/pallas_call | solution.py:869
  588.8 0.7 slice_convert_fusion.3
  589.5 0.1 reshape.212
  589.6 0.7 copy.87
  590.3 1.4 convert_reduce_fusion.3
  591.7 2.0 slice_convert_fusion.1
  593.7 4.4 convert_add_fusion
  598.1 1.7 slice_convert_fusion
  599.8 1.8 bitcast_convert_fusion.2
  601.5 0.7 copy-done.12
  602.2 1.4 fusion.7
  603.6 0.7 copy-done.9
  604.3 0.3 copy-done.10
  604.6 0.8 copy-done.11
  605.4 1.7 fusion.8
  607.0 2.8 bitcast_convert_fusion
  609.9 2.8 bitcast_convert_fusion.1
  (75 shorter events, 0.5 us)
Async XLA Ops:
  7.2 223.0 %all-gather.3.cloned.1.call-start = ((), (), s32[]{:S(2)}) async-start(), calls=%async_computation.2 | async-start | bytes 5898240 | tf_op jit(solution)/shard_map/all_gather | solution.py:2192
  13.4 65.5 %copy-start.19 = (s32[1,3072]{1,0:T(1,128)S(1)}, s32[1,3072]{1,0:T(1,128)}, u32[]{:S(2)}) copy-start(s32[1,3072]{1,0:T(1,128)} %param.17) | copy-start | bytes 36868
  13.4 66.3 %copy-start.21 = (s32[1,3]{1,0:T(1,128)S(1)}, s32[1,3]{1,0:T(1,128)}, u32[]{:S(2)}) copy-start(s32[1,3]{1,0:T(1,128)} %param.18) | copy-start | bytes 40
  77.4 2.8 copy-start
  77.5 3.4 copy-start.20
  77.5 152.7 %all-gather.5.cloned.1.call-start = ((), (), s32[]{:S(2)}) async-start(), calls=%async_computation.3 | async-start | bytes 5898240 | tf_op jit(solution)/shard_map/all_gather | solution.py:2193
  78.2 528.8 %reduce-scatter.9.cloned.1.call-start = ((), (), s32[]{:S(2)}) async-start(), calls=%async_computation.5 | async-start | bytes 5898240
  79.8 273.4 %copy-start.18 = (s32[1,384]{1,0:T(1,128)}, s32[1,384]{1,0:T(1,128)S(1)}, u32[]{:S(2)}) copy-start(s32[1,384]{1,0:T(1,128)S(1)} %get-tuple-element.159.oq_ref) | copy-start | bytes 4612
  82.0 145.1 %copy-start.1 = (f32[384,128]{1,0:T(8,128)}, f32[384,128]{1,0:T(8,128)S(1)}, u32[]{:S(2)}) copy-start(f32[384,128]{1,0:T(8,128)S(1)} %get-tuple-element.167.cos_ref) | copy-start | bytes 589828
  82.0 145.1 %copy-start.2 = (f32[384,128]{1,0:T(8,128)}, f32[384,128]{1,0:T(8,128)S(1)}, u32[]{:S(2)}) copy-start(f32[384,128]{1,0:T(8,128)S(1)} %get-tuple-element.168.sin_ref) | copy-start | bytes 589828
  227.2 1.0 copy-start.3
  228.2 0.7 copy-start.4
  228.9 0.7 copy-start.5
  229.6 0.6 copy-start.6
  350.6 2.4 copy-start.7
  350.7 259.2 %reduce-scatter.7.cloned.1.call-start = ((), (), s32[]{:S(2)}) async-start(), calls=%async_computation.4 | async-start | bytes 5898240
  351.3 2.5 copy-start.14
  356.7 2.8 copy-start.22
  356.7 7.4 %slice-start = ((s8[4718592]{0:T(1024)(128)(4,1)}), s8[4194304]{0:T(1024)(128)(4,1)S(1)}, s32[]{:S(2)}) async-start(s8[4718592]{0:T(1024)(128)(4,1)} %bitcast.75), calls=%async_computation.6 | async-start | bytes 8388608
  359.5 4.6 copy-start.8
  359.5 4.6 slice-start.1
  485.8 1.5 copy-start.17
  487.3 1.1 copy-start.16
  593.7 4.4 copy-start.13
  598.1 1.7 copy-start.15
  599.8 2.5 copy-start.12
  602.2 2.1 copy-start.9
  602.2 2.4 copy-start.10
  602.2 3.2 copy-start.11
Sparse Core Ops, SparseCore 0:
  77.6 85.8 all-gather.2
  165.3 55.8 all-gather.4
  350.8 80.4 reduce-scatter.8
  434.2 55.1 reduce-scatter.6

commit v9 on v8

--- a/solution.py
+++ b/solution.py
@@ -24,6 +24,7 @@
 EXPERT_VMEM_BYTES = 119 * 512 * 1024
 BACK_VMEM_BYTES = 61 * 1024 * 1024
 FRONT_VMEM_BYTES = 50 * 1024 * 1024
+DENSE_VMEM_BYTES = 40 * 1024 * 1024
 MESH = pl.DeviceIdType.MESH
 F32 = jnp.float32
 BF16 = jnp.bfloat16
@@ -397,12 +398,17 @@
     )
 
 
-def gather_kernel(dense, line, resumed, steps, fsdp, chips, *refs):
-    count = dense + line + resumed
-    ins, outs, scratch = refs[:count], refs[count : 2 * count], refs[2 * count :]
+def gather_kernel(dense, line, merged, steps, fsdp, chips, *refs):
+    count = dense + line
+    ins, refs = refs[:count], refs[count:]
+    outs, scratch = list(refs[: count - merged + 1]), refs[count - merged + 1 :]
+    columns, start = [], 0
+    for ref in ins[:merged]:
+        columns.append(outs[0].at[:, pl.ds(start, ref.shape[1])])
+        start += ref.shape[1]
+    outs = columns + outs[1:]
     ctx, me, chip, core, sibling = place()
     greet(chips, peers_of(me, fsdp) if dense else [], line > 0)
-    split = dense + line
     if dense:
         own, scratch = scratch[: 5 * dense + 3], scratch[5 * dense + 3 :]
         first = DenseGather(
@@ -414,7 +420,7 @@
         first.start()
     if line:
         own, scratch = scratch[: line + 7], scratch[line + 7 :]
-        second = LineGather(ins[dense:split], outs[dense:split], own, chips)
+        second = LineGather(ins[dense:], outs[dense:], own, chips)
         for step in range(steps):
             second.send(step)
             if step == 0:
@@ -424,39 +430,26 @@
             second.receive(step)
             if step == 0:
                 second.turn_own()
-    if resumed:
-        third = LineGather([None], outs[split:], scratch, chips)
-        third.send(chips - 2)
-        third.receive(chips - 2)
     if dense:
         first.finish()
     if line:
         second.finish_own()
         for step in range(steps):
             second.finish(step)
-    if resumed:
-        third.finish(chips - 2)
-
-
-def gather(dense, line, steps, fsdp, chips, collective_id, resumed=()):
-    arrays = list(dense) + list(line) + list(resumed)
-    count = len(arrays)
-    scratch = (dense_scratch(dense, fsdp) if dense else []) + (
-        line_scratch(line, chips) if line else []
-    )
-    if resumed:
-        scratch = scratch + line_scratch([None], chips)
+
+
+def gather(dense, merged, line, steps, fsdp, chips, collective_id):
+    arrays = list(dense) + list(line)
+    joined = sum(a.shape[1] for a in dense[:merged])
+    shapes = [(fsdp * dense[0].shape[0], joined)]
+    shapes += [(fsdp * a.shape[0],) + a.shape[1:] for a in dense[merged:]]
+    shapes += [(2, chips) + a.shape for a in line]
     return pl.pallas_call(
-        functools.partial(
-            gather_kernel, len(dense), len(line), len(resumed), steps, fsdp, chips
-        ),
-        out_shape=[jax.ShapeDtypeStruct((fsdp * a.shape[0],) + a.shape[1:], a.dtype) for a in dense]
-        + [jax.ShapeDtypeStruct((2, chips) + a.shape, a.dtype) for a in line]
-        + [jax.ShapeDtypeStruct(a.shape, a.dtype) for a in resumed],
-        in_specs=[pl.BlockSpec(memory_space=pl.ANY)] * count,
-        out_specs=[pl.BlockSpec(memory_space=pl.ANY)] * count,
-        scratch_shapes=scratch,
-        input_output_aliases={count - 1: count - 1} if resumed else {},
+        functools.partial(gather_kernel, len(dense), len(line), merged, steps, fsdp, chips),
+        out_shape=[jax.ShapeDtypeStruct(shape, BF16) for shape in shapes],
+        in_specs=[pl.BlockSpec(memory_space=pl.ANY)] * len(arrays),
+        out_specs=[pl.BlockSpec(memory_space=pl.ANY)] * len(shapes),
+        scratch_shapes=dense_scratch(dense, fsdp) + line_scratch(line, chips),
         compiler_params=pltpu.CompilerParams(
             collective_id=collective_id, has_side_effects=True, vmem_limit_bytes=VMEM_BYTES
         ),
@@ -760,10 +753,18 @@
     count = len(cuts)
     arrays = max(cut[0] for cut in cuts) + 1
     ins, refs = refs[:arrays], refs[arrays:]
-    own_ref, right_ref, left_ref = refs[:3]
-    outs, total_ref, refs = refs[3 : 3 + arrays], refs[3 + arrays], refs[4 + arrays :]
-    from_left, from_right, r_send, r_recv, l_send, l_recv = refs[:6]
-    rest = refs[6:]
+    own_ref, right_ref, left_ref, pre_ref, tokens_ref, middle_ref, gain_ref, qkv_ref = refs[:8]
+    refs = refs[8:]
+    outs, total_ref, input_ref, refs = (
+        refs[:arrays],
+        refs[arrays],
+        refs[arrays + 1],
+        refs[arrays + 2 :],
+    )
+    from_left, from_right, r_send, r_recv, l_send, l_recv, small_v, qkv_v, qkv_sem = refs[:9]
+    rest = refs[9:]
+    qkv_load = pltpu.make_async_copy(qkv_ref, qkv_v, qkv_sem)
+    qkv_load.start()
     ctx, me, chip, core, sibling = place()
     greet(chips, peers_of(me, fsdp), True)
 
@@ -782,7 +783,7 @@
     for i, (which, start, size) in enumerate(cuts):
         buffers = rest[i * DENSE_BUFFERS : (i + 1) * DENSE_BUFFERS]
         sems = rest[count * DENSE_BUFFERS + i * DENSE_SEMS :][:DENSE_SEMS]
-        local = ins[which].at[:, :, :, pl.ds(start, size)]
+        local = (small_v if which == 1 else ins[which]).at[:, :, :, pl.ds(start, size)]
         sums.append(
             DenseSum(
                 local,
@@ -794,16 +795,47 @@
                 chips,
             )
         )
-    for one in sums:
+    large = [one for one, cut in zip(sums, cuts) if cut[0] != 1]
+    small = [one for one, cut in zip(sums, cuts) if cut[0] == 1]
+    for one in large:
         one.start()
-    for one in sums:
+    for one in large:
         one.cross_over()
+
+    rows, width = tokens_ref.shape
+    qkv_load.wait()
+    gain_grad = jnp.zeros((1, width), F32)
+    for part in (pl.ds(0, rows // 2), pl.ds(rows // 2, rows // 2)):
+        grad = dot(pre_ref[part, :], qkv_v[...], NT)
+        value = tokens_ref[part, :].astype(F32)
+        scale = lax.rsqrt(jnp.mean(value * value, axis=-1, keepdims=True) + EPSILON)
+        unit = value * scale
+        scaled = grad * gain_ref[...]
+        slope = jnp.mean(scaled * unit, axis=-1, keepdims=True)
+        input_ref[part, :] = (middle_ref[part, :] + scale * (scaled - unit * slope)).astype(BF16)
+        gain_grad = gain_grad + jnp.sum(grad * unit, axis=0, keepdims=True)
+    small_v[...] = ins[1][...]
+    shard = width // fsdp
+    first_row = lax.broadcasted_iota(jnp.int32, (small_v.shape[2], shard), 0) == 0
+    for f in range(fsdp):
+        held = small_v[f, 1, :, :shard].astype(F32)
+        mine = jnp.broadcast_to(gain_grad[:, f * shard : (f + 1) * shard], held.shape)
+        small_v[f, 1, :, :shard] = jnp.where(first_row, mine, held).astype(BF16)
+    for one in small:
+        one.start()
+    for one in small:
+        one.cross_over()
+
     stages = [one.stages() for one in sums]
     lag = chips - 1
-    for tick in range(len(stages[0]) + lag * (count - 1)):
+    offsets = []
+    for which, start, size in cuts:
+        turn = sum(1 for other in cuts[: len(offsets)] if other[0] != 1)
+        offsets.append(lag * (max(0, turn - 1) if which == 1 else turn))
+    for tick in range(len(stages[0]) + max(offsets)):
         for i in range(count):
-            if 0 <= tick - lag * i < len(stages[i]):
-                stages[i][tick - lag * i]()
+            if 0 <= tick - offsets[i] < len(stages[i]):
+                stages[i][tick - offsets[i]]()
     @pl.when(chip >= 1)
     def _():
         to_right.wait_recv()
@@ -856,7 +888,21 @@
     )
 
 
-def dense_reduce(arrays, own, right, left, piece, fsdp, chips, collective_id):
+def dense_reduce(
+    arrays,
+    own,
+    right,
+    left,
+    pre_grad,
+    tokens,
+    middle_grad,
+    gain,
+    qkv,
+    piece,
+    fsdp,
+    chips,
+    collective_id,
+):
     vmem = pl.BlockSpec(memory_space=pltpu.VMEM)
     cuts, buffers = [], []
     for i, a in enumerate(arrays):
@@ -866,22 +912,28 @@
             cuts.append((i, start, size))
             buffers += dense_buffers(rows, size, fsdp, chips)
     sems = dense_sems(fsdp, chips)
+    anywhere = pl.BlockSpec(memory_space=pl.ANY)
     return pl.pallas_call(
         functools.partial(dense_reduce_kernel, fsdp, chips, tuple(cuts)),
         out_shape=[jax.ShapeDtypeStruct(a.shape[1:], BF16) for a in arrays]
-        + [jax.ShapeDtypeStruct(own.shape, F32)],
-        in_specs=[vmem] * len(arrays) + [vmem, pl.BlockSpec(memory_space=pl.ANY)]
-        + [pl.BlockSpec(memory_space=pl.ANY)],
-        out_specs=[vmem] * (len(arrays) + 1),
+        + [jax.ShapeDtypeStruct(own.shape, F32), jax.ShapeDtypeStruct(tokens.shape, BF16)],
+        in_specs=[vmem] * len(arrays)
+        + [vmem, anywhere, anywhere, vmem, vmem, vmem, vmem, anywhere],
+        out_specs=[vmem] * (len(arrays) + 2),
         scratch_shapes=[pltpu.VMEM(own.shape, BF16)] * 2
         + [pltpu.SemaphoreType.DMA] * 4
+        + [
+            pltpu.VMEM(arrays[1].shape, BF16),
+            pltpu.VMEM(qkv.shape, BF16),
+            pltpu.SemaphoreType.DMA,
+        ]
         + buffers
         + sems * len(cuts),
         compiler_params=pltpu.CompilerParams(
-            collective_id=collective_id, has_side_effects=True, vmem_limit_bytes=VMEM_BYTES
+            collective_id=collective_id, has_side_effects=True, vmem_limit_bytes=DENSE_VMEM_BYTES
         ),
         name="dense_reduce",
-    )(*arrays, own, right, left)
+    )(*arrays, own, right, left, pre_grad, tokens, middle_grad, gain[None, :], qkv)
 
 
 def after(value, *others):
@@ -931,6 +983,7 @@
     kv_hbm,
     attended_hbm,
     middle_hbm,
+    hidden_hbm,
     hidden_all_ref,
     gate_full_ref,
     grad_ref,
@@ -1161,6 +1214,7 @@
     end(1)
     keep(3, attended_ref, attended_hbm).start()
     keep(4, middle_ref, middle_hbm).start()
+    keep(5, hidden_v, hidden_hbm).start()
     for h in range(QUERY_HEADS):
         lse_ref[h] = top[h].T[:1, :]
     for step in late[1:]:
@@ -1187,6 +1241,7 @@
             (kv_ref, kv_hbm),
             (attended_ref, attended_hbm),
             (middle_ref, middle_hbm),
+            (hidden_v, hidden_hbm),
         )
     ):
         keep(k, src, dst).wait()
@@ -1231,6 +1286,7 @@
         ((rows, width), F32),
     ]
     gathered = [
+        ((rows, width), BF16),
         ((2, chips, rows, width), BF16),
         ((w_gate.shape[0], width, w_gate.shape[2]), BF16),
         (grad_all.shape, BF16),
@@ -1242,7 +1298,7 @@
             jax.ShapeDtypeStruct(shape, kind) for shape, kind in shapes + kept + gathered
         ],
         in_specs=[vmem] * 11 + [anywhere] * 4,
-        out_specs=[vmem] * 4 + [anywhere] * 8,
+        out_specs=[vmem] * 4 + [anywhere] * 9,
         scratch_shapes=[pltpu.VMEM(shape, kind) for shape, kind in kept]
         + [
             pltpu.VMEM(qkv.shape, BF16),
@@ -1258,12 +1314,12 @@
             pltpu.SemaphoreType.DMA,
         ]
         + spread_sems(fsdp)
-        + [pltpu.SemaphoreType.DMA((5,))]
+        + [pltpu.SemaphoreType.DMA((6,))]
         + line_scratch([None] * 2, chips)
         + line_scratch([None], chips)
         + line_scratch([None], chips)
         + line_scratch([None] * 2, chips),
-        input_output_aliases={14: 11},
+        input_output_aliases={14: 12},
         compiler_params=pltpu.CompilerParams(
             collective_id=collective_id, has_side_effects=True, vmem_limit_bytes=FRONT_VMEM_BYTES
         ),
@@ -1306,8 +1362,7 @@
     ok_ref,
     cos_ref,
     sin_ref,
-    mine_ref,
-    other_ref,
+    rows_ref,
     dense_ref,
     dq_ref,
     kv_ref,
@@ -1355,12 +1410,12 @@
                 order.append(r)
     order.append(0)
     swaps = [
-        remote(other_ref.at[r], pair.at[r], swap_send.at[r], swap_recv.at[r], (sibling, me))
+        remote(rows_ref.at[1, r], pair.at[r], swap_send.at[r], swap_recv.at[r], (sibling, me))
         for r in range(chips)
     ]
     slots = mine_v.shape[0]
     loads = [
-        pltpu.make_async_copy(mine_ref.at[r], mine_v.at[j % slots], load_sem.at[j % slots])
+        pltpu.make_async_copy(rows_ref.at[0, r], mine_v.at[j % slots], load_sem.at[j % slots])
         for j, r in enumerate(order)
     ]
     line = LineSum(
@@ -1566,8 +1621,7 @@
     order_keys,
     cosine,
     sine,
-    mine,
-    other,
+    out_rows,
     dense,
     fsdp,
     early_dense,
@@ -1575,7 +1629,7 @@
 ):
     rows = queries.shape[0]
     keys = kv.shape[0]
-    chips, unused, width = mine.shape
+    unused, chips, unused, width = out_rows.shape
     per_group = QUERY_HEADS // KVH
     head_rows = pl.BlockSpec((rows, HEAD_SIZE), lambda h: (0, h))
     anywhere = pl.BlockSpec(memory_space=pl.ANY)
@@ -1589,7 +1643,7 @@
             jax.ShapeDtypeStruct((rows, 2 * KVH * HEAD_SIZE), BF16),
         ]
         + [jax.ShapeDtypeStruct((rows, width), BF16)] * 3
-        + [jax.ShapeDtypeStruct(dense.shape[1:], BF16)],
+        + [jax.ShapeDtypeStruct(dense.shape[1:] if early_dense else (16, LANES), BF16)],
         in_specs=[
             head_rows,
             pl.BlockSpec((keys, HEAD_SIZE), lambda h: (0, h // per_group)),
@@ -1602,7 +1656,6 @@
             pl.BlockSpec((1, keys), lambda h: (0, 0)),
             pl.BlockSpec((rows, HEAD_SIZE), lambda h: (0, 0)),
             pl.BlockSpec((rows, HEAD_SIZE), lambda h: (0, 0)),
-            anywhere,
             anywhere,
             anywhere,
         ],
@@ -1664,8 +1717,7 @@
         order_keys[None, :],
         cosine,
         sine,
-        mine,
-        other,
+        out_rows,
         dense,
     )
 
@@ -1685,8 +1737,7 @@
     up_ref,
     down_ref,
     returned_ref,
-    out_mine_ref,
-    out_other_ref,
+    out_ref,
     gate_grad_ref,
     gate_got_ref,
     up_grad_ref,
@@ -1764,8 +1815,7 @@
     def out_copies(i):
         r = chunk_order(chip, i, chips)
         return [
-            pltpu.make_async_copy(out_v.at[0], out_mine_ref.at[r], out_sem.at[0]),
-            pltpu.make_async_copy(out_v.at[1], out_other_ref.at[r], out_sem.at[1]),
+            pltpu.make_async_copy(out_v.at[q], out_ref.at[q, r], out_sem.at[q]) for q in range(2)
         ]
 
     def swap(i):
@@ -2084,20 +2134,20 @@
         ),
         out_shape=[
             jax.ShapeDtypeStruct((tokens, wide), BF16),
-            jax.ShapeDtypeStruct((chips, tokens, width), BF16),
-            jax.ShapeDtypeStruct((chips, tokens, width), BF16),
+            jax.ShapeDtypeStruct(hidden.shape, BF16),
             jax.ShapeDtypeStruct(
                 ((fsdp,) if per > 1 else ()) + (local_experts, shard, units), BF16
             ),
             jax.ShapeDtypeStruct(
-                (fsdp - 1 if per == 1 else 1, local_experts, shard, units), BF16
+                (fsdp - 1, local_experts, shard, units) if per == 1 else (1, 1, 16, LANES), BF16
             ),
             jax.ShapeDtypeStruct((fsdp, local_experts, shard, units), BF16),
             jax.ShapeDtypeStruct((fsdp, local_experts, units, shard), BF16),
         ]
         + [jax.ShapeDtypeStruct(shape, BF16) for shape in saved],
         in_specs=[anywhere, anywhere, vmem, vmem, anywhere, anywhere, anywhere],
-        out_specs=[vmem] + [anywhere] * 11,
+        out_specs=[vmem] + [anywhere] * 10,
+        input_output_aliases={0: 1},
         scratch_shapes=[
             pltpu.VMEM((local_experts * width, units), BF16),
             pltpu.VMEM((local_experts * width, units), BF16),
@@ -2139,7 +2189,7 @@
         up.reshape(local_experts * width, units),
         down.reshape(local_experts * units, width),
     )
-    return outs[:7]
+    return outs[:6]
 
 
 def body(
@@ -2182,9 +2232,8 @@
         ],
         axis=1,
     )
-    qkv_shard = jnp.concatenate([w_query, w_key, w_value], axis=1)
     qkv_full, small_full, out_full, grad_all = gather(
-        [qkv_shard, small, w_out], [grad_out[0]], chips - 2, fsdp, chips, 0
+        [w_query, w_key, w_value, small, w_out], 3, [grad_out[0]], chips - 2, fsdp, chips, 0
     )
 
     qkv_full, w_up, w_down = lax.optimization_barrier((qkv_full, w_up, w_down))
@@ -2232,6 +2281,7 @@
         kv_all,
         attended,
         middle,
+        hidden_two,
         hidden_all,
         gate_full,
         grad_all,
@@ -2257,9 +2307,8 @@
     )
     kv_all = kv_all.reshape(-1, 2 * kv_width)
     gate_weights = gate_weights[:, :expert_count]
-    hidden_two = hidden_all[0, 0]
-
-    returned, out_mine, out_other, gate_local, gate_got, up_local, down_local = experts_pass(
+
+    returned, out_rows, gate_local, gate_got, up_local, down_local = experts_pass(
         hidden_all,
         grad_all,
         table_all,
@@ -2317,20 +2366,14 @@
         order_keys,
         cosine,
         sine,
-        out_mine,
-        out_other,
-        halves(out_local),
+        out_rows,
+        halves(out_local) if early_dense else out_local[:16, :LANES].astype(BF16),
         fsdp,
         early_dense,
         3,
     )
     pre_grad = jnp.concatenate([query_grad, kv_grad], axis=1)
     qkv_local = jnp.einsum("td,tc->dc", hidden_one, pre_grad, preferred_element_type=F32)
-    hidden_one_grad = jnp.einsum("tc,dc->td", pre_grad, qkv_full, preferred_element_type=F32)
-    unused_one, norm_one_back = jax.vjp(rms_scale, inputs, gain_a)
-    input_part, gain_one_local = norm_one_back(hidden_one_grad)
-    input_grad = (middle_grad + input_part).astype(BF16)
-
     span = shard * expert_count // 16
     wide = LANES * chips * -(-max(span, shard) // (LANES * chips))
     small_local = jnp.stack(
@@ -2340,20 +2383,22 @@
                 ((0, 0), (0, 0), (0, wide - span)),
             ),
             jnp.pad(
-                jnp.stack(
-                    [gain_one_local.reshape(fsdp, shard), gain_two_local.reshape(fsdp, shard)],
-                    axis=1,
-                ).astype(BF16),
-                ((0, 0), (0, 14), (0, wide - shard)),
+                gain_two_local.reshape(fsdp, 1, shard).astype(BF16),
+                ((0, 0), (1, 14), (0, wide - shard)),
             ),
         ],
         axis=1,
     )
-    *sums, out_sum = dense_reduce(
+    *sums, out_sum, input_grad = dense_reduce(
         [halves(qkv_local), small_local] + ([] if early_dense else [halves(out_local)]),
         out_own,
         out_right,
         out_left,
+        pre_grad,
+        tokens[0],
+        middle_grad,
+        gain_a,
+        qkv_full,
         DENSE_PIECE,
         fsdp,
         chips,

time: 623 us -> 600 us (0.963)
  Pallas kernels: 530 us -> 518 us
  matrix products: 27.5 us -> 17.3 us
  other arithmetic: 33.3 us -> 23.7 us
  local copies, waits for them, and re-layouts: 13.7 us -> 20.3 us
    pallas_call x1, Pallas kernels: 81.7 us -> 70.1 us  [dense_reduce(): pl.pallas_call(functools.partial(dense_reduce_kernel, fsdp, chips, tuple(...]
    dot_general x1 -> x0, matrix products: 7.83 us -> none  [body(): jnp.einsum('tc,dc->td', pre_grad, qkv_full, preferred_element_type=F32)]
    unnamed x54 -> x69, local copies, waits for them, and re-layouts: 10.2 us -> 16.1 us
  transfers between devices with their start and end apart: 4 -> 4, of which waited for: 0 -> 0; matrix products, arithmetic and copies ran while one was open for 10% -> 7% of each run, Pallas kernels for 56% -> 56%
where the time goes in v9:
time: 600 us; the launch traced here: 596 us
  Pallas kernels  518 us (86%)
  other arithmetic  23.7 us (4%)
  local copies, waits for them, and re-layouts  20.3 us (3%)
  matrix products  17.3 us (3%)
  between operations  14.5 us (2%)
    pallas_call x1, Pallas kernels, front(): pl.pallas_call(functools.partial(front_kernel, HEAD_SIZE ** (-0.5), chips...  145 us
    pallas_call x1, Pallas kernels, experts_pass(): pl.pallas_call(functools.partial(experts_kernel, capacity, local_experts,...  120 us
    pallas_call x1, Pallas kernels, attention_back(): pl.pallas_call(functools.partial(attention_back_kernel, HEAD_SIZE ** (-0....  119 us
    pallas_call x1, Pallas kernels, dense_reduce(): pl.pallas_call(functools.partial(dense_reduce_kernel, fsdp, chips, tuple(...  70.1 us
    pallas_call x1, Pallas kernels, gather(): pl.pallas_call(functools.partial(gather_kernel, len(dense), len(line), me...  64.4 us
    unnamed x69, local copies, waits for them, and re-layouts  16.1 us
  transfers between devices with their start and end apart: 4, of which 0 were waited for; matrix products, arithmetic and copies ran while one was open for 7% of the time, Pallas kernels for 56%

profile of v9, /device:TPU:0, one launch (start us, length us, event | category | flops | bytes accessed | tf_op | source)
XLA Modules:
  0.0 595.7 jit_solution(9093218910921833232)
XLA Ops:
  7.2 0.8 broadcast_in_dim.35
  8.0 0.8 broadcast_in_dim.36
  8.8 0.8 copy.74
  9.7 0.1 pad.26.clone
  9.7 0.8 maximum_maximum_fusion.refs_3_
  10.5 64.4 %gather.1 = (bf16[1536,2048]{1,0:T(8,128)(2,1)}, bf16[1536,128]{1,0:T(8,128)(2,1)}, bf16[1536,1536]{1,0:T(8,128)(2,1)}, bf16[2,4,384,1536]{3,2,1,0:T(8,128)(2,1)}) custom-call(bf16[384,1536]{1,0:T(8,128)(2,1)} %refs_0_.1, bf16[384,256]{1,0:T(8,128)(2,1)} %refs_1_.1, bf16[384,256]{1,0:T(8,128)(2,1)} %refs_2_.1, bf16[384,128]{1,0:T(8,128)(2,1)} %maximum_maximum_fusion.refs_3_, ...), custom_call_target="tpu_custom_call" | custom-call | tf_op jit(solution)/shard_map/gather/pallas_call | solution.py:447
  75.0 0.0 all-gather.5.cloned.1.call-start
  75.0 0.7 all-gather.5.cloned.1.call-update
  75.8 0.5 broadcast.69
  76.3 0.7 reduce.13
  77.1 0.2 reduce-window.8
  77.3 0.1 select_reduce_fusion
  77.5 0.1 copy.81.pq_ref
  77.6 0.2 copy.80.oq_ref
  77.8 0.5 convert_reduce_fusion
  78.4 0.1 copy.79
  78.6 0.8 fusion.10
  79.3 0.2 pad_maximum_fusion
  79.5 0.3 fusion.3.table_ref
  79.8 144.8 %front.1 = (f32[2,4,16,384]{3,2,1,0:T(8,128)S(1)}, f32[12,1,384]{2,1,0:T(1,128)S(1)}, f32[384,128]{1,0:T(8,128)S(1)}, f32[2,4,16,384]{3,2,1,0:T(8,128)S(1)}, bf1...) custom-call(bf16[384,1536]{1,0:T(8,128)(2,1)} %bitcast.59, ...), custom_call_target="tpu_custom_call", output_to_operand_aliasing={{12}: (14, {})} | custom-call | flops 11475615744 | bytes 40000000 | tf_op jit(solution)/shard_map/front/pallas_call | solution.py:1295
  224.7 1.0 copy-done.13
  225.7 0.7 copy-done.14
  226.4 0.7 copy-done.15
  227.0 0.6 copy-done.16
  227.6 120.4 %experts.1 = (bf16[384,1664]{1,0:T(8,128)(2,1)}, bf16[2,4,384,1536]{3,2,1,0:T(8,128)(2,1)}, bf16[2,384,768]{2,1,0:T(8,128)(2,1)}, bf16[3,2,384,768]{3,2,1,0:T(8,...) custom-call(bf16[2,4,384,1536]{3,2,1,0:T(8,128)(2,1)} %get-tuple-ele, ...), custom_call_target="tpu_custom_call", output_to_operand_aliasing={{1}: (0, {})} | custom-call | flops 48318382080 | bytes 100000000 | tf_op jit(solution)/shard_map/experts/pallas_call | solution.py:2131
  348.1 0.0 reduce-scatter.7.cloned.1.call-start
  348.2 0.5 reduce-scatter.7.cloned.1.call-update
  348.7 1.1 copy-done.17
  349.8 0.2 multiply_reduce_fusion.2
  350.1 0.6 broadcast_in_dim_reshape.3.ok_ref
  350.7 0.6 reshape_subtract_fusion.pq_ref
  351.3 1.5 convert_element_type.175
  352.7 0.2 multiply_reduce_fusion.3
  353.0 0.2 multiply_convert_fusion
  353.2 1.0 multiply_reduce_fusion
  354.1 0.7 copy-done.18
  354.8 0.3 copy-done.20
  355.1 0.6 fusion.refs_7_
  355.7 0.7 copy-done.29
  356.4 4.6 convolution_convert_fusion.1
  361.0 3.1 convolution_convert_fusion.2.do_ref
  364.1 118.7 %attention_back.1 = (bf16[384,1536]{1,0:T(8,128)(2,1)}, bf16[384,512]{1,0:T(8,128)(2,1)}, bf16[384,1536]{1,0:T(8,128)(2,1)}, bf16[384,1536]{1,0:T(8,128)(2,1)}, ...) custom-call(bf16[384,1536]{1,0:T(8,128)(2,1)} %copy-done.13, bf16[3072,512]{1,0:T(8,128)(2,1)} %bitcast.75, ...), custom_call_target="tpu_custom_call" | custom-call | flops 18119393280 | bytes 12189696 | tf_op jit(solution)/shard_map/attention_back/pallas_call | solution.py:1636
  482.8 2.5 constant_dynamic-update-slice_fusion.1
  485.3 0.8 constant_dynamic-update-slice_fusion.refs_5_
  486.1 0.3 convolution_convert_fusion.3
  486.4 0.2 copy.82
  486.7 0.3 reshape.194
  487.1 8.0 %convolution_convert_fusion = bf16[1536,2048]{1,0:T(8,128)(2,1)} fusion(bf16[384,1536]{1,0:T(8,128)(2,1)} %get-tuple-element.58, bf16[384,2048]{1,0:T(8,128)(2,1)} %constant_dynamic-update-slice_fusion.refs_5_), kind=kOutput, calls=%fused_computation | convolution fusion | flops 2419064832 | bytes 9043968 | tf_op jit(solution)/shard_map/td,tc->dc/dot_general | solution.py:2376
  495.1 70.1 %dense_reduce.1 = (bf16[2,192,2048]{2,1,0:T(8,128)(2,1)S(1)}, bf16[2,16,512]{2,1,0:T(8,128)(2,1)S(1)}, f32[384,1536]{1,0:T(8,128)S(1)}, bf16[384,1536]{1,0:T(8,128)(2,1)S(1)}) custom-call(bf16[4,2,192,2048]{3,2,1,0:T(8,128)(2,1)} %bitcast.62, bf16[4,2,16,512]{3,2,1,0:T(8,128)(2,1)S(1)} %pad_maximum_fusion.2.refs_1_, bf16[384,1536]{1,0:T(8,128)(2,1)S(1)} %copy-done.6, ...), custom_call_target="tpu_custom_call" | custom-call | tf_op jit(solution)/shard_map/dense_reduce/pallas_call | solution.py:916
  565.2 1.4 copy-done.1
  566.6 1.1 copy-done.3
  567.8 1.0 copy-done.9
  568.8 0.1 reshape.202
  568.9 0.7 copy.84
  569.6 0.6 convert_reduce_fusion.3
  570.2 2.0 slice_convert_fusion.1
  572.2 4.0 convert_add_fusion
  576.2 1.7 slice_convert_fusion
  577.9 1.8 bitcast_convert_fusion.2
  579.7 1.1 copy-done.2
  580.8 1.3 fusion.1
  582.1 2.8 bitcast_convert_fusion
  584.9 2.9 bitcast_convert_fusion.1
  587.9 1.0 copy.89
  (83 shorter events, 0.5 us)
Async XLA Ops:
  7.2 220.5 %all-gather.3.cloned.1.call-start = ((), (), s32[]{:S(2)}) async-start(), calls=%async_computation.2 | async-start | bytes 5898240 | tf_op jit(solution)/shard_map/all_gather | solution.py:2241
  10.5 65.8 %copy-start.26 = (s32[1,3072]{1,0:T(1,128)S(1)}, s32[1,3072]{1,0:T(1,128)}, u32[]{:S(2)}) copy-start(s32[1,3072]{1,0:T(1,128)} %param.17) | copy-start | bytes 36868
  10.5 66.6 %copy-start.28 = (s32[1,3]{1,0:T(1,128)S(1)}, s32[1,3]{1,0:T(1,128)}, u32[]{:S(2)}) copy-start(s32[1,3]{1,0:T(1,128)} %param.18) | copy-start | bytes 40
  74.9 2.8 copy-start
  74.9 3.4 copy-start.27
  75.0 152.7 %all-gather.5.cloned.1.call-start = ((), (), s32[]{:S(2)}) async-start(), calls=%async_computation.3 | async-start | bytes 5898240 | tf_op jit(solution)/shard_map/all_gather | solution.py:2242
  75.7 506.4 %reduce-scatter.9.cloned.1.call-start = ((), (), s32[]{:S(2)}) async-start(), calls=%async_computation.5 | async-start | bytes 5898240
  77.3 273.4 %copy-start.25 = (s32[1,384]{1,0:T(1,128)}, s32[1,384]{1,0:T(1,128)S(1)}, u32[]{:S(2)}) copy-start(s32[1,384]{1,0:T(1,128)S(1)} %get-tuple-element.159.oq_ref) | copy-start | bytes 4612
  79.5 145.1 %copy-start.11 = (f32[384,128]{1,0:T(8,128)}, f32[384,128]{1,0:T(8,128)S(1)}, u32[]{:S(2)}) copy-start(f32[384,128]{1,0:T(8,128)S(1)} %get-tuple-element.166.cos_ref) | copy-start | bytes 589828
  79.5 145.1 %copy-start.12 = (f32[384,128]{1,0:T(8,128)}, f32[384,128]{1,0:T(8,128)S(1)}, u32[]{:S(2)}) copy-start(f32[384,128]{1,0:T(8,128)S(1)} %get-tuple-element.167.sin_ref) | copy-start | bytes 589828
  224.7 1.0 copy-start.13
  225.7 0.7 copy-start.14
  226.4 0.7 copy-start.15
  227.0 0.6 copy-start.16
  348.1 236.8 %reduce-scatter.7.cloned.1.call-start = ((), (), s32[]{:S(2)}) async-start(), calls=%async_computation.4 | async-start | bytes 5898240
  348.2 1.7 copy-start.17
  353.2 1.7 copy-start.18
  353.2 2.0 copy-start.20
  355.1 1.3 copy-start.29
  355.1 5.9 slice-start
  356.4 4.6 slice-start.1
  482.8 2.5 copy-start.24
  482.8 3.3 copy-start.23
  487.0 8.1 %copy-start.5 = (bf16[1,384,1536]{2,1,0:T(8,128)(2,1)S(1)}, bf16[1,384,1536]{2,1,0:T(8,128)(2,1)}, u32[]{:S(2)}) copy-start(bf16[1,384,1536]{2,1,0:T(8,128)(2,1)} %param.15) | copy-start | bytes 3538948
  487.0 8.1 %copy-start.6 = (bf16[384,1536]{1,0:T(8,128)(2,1)S(1)}, bf16[384,1536]{1,0:T(8,128)(2,1)}, u32[]{:S(2)}) copy-start(bf16[384,1536]{1,0:T(8,128)(2,1)} %get-tuple-element.76.refs_2_) | copy-start | bytes 3538948
  487.0 8.1 %copy-start.7 = (bf16[384,1536]{1,0:T(8,128)(2,1)S(1)}, bf16[384,1536]{1,0:T(8,128)(2,1)}, u32[]{:S(2)}) copy-start(bf16[384,1536]{1,0:T(8,128)(2,1)} %get-tuple-element.77.refs_3_) | copy-start | bytes 3538948
  487.0 8.1 %copy-start.8 = (bf16[384,1536]{1,0:T(8,128)(2,1)S(1)}, bf16[384,1536]{1,0:T(8,128)(2,1)}, u32[]{:S(2)}) copy-start(bf16[384,1536]{1,0:T(8,128)(2,1)} %get-tuple-element.78.refs_4_) | copy-start | bytes 3538948
  565.2 1.4 copy-start.1
  566.6 1.1 copy-start.3
  567.8 1.0 copy-start.9
  568.8 3.4 copy-start.21
  572.2 4.0 copy-start.4
  576.2 1.7 copy-start.22
  576.2 3.5 copy-start.19
  577.9 2.9 copy-start.2
  584.9 2.9 copy-start.10
Sparse Core Ops, SparseCore 0:
  75.1 85.8 all-gather.2
  162.8 55.8 all-gather.4
  348.2 73.1 reduce-scatter.8
  424.3 62.7 reduce-scatter.6

commit v10 on v9

--- a/solution.py
+++ b/solution.py
@@ -24,7 +24,7 @@
 EXPERT_VMEM_BYTES = 119 * 512 * 1024
 BACK_VMEM_BYTES = 61 * 1024 * 1024
 FRONT_VMEM_BYTES = 50 * 1024 * 1024
-DENSE_VMEM_BYTES = 40 * 1024 * 1024
+DENSE_VMEM_BYTES = 50 * 1024 * 1024
 MESH = pl.DeviceIdType.MESH
 F32 = jnp.float32
 BF16 = jnp.bfloat16
@@ -752,19 +752,25 @@
 def dense_reduce_kernel(fsdp, chips, cuts, *refs):
     count = len(cuts)
     arrays = max(cut[0] for cut in cuts) + 1
-    ins, refs = refs[:arrays], refs[arrays:]
-    own_ref, right_ref, left_ref, pre_ref, tokens_ref, middle_ref, gain_ref, qkv_ref = refs[:8]
-    refs = refs[8:]
+    ins, refs = [None] + list(refs[: arrays - 1]), refs[arrays - 1 :]
+    right_ref, left_ref, gain_ref = refs[:3]
+    loaded, refs = refs[3:10], refs[10:]
     outs, total_ref, input_ref, refs = (
         refs[:arrays],
         refs[arrays],
         refs[arrays + 1],
         refs[arrays + 2 :],
     )
-    from_left, from_right, r_send, r_recv, l_send, l_recv, small_v, qkv_v, qkv_sem = refs[:9]
-    rest = refs[9:]
-    qkv_load = pltpu.make_async_copy(qkv_ref, qkv_v, qkv_sem)
-    qkv_load.start()
+    from_left, from_right, r_send, r_recv, l_send, l_recv = refs[:6]
+    small_v, local_v, load_sem = refs[6:9]
+    held, rest = refs[9:16], refs[16:]
+    normed_ref, dq_ref, dkv_ref, qkv_v, tokens_ref, middle_ref, own_ref = held
+    loads = [
+        pltpu.make_async_copy(src, dst, load_sem.at[k])
+        for k, (src, dst) in enumerate(zip(loaded, held))
+    ]
+    for copy in loads:
+        copy.start()
     ctx, me, chip, core, sibling = place()
     greet(chips, peers_of(me, fsdp), True)
 
@@ -783,7 +789,7 @@
     for i, (which, start, size) in enumerate(cuts):
         buffers = rest[i * DENSE_BUFFERS : (i + 1) * DENSE_BUFFERS]
         sems = rest[count * DENSE_BUFFERS + i * DENSE_SEMS :][:DENSE_SEMS]
-        local = (small_v if which == 1 else ins[which]).at[:, :, :, pl.ds(start, size)]
+        local = (local_v, small_v, ins[-1])[which].at[:, :, :, pl.ds(start, size)]
         sums.append(
             DenseSum(
                 local,
@@ -797,16 +803,37 @@
         )
     large = [one for one, cut in zip(sums, cuts) if cut[0] != 1]
     small = [one for one, cut in zip(sums, cuts) if cut[0] == 1]
-    for one in large:
-        one.start()
+    rows, width = tokens_ref.shape
+    shard = width // fsdp
+    per = 1 if shard % LANES == 0 else 2
+    for copy in loads[:3]:
+        copy.wait()
+    for one, (which, start, size) in zip(sums, cuts):
+        if which == 0:
+            for f in range(0, fsdp, per):
+                left = normed_ref[:, f * shard : (f + per) * shard]
+                for begin in range(start, start + size, KEY_TILE):
+                    right = (
+                        dq_ref[:, begin : begin + KEY_TILE]
+                        if begin < width
+                        else dkv_ref[:, begin - width : begin - width + KEY_TILE]
+                    )
+                    value = dot(left, right, TN).astype(BF16)
+                    for k in range(2 * per):
+                        local_v[f + k // 2, k % 2, :, begin : begin + KEY_TILE] = value[
+                            k * shard // 2 : (k + 1) * shard // 2, :
+                        ]
+        if which != 1:
+            one.start()
     for one in large:
         one.cross_over()
 
-    rows, width = tokens_ref.shape
-    qkv_load.wait()
+    for copy in loads[3:]:
+        copy.wait()
     gain_grad = jnp.zeros((1, width), F32)
     for part in (pl.ds(0, rows // 2), pl.ds(rows // 2, rows // 2)):
-        grad = dot(pre_ref[part, :], qkv_v[...], NT)
+        grad = dot(dq_ref[part, :], qkv_v[:, :width], NT)
+        grad = grad + dot(dkv_ref[part, :], qkv_v[:, width:], NT)
         value = tokens_ref[part, :].astype(F32)
         scale = lax.rsqrt(jnp.mean(value * value, axis=-1, keepdims=True) + EPSILON)
         unit = value * scale
@@ -815,7 +842,6 @@
         input_ref[part, :] = (middle_ref[part, :] + scale * (scaled - unit * slope)).astype(BF16)
         gain_grad = gain_grad + jnp.sum(grad * unit, axis=0, keepdims=True)
     small_v[...] = ins[1][...]
-    shard = width // fsdp
     first_row = lax.broadcasted_iota(jnp.int32, (small_v.shape[2], shard), 0) == 0
     for f in range(fsdp):
         held = small_v[f, 1, :, :shard].astype(F32)
@@ -893,7 +919,9 @@
     own,
     right,
     left,
-    pre_grad,
+    query_grad,
+    kv_grad,
+    normed,
     tokens,
     middle_grad,
     gain,
@@ -912,28 +940,37 @@
             cuts.append((i, start, size))
             buffers += dense_buffers(rows, size, fsdp, chips)
     sems = dense_sems(fsdp, chips)
+    loaded = [normed, query_grad, kv_grad, qkv, tokens, middle_grad, own]
     anywhere = pl.BlockSpec(memory_space=pl.ANY)
     return pl.pallas_call(
         functools.partial(dense_reduce_kernel, fsdp, chips, tuple(cuts)),
         out_shape=[jax.ShapeDtypeStruct(a.shape[1:], BF16) for a in arrays]
         + [jax.ShapeDtypeStruct(own.shape, F32), jax.ShapeDtypeStruct(tokens.shape, BF16)],
-        in_specs=[vmem] * len(arrays)
-        + [vmem, anywhere, anywhere, vmem, vmem, vmem, vmem, anywhere],
+        in_specs=[vmem] * (len(arrays) - 1)
+        + [anywhere, anywhere, vmem]
+        + [anywhere] * 7,
         out_specs=[vmem] * (len(arrays) + 2),
         scratch_shapes=[pltpu.VMEM(own.shape, BF16)] * 2
         + [pltpu.SemaphoreType.DMA] * 4
         + [
             pltpu.VMEM(arrays[1].shape, BF16),
-            pltpu.VMEM(qkv.shape, BF16),
-            pltpu.SemaphoreType.DMA,
+            pltpu.VMEM(arrays[0].shape, BF16),
+            pltpu.SemaphoreType.DMA((len(loaded),)),
         ]
+        + [pltpu.VMEM(a.shape, a.dtype) for a in loaded]
         + buffers
         + sems * len(cuts),
         compiler_params=pltpu.CompilerParams(
             collective_id=collective_id, has_side_effects=True, vmem_limit_bytes=DENSE_VMEM_BYTES
         ),
         name="dense_reduce",
-    )(*arrays, own, right, left, pre_grad, tokens, middle_grad, gain[None, :], qkv)
+    )(
+        *arrays[1:],
+        right,
+        left,
+        gain[None, :],
+        *loaded,
+    )
 
 
 def after(value, *others):
@@ -2372,8 +2409,6 @@
         early_dense,
         3,
     )
-    pre_grad = jnp.concatenate([query_grad, kv_grad], axis=1)
-    qkv_local = jnp.einsum("td,tc->dc", hidden_one, pre_grad, preferred_element_type=F32)
     span = shard * expert_count // 16
     wide = LANES * chips * -(-max(span, shard) // (LANES * chips))
     small_local = jnp.stack(
@@ -2390,11 +2425,17 @@
         axis=1,
     )
     *sums, out_sum, input_grad = dense_reduce(
-        [halves(qkv_local), small_local] + ([] if early_dense else [halves(out_local)]),
+        [
+            jax.ShapeDtypeStruct((fsdp, 2, shard // 2, width + 2 * kv_width), BF16),
+            small_local,
+        ]
+        + ([] if early_dense else [halves(out_local)]),
         out_own,
         out_right,
         out_left,
-        pre_grad,
+        query_grad,
+        kv_grad,
+        hidden_one,
         tokens[0],
         middle_grad,
         gain_a,
@@ -2411,13 +2452,13 @@
     qkv_grads = qkv_sum.reshape(shard, -1)
     out_proj_grad = out_proj_sum.reshape(shard, -1)[:, :width]
     up_grad_out, down_grad_out = (
-        after(part, pre_grad)[0].astype(F32) for part in (up_sum, down_sum)
+        after(part, kv_grad)[0].astype(F32) for part in (up_sum, down_sum)
     )
     if direct:
-        gate_local, gate_got = lax.optimization_barrier((gate_local, gate_got, pre_grad))[:2]
+        gate_local, gate_got = lax.optimization_barrier((gate_local, gate_got, kv_grad))[:2]
         gate_grad_out = add(gate_local, *[gate_got[j] for j in range(fsdp - 1)])
     else:
-        gate_grad_out = after(gate_local, pre_grad).astype(F32)
+        gate_grad_out = after(gate_local, kv_grad).astype(F32)
     result = middle + out_sum
     return (
         result.astype(BF16)[None],

time: 600 us -> 588 us (0.980)
  matrix products: 17.3 us -> 10.9 us
  local copies, waits for them, and re-layouts: 20.3 us -> 14.1 us
    dot_general x1 -> x0, matrix products: 8.03 us -> none  [body(): jnp.einsum('td,tc->dc', hidden_one, pre_grad, preferred_element_type=F32)]
    unnamed x69 -> x60, local copies, waits for them, and re-layouts: 16.1 us -> 9.83 us
  transfers between devices with their start and end apart: 4 -> 4, of which waited for: 0 -> 0; matrix products, arithmetic and copies ran while one was open for 7% -> 6% of each run, Pallas kernels for 56% -> 57%
where the time goes in v10:
time: 588 us; the launch traced here: 584 us
  Pallas kernels  519 us (88%)
  other arithmetic  23.9 us (4%)
  between operations  14.5 us (2%)
  local copies, waits for them, and re-layouts  14.1 us (2%)
  matrix products  10.9 us (2%)
    pallas_call x1, Pallas kernels, front(): pl.pallas_call(functools.partial(front_kernel, HEAD_SIZE ** (-0.5), chips...  145 us
    pallas_call x1, Pallas kernels, experts_pass(): pl.pallas_call(functools.partial(experts_kernel, capacity, local_experts,...  120 us
    pallas_call x1, Pallas kernels, attention_back(): pl.pallas_call(functools.partial(attention_back_kernel, HEAD_SIZE ** (-0....  119 us
    pallas_call x1, Pallas kernels, dense_reduce(): pl.pallas_call(functools.partial(dense_reduce_kernel, fsdp, chips, tuple(...  70.5 us
    pallas_call x1, Pallas kernels, gather(): pl.pallas_call(functools.partial(gather_kernel, len(dense), len(line), me...  64.4 us
  transfers between devices with their start and end apart: 4, of which 0 were waited for; matrix products, arithmetic and copies ran while one was open for 6% of the time, Pallas kernels for 57%

profile of v10, /device:TPU:0, one launch (start us, length us, event | category | flops | bytes accessed | tf_op | source)
XLA Modules:
  0.0 584.2 jit_solution(8799111878684091694)
XLA Ops:
  7.2 0.0 all-gather.3.cloned.1.call-start
  7.2 0.8 broadcast_in_dim.35
  8.0 0.8 broadcast_in_dim.36
  8.8 0.8 copy.74
  9.7 0.1 pad.26.clone
  9.7 0.8 maximum_maximum_fusion.refs_3_
  10.5 64.4 %gather.1 = (bf16[1536,2048]{1,0:T(8,128)(2,1)}, bf16[1536,128]{1,0:T(8,128)(2,1)}, bf16[1536,1536]{1,0:T(8,128)(2,1)}, bf16[2,4,384,1536]{3,2,1,0:T(8,128)(2,1)}) custom-call(bf16[384,1536]{1,0:T(8,128)(2,1)} %refs_0_.1, bf16[384,256]{1,0:T(8,128)(2,1)} %refs_1_.1, bf16[384,256]{1,0:T(8,128)(2,1)} %refs_2_.1, bf16[384,128]{1,0:T(8,128)(2,1)} %maximum_maximum_fusion.refs_3_, ...), custom_call_target="tpu_custom_call" | custom-call | tf_op jit(solution)/shard_map/gather/pallas_call | solution.py:447
  75.0 0.0 all-gather.3.cloned.1.call-update
  75.0 0.0 all-gather.5.cloned.1.call-start
  75.0 0.7 all-gather.5.cloned.1.call-update
  75.7 0.0 reduce-scatter.9.cloned.1.call-start
  75.8 0.5 broadcast.69
  76.3 0.7 reduce.13
  77.1 0.2 reduce-window.8
  77.3 0.1 select_reduce_fusion
  77.5 0.1 copy.81.pq_ref
  77.6 0.2 copy.80.oq_ref
  77.8 0.5 convert_reduce_fusion
  78.4 0.1 copy.79
  78.6 0.8 fusion.10
  79.3 0.2 pad_maximum_fusion
  79.5 0.3 fusion.3.table_ref
  79.8 144.8 %front.1 = (f32[2,4,16,384]{3,2,1,0:T(8,128)S(1)}, f32[12,1,384]{2,1,0:T(1,128)S(1)}, f32[384,128]{1,0:T(8,128)S(1)}, f32[2,4,16,384]{3,2,1,0:T(8,128)S(1)}, bf1...) custom-call(bf16[384,1536]{1,0:T(8,128)(2,1)} %bitcast.58, ...), custom_call_target="tpu_custom_call", output_to_operand_aliasing={{12}: (14, {})} | custom-call | flops 11475615744 | bytes 40000000 | tf_op jit(solution)/shard_map/front/pallas_call | solution.py:1332
  224.7 1.0 copy-done.6
  225.7 0.7 copy-done.7
  226.3 0.7 copy-done.8
  227.0 0.6 copy-done.9
  227.6 120.5 %experts.1 = (bf16[384,1664]{1,0:T(8,128)(2,1)}, bf16[2,4,384,1536]{3,2,1,0:T(8,128)(2,1)}, bf16[2,384,768]{2,1,0:T(8,128)(2,1)}, bf16[3,2,384,768]{3,2,1,0:T(8,...) custom-call(bf16[2,4,384,1536]{3,2,1,0:T(8,128)(2,1)} %get-tuple-ele, ...), custom_call_target="tpu_custom_call", output_to_operand_aliasing={{1}: (0, {})} | custom-call | flops 48318382080 | bytes 100000000 | tf_op jit(solution)/shard_map/experts/pallas_call | solution.py:2168
  348.1 0.0 reduce-scatter.9.cloned.1.call-update
  348.1 0.0 reduce-scatter.7.cloned.1.call-start
  348.2 0.5 reduce-scatter.7.cloned.1.call-update
  348.7 0.6 broadcast_in_dim_reshape.3.ok_ref
  349.3 0.5 copy-done.10
  349.9 0.2 multiply_reduce_fusion.2
  350.1 0.6 reshape_subtract_fusion.pq_ref
  350.7 0.1 copy-done.16
  350.8 0.2 convert_element_type.171
  350.9 0.2 multiply_reduce_fusion.3
  351.2 0.2 multiply_convert_fusion
  351.4 0.9 multiply_reduce_fusion
  352.3 0.4 copy-done.13
  352.7 0.6 fusion.refs_9_
  353.3 0.7 copy-done.25
  353.9 4.6 convolution_convert_fusion
  358.6 3.0 convolution_convert_fusion.1.do_ref
  361.6 119.3 %attention_back.1 = (bf16[384,1536]{1,0:T(8,128)(2,1)}, bf16[384,512]{1,0:T(8,128)(2,1)}, bf16[384,1536]{1,0:T(8,128)(2,1)}, bf16[384,1536]{1,0:T(8,128)(2,1)}, ...) custom-call(bf16[384,1536]{1,0:T(8,128)(2,1)} %copy-done.6, bf16[3072,512]{1,0:T(8,128)(2,1)} %bitcast.71, ...), custom_call_target="tpu_custom_call" | custom-call | flops 18119393280 | bytes 12189696 | tf_op jit(solution)/shard_map/attention_back/pallas_call | solution.py:1673
  481.0 2.0 convolution_convert_fusion.2
  483.0 1.0 copy.82
  484.0 0.3 reshape.188
  484.4 1.0 copy-done.3
  485.4 70.5 %dense_reduce.1 = (bf16[2,192,2048]{2,1,0:T(8,128)(2,1)}, bf16[2,16,512]{2,1,0:T(8,128)(2,1)}, f32[384,1536]{1,0:T(8,128)}, bf16[384,1536]{1,0:T(8,128)(2,1)S(1)}) custom-call(bf16[4,2,16,512]{3,2,1,0:T(8,128)(2,1)S(1)} %pad_maximum_fusion.2.refs_0_, bf16[384,1536]{1,0:T(8,128)(2,1)S(1)} %copy-done.1, bf16[384,1536]{1,0:T(8,128)(2,1)S(1)} %copy-done.2, ...), custom_call_target="tpu_custom_call" | custom-call | tf_op jit(solution)/shard_map/dense_reduce/pallas_call | solution.py:945
  555.9 0.8 slice_convert_fusion.3
  556.7 0.1 reshape.198
  556.8 0.7 copy.84
  557.5 1.4 convert_reduce_fusion.3
  558.9 2.0 slice_convert_fusion.1
  560.9 4.0 convert_add_fusion
  564.9 1.7 slice_convert_fusion
  566.6 1.8 bitcast_convert_fusion.2
  568.4 1.1 copy-done.11
  569.4 1.3 fusion.1
  570.7 2.8 bitcast_convert_fusion
  573.6 2.8 bitcast_convert_fusion.1
  576.4 1.0 copy.88
  (72 shorter events, 0.4 us)
Async XLA Ops:
  7.2 220.4 %all-gather.3.cloned.1.call-start = ((), (), s32[]{:S(2)}) async-start(), calls=%async_computation.2 | async-start | bytes 5898240 | tf_op jit(solution)/shard_map/all_gather | solution.py:2278
  10.5 65.8 %copy-start.22 = (s32[1,3072]{1,0:T(1,128)S(1)}, s32[1,3072]{1,0:T(1,128)}, u32[]{:S(2)}) copy-start(s32[1,3072]{1,0:T(1,128)} %param.17) | copy-start | bytes 36868
  10.5 66.6 %copy-start.24 = (s32[1,3]{1,0:T(1,128)S(1)}, s32[1,3]{1,0:T(1,128)}, u32[]{:S(2)}) copy-start(s32[1,3]{1,0:T(1,128)} %param.18) | copy-start | bytes 40
  74.9 2.8 copy-start
  74.9 3.4 copy-start.23
  75.0 152.6 %all-gather.5.cloned.1.call-start = ((), (), s32[]{:S(2)}) async-start(), calls=%async_computation.3 | async-start | bytes 5898240 | tf_op jit(solution)/shard_map/all_gather | solution.py:2279
  75.7 495.0 %reduce-scatter.9.cloned.1.call-start = ((), (), s32[]{:S(2)}) async-start(), calls=%async_computation.5 | async-start | bytes 5898240
  77.3 272.8 %copy-start.21 = (s32[1,384]{1,0:T(1,128)}, s32[1,384]{1,0:T(1,128)S(1)}, u32[]{:S(2)}) copy-start(s32[1,384]{1,0:T(1,128)S(1)} %get-tuple-element.159.oq_ref) | copy-start | bytes 4612
  79.5 145.1 %copy-start.4 = (f32[384,128]{1,0:T(8,128)}, f32[384,128]{1,0:T(8,128)S(1)}, u32[]{:S(2)}) copy-start(f32[384,128]{1,0:T(8,128)S(1)} %get-tuple-element.166.cos_ref) | copy-start | bytes 589828
  79.5 145.1 %copy-start.5 = (f32[384,128]{1,0:T(8,128)}, f32[384,128]{1,0:T(8,128)S(1)}, u32[]{:S(2)}) copy-start(f32[384,128]{1,0:T(8,128)S(1)} %get-tuple-element.167.sin_ref) | copy-start | bytes 589828
  224.6 1.0 copy-start.6
  225.7 0.7 copy-start.7
  226.3 0.7 copy-start.8
  227.0 0.6 copy-start.9
  348.1 225.4 %reduce-scatter.7.cloned.1.call-start = ((), (), s32[]{:S(2)}) async-start(), calls=%async_computation.4 | async-start | bytes 5898240
  348.2 1.7 copy-start.10
  349.3 1.4 copy-start.16
  351.4 0.9 copy-start.20
  351.4 1.3 copy-start.13
  352.7 1.3 copy-start.25
  352.7 5.9 %slice-start = ((s8[4718592]{0:T(1024)(128)(4,1)}), s8[4194304]{0:T(1024)(128)(4,1)S(1)}, s32[]{:S(2)}) async-start(s8[4718592]{0:T(1024)(128)(4,1)} %bitcast.64), calls=%async_computation.6 | async-start | bytes 8388608
  353.3 5.3 copy-start.12
  353.9 4.6 slice-start.1
  361.6 119.4 %copy-start.19 = (bf16[384,1536]{1,0:T(8,128)(2,1)S(1)}, bf16[384,1536]{1,0:T(8,128)(2,1)}, u32[]{:S(2)}) copy-start(bf16[384,1536]{1,0:T(8,128)(2,1)} %get-tuple-element.58) | copy-start | bytes 3538948
  481.0 3.4 copy-start.1
  481.0 3.4 copy-start.2
  484.4 1.0 copy-start.3
  555.9 5.0 copy-start.17
  560.9 4.0 copy-start.15
  564.9 1.7 copy-start.18
  564.9 3.5 copy-start.14
  566.6 2.9 copy-start.11
Sparse Core Ops, SparseCore 0:
  75.1 85.8 all-gather.2
  162.8 55.8 all-gather.4
  348.3 78.0 reduce-scatter.8
  429.2 55.1 reduce-scatter.6

commit v11 on v10

--- a/solution.py
+++ b/solution.py
@@ -1214,7 +1214,7 @@
                 kv_line.receive(k - 1)
                 if k < chips - 1:
                     kv_line.send(k)
-                else:
+                if k == chips - 2:
                     grad_line.send(chips - 2)
 
         r = chunk_order(chip, chips - 1 - t, chips)
@@ -1487,7 +1487,8 @@
             for j, owner in enumerate(dense.owners)
         ]
         stages = dense.stages()
-        at_head = {QUERY_HEADS - 1 - len(stages) // 2 + k: k for k in range(len(stages) // 2)}
+        ahead = len(stages) // 2 + 1
+        at_head = {QUERY_HEADS - 1 - ahead + k: k for k in range(ahead)}
 
     def kv_swap(group, r):
         return remote(
@@ -1613,7 +1614,7 @@
             store(2, chips - 1, left_ref),
         ):
             copy.start()
-        rest = stages[len(stages) // 2 :] if early_dense else []
+        rest = stages[ahead:] if early_dense else []
         for group in range(KVH):
             one = kv_line(group)
             for s in range(chips - 1):
@@ -2104,13 +2105,29 @@
             ).astype(BF16)
             tile_copy(e, j).start()
 
+    def held_rows(k):
+        return pl.ds(k * total_rows, total_rows)
+
+    later = [
+        pltpu.make_async_copy(db_ref.at[k], up_v.at[held_rows(k)], save_sem.at[1 + local_experts + k])
+        for k in range(local_experts)
+    ]
+
     def fetch_x(e):
         copies = [(x_ref.at[e], down_v.at[:total_rows])]
         if e == 0:
-            for k in range(local_experts):
-                held = pl.ds(k * total_rows, total_rows)
-                copies += [(da_ref.at[k], gate_v.at[held]), (db_ref.at[k], up_v.at[held])]
-        return lambda: fetch(copies)
+            copies += [(da_ref.at[k], gate_v.at[held_rows(k)]) for k in range(local_experts)]
+
+        def run():
+            if e == 0:
+                for copy in later:
+                    copy.start()
+            fetch(copies)
+            if e == 1:
+                for copy in later:
+                    copy.wait()
+
+        return run
 
     def stage_up(slot, p):
         return out_v.at[slot, pl.ds(p * shard, shard), pl.ds(0, units)]

time: 588 us -> 587 us (level)
  no operation moved by 1% of the time
where the time goes in v11:
time: 587 us; the launch traced here: 583 us
  Pallas kernels  519 us (88%)
  other arithmetic  23.9 us (4%)
  between operations  14.5 us (2%)
  local copies, waits for them, and re-layouts  14.1 us (2%)
  matrix products  10.9 us (2%)
    pallas_call x1, Pallas kernels, front(): pl.pallas_call(functools.partial(front_kernel, HEAD_SIZE ** (-0.5), chips...  145 us
    pallas_call x1, Pallas kernels, experts_pass(): pl.pallas_call(functools.partial(experts_kernel, capacity, local_experts,...  120 us
    pallas_call x1, Pallas kernels, attention_back(): pl.pallas_call(functools.partial(attention_back_kernel, HEAD_SIZE ** (-0....  119 us
    pallas_call x1, Pallas kernels, dense_reduce(): pl.pallas_call(functools.partial(dense_reduce_kernel, fsdp, chips, tuple(...  69.6 us
    pallas_call x1, Pallas kernels, gather(): pl.pallas_call(functools.partial(gather_kernel, len(dense), len(line), me...  64.4 us
  transfers between devices with their start and end apart: 4, of which 0 were waited for; matrix products, arithmetic and copies ran while one was open for 6% of the time, Pallas kernels for 57%

profile of v11, /device:TPU:0, one launch (start us, length us, event | category | flops | bytes accessed | tf_op | source)
XLA Modules:
  0.0 583.3 jit_solution(14090493965201290771)
XLA Ops:
  7.2 0.0 all-gather.3.cloned.1.call-start
  7.2 0.8 broadcast_in_dim.35
  8.0 0.8 broadcast_in_dim.36
  8.8 0.8 copy.74
  9.7 0.1 pad.26.clone
  9.7 0.8 maximum_maximum_fusion.refs_3_
  10.5 64.4 %gather.1 = (bf16[1536,2048]{1,0:T(8,128)(2,1)}, bf16[1536,128]{1,0:T(8,128)(2,1)}, bf16[1536,1536]{1,0:T(8,128)(2,1)}, bf16[2,4,384,1536]{3,2,1,0:T(8,128)(2,1)}) custom-call(bf16[384,1536]{1,0:T(8,128)(2,1)} %refs_0_.1, bf16[384,256]{1,0:T(8,128)(2,1)} %refs_1_.1, bf16[384,256]{1,0:T(8,128)(2,1)} %refs_2_.1, bf16[384,128]{1,0:T(8,128)(2,1)} %maximum_maximum_fusion.refs_3_, ...), custom_call_target="tpu_custom_call" | custom-call | tf_op jit(solution)/shard_map/gather/pallas_call | solution.py:447
  75.0 0.0 all-gather.3.cloned.1.call-update
  75.0 0.0 all-gather.5.cloned.1.call-start
  75.0 0.7 all-gather.5.cloned.1.call-update
  75.7 0.0 reduce-scatter.9.cloned.1.call-start
  75.8 0.5 broadcast.69
  76.3 0.7 reduce.13
  77.1 0.2 reduce-window.8
  77.3 0.1 select_reduce_fusion
  77.5 0.1 copy.81.pq_ref
  77.6 0.2 copy.80.oq_ref
  77.8 0.5 convert_reduce_fusion
  78.4 0.1 copy.79
  78.6 0.8 fusion.10
  79.3 0.2 pad_maximum_fusion
  79.5 0.3 fusion.3.table_ref
  79.8 144.8 %front.1 = (f32[2,4,16,384]{3,2,1,0:T(8,128)S(1)}, f32[12,1,384]{2,1,0:T(1,128)S(1)}, f32[384,128]{1,0:T(8,128)S(1)}, f32[2,4,16,384]{3,2,1,0:T(8,128)S(1)}, bf1...) custom-call(bf16[384,1536]{1,0:T(8,128)(2,1)} %bitcast.58, ...), custom_call_target="tpu_custom_call", output_to_operand_aliasing={{12}: (14, {})} | custom-call | flops 11475615744 | bytes 40000000 | tf_op jit(solution)/shard_map/front/pallas_call | solution.py:1332
  224.7 1.0 copy-done.6
  225.7 0.7 copy-done.7
  226.3 0.7 copy-done.8
  227.0 0.6 copy-done.9
  227.6 120.5 %experts.1 = (bf16[384,1664]{1,0:T(8,128)(2,1)}, bf16[2,4,384,1536]{3,2,1,0:T(8,128)(2,1)}, bf16[2,384,768]{2,1,0:T(8,128)(2,1)}, bf16[3,2,384,768]{3,2,1,0:T(8,...) custom-call(bf16[2,4,384,1536]{3,2,1,0:T(8,128)(2,1)} %get-tuple-ele, ...), custom_call_target="tpu_custom_call", output_to_operand_aliasing={{1}: (0, {})} | custom-call | flops 48318382080 | bytes 100000000 | tf_op jit(solution)/shard_map/experts/pallas_call | solution.py:2185
  348.1 0.0 reduce-scatter.9.cloned.1.call-update
  348.1 0.0 reduce-scatter.7.cloned.1.call-start
  348.2 0.5 reduce-scatter.7.cloned.1.call-update
  348.7 0.6 broadcast_in_dim_reshape.3.ok_ref
  349.3 0.5 copy-done.10
  349.8 0.2 multiply_reduce_fusion.2
  350.1 0.6 reshape_subtract_fusion.pq_ref
  350.6 0.1 copy-done.16
  350.8 0.2 convert_element_type.171
  350.9 0.2 multiply_reduce_fusion.3
  351.1 0.2 multiply_convert_fusion
  351.4 0.9 multiply_reduce_fusion
  352.3 0.4 copy-done.13
  352.7 0.6 fusion.refs_9_
  353.3 0.7 copy-done.25
  353.9 4.6 convolution_convert_fusion
  358.6 3.1 convolution_convert_fusion.1.do_ref
  361.6 119.2 %attention_back.1 = (bf16[384,1536]{1,0:T(8,128)(2,1)}, bf16[384,512]{1,0:T(8,128)(2,1)}, bf16[384,1536]{1,0:T(8,128)(2,1)}, bf16[384,1536]{1,0:T(8,128)(2,1)}, ...) custom-call(bf16[384,1536]{1,0:T(8,128)(2,1)} %copy-done.6, bf16[3072,512]{1,0:T(8,128)(2,1)} %bitcast.71, ...), custom_call_target="tpu_custom_call" | custom-call | flops 18119393280 | bytes 12189696 | tf_op jit(solution)/shard_map/attention_back/pallas_call | solution.py:1674
  480.9 2.0 convolution_convert_fusion.2
  482.9 1.0 copy.82
  483.9 0.3 reshape.188
  484.3 1.0 copy-done.3
  485.3 69.6 %dense_reduce.1 = (bf16[2,192,2048]{2,1,0:T(8,128)(2,1)}, bf16[2,16,512]{2,1,0:T(8,128)(2,1)}, f32[384,1536]{1,0:T(8,128)}, bf16[384,1536]{1,0:T(8,128)(2,1)S(1)}) custom-call(bf16[4,2,16,512]{3,2,1,0:T(8,128)(2,1)S(1)} %pad_maximum_fusion.2.refs_0_, bf16[384,1536]{1,0:T(8,128)(2,1)S(1)} %copy-done.1, bf16[384,1536]{1,0:T(8,128)(2,1)S(1)} %copy-done.2, ...), custom_call_target="tpu_custom_call" | custom-call | tf_op jit(solution)/shard_map/dense_reduce/pallas_call | solution.py:945
  554.9 0.8 slice_convert_fusion.3
  555.7 0.1 reshape.198
  555.8 0.7 copy.84
  556.6 1.4 convert_reduce_fusion.3
  557.9 2.0 slice_convert_fusion.1
  559.9 4.0 convert_add_fusion
  563.9 1.7 slice_convert_fusion
  565.6 1.8 bitcast_convert_fusion.2
  567.4 1.1 copy-done.11
  568.5 1.3 fusion.1
  569.8 2.8 bitcast_convert_fusion
  572.6 2.8 bitcast_convert_fusion.1
  575.5 1.0 copy.88
  (72 shorter events, 0.4 us)
Async XLA Ops:
  7.2 220.4 %all-gather.3.cloned.1.call-start = ((), (), s32[]{:S(2)}) async-start(), calls=%async_computation.2 | async-start | bytes 5898240 | tf_op jit(solution)/shard_map/all_gather | solution.py:2295
  10.5 65.8 %copy-start.22 = (s32[1,3072]{1,0:T(1,128)S(1)}, s32[1,3072]{1,0:T(1,128)}, u32[]{:S(2)}) copy-start(s32[1,3072]{1,0:T(1,128)} %param.17) | copy-start | bytes 36868
  10.5 66.6 %copy-start.24 = (s32[1,3]{1,0:T(1,128)S(1)}, s32[1,3]{1,0:T(1,128)}, u32[]{:S(2)}) copy-start(s32[1,3]{1,0:T(1,128)} %param.18) | copy-start | bytes 40
  74.9 2.8 copy-start
  74.9 3.4 copy-start.23
  75.0 152.6 %all-gather.5.cloned.1.call-start = ((), (), s32[]{:S(2)}) async-start(), calls=%async_computation.3 | async-start | bytes 5898240 | tf_op jit(solution)/shard_map/all_gather | solution.py:2296
  75.7 494.0 %reduce-scatter.9.cloned.1.call-start = ((), (), s32[]{:S(2)}) async-start(), calls=%async_computation.5 | async-start | bytes 5898240
  77.3 272.7 %copy-start.21 = (s32[1,384]{1,0:T(1,128)}, s32[1,384]{1,0:T(1,128)S(1)}, u32[]{:S(2)}) copy-start(s32[1,384]{1,0:T(1,128)S(1)} %get-tuple-element.159.oq_ref) | copy-start | bytes 4612
  79.5 145.1 %copy-start.4 = (f32[384,128]{1,0:T(8,128)}, f32[384,128]{1,0:T(8,128)S(1)}, u32[]{:S(2)}) copy-start(f32[384,128]{1,0:T(8,128)S(1)} %get-tuple-element.166.cos_ref) | copy-start | bytes 589828
  79.5 145.1 %copy-start.5 = (f32[384,128]{1,0:T(8,128)}, f32[384,128]{1,0:T(8,128)S(1)}, u32[]{:S(2)}) copy-start(f32[384,128]{1,0:T(8,128)S(1)} %get-tuple-element.167.sin_ref) | copy-start | bytes 589828
  224.6 1.0 copy-start.6
  225.7 0.7 copy-start.7
  226.3 0.7 copy-start.8
  227.0 0.6 copy-start.9
  348.1 224.5 %reduce-scatter.7.cloned.1.call-start = ((), (), s32[]{:S(2)}) async-start(), calls=%async_computation.4 | async-start | bytes 5898240
  348.2 1.7 copy-start.10
  349.3 1.4 copy-start.16
  351.3 0.9 copy-start.20
  351.3 1.3 copy-start.13
  352.7 1.3 copy-start.25
  352.7 5.9 %slice-start = ((s8[4718592]{0:T(1024)(128)(4,1)}), s8[4194304]{0:T(1024)(128)(4,1)S(1)}, s32[]{:S(2)}) async-start(s8[4718592]{0:T(1024)(128)(4,1)} %bitcast.64), calls=%async_computation.6 | async-start | bytes 8388608
  353.3 5.3 copy-start.12
  353.9 4.6 slice-start.1
  361.6 119.3 %copy-start.19 = (bf16[384,1536]{1,0:T(8,128)(2,1)S(1)}, bf16[384,1536]{1,0:T(8,128)(2,1)}, u32[]{:S(2)}) copy-start(bf16[384,1536]{1,0:T(8,128)(2,1)} %get-tuple-element.58) | copy-start | bytes 3538948
  480.9 3.4 copy-start.1
  480.9 3.4 copy-start.2
  484.3 1.0 copy-start.3
  554.9 5.0 copy-start.17
  559.9 4.0 copy-start.15
  563.9 1.7 copy-start.18
  563.9 3.5 copy-start.14
  565.6 2.9 copy-start.11
Sparse Core Ops, SparseCore 0:
  75.1 85.8 all-gather.2
  162.8 55.8 all-gather.4
  348.2 78.0 reduce-scatter.8
  429.2 55.1 reduce-scatter.6
